TPU v7x, 1024 devices: a whole 4x4x32 slice. The times are simulated.
1024 devices in a mesh: dp: 32 (over z_hi, y, core), mp: 32 (over x, z_lo).
Axes of the slice: x: 4, y: 4, z: 32 (z_hi: 4, z_lo: 8; z = z_hi * 8 + z_lo), core: 2. Of those that a mesh axis runs over, the one named last changes fastest.
Arguments:
- layer_input: bfloat16 [6144, 3072], P(('dp', 'mp')), may hold values from -24 to 24
- out_grad: bfloat16 [6144, 3072], P(('dp', 'mp')), may hold values from -24 to 24
- norm_gain_vector: float32 [3072], replicated, may hold values from 0.5 to 1.5
- up_weight: bfloat16 [3072, 12288], P(None, 'mp'), may hold values from -0.109375 to 0.109375
- down_weight: bfloat16 [12288, 3072], P('mp'), may hold values from -0.0546875 to 0.0546875
Outputs:
- input_grad: bfloat16 [6144, 3072], P(('dp', 'mp'))
- up_grad: float32 [3072, 12288], P('dp', 'mp')
- down_grad: float32 [12288, 3072], P('mp', 'dp')
All inputs are finite; a program needn't handle non-finite values.
Results may differ from a plain program's by a relative error of at most 0.02.
Values may be sent and summed in bfloat16 or wider, within the bound.
No kernel may reach another device: no remote copies, remote signals or barrier semaphores. Data moves between devices by JAX's collectives and lax.ppermute only.
A program may use at most 32 MiB of HBM per device.

v0:
```python
import math

import jax
import jax.numpy as jnp
from jax import lax
from jax.sharding import PartitionSpec as P


def gelu_value(v):
    return 0.5 * v * (1.0 + jax.scipy.special.erf(v / math.sqrt(2.0)))


def gelu_slope(v):
    return 0.5 * (1.0 + jax.scipy.special.erf(v / math.sqrt(2.0))) + v * jnp.exp(
        -0.5 * v * v
    ) / math.sqrt(2.0 * math.pi)


def shards(layer_input, out_grad, norm_gain_vector, up_weight, down_weight):
    xf = layer_input.astype(jnp.float32)
    mean_val = jnp.mean(xf, axis=1, keepdims=True)
    centered_input = xf - mean_val
    inverse_deviation = 1.0 / jnp.sqrt(
        jnp.mean(centered_input * centered_input, axis=1, keepdims=True) + 1e-06
    )
    standardized_input = centered_input * inverse_deviation
    normalized_input = (standardized_input * norm_gain_vector).astype(jnp.bfloat16)
    normed_all, grad_all = (
        lax.all_gather(normalized_input, "mp", axis=0, tiled=True),
        lax.all_gather(out_grad, "mp", axis=0, tiled=True),
    )
    pre = jnp.dot(normed_all, up_weight, preferred_element_type=jnp.float32)
    hidden = gelu_value(pre).astype(jnp.bfloat16)
    down_term = jnp.einsum("tf,td->fd", hidden, grad_all, preferred_element_type=jnp.float32)
    hidden_grad = jnp.einsum("td,fd->tf", grad_all, down_weight, preferred_element_type=jnp.float32)
    pre_grad = (hidden_grad * gelu_slope(pre)).astype(jnp.bfloat16)
    up_term = jnp.einsum("td,tf->df", normed_all, pre_grad, preferred_element_type=jnp.float32)
    full_term = jnp.einsum("tf,df->td", pre_grad, up_weight, preferred_element_type=jnp.float32)
    normed_grad = lax.psum_scatter(
        full_term.astype(jnp.bfloat16), "mp", scatter_dimension=0, tiled=True
    ).astype(jnp.float32)
    up_grad, down_grad = (
        lax.psum_scatter(
            up_term.astype(jnp.bfloat16), "dp", scatter_dimension=0, tiled=True
        ).astype(jnp.float32),
        lax.psum_scatter(
            down_term.astype(jnp.bfloat16), "dp", scatter_dimension=1, tiled=True
        ).astype(jnp.float32),
    )
    scaled_input = normed_grad * norm_gain_vector
    backward_pass = inverse_deviation * (
        scaled_input
        - jnp.mean(scaled_input, axis=1, keepdims=True)
        - standardized_input * jnp.mean(scaled_input * standardized_input, axis=1, keepdims=True)
    )
    input_grad = (out_grad.astype(jnp.float32) + backward_pass).astype(jnp.bfloat16)
    return (input_grad, up_grad, down_grad)


def solution(mesh):
    return jax.shard_map(
        shards,
        mesh=mesh,
        in_specs=(P(("dp", "mp"), None), P(("dp", "mp"), None), P(), P(None, "mp"), P("mp", None)),
        out_specs=(P(("dp", "mp"), None), P("dp", "mp"), P("mp", "dp")),
        check_vma=False,
    )
```

profile of v0, /device:TPU:6, one launch (start us, length us, event | category | flops | bytes accessed | tf_op | source)
XLA Modules:
  0.0 883.9 jit_solution(2447666210779875753)
XLA Ops:
  7.2 1.1 convert_reduce_fusion
  8.3 1.0 fusion.18
  9.9 1.5 fusion.20
  12.2 224.2 %all-gather.7.cloned.1.call-done = bf16[32,6,3072]{2,1,0:T(8,128)(2,1)} async-done(((bf16[1,6,3072]{2,1,0:T(8,128)(2,1)}), bf16[32,6,3072]{2,1,0:T(8,128)(2,1)}) %all-gather.7.cloned.1.call-update) | async-done | bytes 1179664 | tf_op jit(solution)/shard_map/all_gather | solution.py:29
  236.4 1.6 reshape.31
  238.0 1.5 fusion.22
  239.4 233.2 %all-gather.5.cloned.1.call-done = bf16[32,6,3072]{2,1,0:T(8,128)(2,1)} async-done(((bf16[1,6,3072]{2,1,0:T(8,128)(2,1)}), bf16[32,6,3072]{2,1,0:T(8,128)(2,1)}) %all-gather.5.cloned.1.call-update) | async-done | bytes 1179664 | tf_op jit(solution)/shard_map/all_gather | solution.py:30
  472.6 2.4 reshape.29
  475.0 3.9 convolution_convert_fusion
  479.0 3.0 fusion.1
  482.6 2.4 convolution_convert_fusion.1
  485.1 1.9 convolution_convert_fusion.2
  487.0 148.0 %fusion = bf16[8,3072]{1,0:T(8,128)(2,1)} fusion(bf16[192,3072]{1,0:T(8,128)(2,1)S(1)} %convolution_convert_fusion.2), kind=kCustom, calls=%all-reduce-scatter | all-reduce-scatter fusion | flops 786433 | bytes 1232896
  635.0 31.7 %collective-permute-start.6 = (bf16[8,3072]{1,0:T(8,128)(2,1)}, bf16[8,3072]{1,0:T(8,128)(2,1)S(1)}, u32[]{:S(2)}, u32[]{:S(2)}) collective-permute-start(bf16[8,3072]{1,0:T(8,128)(2,1)} %fusion), channel_id=1, source_target_pairs={{0,7},{1,8},{2,9},{3,10},{4,11},{5,12},{6,13},{7,14},{8,15},{9,16}... | collective-permute-start | bytes 147464
  666.7 1.9 collective-permute-start.5
  669.4 1.3 collective-permute-start.7
  670.7 1.9 collective-permute-start.4
  672.6 1.9 collective-permute-start.3
  674.6 0.8 collective-permute-done.7
  675.4 1.9 collective-permute-start.2
  677.3 4.3 collective-permute-start.1
  681.6 1.9 collective-permute-start
  683.5 1.3 dynamic-slice.4
  685.5 3.9 collective-permute-done.3
  689.4 0.9 collective-permute-done.1
  690.3 5.0 collective-permute-done
  695.3 2.1 concatenate
  697.5 1.1 fusion.19
  698.5 1.5 fusion.17
  700.1 1.6 convert_element_type.47
  701.6 174.2 %reduce-scatter.5.cloned.1.call-done = bf16[96,384]{1,0:T(8,128)(2,1)} async-done(((bf16[3072,384]{1,0:T(8,128)(2,1)}), bf16[96,384]{1,0:T(8,128)(2,1)}) %reduce-scatter.5.cloned.1.call-update) | async-done | bytes 73744 | tf_op jit(solution)/shard_map/reduce_scatter | solution.py:43
  875.8 1.6 convert_element_type.44
  (25 shorter events, 2.9 us)
Async XLA Ops:
  7.2 230.8 %copy-start = (bf16[3072,384]{1,0:T(8,128)(2,1)S(1)}, bf16[3072,384]{1,0:T(8,128)(2,1)}, u32[]{:S(2)}) copy-start(bf16[3072,384]{1,0:T(8,128)(2,1)} %param.8) | copy-start | bytes 7077892
  7.2 229.2 %all-gather.7.cloned.1.call-start = ((), (), s32[]{:S(2)}) async-start(), calls=%async_computation.5 | async-start | bytes 1622016 | tf_op jit(solution)/shard_map/all_gather | solution.py:29
  9.3 0.5 copy-start.3
  11.4 461.2 %all-gather.5.cloned.1.call-start = ((), (), s32[]{:S(2)}) async-start(), calls=%async_computation.4 | async-start | bytes 1622016 | tf_op jit(solution)/shard_map/all_gather | solution.py:30
  12.1 687.9 %reduce-scatter.7.cloned.1.call-start = ((), (), s32[]{:S(2)}) async-start(), calls=%async_computation.3 | async-start | bytes 2433024 | tf_op jit(solution)/shard_map/reduce_scatter | solution.py:46
  478.9 396.9 %reduce-scatter.5.cloned.1.call-start = ((), (), s32[]{:S(2)}) async-start(), calls=%async_computation.2 | async-start | bytes 2433024 | tf_op jit(solution)/shard_map/reduce_scatter | solution.py:43
  481.9 0.7 copy-start.1
  487.0 210.5 %copy-start.2 = (f32[3072]{0:T(1024)S(1)}, f32[3072]{0:T(1024)}, u32[]{:S(2)}) copy-start(f32[3072]{0:T(1024)} %param.7) | copy-start | bytes 36868
  635.0 42.3 %collective-permute-start.6 = (bf16[8,3072]{1,0:T(8,128)(2,1)}, bf16[8,3072]{1,0:T(8,128)(2,1)S(1)}, u32[]{:S(2)}, u32[]{:S(2)}) collective-permute-start(bf16[8,3072]{1,0:T(8,128)(2,1)} %fusion), channel_id=1, source_target_pairs={{0,7},{1,8},{2,9},{3,10},{4,11},{5,12},{6,13},{7,14},{8,15},{9,16}... | collective-permute-start | bytes 147464
  666.7 14.9 %collective-permute-start.5 = (bf16[8,3072]{1,0:T(8,128)(2,1)}, bf16[8,3072]{1,0:T(8,128)(2,1)S(1)}, u32[]{:S(2)}, u32[]{:S(2)}) collective-permute-start(bf16[8,3072]{1,0:T(8,128)(2,1)} %fusion), channel_id=1, source_target_pairs={{0,6},{1,7},{2,8},{3,9},{4,10},{5,11},{6,12},{7,13},{8,14},{9,15},... | collective-permute-start | bytes 147464
  669.4 6.0 collective-permute-start.7
  670.7 14.8 %collective-permute-start.4 = (bf16[8,3072]{1,0:T(8,128)(2,1)}, bf16[8,3072]{1,0:T(8,128)(2,1)S(1)}, u32[]{:S(2)}, u32[]{:S(2)}) collective-permute-start(bf16[8,3072]{1,0:T(8,128)(2,1)} %fusion), channel_id=1, source_target_pairs={{0,5},{1,6},{2,7},{3,8},{4,9},{5,10},{6,11},{7,12},{8,13},{9,14},{... | collective-permute-start | bytes 147464
  672.6 16.7 %collective-permute-start.3 = (bf16[8,3072]{1,0:T(8,128)(2,1)}, bf16[8,3072]{1,0:T(8,128)(2,1)S(1)}, u32[]{:S(2)}, u32[]{:S(2)}) collective-permute-start(bf16[8,3072]{1,0:T(8,128)(2,1)} %fusion), channel_id=1, source_target_pairs={{0,4},{1,5},{2,6},{3,7},{4,8},{5,9},{6,10},{7,11},{8,12},{9,13},{1... | collective-permute-start | bytes 147464
  675.4 14.0 %collective-permute-start.2 = (bf16[8,3072]{1,0:T(8,128)(2,1)}, bf16[8,3072]{1,0:T(8,128)(2,1)S(1)}, u32[]{:S(2)}, u32[]{:S(2)}) collective-permute-start(bf16[8,3072]{1,0:T(8,128)(2,1)} %fusion), channel_id=1, source_target_pairs={{0,3},{1,4},{2,5},{3,6},{4,7},{5,8},{6,9},{7,10},{8,11},{9,12},{10... | collective-permute-start | bytes 147464
  677.3 13.0 %collective-permute-start.1 = (bf16[8,3072]{1,0:T(8,128)(2,1)}, bf16[8,3072]{1,0:T(8,128)(2,1)S(1)}, u32[]{:S(2)}, u32[]{:S(2)}) collective-permute-start(bf16[8,3072]{1,0:T(8,128)(2,1)} %fusion), channel_id=1, source_target_pairs={{0,2},{1,3},{2,4},{3,5},{4,6},{5,7},{6,8},{7,9},{8,10},{9,11},{10,... | collective-permute-start | bytes 147464
  681.6 13.7 %collective-permute-start = (bf16[8,3072]{1,0:T(8,128)(2,1)}, bf16[8,3072]{1,0:T(8,128)(2,1)S(1)}, u32[]{:S(2)}, u32[]{:S(2)}) collective-permute-start(bf16[8,3072]{1,0:T(8,128)(2,1)} %fusion), channel_id=1, source_target_pairs={{0,1},{1,2},{2,3},{3,4},{4,5},{5,6},{6,7},{7,8},{8,9},{9,10},{10,1... | collective-permute-start | bytes 147464
Sparse Core Ops, SparseCore 0:
  11.5 224.8 all-gather.6
  239.0 233.5 all-gather.4
  479.0 210.9 reduce-scatter.6
  696.4 179.3 reduce-scatter.4
where the time goes:
time: 885 us; the launch traced here: 884 us
  waiting for transfers between devices  643 us (73%)
  blocking collectives  148 us (17%)
  starting transfers between devices  47 us (5%)
  between operations  14.6 us (2%)
  matrix products  12.7 us (1%)
  local copies, waits for them, and re-layouts  9.38 us (1%)
  other arithmetic  9.33 us (1%)
    all_gather x1, waiting for transfers between devices, shards(): lax.all_gather(out_grad, 'mp', axis=0, tiled=True)  233 us
    all_gather x1, waiting for transfers between devices, shards(): lax.all_gather(normalized_input, 'mp', axis=0, tiled=True)  224 us
    reduce_scatter x1, waiting for transfers between devices, shards(): lax.psum_scatter(up_term.astype(jnp.bfloat16), 'dp', scatter_dimension=0,...  174 us
    unnamed x1, blocking collectives  148 us
    unnamed x8, starting transfers between devices  46.8 us
  transfers between devices with their start and end apart: 12, of which 7 were waited for; matrix products, arithmetic and copies ran while one was open for 19% of the time, Pallas kernels for 0%

commit v1 on v0

v1 whole, which is shorter than its diff:
```python
import math

import jax
import jax.numpy as jnp
from jax import lax
from jax.sharding import Mesh
from jax.sharding import PartitionSpec as P

BF16, F32 = jnp.bfloat16, jnp.float32
NAMES = ("zh", "y", "c", "x", "zl")
SIZES = (4, 4, 2, 4, 8)


def gelu_parts(v):
    cdf = 0.5 * (1.0 + jax.scipy.special.erf(v / math.sqrt(2.0)))
    return v * cdf, cdf + v * jnp.exp(-0.5 * v * v) / math.sqrt(2.0 * math.pi)


def gather(block, axis, size):
    return lax.all_to_all(jnp.broadcast_to(block[None], (size,) + block.shape), axis, 0, 0)


def scatter_sum(parts, axis):
    got = lax.all_to_all(parts, axis, 0, 0)
    return jnp.sum(got.astype(F32), axis=0)


def shards(layer_input, out_grad, norm_gain_vector, up_weight, down_weight):
    nzh, ny, nc, nx, nzl = SIZES
    rows, width = layer_input.shape
    hidden_width = up_weight.shape[1]
    part = width // (nzh * ny * nc)
    xf = layer_input.astype(F32)
    centered = xf - jnp.mean(xf, axis=1, keepdims=True)
    rstd = 1.0 / jnp.sqrt(jnp.mean(centered * centered, axis=1, keepdims=True) + 1e-06)
    xhat = centered * rstd
    normed = (xhat * norm_gain_vector).astype(BF16)

    pair = jnp.stack([normed, out_grad])
    pair = gather(pair, "zl", nzl)
    pair = pair.transpose(1, 0, 2, 3).reshape(2, nzl * rows, width)
    pair = gather(pair, "x", nx)
    normed_all = pair[:, 0].reshape(nx * nzl * rows, width)
    grad_all = pair[:, 1].reshape(nx * nzl * rows, width)

    pre = jnp.dot(normed_all, up_weight, preferred_element_type=F32)
    hidden_grad = jnp.einsum("td,fd->tf", grad_all, down_weight, preferred_element_type=F32)
    value, slope = gelu_parts(pre)
    hidden = value.astype(BF16)
    pre_grad = (hidden_grad * slope).astype(BF16)
    down_term = jnp.einsum("td,tf->df", grad_all, hidden, preferred_element_type=F32).astype(BF16)
    up_term = jnp.einsum("td,tf->df", normed_all, pre_grad, preferred_element_type=F32).astype(BF16)
    full_term = jnp.einsum("tf,df->td", pre_grad, up_weight, preferred_element_type=F32).astype(BF16)

    terms = jnp.stack([up_term, down_term]).reshape(2, nzh, ny, nc, part, hidden_width)
    terms = terms.transpose(3, 2, 1, 0, 4, 5)
    terms = scatter_sum(terms, "c").astype(BF16)
    terms = scatter_sum(terms, "y").astype(BF16)
    terms = scatter_sum(terms, "zh")
    up_grad, down_grad = terms[0], terms[1].T

    full_term = full_term.reshape(nx, nzl * rows, width)
    full_term = scatter_sum(full_term, "x").astype(BF16)
    normed_grad = scatter_sum(full_term.reshape(nzl, rows, width), "zl")

    g = normed_grad * norm_gain_vector
    back = rstd * (
        g
        - jnp.mean(g, axis=1, keepdims=True)
        - xhat * jnp.mean(g * xhat, axis=1, keepdims=True)
    )
    input_grad = (out_grad.astype(F32) + back).astype(BF16)
    return (input_grad, up_grad, down_grad)


def solution(mesh):
    fine = Mesh(mesh.devices.reshape(SIZES), NAMES)
    dp, mp, both = ("zh", "y", "c"), ("x", "zl"), NAMES
    return jax.shard_map(
        shards,
        mesh=fine,
        in_specs=(P(both, None), P(both, None), P(), P(None, mp), P(mp, None)),
        out_specs=(P(both, None), P(dp, mp), P(mp, dp)),
        check_vma=False,
    )
```

time: 885 us -> 264 us (0.30)
  the two profiles are of different devices: /device:TPU:6 before, /device:TPU:33 now
where the time goes in v1:
time: 264 us; the launch traced here: 263 us
  waiting for transfers between devices  115 us (44%)
  blocking collectives  82.6 us (31%)
  starting transfers between devices  35.7 us (14%)
  other arithmetic  14.1 us (5%)
  local copies, waits for them, and re-layouts  8.59 us (3%)
  matrix products  5.85 us (2%)
    all_to_all x4, waiting for transfers between devices, scatter_sum(): got = lax.all_to_all(parts, axis, 0, 0)  115 us
    all_to_all x2, blocking collectives, gather(): lax.all_to_all(jnp.broadcast_to(block[None], (size,) + block.shape), axis...  70.4 us
    all_to_all x4, starting transfers between devices, scatter_sum(): got = lax.all_to_all(parts, axis, 0, 0)  35.7 us
    all_to_all x1, blocking collectives, scatter_sum(): got = lax.all_to_all(parts, axis, 0, 0)  12.2 us
    reduce_sum x5, other arithmetic, scatter_sum(): return jnp.sum(got.astype(F32), axis=0)  8.52 us
  transfers between devices with their start and end apart: 4, of which 4 were waited for; matrix products, arithmetic and copies ran while one was open for 6% of the time, Pallas kernels for 0%

profile of v1, /device:TPU:33, one launch (start us, length us, event | category | flops | bytes accessed | tf_op | source)
XLA Modules:
  0.0 263.1 jit_solution(18270055490189749978)
XLA Ops:
  0.6 1.1 convert_reduce_fusion.2
  1.7 1.0 fusion.16
  2.8 0.9 fusion.17
  3.6 0.8 pad_maximum_fusion.1
  4.6 0.3 broadcast_in_dim.6
  4.9 40.1 %all_to_all.35 = bf16[8,2,6,3072]{3,1,2,0:T(2,128)(2,1)S(1)} all-to-all(bf16[8,2,6,3072]{3,1,2,0:T(2,128)(2,1)S(1)} %broadcast_in_dim.6), channel_id=1, replica_groups=mesh['zh'=4,'y'=4,'c'=2,'x'=4,'zl'=8] {'zl'}, dimensions={0} | all-to-all | bytes 1179648 | tf_op jit(solution)/shard_map/all_to_all | solution.py:20
  45.1 0.3 broadcast_in_dim.8
  45.4 30.2 %all_to_all.36 = bf16[4,2,48,3072]{3,2,1,0:T(8,128)(2,1)S(1)} all-to-all(bf16[4,2,48,3072]{3,2,1,0:T(8,128)(2,1)S(1)} %broadcast_in_dim.8), channel_id=1, replica_groups=mesh['zh'=4,'y'=4,'c'=2,'x'=4,'zl'=8] {'x'}, dimensions={0} | all-to-all | bytes 4718592 | tf_op jit(solution)/shard_map/all_to_all | solution.py:20
  75.8 0.8 fusion.19
  76.6 0.8 copy-done.4
  77.5 0.9 fusion
  78.4 2.0 convolution_convert_fusion.2
  80.4 1.0 convolution_convert_fusion.1
  81.5 1.0 convolution_convert_fusion
  82.5 0.8 copy_bitcast_fusion
  83.3 12.2 %all_to_all.37 = bf16[2,4,4,2,96,384]{5,4,1,2,3,0:T(8,128)(2,1)} all-to-all(bf16[2,4,4,2,96,384]{5,4,1,2,3,0:T(8,128)(2,1)S(1)} %copy_bitcast_fusion), channel_id=1, replica_groups=mesh['zh'=4,'y'=4,'c'=2,'x'=4,'zl'=8] {'c'}, dimensions={0} | all-to-all | bytes 9437184 | tf_op jit(solution)/shard_map/all_to_all | solution.py:24
  95.5 3.5 %all-to-all-start.2 = ((bf16[4,48,3072]{2,1,0:T(8,128)(2,1)}), bf16[4,48,3072]{2,1,0:T(8,128)(2,1)S(1)}, u32[]{:S(2)}, u32[]{:S(2)}) async-start(bf16[4,48,3072]{2,1,0:T(8,128)(2,1)} %bitcast.6), calls=%async_computation.2 | async-start | bytes 2359296 | tf_op jit(solution)/shard_map/all_to_all | solution.py:24
  99.1 5.3 %reduce_sum.96 = bf16[4,4,2,96,384]{4,3,0,1,2:T(8,128)(2,1)} reduce(bf16[2,4,4,2,96,384]{5,4,1,2,3,0:T(8,128)(2,1)} %all_to_all.37, bf16[]{:T(256)} %constant.26.clone.1), dimensions={0}, to_apply=%region_6.0 | reduce | flops 1179648 | bytes 7077890 | tf_op jit(solution)/shard_map/reduce_sum | solution.py:25
  104.4 3.4 %copy.27 = bf16[4,4,2,96,384]{4,3,1,2,0:T(8,128)(2,1)} copy(bf16[4,4,2,96,384]{4,3,0,1,2:T(8,128)(2,1)} %reduce_sum.96) | data formatting | bytes 4718592 | tf_op jit(solution)/shard_map/reduce_sum | solution.py:25
  107.8 7.5 %all-to-all-done.2 = bf16[4,48,3072]{2,1,0:T(8,128)(2,1)S(1)} async-done(((bf16[4,48,3072]{2,1,0:T(8,128)(2,1)}), bf16[4,48,3072]{2,1,0:T(8,128)(2,1)S(1)}, u32[]{:S(2)}, u32[]{:S(2)}) %all-to-all-start.2) | async-done | bytes 1179680 | tf_op jit(solution)/shard_map/all_to_all | solution.py:24
  115.3 4.5 %all-to-all-start.5 = ((bf16[4,4,2,96,384]{4,3,1,2,0:T(8,128)(2,1)}), bf16[4,4,2,96,384]{4,3,1,2,0:T(8,128)(2,1)}, u32[]{:S(2)}, u32[]{:S(2)}) async-start(bf16[4,4,2,96,384]{4,3,1,2,0:T(8,128)(2,1)} %copy.27), calls=%async_computation.5 | async-start | bytes 4718592 | tf_op jit(solution)/shard_map/all_to_all | solution.py:24
  119.8 0.9 reduce_sum.92
  120.7 1.8 reshape.42
  122.6 25.3 %all-to-all-done.5 = bf16[4,4,2,96,384]{4,3,1,2,0:T(8,128)(2,1)} async-done(((bf16[4,4,2,96,384]{4,3,1,2,0:T(8,128)(2,1)}), bf16[4,4,2,96,384]{4,3,1,2,0:T(8,128)(2,1)}, u32[]{:S(2)}, u32[]{:S(2)}) %all-to-all-start.5) | async-done | bytes 2359328 | tf_op jit(solution)/shard_map/all_to_all | solution.py:24
  147.8 7.1 %all-to-all-start.3 = ((bf16[8,6,3072]{2,1,0:T(8,128)(2,1)}), bf16[8,6,3072]{2,1,0:T(8,128)(2,1)S(1)}, u32[]{:S(2)}, u32[]{:S(2)}) async-start(bf16[8,6,3072]{2,1,0:T(8,128)(2,1)} %reshape.42), calls=%async_computation.3 | async-start | bytes 786432 | tf_op jit(solution)/shard_map/all_to_all | solution.py:24
  155.0 2.1 reduce_sum.97
  157.1 0.9 copy.29
  157.9 17.5 %all-to-all-done.3 = bf16[8,6,3072]{2,1,0:T(8,128)(2,1)S(1)} async-done(((bf16[8,6,3072]{2,1,0:T(8,128)(2,1)}), bf16[8,6,3072]{2,1,0:T(8,128)(2,1)S(1)}, u32[]{:S(2)}, u32[]{:S(2)}) %all-to-all-start.3) | async-done | bytes 294944 | tf_op jit(solution)/shard_map/all_to_all | solution.py:24
  175.4 20.5 %all-to-all-start.6 = ((bf16[4,2,96,384]{3,2,1,0:T(8,128)(2,1)}), bf16[4,2,96,384]{3,2,1,0:T(8,128)(2,1)S(1)}, u32[]{:S(2)}, u32[]{:S(2)}) async-start(bf16[4,2,96,384]{3,2,1,0:T(8,128)(2,1)} %copy.29), calls=%async_computation.6 | async-start | bytes 1179648 | tf_op jit(solution)/shard_map/all_to_all | solution.py:24
  196.3 0.7 fusion.15
  197.0 65.2 %all-to-all-done.6 = bf16[4,2,96,384]{3,2,1,0:T(8,128)(2,1)S(1)} async-done(((bf16[4,2,96,384]{3,2,1,0:T(8,128)(2,1)}), bf16[4,2,96,384]{3,2,1,0:T(8,128)(2,1)S(1)}, u32[]{:S(2)}, u32[]{:S(2)}) %all-to-all-start.6) | async-done | bytes 589856 | tf_op jit(solution)/shard_map/all_to_all | solution.py:24
  262.3 0.7 slice_bitcast_fusion
  (18 shorter events, 0.7 us)
Async XLA Ops:
  0.6 75.2 %copy-start = (bf16[3072,384]{1,0:T(8,128)(2,1)S(1)}, bf16[3072,384]{1,0:T(8,128)(2,1)}, u32[]{:S(2)}) copy-start(bf16[3072,384]{1,0:T(8,128)(2,1)} %param.8) | copy-start | bytes 7077892
  75.8 1.7 copy-start.4
  95.5 19.8 %all-to-all-start.2 = ((bf16[4,48,3072]{2,1,0:T(8,128)(2,1)}), bf16[4,48,3072]{2,1,0:T(8,128)(2,1)S(1)}, u32[]{:S(2)}, u32[]{:S(2)}) async-start(bf16[4,48,3072]{2,1,0:T(8,128)(2,1)} %bitcast.6), calls=%async_computation.2 | async-start | bytes 2359296 | tf_op jit(solution)/shard_map/all_to_all | solution.py:24
  115.3 32.5 %all-to-all-start.5 = ((bf16[4,4,2,96,384]{4,3,1,2,0:T(8,128)(2,1)}), bf16[4,4,2,96,384]{4,3,1,2,0:T(8,128)(2,1)}, u32[]{:S(2)}, u32[]{:S(2)}) async-start(bf16[4,4,2,96,384]{4,3,1,2,0:T(8,128)(2,1)} %copy.27), calls=%async_computation.5 | async-start | bytes 4718592 | tf_op jit(solution)/shard_map/all_to_all | solution.py:24
  147.8 27.6 %all-to-all-start.3 = ((bf16[8,6,3072]{2,1,0:T(8,128)(2,1)}), bf16[8,6,3072]{2,1,0:T(8,128)(2,1)S(1)}, u32[]{:S(2)}, u32[]{:S(2)}) async-start(bf16[8,6,3072]{2,1,0:T(8,128)(2,1)} %reshape.42), calls=%async_computation.3 | async-start | bytes 786432 | tf_op jit(solution)/shard_map/all_to_all | solution.py:24
  154.9 41.1 %copy-start.1 = (bf16[6,3072]{1,0:T(8,128)(2,1)S(1)}, bf16[6,3072]{1,0:T(8,128)(2,1)}, u32[]{:S(2)}) copy-start(bf16[6,3072]{1,0:T(8,128)(2,1)} %param.5) | copy-start | bytes 110596
  154.9 41.1 %copy-start.3 = (f32[3072]{0:T(1024)S(1)}, f32[3072]{0:T(1024)}, u32[]{:S(2)}) copy-start(f32[3072]{0:T(1024)} %param.7) | copy-start | bytes 36868
  155.0 41.4 %copy-start.2 = (bf16[6,3072]{1,0:T(8,128)(2,1)S(1)}, bf16[6,3072]{1,0:T(8,128)(2,1)}, u32[]{:S(2)}) copy-start(bf16[6,3072]{1,0:T(8,128)(2,1)} %param.6) | copy-start | bytes 110596
  175.4 86.8 %all-to-all-start.6 = ((bf16[4,2,96,384]{3,2,1,0:T(8,128)(2,1)}), bf16[4,2,96,384]{3,2,1,0:T(8,128)(2,1)S(1)}, u32[]{:S(2)}, u32[]{:S(2)}) async-start(bf16[4,2,96,384]{3,2,1,0:T(8,128)(2,1)} %copy.29), calls=%async_computation.6 | async-start | bytes 1179648 | tf_op jit(solution)/shard_map/all_to_all | solution.py:24

commit v2 on v1

v2 whole, which is shorter than its diff:
```python
import math

import jax
import jax.numpy as jnp
from jax import lax
from jax.sharding import Mesh
from jax.sharding import PartitionSpec as P

BF16, F32 = jnp.bfloat16, jnp.float32
NAMES = ("zh", "y", "c", "x", "zl")
SIZES = (4, 4, 2, 4, 8)
FAR = [(i, i ^ 4) for i in range(8)]
FOURS = [[0, 1, 2, 3], [4, 5, 6, 7]]
AROUND = [(2 * i + c, 2 * ((i + 1 - 2 * c) % 4) + c) for i in range(4) for c in range(2)]


def gelu_parts(v):
    cdf = 0.5 * (1.0 + jax.scipy.special.erf(v / math.sqrt(2.0)))
    return v * cdf, cdf + v * jnp.exp(-0.5 * v * v) / math.sqrt(2.0 * math.pi)


def copies(block, n):
    return jnp.broadcast_to(block[None], (n,) + block.shape)


def added(*terms):
    total = terms[0].astype(F32)
    for term in terms[1:]:
        total = total + term.astype(F32)
    return total


def pick(array, index, axis):
    return lax.dynamic_index_in_dim(array, index, axis, keepdims=False)


def shards(layer_input, out_grad, norm_gain_vector, up_weight, down_weight):
    nzh, ny, nc, nx, nzl = SIZES
    rows, width = layer_input.shape
    hidden_width = up_weight.shape[1]
    part = width // (nzh * ny * nc)
    zh, c = lax.axis_index("zh"), lax.axis_index("c")

    xf = layer_input.astype(F32)
    centered = xf - jnp.mean(xf, axis=1, keepdims=True)
    rstd = 1.0 / jnp.sqrt(jnp.mean(centered * centered, axis=1, keepdims=True) + 1e-06)
    xhat = centered * rstd
    normed = (xhat * norm_gain_vector).astype(BF16)

    pair = jnp.concatenate([normed, out_grad], axis=1)
    pair = jnp.concatenate([pair, lax.ppermute(pair, "zl", FAR)], axis=0)
    pair = lax.all_to_all(copies(pair, 4), "zl", 0, 0, axis_index_groups=FOURS)
    pair = pair.reshape(nzl * rows, 2 * width)
    pair = jnp.stack([pair[:, :width], pair[:, width:]])
    pair = lax.all_to_all(copies(pair, nx), "x", 0, 0)
    normed_all = pair[:, 0].reshape(nx * nzl * rows, width)
    grad_all = pair[:, 1].reshape(nx * nzl * rows, width)

    pre = jnp.dot(normed_all, up_weight, preferred_element_type=F32)
    value, slope = gelu_parts(pre)
    hidden = value.astype(BF16)
    hidden_grad = jnp.einsum("td,fd->tf", grad_all, down_weight, preferred_element_type=F32)
    pre_grad = (hidden_grad * slope).astype(BF16)

    def half(left, right):
        term = jnp.einsum("td,tf->df", left, right, preferred_element_type=F32).astype(BF16)
        term = term.reshape(nzh, ny, nc, part, hidden_width)
        got = lax.ppermute(pick(term, 1 - c, 2), "c", [(0, 1), (1, 0)])
        return added(pick(term, c, 2), got).astype(BF16).transpose(1, 0, 2, 3)

    terms = jnp.stack([half(grad_all, hidden), half(normed_all, pre_grad)], axis=2)
    terms = lax.all_to_all(terms, "y", 0, 0)
    terms = added(*[terms[i] for i in range(ny)]).astype(BF16)
    terms, pre_grad = lax.optimization_barrier((terms, pre_grad))

    step = 1 - 2 * c
    total = pick(terms, (zh - step) % nzh, 0)

    def hop(total, k, fence):
        got = lax.ppermute(total, ("zh", "c"), AROUND)
        got, fence = lax.optimization_barrier((got, fence))
        return added(got, pick(terms, (zh - k * step) % nzh, 0)), fence

    full_term = jnp.einsum("tf,df->td", pre_grad, up_weight, preferred_element_type=F32)
    full_term = full_term.astype(BF16).reshape(nx, nzl * rows, width)
    total, full_term = hop(total, 2, full_term)
    full_term = lax.all_to_all(full_term, "x", 0, 0)
    full_term = added(*[full_term[i] for i in range(nx)]).astype(BF16)
    total, full_term = hop(total.astype(BF16), 3, full_term)
    full_term = lax.all_to_all(
        full_term.reshape(4, 2 * rows, width), "zl", 0, 0, axis_index_groups=FOURS
    )
    full_term = added(*[full_term[i] for i in range(4)])
    far = lax.ppermute(full_term[rows:].astype(BF16), "zl", FAR)
    total, far = hop(total.astype(BF16), 4, far)
    normed_grad = added(full_term[:rows], far)
    up_grad, down_grad = total[1], total[0].T

    g = normed_grad * norm_gain_vector
    back = rstd * (
        g
        - jnp.mean(g, axis=1, keepdims=True)
        - xhat * jnp.mean(g * xhat, axis=1, keepdims=True)
    )
    input_grad = (out_grad.astype(F32) + back).astype(BF16)
    return (input_grad, up_grad, down_grad)


def solution(mesh):
    fine = Mesh(mesh.devices.reshape(SIZES), NAMES)
    dp, mp, both = ("zh", "y", "c"), ("x", "zl"), NAMES
    return jax.shard_map(
        shards,
        mesh=fine,
        in_specs=(P(both, None), P(both, None), P(), P(None, mp), P(mp, None)),
        out_specs=(P(both, None), P(dp, mp), P(mp, dp)),
        check_vma=False,
    )
```

time: 264 us -> 238 us (0.902)
  the two profiles are of different devices: /device:TPU:33 before, /device:TPU:6 now
where the time goes in v2:
time: 238 us; the launch traced here: 236 us
  starting transfers between devices  90 us (38%)
  waiting for transfers between devices  88 us (37%)
  blocking collectives  23.9 us (10%)
  other arithmetic  15.1 us (6%)
  local copies, waits for them, and re-layouts  11.8 us (5%)
  matrix products  5.88 us (2%)
    ppermute x3, starting transfers between devices, hop(): got = lax.ppermute(total, ('zh', 'c'), AROUND)  39.8 us
    all_to_all x1, waiting for transfers between devices, shards(): terms = lax.all_to_all(terms, 'y', 0, 0)  30 us
    all_to_all x1, waiting for transfers between devices, shards(): pair = lax.all_to_all(copies(pair, nx), 'x', 0, 0)  26.6 us
    all_to_all x1, blocking collectives, shards(): pair = lax.all_to_all(copies(pair, 4), 'zl', 0, 0, axis_index_groups=FOURS)  23.9 us
    all_to_all x1, starting transfers between devices, shards(): lax.all_to_all(full_term.reshape(4, 2 * rows, width), 'zl', 0, 0, axis_in...  13.1 us
    ppermute x1, waiting for transfers between devices, shards(): far = lax.ppermute(full_term[rows:].astype(BF16), 'zl', FAR)  11.3 us
    ppermute x1, waiting for transfers between devices, shards(): pair = jnp.concatenate([pair, lax.ppermute(pair, 'zl', FAR)], axis=0)  9.1 us
    ppermute x1, starting transfers between devices, shards(): pair = jnp.concatenate([pair, lax.ppermute(pair, 'zl', FAR)], axis=0)  9.1 us
  transfers between devices with their start and end apart: 11, of which 8 were waited for; matrix products, arithmetic and copies ran while one was open for 3% of the time, Pallas kernels for 0%

profile of v2, /device:TPU:6, one launch (start us, length us, event | category | flops | bytes accessed | tf_op | source)
XLA Modules:
  0.0 235.6 jit_solution(9938678478743219030)
XLA Ops:
  0.6 1.1 convert_reduce_fusion
  1.7 1.0 fusion.24
  4.5 9.1 %collective-permute-start = (bf16[6,6144]{1,0:T(8,128)(2,1)S(1)}, bf16[6,6144]{1,0:T(8,128)(2,1)S(1)}, u32[]{:S(2)}, u32[]{:S(2)}) collective-permute-start(bf16[6,6144]{1,0:T(8,128)(2,1)S(1)} %pad_maximum_fusion.3), channel_id=1, source_target_pairs={{0,4},{1,5},{2,6},{3,7},{4,0},{5,1},{6,2},{7,3},{8,12},{9,13},{10,... | collective-permute-start | bytes 221192 | tf_op jit(solution)/shard_map/ppermute | solution.py:51
  13.6 9.1 %collective-permute-done = bf16[6,6144]{1,0:T(8,128)(2,1)S(1)} collective-permute-done((bf16[6,6144]{1,0:T(8,128)(2,1)S(1)}, bf16[6,6144]{1,0:T(8,128)(2,1)S(1)}, u32[]{:S(2)}, u32[]{:S(2)}) %collective-permute-start) | collective-permute-done | bytes 73760 | tf_op jit(solution)/shard_map/ppermute | solution.py:51
  23.6 23.9 %all_to_all.25 = bf16[4,12,6144]{2,1,0:T(8,128)(2,1)S(1)} all-to-all(bf16[4,12,6144]{2,1,0:T(8,128)(2,1)S(1)} %broadcast_in_dim.4), channel_id=1, replica_groups={{0,1,2,3},{4,5,6,7},{8,9,10,11},{12,13,14,15},{16,17,18,19},{20,21,22,2..., dimensions={0} | all-to-all | bytes 1179648 | tf_op jit(solution)/shard_map/all_to_all | solution.py:52
  48.4 1.1 slice_bitcast_fusion.1
  49.6 1.7 broadcast_in_dim.5
  51.3 4.8 %all-to-all-start.1 = ((bf16[4,2,48,3072]{3,2,1,0:T(8,128)(2,1)}), bf16[4,2,48,3072]{3,2,1,0:T(8,128)(2,1)}, u32[]{:S(2)}, u32[]{:S(2)}) async-start(bf16[4,2,48,3072]{3,2,1,0:T(8,128)(2,1)} %broadcast_in_dim.5), calls=%async_computation.1 | async-start | bytes 4718592 | tf_op jit(solution)/shard_map/all_to_all | solution.py:55
  56.1 26.6 %all-to-all-done.1 = bf16[4,2,48,3072]{3,2,1,0:T(8,128)(2,1)} async-done(((bf16[4,2,48,3072]{3,2,1,0:T(8,128)(2,1)}), bf16[4,2,48,3072]{3,2,1,0:T(8,128)(2,1)}, u32[]{:S(2)}, u32[]{:S(2)}) %all-to-all-start.1) | async-done | bytes 2359328 | tf_op jit(solution)/shard_map/all_to_all | solution.py:55
  82.7 1.8 fusion.29
  85.3 1.0 convolution_convert_fusion.1
  87.9 1.0 convolution_convert_fusion
  89.7 1.9 collective-permute-start.1
  91.8 2.4 %collective-permute-start.2 = (bf16[4,4,96,384]{3,2,0,1:T(8,128)(2,1)S(1)}, bf16[4,4,96,384]{3,2,0,1:T(8,128)(2,1)S(1)}, u32[]{:S(2)}, u32[]{:S(2)}) collective-permute-start(bf16[4,4,96,384]{3,2,0,1:T(8,128)(2,1)S(1)} %bitcast.83), channel_id=1, source_target_pairs={{0,32},{32,0},{1,33},{33,1},{2,34},{34,2},{3,35},{35,3},{4,36},{36... | collective-permute-start | bytes 3538952 | tf_op jit(solution)/shard_map/ppermute | solution.py:68
  94.8 1.9 collective-permute-done.2
  97.0 1.7 pad_maximum_fusion
  98.7 4.7 %all-to-all-start.2 = ((bf16[4,4,2,96,384]{4,3,2,1,0:T(8,128)(2,1)}), bf16[4,4,2,96,384]{4,3,2,1,0:T(8,128)(2,1)}, u32[]{:S(2)}, u32[]{:S(2)}) async-start(bf16[4,4,2,96,384]{4,3,2,1,0:T(8,128)(2,1)} %pad_maximum_fusion), calls=%async_computation.2 | async-start | bytes 4718592 | tf_op jit(solution)/shard_map/all_to_all | solution.py:72
  103.4 30.0 %all-to-all-done.2 = bf16[4,4,2,96,384]{4,3,2,1,0:T(8,128)(2,1)} async-done(((bf16[4,4,2,96,384]{4,3,2,1,0:T(8,128)(2,1)}), bf16[4,4,2,96,384]{4,3,2,1,0:T(8,128)(2,1)}, u32[]{:S(2)}, u32[]{:S(2)}) %all-to-all-start.2) | async-done | bytes 2359328 | tf_op jit(solution)/shard_map/all_to_all | solution.py:72
  133.4 1.9 fusion.5
  136.2 15.7 %collective-permute-start.3 = (bf16[2,96,384]{2,1,0:T(8,128)(2,1)S(1)}, bf16[2,96,384]{2,1,0:T(8,128)(2,1)S(1)}, u32[]{:S(2)}, u32[]{:S(2)}) collective-permute-start(bf16[2,96,384]{2,1,0:T(8,128)(2,1)S(1)} %dynamic-slice_bitcast_fusion), channel_id=1, source_target_pairs={{0,256},{32,800},{256,512},{288,32},{512,768},{544,288},{768,0},{8... | collective-permute-start | bytes 442376 | tf_op jit(solution)/shard_map/ppermute | solution.py:80
  152.0 2.0 convolution_convert_fusion.2
  154.0 5.7 %collective-permute-done.3 = bf16[2,96,384]{2,1,0:T(8,128)(2,1)S(1)} collective-permute-done((bf16[2,96,384]{2,1,0:T(8,128)(2,1)S(1)}, bf16[2,96,384]{2,1,0:T(8,128)(2,1)S(1)}, u32[]{:S(2)}, u32[]{:S(2)}) %collective-permute-start.3) | collective-permute-done | bytes 147488 | tf_op jit(solution)/shard_map/ppermute | solution.py:80
  160.3 5.5 %all-to-all-start.3 = ((bf16[4,48,3072]{2,1,0:T(8,128)(2,1)}), bf16[4,48,3072]{2,1,0:T(8,128)(2,1)S(1)}, u32[]{:S(2)}, u32[]{:S(2)}) async-start(bf16[4,48,3072]{2,1,0:T(8,128)(2,1)} %bitcast.16), calls=%async_computation.3 | async-start | bytes 2359296 | tf_op jit(solution)/shard_map/all_to_all | solution.py:87
  165.9 1.7 fusion.12
  167.5 12.2 %collective-permute-start.4 = (bf16[2,96,384]{2,1,0:T(8,128)(2,1)}, bf16[2,96,384]{2,1,0:T(8,128)(2,1)}, u32[]{:S(2)}, u32[]{:S(2)}) collective-permute-start(bf16[2,96,384]{2,1,0:T(8,128)(2,1)} %fusion.12), channel_id=1, source_target_pairs={{0,256},{32,800},{256,512},{288,32},{512,768},{544,288},{768,0},{8... | collective-permute-start | bytes 442376 | tf_op jit(solution)/shard_map/ppermute | solution.py:80
  180.6 3.1 %collective-permute-done.4 = bf16[2,96,384]{2,1,0:T(8,128)(2,1)} collective-permute-done((bf16[2,96,384]{2,1,0:T(8,128)(2,1)}, bf16[2,96,384]{2,1,0:T(8,128)(2,1)}, u32[]{:S(2)}, u32[]{:S(2)}) %collective-permute-start.4) | collective-permute-done | bytes 147488 | tf_op jit(solution)/shard_map/ppermute | solution.py:80
  183.7 1.8 reshape.85
  185.5 13.1 %all-to-all-start.4 = ((bf16[4,12,3072]{2,1,0:T(8,128)(2,1)}), bf16[4,12,3072]{2,1,0:T(8,128)(2,1)S(1)}, u32[]{:S(2)}, u32[]{:S(2)}) async-start(bf16[4,12,3072]{2,1,0:T(8,128)(2,1)} %reshape.85), calls=%async_computation.4 | async-start | bytes 786432 | tf_op jit(solution)/shard_map/all_to_all | solution.py:90
  198.6 1.7 fusion.11
  200.2 11.9 %collective-permute-start.5 = (bf16[2,96,384]{2,1,0:T(8,128)(2,1)}, bf16[2,96,384]{2,1,0:T(8,128)(2,1)}, u32[]{:S(2)}, u32[]{:S(2)}) collective-permute-start(bf16[2,96,384]{2,1,0:T(8,128)(2,1)} %fusion.11), channel_id=1, source_target_pairs={{0,256},{32,800},{256,512},{288,32},{512,768},{544,288},{768,0},{8... | collective-permute-start | bytes 442376 | tf_op jit(solution)/shard_map/ppermute | solution.py:80
  212.9 8.7 %collective-permute-start.6 = (bf16[6,3072]{1,0:T(8,128)(2,1)S(1)}, bf16[6,3072]{1,0:T(8,128)(2,1)S(1)}, u32[]{:S(2)}, u32[]{:S(2)}) collective-permute-start(bf16[6,3072]{1,0:T(8,128)(2,1)S(1)} %fusion.27), channel_id=1, source_target_pairs={{0,4},{1,5},{2,6},{3,7},{4,0},{5,1},{6,2},{7,3},{8,12},{9,13},{10,... | collective-permute-start | bytes 110600 | tf_op jit(solution)/shard_map/ppermute | solution.py:94
  221.6 11.3 %collective-permute-done.6 = bf16[6,3072]{1,0:T(8,128)(2,1)S(1)} collective-permute-done((bf16[6,3072]{1,0:T(8,128)(2,1)S(1)}, bf16[6,3072]{1,0:T(8,128)(2,1)S(1)}, u32[]{:S(2)}, u32[]{:S(2)}) %collective-permute-start.6) | collective-permute-done | bytes 36896 | tf_op jit(solution)/shard_map/ppermute | solution.py:94
  (49 shorter events, 13.6 us)
Async XLA Ops:
  0.6 83.9 %copy-start = (bf16[3072,384]{1,0:T(8,128)(2,1)S(1)}, bf16[3072,384]{1,0:T(8,128)(2,1)}, u32[]{:S(2)}) copy-start(bf16[3072,384]{1,0:T(8,128)(2,1)} %param.8) | copy-start | bytes 7077892
  4.5 18.2 %collective-permute-start = (bf16[6,6144]{1,0:T(8,128)(2,1)S(1)}, bf16[6,6144]{1,0:T(8,128)(2,1)S(1)}, u32[]{:S(2)}, u32[]{:S(2)}) collective-permute-start(bf16[6,6144]{1,0:T(8,128)(2,1)S(1)} %pad_maximum_fusion.3), channel_id=1, source_target_pairs={{0,4},{1,5},{2,6},{3,7},{4,0},{5,1},{6,2},{7,3},{8,12},{9,13},{10,... | collective-permute-start | bytes 221192 | tf_op jit(solution)/shard_map/ppermute | solution.py:51
  51.3 31.4 %all-to-all-start.1 = ((bf16[4,2,48,3072]{3,2,1,0:T(8,128)(2,1)}), bf16[4,2,48,3072]{3,2,1,0:T(8,128)(2,1)}, u32[]{:S(2)}, u32[]{:S(2)}) async-start(bf16[4,2,48,3072]{3,2,1,0:T(8,128)(2,1)} %broadcast_in_dim.5), calls=%async_computation.1 | async-start | bytes 4718592 | tf_op jit(solution)/shard_map/all_to_all | solution.py:55
  85.3 1.7 copy-start.9
  89.7 4.7 %collective-permute-start.1 = (bf16[4,4,96,384]{3,2,0,1:T(8,128)(2,1)S(1)}, bf16[4,4,96,384]{3,2,0,1:T(8,128)(2,1)S(1)}, u32[]{:S(2)}, u32[]{:S(2)}) collective-permute-start(bf16[4,4,96,384]{3,2,0,1:T(8,128)(2,1)S(1)} %bitcast.84), channel_id=1, source_target_pairs={{0,32},{32,0},{1,33},{33,1},{2,34},{34,2},{3,35},{35,3},{4,36},{36... | collective-permute-start | bytes 3538952 | tf_op jit(solution)/shard_map/ppermute | solution.py:68
  91.8 4.9 %collective-permute-start.2 = (bf16[4,4,96,384]{3,2,0,1:T(8,128)(2,1)S(1)}, bf16[4,4,96,384]{3,2,0,1:T(8,128)(2,1)S(1)}, u32[]{:S(2)}, u32[]{:S(2)}) collective-permute-start(bf16[4,4,96,384]{3,2,0,1:T(8,128)(2,1)S(1)} %bitcast.83), channel_id=1, source_target_pairs={{0,32},{32,0},{1,33},{33,1},{2,34},{34,2},{3,35},{35,3},{4,36},{36... | collective-permute-start | bytes 3538952 | tf_op jit(solution)/shard_map/ppermute | solution.py:68
  98.7 34.8 %all-to-all-start.2 = ((bf16[4,4,2,96,384]{4,3,2,1,0:T(8,128)(2,1)}), bf16[4,4,2,96,384]{4,3,2,1,0:T(8,128)(2,1)}, u32[]{:S(2)}, u32[]{:S(2)}) async-start(bf16[4,4,2,96,384]{4,3,2,1,0:T(8,128)(2,1)} %pad_maximum_fusion), calls=%async_computation.2 | async-start | bytes 4718592 | tf_op jit(solution)/shard_map/all_to_all | solution.py:72
  135.3 0.9 copy-start.1
  136.2 23.5 %collective-permute-start.3 = (bf16[2,96,384]{2,1,0:T(8,128)(2,1)S(1)}, bf16[2,96,384]{2,1,0:T(8,128)(2,1)S(1)}, u32[]{:S(2)}, u32[]{:S(2)}) collective-permute-start(bf16[2,96,384]{2,1,0:T(8,128)(2,1)S(1)} %dynamic-slice_bitcast_fusion), channel_id=1, source_target_pairs={{0,256},{32,800},{256,512},{288,32},{512,768},{544,288},{768,0},{8... | collective-permute-start | bytes 442376 | tf_op jit(solution)/shard_map/ppermute | solution.py:80
  159.7 0.7 copy-start.7
  160.3 19.4 %all-to-all-start.3 = ((bf16[4,48,3072]{2,1,0:T(8,128)(2,1)}), bf16[4,48,3072]{2,1,0:T(8,128)(2,1)S(1)}, u32[]{:S(2)}, u32[]{:S(2)}) async-start(bf16[4,48,3072]{2,1,0:T(8,128)(2,1)} %bitcast.16), calls=%async_computation.3 | async-start | bytes 2359296 | tf_op jit(solution)/shard_map/all_to_all | solution.py:87
  167.5 16.1 %collective-permute-start.4 = (bf16[2,96,384]{2,1,0:T(8,128)(2,1)}, bf16[2,96,384]{2,1,0:T(8,128)(2,1)}, u32[]{:S(2)}, u32[]{:S(2)}) collective-permute-start(bf16[2,96,384]{2,1,0:T(8,128)(2,1)} %fusion.12), channel_id=1, source_target_pairs={{0,256},{32,800},{256,512},{288,32},{512,768},{544,288},{768,0},{8... | collective-permute-start | bytes 442376 | tf_op jit(solution)/shard_map/ppermute | solution.py:80
  180.6 18.0 %copy-start.2 = (bf16[4,2,96,384]{3,2,1,0:T(8,128)(2,1)S(1)}, bf16[4,2,96,384]{3,2,1,0:T(8,128)(2,1)}, u32[]{:S(2)}) copy-start(bf16[4,2,96,384]{3,2,1,0:T(8,128)(2,1)} %copy-done.1) | copy-start | bytes 1769476
  185.5 26.7 %all-to-all-start.4 = ((bf16[4,12,3072]{2,1,0:T(8,128)(2,1)}), bf16[4,12,3072]{2,1,0:T(8,128)(2,1)S(1)}, u32[]{:S(2)}, u32[]{:S(2)}) async-start(bf16[4,12,3072]{2,1,0:T(8,128)(2,1)} %reshape.85), calls=%async_computation.4 | async-start | bytes 786432 | tf_op jit(solution)/shard_map/all_to_all | solution.py:90
  198.5 36.1 %copy-start.3 = (bf16[6,3072]{1,0:T(8,128)(2,1)S(1)}, bf16[6,3072]{1,0:T(8,128)(2,1)}, u32[]{:S(2)}) copy-start(bf16[6,3072]{1,0:T(8,128)(2,1)} %param.5) | copy-start | bytes 110596
  198.6 36.1 %copy-start.8 = (f32[3072]{0:T(1024)S(1)}, f32[3072]{0:T(1024)}, u32[]{:S(2)}) copy-start(f32[3072]{0:T(1024)} %param.7) | copy-start | bytes 36868
  198.6 36.3 %copy-start.6 = (bf16[6,3072]{1,0:T(8,128)(2,1)S(1)}, bf16[6,3072]{1,0:T(8,128)(2,1)}, u32[]{:S(2)}) copy-start(bf16[6,3072]{1,0:T(8,128)(2,1)} %param.6) | copy-start | bytes 110596
  200.2 21.4 %collective-permute-start.5 = (bf16[2,96,384]{2,1,0:T(8,128)(2,1)}, bf16[2,96,384]{2,1,0:T(8,128)(2,1)}, u32[]{:S(2)}, u32[]{:S(2)}) collective-permute-start(bf16[2,96,384]{2,1,0:T(8,128)(2,1)} %fusion.11), channel_id=1, source_target_pairs={{0,256},{32,800},{256,512},{288,32},{512,768},{544,288},{768,0},{8... | collective-permute-start | bytes 442376 | tf_op jit(solution)/shard_map/ppermute | solution.py:80
  212.2 0.7 copy-start.4
  212.9 20.1 %collective-permute-start.6 = (bf16[6,3072]{1,0:T(8,128)(2,1)S(1)}, bf16[6,3072]{1,0:T(8,128)(2,1)S(1)}, u32[]{:S(2)}, u32[]{:S(2)}) collective-permute-start(bf16[6,3072]{1,0:T(8,128)(2,1)S(1)} %fusion.27), channel_id=1, source_target_pairs={{0,4},{1,5},{2,6},{3,7},{4,0},{5,1},{6,2},{7,3},{8,12},{9,13},{10,... | collective-permute-start | bytes 110600 | tf_op jit(solution)/shard_map/ppermute | solution.py:94
  221.6 13.0 %copy-start.5 = (f32[1,12,3072]{2,1,0:T(8,128)S(1)}, f32[1,12,3072]{2,1,0:T(8,128)}, u32[]{:S(2)}) copy-start(f32[1,12,3072]{2,1,0:T(8,128)} %copy-done.4) | copy-start | bytes 442372

commit v3 on v2

--- a/solution.py
+++ b/solution.py
@@ -9,8 +9,6 @@
 BF16, F32 = jnp.bfloat16, jnp.float32
 NAMES = ("zh", "y", "c", "x", "zl")
 SIZES = (4, 4, 2, 4, 8)
-FAR = [(i, i ^ 4) for i in range(8)]
-FOURS = [[0, 1, 2, 3], [4, 5, 6, 7]]
 AROUND = [(2 * i + c, 2 * ((i + 1 - 2 * c) % 4) + c) for i in range(4) for c in range(2)]
 
 
@@ -19,8 +17,12 @@
     return v * cdf, cdf + v * jnp.exp(-0.5 * v * v) / math.sqrt(2.0 * math.pi)
 
 
-def copies(block, n):
-    return jnp.broadcast_to(block[None], (n,) + block.shape)
+def swap(block, distance):
+    return lax.ppermute(block, "zl", [(i, i ^ distance) for i in range(8)])
+
+
+def shift(block, distance):
+    return lax.ppermute(block, "x", [(i, (i + distance) % 4) for i in range(4)])
 
 
 def added(*terms):
@@ -47,14 +49,15 @@
     xhat = centered * rstd
     normed = (xhat * norm_gain_vector).astype(BF16)
 
-    pair = jnp.concatenate([normed, out_grad], axis=1)
-    pair = jnp.concatenate([pair, lax.ppermute(pair, "zl", FAR)], axis=0)
-    pair = lax.all_to_all(copies(pair, 4), "zl", 0, 0, axis_index_groups=FOURS)
-    pair = pair.reshape(nzl * rows, 2 * width)
-    pair = jnp.stack([pair[:, :width], pair[:, width:]])
-    pair = lax.all_to_all(copies(pair, nx), "x", 0, 0)
-    normed_all = pair[:, 0].reshape(nx * nzl * rows, width)
-    grad_all = pair[:, 1].reshape(nx * nzl * rows, width)
+    def gathered(block):
+        for distance in (4, 2, 1):
+            block = jnp.concatenate([block, swap(block, distance)])
+        left, right = shift(block, 1), shift(block, -1)
+        middle = block.shape[0] // 2
+        across = shift(left[:middle], 1), shift(right[middle:], -1)
+        return jnp.concatenate([block, left, *across, right])
+
+    grad_all, normed_all = gathered(out_grad), gathered(normed)
 
     pre = jnp.dot(normed_all, up_weight, preferred_element_type=F32)
     value, slope = gelu_parts(pre)
@@ -68,32 +71,24 @@
         got = lax.ppermute(pick(term, 1 - c, 2), "c", [(0, 1), (1, 0)])
         return added(pick(term, c, 2), got).astype(BF16).transpose(1, 0, 2, 3)
 
+    full_term = jnp.einsum("tf,df->td", pre_grad, up_weight, preferred_element_type=F32)
+    full_term, pre_grad = lax.optimization_barrier((full_term.astype(BF16), pre_grad))
+    own, left, across, right = jnp.split(full_term, nx)
+    own = added(own, shift(left, -1), shift(across, 2), shift(right, 1))
+    for distance in (1, 2, 4):
+        middle = own.shape[0] // 2
+        own = added(own[:middle], swap(own[middle:].astype(BF16), distance))
+    normed_grad = own
+
     terms = jnp.stack([half(grad_all, hidden), half(normed_all, pre_grad)], axis=2)
     terms = lax.all_to_all(terms, "y", 0, 0)
     terms = added(*[terms[i] for i in range(ny)]).astype(BF16)
-    terms, pre_grad = lax.optimization_barrier((terms, pre_grad))
 
     step = 1 - 2 * c
     total = pick(terms, (zh - step) % nzh, 0)
-
-    def hop(total, k, fence):
-        got = lax.ppermute(total, ("zh", "c"), AROUND)
-        got, fence = lax.optimization_barrier((got, fence))
-        return added(got, pick(terms, (zh - k * step) % nzh, 0)), fence
-
-    full_term = jnp.einsum("tf,df->td", pre_grad, up_weight, preferred_element_type=F32)
-    full_term = full_term.astype(BF16).reshape(nx, nzl * rows, width)
-    total, full_term = hop(total, 2, full_term)
-    full_term = lax.all_to_all(full_term, "x", 0, 0)
-    full_term = added(*[full_term[i] for i in range(nx)]).astype(BF16)
-    total, full_term = hop(total.astype(BF16), 3, full_term)
-    full_term = lax.all_to_all(
-        full_term.reshape(4, 2 * rows, width), "zl", 0, 0, axis_index_groups=FOURS
-    )
-    full_term = added(*[full_term[i] for i in range(4)])
-    far = lax.ppermute(full_term[rows:].astype(BF16), "zl", FAR)
-    total, far = hop(total.astype(BF16), 4, far)
-    normed_grad = added(full_term[:rows], far)
+    for hop in range(2, nzh + 1):
+        got = lax.ppermute(total.astype(BF16), ("zh", "c"), AROUND)
+        total = added(got, pick(terms, (zh - hop * step) % nzh, 0))
     up_grad, down_grad = total[1], total[0].T
 
     g = normed_grad * norm_gain_vector

time: 238 us -> 237 us (level)
  starting transfers between devices: 90 us -> 131 us
  waiting for transfers between devices: 88 us -> 50.2 us
  blocking collectives: 23.9 us -> 0 us
  local copies, waits for them, and re-layouts: 11.8 us -> 30.4 us
  other arithmetic: 15.1 us -> 12.5 us
    ppermute x5 -> x23, starting transfers between devices: 57.6 us -> 122 us  [the longest x9 41.8 us: swap(): return lax.ppermute(block, 'zl', [(i, i ^ distance) for i in range(8)])]
    all_to_all x1, waiting for transfers between devices: 30 us -> 0.01 us  [shards(): terms = lax.all_to_all(terms, 'y', 0, 0)]
    all_to_all x3 -> x0, waiting for transfers between devices: 26.6 us -> none  [the longest x1 26.6 us: shards(): pair = lax.all_to_all(copies(pair, nx), 'x', 0, 0)]
    concatenate x0 -> x2, local copies, waits for them, and re-layouts: none -> 23.9 us  [gathered(): return jnp.concatenate([block, left, *across, right])]
    all_to_all x1 -> x0, blocking collectives: 23.9 us -> none  [shards(): pair = lax.all_to_all(copies(pair, 4), 'zl', 0, 0, axis_index_groups=FOURS)]
    all_to_all x3 -> x0, starting transfers between devices: 23.4 us -> none  [the longest x1 13.1 us: shards(): lax.all_to_all(full_term.reshape(4, 2 * rows, width), 'zl', 0, 0, axis_in...]
    ppermute x5 -> x23, waiting for transfers between devices: 29.2 us -> 50.2 us  [the longest x3 30.1 us: shards(): got = lax.ppermute(total.astype(BF16), ('zh', 'c'), AROUND)]
    reshape x2 -> x0, local copies, waits for them, and re-layouts: 2.75 us -> none  [the longest x1 1.78 us: shards(): full_term.reshape(4, 2 * rows, width)]
  transfers between devices with their start and end apart: 11 -> 26, of which waited for: 8 -> 11; matrix products, arithmetic and copies ran while one was open for 3% -> 11% of each run, Pallas kernels for 0% -> 0%
where the time goes in v3:
time: 237 us; the launch traced here: 233 us
  starting transfers between devices  131 us (55%)
  waiting for transfers between devices  50.2 us (21%)
  local copies, waits for them, and re-layouts  30.4 us (13%)
  other arithmetic  12.5 us (5%)
  matrix products  6.63 us (3%)
    ppermute x9, starting transfers between devices, swap(): return lax.ppermute(block, 'zl', [(i, i ^ distance) for i in range(8)])  41.8 us
    ppermute x3, starting transfers between devices, shards(): got = lax.ppermute(total.astype(BF16), ('zh', 'c'), AROUND)  40.9 us
    ppermute x11, starting transfers between devices, shift(): return lax.ppermute(block, 'x', [(i, (i + distance) % 4) for i in range(4)])  39.7 us
    ppermute x3, waiting for transfers between devices, shards(): got = lax.ppermute(total.astype(BF16), ('zh', 'c'), AROUND)  30.1 us
    concatenate x2, local copies, waits for them, and re-layouts, gathered(): return jnp.concatenate([block, left, *across, right])  23.9 us
    ppermute x9, waiting for transfers between devices, swap(): return lax.ppermute(block, 'zl', [(i, i ^ distance) for i in range(8)])  12.9 us
    ppermute x11, waiting for transfers between devices, shift(): return lax.ppermute(block, 'x', [(i, (i + distance) % 4) for i in range(4)])  7.14 us
  transfers between devices with their start and end apart: 26, of which 11 were waited for; matrix products, arithmetic and copies ran while one was open for 11% of the time, Pallas kernels for 0%

profile of v3, /device:TPU:6, one launch (start us, length us, event | category | flops | bytes accessed | tf_op | source)
XLA Modules:
  0.0 232.5 jit_solution(3112915925536371507)
XLA Ops:
  3.7 9.1 %collective-permute-start.7 = (bf16[6,3072]{1,0:T(8,128)(2,1)S(1)}, bf16[6,3072]{1,0:T(8,128)(2,1)S(1)}, u32[]{:S(2)}, u32[]{:S(2)}) collective-permute-start(bf16[6,3072]{1,0:T(8,128)(2,1)S(1)} %fusion.16), channel_id=1, source_target_pairs={{0,4},{1,5},{2,6},{3,7},{4,0},{5,1},{6,2},{7,3},{8,12},{9,13},{10,... | collective-permute-start | bytes 110600 | tf_op jit(solution)/shard_map/ppermute | solution.py:21
  12.8 1.9 collective-permute-start
  14.9 7.5 %collective-permute-start.8 = (bf16[12,3072]{1,0:T(8,128)(2,1)S(1)}, bf16[12,3072]{1,0:T(8,128)(2,1)S(1)}, u32[]{:S(2)}, u32[]{:S(2)}) collective-permute-start(bf16[12,3072]{1,0:T(8,128)(2,1)S(1)} %pad_maximum_fusion.6), channel_id=1, source_target_pairs={{0,2},{1,3},{2,0},{3,1},{4,6},{5,7},{6,4},{7,5},{8,10},{9,11},{10,... | collective-permute-start | bytes 221192 | tf_op jit(solution)/shard_map/ppermute | solution.py:21
  24.2 5.2 %collective-permute-start.1 = (bf16[12,3072]{1,0:T(8,128)(2,1)S(1)}, bf16[12,3072]{1,0:T(8,128)(2,1)S(1)}, u32[]{:S(2)}, u32[]{:S(2)}) collective-permute-start(bf16[12,3072]{1,0:T(8,128)(2,1)S(1)} %pad_maximum_fusion.5), channel_id=1, source_target_pairs={{0,2},{1,3},{2,0},{3,1},{4,6},{5,7},{6,4},{7,5},{8,10},{9,11},{10,... | collective-permute-start | bytes 221192 | tf_op jit(solution)/shard_map/ppermute | solution.py:21
  29.5 3.4 %collective-permute-start.9 = (bf16[24,3072]{1,0:T(8,128)(2,1)S(1)}, bf16[24,3072]{1,0:T(8,128)(2,1)S(1)}, u32[]{:S(2)}, u32[]{:S(2)}) collective-permute-start(bf16[24,3072]{1,0:T(8,128)(2,1)S(1)} %pad_maximum_fusion.4), channel_id=1, source_target_pairs={{0,1},{1,0},{2,3},{3,2},{4,5},{5,4},{6,7},{7,6},{8,9},{9,8},{10,11... | collective-permute-start | bytes 442376 | tf_op jit(solution)/shard_map/ppermute | solution.py:21
  34.9 2.5 %collective-permute-start.2 = (bf16[24,3072]{1,0:T(8,128)(2,1)S(1)}, bf16[24,3072]{1,0:T(8,128)(2,1)S(1)}, u32[]{:S(2)}, u32[]{:S(2)}) collective-permute-start(bf16[24,3072]{1,0:T(8,128)(2,1)S(1)} %pad_maximum_fusion.3), channel_id=1, source_target_pairs={{0,1},{1,0},{2,3},{3,2},{4,5},{5,4},{6,7},{7,6},{8,9},{9,8},{10,11... | collective-permute-start | bytes 442376 | tf_op jit(solution)/shard_map/ppermute | solution.py:21
  38.2 6.9 %collective-permute-start.10 = (bf16[48,3072]{1,0:T(8,128)(2,1)S(1)}, bf16[48,3072]{1,0:T(8,128)(2,1)S(1)}, u32[]{:S(2)}, u32[]{:S(2)}) collective-permute-start(bf16[48,3072]{1,0:T(8,128)(2,1)S(1)} %pad_maximum_fusion.2), channel_id=1, source_target_pairs={{0,8},{8,16},{16,24},{24,0},{1,9},{9,17},{17,25},{25,1},{2,10},{10... | collective-permute-start | bytes 884744 | tf_op jit(solution)/shard_map/ppermute | solution.py:25
  45.1 1.9 collective-permute-start.12
  47.2 5.1 %collective-permute-start.3 = (bf16[48,3072]{1,0:T(8,128)(2,1)S(1)}, bf16[48,3072]{1,0:T(8,128)(2,1)S(1)}, u32[]{:S(2)}, u32[]{:S(2)}) collective-permute-start(bf16[48,3072]{1,0:T(8,128)(2,1)S(1)} %pad_maximum_fusion.1), channel_id=1, source_target_pairs={{0,8},{8,16},{16,24},{24,0},{1,9},{9,17},{17,25},{25,1},{2,10},{10... | collective-permute-start | bytes 884744 | tf_op jit(solution)/shard_map/ppermute | solution.py:25
  54.3 5.1 %collective-permute-start.11 = (bf16[24,3072]{1,0:T(8,128)(2,1)S(1)}, bf16[24,3072]{1,0:T(8,128)(2,1)S(1)}, u32[]{:S(2)}, u32[]{:S(2)}) collective-permute-start(bf16[24,3072]{1,0:T(8,128)(2,1)S(1)} %slice.69), channel_id=1, source_target_pairs={{0,8},{8,16},{16,24},{24,0},{1,9},{9,17},{17,25},{25,1},{2,10},{10... | collective-permute-start | bytes 442376 | tf_op jit(solution)/shard_map/ppermute | solution.py:25
  62.9 5.1 %collective-permute-start.4 = (bf16[24,3072]{1,0:T(8,128)(2,1)}, bf16[24,3072]{1,0:T(8,128)(2,1)}, u32[]{:S(2)}, u32[]{:S(2)}) collective-permute-start(bf16[24,3072]{1,0:T(8,128)(2,1)} %slice.67), channel_id=1, source_target_pairs={{0,8},{8,16},{16,24},{24,0},{1,9},{9,17},{17,25},{25,1},{2,10},{10... | collective-permute-start | bytes 442376 | tf_op jit(solution)/shard_map/ppermute | solution.py:25
  71.4 11.9 %concatenate.37 = bf16[192,3072]{1,0:T(8,128)(2,1)S(1)} concatenate(bf16[6,3072]{1,0:T(8,128)(2,1)} %copy-done.6, bf16[6,3072]{1,0:T(8,128)(2,1)} %copy-done.10, bf16[12,3072]{1,0:T(8,128)(2,1)} %copy-done.8, bf16[24,3072]{1,0:T(8,128)(2,1)} %copy-done.16, bf16[48,3072]{1,0:T(8,128)(2,1)} %copy-done.13, bf16[24,3072]{1,0:T(8,128)(2,1)} %copy-done.18, ...), dimensions={0} | concatenate | bytes 2359296 | tf_op jit(solution)/shard_map/concatenate | solution.py:58
  84.9 11.9 %concatenate.33 = bf16[192,3072]{1,0:T(8,128)(2,1)S(1)} concatenate(bf16[6,3072]{1,0:T(8,128)(2,1)} %param.6, bf16[6,3072]{1,0:T(8,128)(2,1)} %copy-done.9, bf16[12,3072]{1,0:T(8,128)(2,1)} %copy-done.7, bf16[24,3072]{1,0:T(8,128)(2,1)} %copy-done.15, bf16[48,3072]{1,0:T(8,128)(2,1)} %copy-done.11, bf16[24,3072]{1,0:T(8,128)(2,1)} %collective-permute-done.4, ...), dimensions={0} | concatenate | bytes 2359296 | tf_op jit(solution)/shard_map/concatenate | solution.py:58
  96.8 2.1 convolution_convert_fusion.1
  103.1 1.9 collective-permute-start.21
  105.1 2.4 %collective-permute-start.20 = (bf16[4,4,96,384]{3,2,0,1:T(8,128)(2,1)S(1)}, bf16[4,4,96,384]{3,2,0,1:T(8,128)(2,1)S(1)}, u32[]{:S(2)}, u32[]{:S(2)}) collective-permute-start(bf16[4,4,96,384]{3,2,0,1:T(8,128)(2,1)S(1)} %bitcast.54), channel_id=1, source_target_pairs={{0,32},{32,0},{1,33},{33,1},{2,34},{34,2},{3,35},{35,3},{4,36},{36... | collective-permute-start | bytes 3538952 | tf_op jit(solution)/shard_map/ppermute | solution.py:71
  108.5 5.1 %collective-permute-start.16 = (bf16[48,3072]{1,0:T(8,128)(2,1)}, bf16[48,3072]{1,0:T(8,128)(2,1)}, u32[]{:S(2)}, u32[]{:S(2)}) collective-permute-start(bf16[48,3072]{1,0:T(8,128)(2,1)} %get-tuple-element.14), channel_id=1, source_target_pairs={{0,8},{8,16},{16,24},{24,0},{1,9},{9,17},{17,25},{25,1},{2,10},{10... | collective-permute-start | bytes 884744 | tf_op jit(solution)/shard_map/ppermute | solution.py:25
  113.6 1.9 collective-permute-start.15
  115.6 2.8 %collective-permute-start.14 = (bf16[48,3072]{1,0:T(8,128)(2,1)}, bf16[48,3072]{1,0:T(8,128)(2,1)}, u32[]{:S(2)}, u32[]{:S(2)}) collective-permute-start(bf16[48,3072]{1,0:T(8,128)(2,1)} %get-tuple-element.13), channel_id=1, source_target_pairs={{0,24},{8,0},{16,8},{24,16},{1,25},{9,1},{17,9},{25,17},{2,26},{10... | collective-permute-start | bytes 884744 | tf_op jit(solution)/shard_map/ppermute | solution.py:25
  120.7 4.5 %all-to-all-start = ((bf16[4,4,2,96,384]{4,3,2,1,0:T(8,128)(2,1)}), bf16[4,4,2,96,384]{4,3,2,1,0:T(8,128)(2,1)}, u32[]{:S(2)}, u32[]{:S(2)}) async-start(bf16[4,4,2,96,384]{4,3,2,1,0:T(8,128)(2,1)} %pad_maximum_fusion), calls=%async_computation | async-start | bytes 4718592 | tf_op jit(solution)/shard_map/all_to_all | solution.py:84
  127.3 5.0 %collective-permute-done.14 = bf16[48,3072]{1,0:T(8,128)(2,1)} collective-permute-done((bf16[48,3072]{1,0:T(8,128)(2,1)}, bf16[48,3072]{1,0:T(8,128)(2,1)}, u32[]{:S(2)}, u32[]{:S(2)}) %collective-permute-start.14) | collective-permute-done | bytes 294944 | tf_op jit(solution)/shard_map/ppermute | solution.py:25
  133.6 2.3 collective-permute-start.17
  135.9 5.3 %collective-permute-done.17 = bf16[24,3072]{1,0:T(8,128)(2,1)S(1)} collective-permute-done((bf16[24,3072]{1,0:T(8,128)(2,1)S(1)}, bf16[24,3072]{1,0:T(8,128)(2,1)S(1)}, u32[]{:S(2)}, u32[]{:S(2)}) %collective-permute-start.17) | collective-permute-done | bytes 147488 | tf_op jit(solution)/shard_map/ppermute | solution.py:21
  141.3 3.5 %collective-permute-start.18 = (bf16[12,3072]{1,0:T(8,128)(2,1)S(1)}, bf16[12,3072]{1,0:T(8,128)(2,1)S(1)}, u32[]{:S(2)}, u32[]{:S(2)}) collective-permute-start(bf16[12,3072]{1,0:T(8,128)(2,1)S(1)} %slice.104), channel_id=1, source_target_pairs={{0,2},{1,3},{2,0},{3,1},{4,6},{5,7},{6,4},{7,5},{8,10},{9,11},{10,... | collective-permute-start | bytes 221192 | tf_op jit(solution)/shard_map/ppermute | solution.py:21
  144.9 5.3 %collective-permute-done.18 = bf16[12,3072]{1,0:T(8,128)(2,1)S(1)} collective-permute-done((bf16[12,3072]{1,0:T(8,128)(2,1)S(1)}, bf16[12,3072]{1,0:T(8,128)(2,1)S(1)}, u32[]{:S(2)}, u32[]{:S(2)}) %collective-permute-start.18) | collective-permute-done | bytes 73760 | tf_op jit(solution)/shard_map/ppermute | solution.py:21
  150.3 6.4 %collective-permute-start.19 = (bf16[6,3072]{1,0:T(8,128)(2,1)S(1)}, bf16[6,3072]{1,0:T(8,128)(2,1)S(1)}, u32[]{:S(2)}, u32[]{:S(2)}) collective-permute-start(bf16[6,3072]{1,0:T(8,128)(2,1)S(1)} %slice.105), channel_id=1, source_target_pairs={{0,4},{1,5},{2,6},{3,7},{4,0},{5,1},{6,2},{7,3},{8,12},{9,13},{10,... | collective-permute-start | bytes 110600 | tf_op jit(solution)/shard_map/ppermute | solution.py:21
  158.6 14.4 %collective-permute-start.22 = (bf16[2,96,384]{2,1,0:T(8,128)(2,1)S(1)}, bf16[2,96,384]{2,1,0:T(8,128)(2,1)}, u32[]{:S(2)}, u32[]{:S(2)}) collective-permute-start(bf16[2,96,384]{2,1,0:T(8,128)(2,1)S(1)} %dynamic-slice_bitcast_fusion), channel_id=1, source_target_pairs={{0,256},{32,800},{256,512},{288,32},{512,768},{544,288},{768,0},{8... | collective-permute-start | bytes 442376 | tf_op jit(solution)/shard_map/ppermute | solution.py:90
  173.3 8.4 %collective-permute-done.22 = bf16[2,96,384]{2,1,0:T(8,128)(2,1)} collective-permute-done((bf16[2,96,384]{2,1,0:T(8,128)(2,1)S(1)}, bf16[2,96,384]{2,1,0:T(8,128)(2,1)}, u32[]{:S(2)}, u32[]{:S(2)}) %collective-permute-start.22) | collective-permute-done | bytes 147488 | tf_op jit(solution)/shard_map/ppermute | solution.py:90
  182.7 13.2 %collective-permute-start.23 = (bf16[2,96,384]{2,1,0:T(8,128)(2,1)S(1)}, bf16[2,96,384]{2,1,0:T(8,128)(2,1)S(1)}, u32[]{:S(2)}, u32[]{:S(2)}) collective-permute-start(bf16[2,96,384]{2,1,0:T(8,128)(2,1)S(1)} %fusion.10), channel_id=1, source_target_pairs={{0,256},{32,800},{256,512},{288,32},{512,768},{544,288},{768,0},{8... | collective-permute-start | bytes 442376 | tf_op jit(solution)/shard_map/ppermute | solution.py:90
  196.0 9.9 %collective-permute-done.23 = bf16[2,96,384]{2,1,0:T(8,128)(2,1)S(1)} collective-permute-done((bf16[2,96,384]{2,1,0:T(8,128)(2,1)S(1)}, bf16[2,96,384]{2,1,0:T(8,128)(2,1)S(1)}, u32[]{:S(2)}, u32[]{:S(2)}) %collective-permute-start.23) | collective-permute-done | bytes 147488 | tf_op jit(solution)/shard_map/ppermute | solution.py:90
  205.9 13.3 %collective-permute-start.24 = (bf16[2,96,384]{2,1,0:T(8,128)(2,1)S(1)}, bf16[2,96,384]{2,1,0:T(8,128)(2,1)S(1)}, u32[]{:S(2)}, u32[]{:S(2)}) collective-permute-start(bf16[2,96,384]{2,1,0:T(8,128)(2,1)S(1)} %fusion.9), channel_id=1, source_target_pairs={{0,256},{32,800},{256,512},{288,32},{512,768},{544,288},{768,0},{8... | collective-permute-start | bytes 442376 | tf_op jit(solution)/shard_map/ppermute | solution.py:90
  219.9 11.8 %collective-permute-done.24 = bf16[2,96,384]{2,1,0:T(8,128)(2,1)S(1)} collective-permute-done((bf16[2,96,384]{2,1,0:T(8,128)(2,1)S(1)}, bf16[2,96,384]{2,1,0:T(8,128)(2,1)S(1)}, u32[]{:S(2)}, u32[]{:S(2)}) %collective-permute-start.24) | collective-permute-done | bytes 147488 | tf_op jit(solution)/shard_map/ppermute | solution.py:90
  (106 shorter events, 33.7 us)
Async XLA Ops:
  0.6 82.7 %copy-start = (bf16[3072,384]{1,0:T(8,128)(2,1)S(1)}, bf16[3072,384]{1,0:T(8,128)(2,1)}, u32[]{:S(2)}) copy-start(bf16[3072,384]{1,0:T(8,128)(2,1)} %param.8) | copy-start | bytes 7077892
  0.6 46.4 %copy-start.4 = (bf16[6,3072]{1,0:T(8,128)(2,1)S(1)}, bf16[6,3072]{1,0:T(8,128)(2,1)}, u32[]{:S(2)}) copy-start(bf16[6,3072]{1,0:T(8,128)(2,1)} %param.6) | copy-start | bytes 110596
  3.7 43.5 %copy-start.6 = (bf16[6,3072]{1,0:T(8,128)(2,1)}, bf16[6,3072]{1,0:T(8,128)(2,1)S(1)}, u32[]{:S(2)}) copy-start(bf16[6,3072]{1,0:T(8,128)(2,1)S(1)} %fusion.16) | copy-start | bytes 110596
  3.7 11.2 %collective-permute-start.7 = (bf16[6,3072]{1,0:T(8,128)(2,1)S(1)}, bf16[6,3072]{1,0:T(8,128)(2,1)S(1)}, u32[]{:S(2)}, u32[]{:S(2)}) collective-permute-start(bf16[6,3072]{1,0:T(8,128)(2,1)S(1)} %fusion.16), channel_id=1, source_target_pairs={{0,4},{1,5},{2,6},{3,7},{4,0},{5,1},{6,2},{7,3},{8,12},{9,13},{10,... | collective-permute-start | bytes 110600 | tf_op jit(solution)/shard_map/ppermute | solution.py:21
  12.8 10.6 %collective-permute-start = (bf16[6,3072]{1,0:T(8,128)(2,1)}, bf16[6,3072]{1,0:T(8,128)(2,1)S(1)}, u32[]{:S(2)}, u32[]{:S(2)}) collective-permute-start(bf16[6,3072]{1,0:T(8,128)(2,1)} %param.6), channel_id=1, source_target_pairs={{0,4},{1,5},{2,6},{3,7},{4,0},{5,1},{6,2},{7,3},{8,12},{9,13},{10,... | collective-permute-start | bytes 110600 | tf_op jit(solution)/shard_map/ppermute | solution.py:21
  14.9 32.3 %copy-start.10 = (bf16[6,3072]{1,0:T(8,128)(2,1)}, bf16[6,3072]{1,0:T(8,128)(2,1)S(1)}, u32[]{:S(2)}) copy-start(bf16[6,3072]{1,0:T(8,128)(2,1)S(1)} %collective-permute-done.7) | copy-start | bytes 110596
  14.9 14.5 %collective-permute-start.8 = (bf16[12,3072]{1,0:T(8,128)(2,1)S(1)}, bf16[12,3072]{1,0:T(8,128)(2,1)S(1)}, u32[]{:S(2)}, u32[]{:S(2)}) collective-permute-start(bf16[12,3072]{1,0:T(8,128)(2,1)S(1)} %pad_maximum_fusion.6), channel_id=1, source_target_pairs={{0,2},{1,3},{2,0},{3,1},{4,6},{5,7},{6,4},{7,5},{8,10},{9,11},{10,... | collective-permute-start | bytes 221192 | tf_op jit(solution)/shard_map/ppermute | solution.py:21
  23.4 30.9 %copy-start.9 = (bf16[6,3072]{1,0:T(8,128)(2,1)}, bf16[6,3072]{1,0:T(8,128)(2,1)S(1)}, u32[]{:S(2)}) copy-start(bf16[6,3072]{1,0:T(8,128)(2,1)S(1)} %collective-permute-done) | copy-start | bytes 110596
  24.2 9.8 %collective-permute-start.1 = (bf16[12,3072]{1,0:T(8,128)(2,1)S(1)}, bf16[12,3072]{1,0:T(8,128)(2,1)S(1)}, u32[]{:S(2)}, u32[]{:S(2)}) collective-permute-start(bf16[12,3072]{1,0:T(8,128)(2,1)S(1)} %pad_maximum_fusion.5), channel_id=1, source_target_pairs={{0,2},{1,3},{2,0},{3,1},{4,6},{5,7},{6,4},{7,5},{8,10},{9,11},{10,... | collective-permute-start | bytes 221192 | tf_op jit(solution)/shard_map/ppermute | solution.py:21
  29.5 8.0 %collective-permute-start.9 = (bf16[24,3072]{1,0:T(8,128)(2,1)S(1)}, bf16[24,3072]{1,0:T(8,128)(2,1)S(1)}, u32[]{:S(2)}, u32[]{:S(2)}) collective-permute-start(bf16[24,3072]{1,0:T(8,128)(2,1)S(1)} %pad_maximum_fusion.4), channel_id=1, source_target_pairs={{0,1},{1,0},{2,3},{3,2},{4,5},{5,4},{6,7},{7,6},{8,9},{9,8},{10,11... | collective-permute-start | bytes 442376 | tf_op jit(solution)/shard_map/ppermute | solution.py:21
  34.9 12.1 %collective-permute-start.2 = (bf16[24,3072]{1,0:T(8,128)(2,1)S(1)}, bf16[24,3072]{1,0:T(8,128)(2,1)S(1)}, u32[]{:S(2)}, u32[]{:S(2)}) collective-permute-start(bf16[24,3072]{1,0:T(8,128)(2,1)S(1)} %pad_maximum_fusion.3), channel_id=1, source_target_pairs={{0,1},{1,0},{2,3},{3,2},{4,5},{5,4},{6,7},{7,6},{8,9},{9,8},{10,11... | collective-permute-start | bytes 442376 | tf_op jit(solution)/shard_map/ppermute | solution.py:21
  38.2 16.0 %collective-permute-start.10 = (bf16[48,3072]{1,0:T(8,128)(2,1)S(1)}, bf16[48,3072]{1,0:T(8,128)(2,1)S(1)}, u32[]{:S(2)}, u32[]{:S(2)}) collective-permute-start(bf16[48,3072]{1,0:T(8,128)(2,1)S(1)} %pad_maximum_fusion.2), channel_id=1, source_target_pairs={{0,8},{8,16},{16,24},{24,0},{1,9},{9,17},{17,25},{25,1},{2,10},{10... | collective-permute-start | bytes 884744 | tf_op jit(solution)/shard_map/ppermute | solution.py:25
  45.1 14.3 %collective-permute-start.12 = (bf16[48,3072]{1,0:T(8,128)(2,1)S(1)}, bf16[48,3072]{1,0:T(8,128)(2,1)S(1)}, u32[]{:S(2)}, u32[]{:S(2)}) collective-permute-start(bf16[48,3072]{1,0:T(8,128)(2,1)S(1)} %pad_maximum_fusion.2), channel_id=1, source_target_pairs={{0,24},{8,0},{16,8},{24,16},{1,25},{9,1},{17,9},{25,17},{2,26},{10... | collective-permute-start | bytes 884744 | tf_op jit(solution)/shard_map/ppermute | solution.py:25
  47.2 15.0 %collective-permute-start.3 = (bf16[48,3072]{1,0:T(8,128)(2,1)S(1)}, bf16[48,3072]{1,0:T(8,128)(2,1)S(1)}, u32[]{:S(2)}, u32[]{:S(2)}) collective-permute-start(bf16[48,3072]{1,0:T(8,128)(2,1)S(1)} %pad_maximum_fusion.1), channel_id=1, source_target_pairs={{0,8},{8,16},{16,24},{24,0},{1,9},{9,17},{17,25},{25,1},{2,10},{10... | collective-permute-start | bytes 884744 | tf_op jit(solution)/shard_map/ppermute | solution.py:25
  52.4 15.7 %collective-permute-start.5 = (bf16[48,3072]{1,0:T(8,128)(2,1)S(1)}, bf16[48,3072]{1,0:T(8,128)(2,1)S(1)}, u32[]{:S(2)}, u32[]{:S(2)}) collective-permute-start(bf16[48,3072]{1,0:T(8,128)(2,1)S(1)} %pad_maximum_fusion.1), channel_id=1, source_target_pairs={{0,24},{8,0},{16,8},{24,16},{1,25},{9,1},{17,9},{25,17},{2,26},{10... | collective-permute-start | bytes 884744 | tf_op jit(solution)/shard_map/ppermute | solution.py:25
  54.3 16.4 %collective-permute-start.11 = (bf16[24,3072]{1,0:T(8,128)(2,1)S(1)}, bf16[24,3072]{1,0:T(8,128)(2,1)S(1)}, u32[]{:S(2)}, u32[]{:S(2)}) collective-permute-start(bf16[24,3072]{1,0:T(8,128)(2,1)S(1)} %slice.69), channel_id=1, source_target_pairs={{0,8},{8,16},{16,24},{24,0},{1,9},{9,17},{17,25},{25,1},{2,10},{10... | collective-permute-start | bytes 442376 | tf_op jit(solution)/shard_map/ppermute | solution.py:25
  60.2 11.2 %collective-permute-start.13 = (bf16[24,3072]{1,0:T(8,128)(2,1)}, bf16[24,3072]{1,0:T(8,128)(2,1)}, u32[]{:S(2)}, u32[]{:S(2)}) collective-permute-start(bf16[24,3072]{1,0:T(8,128)(2,1)} %slice.70), channel_id=1, source_target_pairs={{0,24},{8,0},{16,8},{24,16},{1,25},{9,1},{17,9},{25,17},{2,26},{10... | collective-permute-start | bytes 442376 | tf_op jit(solution)/shard_map/ppermute | solution.py:25
  62.9 21.9 %collective-permute-start.4 = (bf16[24,3072]{1,0:T(8,128)(2,1)}, bf16[24,3072]{1,0:T(8,128)(2,1)}, u32[]{:S(2)}, u32[]{:S(2)}) collective-permute-start(bf16[24,3072]{1,0:T(8,128)(2,1)} %slice.67), channel_id=1, source_target_pairs={{0,8},{8,16},{16,24},{24,0},{1,9},{9,17},{17,25},{25,1},{2,10},{10... | collective-permute-start | bytes 442376 | tf_op jit(solution)/shard_map/ppermute | solution.py:25
  68.8 16.1 %collective-permute-start.6 = (bf16[24,3072]{1,0:T(8,128)(2,1)}, bf16[24,3072]{1,0:T(8,128)(2,1)}, u32[]{:S(2)}, u32[]{:S(2)}) collective-permute-start(bf16[24,3072]{1,0:T(8,128)(2,1)} %slice.68), channel_id=1, source_target_pairs={{0,24},{8,0},{16,8},{24,16},{1,25},{9,1},{17,9},{25,17},{2,26},{10... | collective-permute-start | bytes 442376 | tf_op jit(solution)/shard_map/ppermute | solution.py:25
  103.1 15.3 %collective-permute-start.21 = (bf16[4,4,96,384]{3,2,0,1:T(8,128)(2,1)S(1)}, bf16[4,4,96,384]{3,2,0,1:T(8,128)(2,1)S(1)}, u32[]{:S(2)}, u32[]{:S(2)}) collective-permute-start(bf16[4,4,96,384]{3,2,0,1:T(8,128)(2,1)S(1)} %bitcast.55), channel_id=1, source_target_pairs={{0,32},{32,0},{1,33},{33,1},{2,34},{34,2},{3,35},{35,3},{4,36},{36... | collective-permute-start | bytes 3538952 | tf_op jit(solution)/shard_map/ppermute | solution.py:71
  105.1 13.5 %collective-permute-start.20 = (bf16[4,4,96,384]{3,2,0,1:T(8,128)(2,1)S(1)}, bf16[4,4,96,384]{3,2,0,1:T(8,128)(2,1)S(1)}, u32[]{:S(2)}, u32[]{:S(2)}) collective-permute-start(bf16[4,4,96,384]{3,2,0,1:T(8,128)(2,1)S(1)} %bitcast.54), channel_id=1, source_target_pairs={{0,32},{32,0},{1,33},{33,1},{2,34},{34,2},{3,35},{35,3},{4,36},{36... | collective-permute-start | bytes 3538952 | tf_op jit(solution)/shard_map/ppermute | solution.py:71
  108.5 18.2 %collective-permute-start.16 = (bf16[48,3072]{1,0:T(8,128)(2,1)}, bf16[48,3072]{1,0:T(8,128)(2,1)}, u32[]{:S(2)}, u32[]{:S(2)}) collective-permute-start(bf16[48,3072]{1,0:T(8,128)(2,1)} %get-tuple-element.14), channel_id=1, source_target_pairs={{0,8},{8,16},{16,24},{24,0},{1,9},{9,17},{17,25},{25,1},{2,10},{10... | collective-permute-start | bytes 884744 | tf_op jit(solution)/shard_map/ppermute | solution.py:25
  113.6 13.7 %collective-permute-start.15 = (bf16[48,3072]{1,0:T(8,128)(2,1)}, bf16[48,3072]{1,0:T(8,128)(2,1)}, u32[]{:S(2)}, u32[]{:S(2)}) collective-permute-start(bf16[48,3072]{1,0:T(8,128)(2,1)} %get-tuple-element.15), channel_id=1, source_target_pairs={{0,16},{8,24},{16,0},{24,8},{1,17},{9,25},{17,1},{25,9},{2,18},{10... | collective-permute-start | bytes 884744 | tf_op jit(solution)/shard_map/ppermute | solution.py:25
  115.6 16.8 %collective-permute-start.14 = (bf16[48,3072]{1,0:T(8,128)(2,1)}, bf16[48,3072]{1,0:T(8,128)(2,1)}, u32[]{:S(2)}, u32[]{:S(2)}) collective-permute-start(bf16[48,3072]{1,0:T(8,128)(2,1)} %get-tuple-element.13), channel_id=1, source_target_pairs={{0,24},{8,0},{16,8},{24,16},{1,25},{9,1},{17,9},{25,17},{2,26},{10... | collective-permute-start | bytes 884744 | tf_op jit(solution)/shard_map/ppermute | solution.py:25
  120.7 36.0 %all-to-all-start = ((bf16[4,4,2,96,384]{4,3,2,1,0:T(8,128)(2,1)}), bf16[4,4,2,96,384]{4,3,2,1,0:T(8,128)(2,1)}, u32[]{:S(2)}, u32[]{:S(2)}) async-start(bf16[4,4,2,96,384]{4,3,2,1,0:T(8,128)(2,1)} %pad_maximum_fusion), calls=%async_computation | async-start | bytes 4718592 | tf_op jit(solution)/shard_map/all_to_all | solution.py:84
  133.6 7.7 %collective-permute-start.17 = (bf16[24,3072]{1,0:T(8,128)(2,1)S(1)}, bf16[24,3072]{1,0:T(8,128)(2,1)S(1)}, u32[]{:S(2)}, u32[]{:S(2)}) collective-permute-start(bf16[24,3072]{1,0:T(8,128)(2,1)S(1)} %slice.103), channel_id=1, source_target_pairs={{0,1},{1,0},{2,3},{3,2},{4,5},{5,4},{6,7},{7,6},{8,9},{9,8},{10,11... | collective-permute-start | bytes 442376 | tf_op jit(solution)/shard_map/ppermute | solution.py:21
  141.3 8.9 %collective-permute-start.18 = (bf16[12,3072]{1,0:T(8,128)(2,1)S(1)}, bf16[12,3072]{1,0:T(8,128)(2,1)S(1)}, u32[]{:S(2)}, u32[]{:S(2)}) collective-permute-start(bf16[12,3072]{1,0:T(8,128)(2,1)S(1)} %slice.104), channel_id=1, source_target_pairs={{0,2},{1,3},{2,0},{3,1},{4,6},{5,7},{6,4},{7,5},{8,10},{9,11},{10,... | collective-permute-start | bytes 221192 | tf_op jit(solution)/shard_map/ppermute | solution.py:21
  150.3 22.8 %collective-permute-start.19 = (bf16[6,3072]{1,0:T(8,128)(2,1)S(1)}, bf16[6,3072]{1,0:T(8,128)(2,1)S(1)}, u32[]{:S(2)}, u32[]{:S(2)}) collective-permute-start(bf16[6,3072]{1,0:T(8,128)(2,1)S(1)} %slice.105), channel_id=1, source_target_pairs={{0,4},{1,5},{2,6},{3,7},{4,0},{5,1},{6,2},{7,3},{8,12},{9,13},{10,... | collective-permute-start | bytes 110600 | tf_op jit(solution)/shard_map/ppermute | solution.py:21
  158.6 60.6 %copy-start.5 = (bf16[6,3072]{1,0:T(8,128)(2,1)S(1)}, bf16[6,3072]{1,0:T(8,128)(2,1)}, u32[]{:S(2)}) copy-start(bf16[6,3072]{1,0:T(8,128)(2,1)} %param.6) | copy-start | bytes 110596
  158.6 23.1 %collective-permute-start.22 = (bf16[2,96,384]{2,1,0:T(8,128)(2,1)S(1)}, bf16[2,96,384]{2,1,0:T(8,128)(2,1)}, u32[]{:S(2)}, u32[]{:S(2)}) collective-permute-start(bf16[2,96,384]{2,1,0:T(8,128)(2,1)S(1)} %dynamic-slice_bitcast_fusion), channel_id=1, source_target_pairs={{0,256},{32,800},{256,512},{288,32},{512,768},{544,288},{768,0},{8... | collective-permute-start | bytes 442376 | tf_op jit(solution)/shard_map/ppermute | solution.py:90
  182.7 23.1 %collective-permute-start.23 = (bf16[2,96,384]{2,1,0:T(8,128)(2,1)S(1)}, bf16[2,96,384]{2,1,0:T(8,128)(2,1)S(1)}, u32[]{:S(2)}, u32[]{:S(2)}) collective-permute-start(bf16[2,96,384]{2,1,0:T(8,128)(2,1)S(1)} %fusion.10), channel_id=1, source_target_pairs={{0,256},{32,800},{256,512},{288,32},{512,768},{544,288},{768,0},{8... | collective-permute-start | bytes 442376 | tf_op jit(solution)/shard_map/ppermute | solution.py:90
  205.9 25.9 %collective-permute-start.24 = (bf16[2,96,384]{2,1,0:T(8,128)(2,1)S(1)}, bf16[2,96,384]{2,1,0:T(8,128)(2,1)S(1)}, u32[]{:S(2)}, u32[]{:S(2)}) collective-permute-start(bf16[2,96,384]{2,1,0:T(8,128)(2,1)S(1)} %fusion.9), channel_id=1, source_target_pairs={{0,256},{32,800},{256,512},{288,32},{512,768},{544,288},{768,0},{8... | collective-permute-start | bytes 442376 | tf_op jit(solution)/shard_map/ppermute | solution.py:90
  (15 other events, 139.9 us)

commit v4 on v3

v4 whole, which is shorter than its diff:
```python
import math

import jax
import jax.numpy as jnp
from jax import lax
from jax.experimental import pallas as pl
from jax.experimental.pallas import tpu as pltpu
from jax.sharding import Mesh
from jax.sharding import PartitionSpec as P

BF16, F32 = jnp.bfloat16, jnp.float32
NAMES = ("zh", "y", "c", "x", "zl")
SIZES = (4, 4, 2, 4, 8)


def gelu_parts(v):
    cdf = 0.5 * (1.0 + jax.scipy.special.erf(v / math.sqrt(2.0)))
    return v * cdf, cdf + v * jnp.exp(-0.5 * v * v) / math.sqrt(2.0 * math.pi)


def swap(block, distance):
    return lax.ppermute(block, "zl", [(i, i ^ distance) for i in range(8)])


def shift(block, distance):
    return lax.ppermute(block, "x", [(i, (i + distance) % 4) for i in range(4)])


def pairs(axis, step):
    flip = {(c, s): 1 if c == s else 3 for c in range(2) for s in range(2)}
    if axis == "x":
        return ("c", "x"), [
            (4 * c + i, 4 * c + (i ^ flip[c, step])) for c in range(2) for i in range(4)
        ]
    return (axis, "c"), [
        (2 * i + c, 2 * (i ^ flip[c, step]) + c) for c in range(2) for i in range(4)
    ]


def paired(block, axis, step):
    names, moves = pairs(axis, step)
    return lax.ppermute(block, names, moves)


def place(own, other, c):
    apart = own ^ other
    odd = jnp.where(c == 0, (5 - apart) // 2, (apart + 1) // 2)
    return jnp.where(apart == 0, 0, jnp.where(apart == 2, 3, odd))


def added(*terms):
    total = terms[0].astype(F32)
    for term in terms[1:]:
        total = total + term.astype(F32)
    return total


def pick(array, index, axis):
    return lax.dynamic_index_in_dim(array, index, axis, keepdims=False)


def terms_kernel(where, grad, hidden, normed, pre_grad, keep, send):
    part = keep.shape[3]
    c = where[16]

    def block(g, _):
        columns = pl.ds(pl.multiple_of(g * 4 * part, 4 * part), 4 * part)
        at_z, there_z = where[4 + g // 2], where[12 + g // 2]
        for k, (left, right) in enumerate(((grad, hidden), (normed, pre_grad))):
            term = lax.dot_general(
                left[:, columns], right[...], (((0,), (0,)), ((), ())), preferred_element_type=F32
            ).astype(BF16)
            for pair in range(2):
                at_y = where[2 * (g % 2) + pair]
                there_y = where[8 + 2 * (g % 2) + pair]
                low = term[2 * pair * part : (2 * pair + 1) * part]
                high = term[(2 * pair + 1) * part : (2 * pair + 2) * part]

                @pl.when(c == 0)
                def _():
                    keep[at_y, at_z, k] = low
                    send[there_y, there_z, k] = high

                @pl.when(c == 1)
                def _():
                    keep[at_y, at_z, k] = high
                    send[there_y, there_z, k] = low

        return 0

    lax.fori_loop(0, 8, block, 0)


def term_halves(where, grad, hidden, normed, pre_grad):
    tokens, width = grad.shape
    hidden_width = hidden.shape[1]
    half = jax.ShapeDtypeStruct((4, 4, 2, width // 32, hidden_width), BF16)
    vmem = pl.BlockSpec(memory_space=pltpu.VMEM)
    return pl.pallas_call(
        terms_kernel,
        out_shape=(half, half),
        in_specs=[pl.BlockSpec(memory_space=pltpu.SMEM)] + [vmem] * 4,
        out_specs=(vmem, vmem),
        compiler_params=pltpu.CompilerParams(vmem_limit_bytes=32 * 1024 * 1024),
        cost_estimate=pl.CostEstimate(
            flops=4 * tokens * width * hidden_width,
            bytes_accessed=8 * width * hidden_width,
            transcendentals=0,
        ),
    )(where, grad, hidden, normed, pre_grad)


def shards(layer_input, out_grad, norm_gain_vector, up_weight, down_weight):
    nx, nzl = SIZES[3:]
    rows, width = layer_input.shape
    hidden_width = up_weight.shape[1]
    zh, y, c = lax.axis_index("zh"), lax.axis_index("y"), lax.axis_index("c")
    x, zl = lax.axis_index("x"), lax.axis_index("zl")

    xf = layer_input.astype(F32)
    centered = xf - jnp.mean(xf, axis=1, keepdims=True)
    rstd = 1.0 / jnp.sqrt(jnp.mean(centered * centered, axis=1, keepdims=True) + 1e-06)
    xhat = centered * rstd
    normed = (xhat * norm_gain_vector).astype(BF16)

    pair = jnp.stack([normed, out_grad])
    for distance in (4, 2, 1):
        pair = jnp.concatenate([pair, swap(pair, distance)], axis=1)
    middle = nzl * rows
    pair = lax.optimization_barrier(pair.reshape(2 * middle, width))
    left, right = shift(pair, 1), shift(pair, -1)
    across_normed, across_grad = shift(left[:middle], 1), shift(right[middle:], -1)
    normed_all = jnp.concatenate([pair[:middle], left[:middle], right[:middle], across_normed])
    grad_all = jnp.concatenate([pair[middle:], left[middle:], right[middle:], across_grad])

    pre = jnp.dot(normed_all, up_weight, preferred_element_type=F32)
    value, slope = gelu_parts(pre)
    hidden = value.astype(BF16)
    hidden_grad = jnp.einsum("td,fd->tf", grad_all, down_weight, preferred_element_type=F32)
    pre_grad = (hidden_grad * slope).astype(BF16)

    blocks = pre_grad.reshape(nx, middle, hidden_width)
    near, far = jnp.where(x % 2 == 0, 2, 1), jnp.where(x % 2 == 0, 1, 2)
    first, second = jnp.where(c == 0, near, far), jnp.where(c == 0, far, near)
    blocks = jnp.stack([blocks[0], pick(blocks, second, 0), pick(blocks, first, 0), blocks[3]])
    full_term = jnp.einsum("xtf,df->xtd", blocks, up_weight, preferred_element_type=F32)
    full_term = full_term.astype(BF16)
    x_first = paired(full_term[2:], "x", 0)
    x_second = paired(added(full_term[1], x_first[1]).astype(BF16), "x", 1)
    own = added(full_term[0], x_first[0], x_second)
    for distance in (1, 2, 4):
        half = own.shape[0] // 2
        own = added(own[:half], swap(own[half:].astype(BF16), distance))
    normed_grad = own


    four = jnp.arange(4)
    where = [place(own, four, core) for core in (c, 1 - c) for own in (y, zh)]
    where = jnp.concatenate(where + [c[None]]).astype(jnp.int32)
    keep, send = term_halves(where, grad_all, hidden, normed_all, pre_grad)
    core = lax.ppermute(send, "c", [(0, 1), (1, 0)])

    y_first = paired(added(keep[2:], core[2:]).astype(BF16), "y", 0)
    y_second = paired(added(keep[1], core[1], y_first[1]).astype(BF16), "y", 1)

    def summed(at):
        return added(keep[0, at], core[0, at], y_first[0, at], y_second[at])

    z_first = paired(summed(slice(2, 4)).astype(BF16), "zh", 0)
    z_second = paired(added(summed(1), z_first[1]).astype(BF16), "zh", 1)
    total = added(summed(0), z_first[0], z_second)
    down_grad, up_grad = total[0].T, total[1]

    g = normed_grad * norm_gain_vector
    back = rstd * (
        g
        - jnp.mean(g, axis=1, keepdims=True)
        - xhat * jnp.mean(g * xhat, axis=1, keepdims=True)
    )
    input_grad = (out_grad.astype(F32) + back).astype(BF16)
    return (input_grad, up_grad, down_grad)


def solution(mesh):
    fine = Mesh(mesh.devices.reshape(SIZES), NAMES)
    dp, mp, both = ("zh", "y", "c"), ("x", "zl"), NAMES
    return jax.shard_map(
        shards,
        mesh=fine,
        in_specs=(P(both, None), P(both, None), P(), P(None, mp), P(mp, None)),
        out_specs=(P(both, None), P(dp, mp), P(mp, dp)),
        check_vma=False,
    )
```

time: 237 us -> 211 us (0.89)
  starting transfers between devices: 131 us -> 88.6 us
  waiting for transfers between devices: 50.2 us -> 92.1 us
  local copies, waits for them, and re-layouts: 30.4 us -> 2.52 us
  Pallas kernels: 0 us -> 7.32 us
  matrix products: 6.63 us -> 2.76 us
    ppermute x11 -> x4, starting transfers between devices: 39.7 us -> 11.7 us  [shift(): return lax.ppermute(block, 'x', [(i, (i + distance) % 4) for i in range(4)])]
    concatenate x2 -> x1, local copies, waits for them, and re-layouts: 23.9 us -> 0.08 us  [shards(): where = jnp.concatenate(where + [c[None]]).astype(jnp.int32)]
    ppermute x5 -> x7, waiting for transfers between devices: 30.1 us -> 47.4 us  [the longest x6 47.4 us: paired(): return lax.ppermute(block, names, moves)]
    ppermute x9 -> x6, waiting for transfers between devices: 12.9 us -> 28.8 us  [swap(): return lax.ppermute(block, 'zl', [(i, i ^ distance) for i in range(8)])]
    ppermute x9 -> x6, starting transfers between devices: 41.8 us -> 32.6 us  [swap(): return lax.ppermute(block, 'zl', [(i, i ^ distance) for i in range(8)])]
    ppermute x11 -> x4, waiting for transfers between devices: 7.14 us -> 15.9 us  [shift(): return lax.ppermute(block, 'x', [(i, (i + distance) % 4) for i in range(4)])]
    pallas_call x0 -> x1, Pallas kernels: none -> 7.32 us  [term_halves(): pl.pallas_call(terms_kernel, out_shape=(half, half), in_specs=[pl.BlockSp...]
    all_to_all x1 -> x0, starting transfers between devices: 4.49 us -> none  [shards(): terms = lax.all_to_all(terms, 'y', 0, 0)]
  transfers between devices with their start and end apart: 26 -> 17, of which waited for: 11 -> 11; matrix products, arithmetic and copies ran while one was open for 11% -> 4% of each run, Pallas kernels for 0% -> 0%
where the time goes in v4:
time: 211 us; the launch traced here: 208 us
  waiting for transfers between devices  92.1 us (44%)
  starting transfers between devices  88.6 us (42%)
  other arithmetic  13.9 us (7%)
  Pallas kernels  7.32 us (3%)
  matrix products  2.76 us (1%)
  local copies, waits for them, and re-layouts  2.52 us (1%)
    ppermute x6, waiting for transfers between devices, paired(): return lax.ppermute(block, names, moves)  47.4 us
    ppermute x6, starting transfers between devices, paired(): return lax.ppermute(block, names, moves)  42.4 us
    ppermute x6, starting transfers between devices, swap(): return lax.ppermute(block, 'zl', [(i, i ^ distance) for i in range(8)])  32.6 us
    ppermute x6, waiting for transfers between devices, swap(): return lax.ppermute(block, 'zl', [(i, i ^ distance) for i in range(8)])  28.8 us
    ppermute x4, waiting for transfers between devices, shift(): return lax.ppermute(block, 'x', [(i, (i + distance) % 4) for i in range(4)])  15.9 us
    ppermute x4, starting transfers between devices, shift(): return lax.ppermute(block, 'x', [(i, (i + distance) % 4) for i in range(4)])  11.7 us
    pallas_call x1, Pallas kernels, term_halves(): pl.pallas_call(terms_kernel, out_shape=(half, half), in_specs=[pl.BlockSp...  7.32 us
  transfers between devices with their start and end apart: 17, of which 11 were waited for; matrix products, arithmetic and copies ran while one was open for 4% of the time, Pallas kernels for 0%

profile of v4, /device:TPU:6, one launch (start us, length us, event | category | flops | bytes accessed | tf_op | source)
XLA Modules:
  0.0 208.4 jit_solution(10125561848878858836)
XLA Ops:
  4.5 9.1 %collective-permute-start = (bf16[2,6,3072]{2,1,0:T(8,128)(2,1)S(1)}, bf16[2,6,3072]{2,1,0:T(8,128)(2,1)S(1)}, u32[]{:S(2)}, u32[]{:S(2)}) collective-permute-start(bf16[2,6,3072]{2,1,0:T(8,128)(2,1)S(1)} %pad_maximum_fusion.5), channel_id=1, source_target_pairs={{0,4},{1,5},{2,6},{3,7},{4,0},{5,1},{6,2},{7,3},{8,12},{9,13},{10,... | collective-permute-start | bytes 221192 | tf_op jit(solution)/shard_map/ppermute | solution.py:22
  13.6 9.1 %collective-permute-done = bf16[2,6,3072]{2,1,0:T(8,128)(2,1)S(1)} collective-permute-done((bf16[2,6,3072]{2,1,0:T(8,128)(2,1)S(1)}, bf16[2,6,3072]{2,1,0:T(8,128)(2,1)S(1)}, u32[]{:S(2)}, u32[]{:S(2)}) %collective-permute-start) | collective-permute-done | bytes 73760 | tf_op jit(solution)/shard_map/ppermute | solution.py:22
  23.5 1.9 collective-permute-start.1
  25.5 9.7 %collective-permute-done.1 = bf16[2,12,3072]{2,1,0:T(8,128)(2,1)S(1)} collective-permute-done((bf16[2,12,3072]{2,1,0:T(8,128)(2,1)S(1)}, bf16[2,12,3072]{2,1,0:T(8,128)(2,1)S(1)}, u32[]{:S(2)}, u32[]{:S(2)}) %collective-permute-start.1) | collective-permute-done | bytes 147488 | tf_op jit(solution)/shard_map/ppermute | solution.py:22
  36.1 1.9 collective-permute-start.2
  38.1 6.9 %collective-permute-done.2 = bf16[2,24,3072]{2,1,0:T(8,128)(2,1)S(1)} collective-permute-done((bf16[2,24,3072]{2,1,0:T(8,128)(2,1)S(1)}, bf16[2,24,3072]{2,1,0:T(8,128)(2,1)S(1)}, u32[]{:S(2)}, u32[]{:S(2)}) %collective-permute-start.2) | collective-permute-done | bytes 294944 | tf_op jit(solution)/shard_map/ppermute | solution.py:22
  46.0 3.9 %collective-permute-start.3 = (bf16[96,3072]{1,0:T(8,128)(2,1)S(1)}, bf16[96,3072]{1,0:T(8,128)(2,1)S(1)}, u32[]{:S(2)}, u32[]{:S(2)}) collective-permute-start(bf16[96,3072]{1,0:T(8,128)(2,1)S(1)} %bitcast.56), channel_id=1, source_target_pairs={{0,8},{8,16},{16,24},{24,0},{1,9},{9,17},{17,25},{25,1},{2,10},{10... | collective-permute-start | bytes 1769480 | tf_op jit(solution)/shard_map/ppermute | solution.py:26
  49.9 1.9 collective-permute-start.4
  51.9 9.5 %collective-permute-done.3 = bf16[96,3072]{1,0:T(8,128)(2,1)S(1)} collective-permute-done((bf16[96,3072]{1,0:T(8,128)(2,1)S(1)}, bf16[96,3072]{1,0:T(8,128)(2,1)S(1)}, u32[]{:S(2)}, u32[]{:S(2)}) %collective-permute-start.3) | collective-permute-done | bytes 589856 | tf_op jit(solution)/shard_map/ppermute | solution.py:26
  61.4 3.4 %collective-permute-start.6 = (bf16[48,3072]{1,0:T(8,128)(2,1)S(1)}, bf16[48,3072]{1,0:T(8,128)(2,1)S(1)}, u32[]{:S(2)}, u32[]{:S(2)}) collective-permute-start(bf16[48,3072]{1,0:T(8,128)(2,1)S(1)} %get-tuple-element.12), channel_id=1, source_target_pairs={{0,8},{8,16},{16,24},{24,0},{1,9},{9,17},{17,25},{25,1},{2,10},{10... | collective-permute-start | bytes 884744 | tf_op jit(solution)/shard_map/ppermute | solution.py:26
  64.9 2.4 %collective-permute-start.5 = (bf16[48,3072]{1,0:T(8,128)(2,1)S(1)}, bf16[48,3072]{1,0:T(8,128)(2,1)S(1)}, u32[]{:S(2)}, u32[]{:S(2)}) collective-permute-start(bf16[48,3072]{1,0:T(8,128)(2,1)S(1)} %get-tuple-element.13), channel_id=1, source_target_pairs={{0,24},{8,0},{16,8},{24,16},{1,25},{9,1},{17,9},{25,17},{2,26},{10... | collective-permute-start | bytes 884744 | tf_op jit(solution)/shard_map/ppermute | solution.py:26
  67.3 2.7 %collective-permute-done.6 = bf16[48,3072]{1,0:T(8,128)(2,1)S(1)} collective-permute-done((bf16[48,3072]{1,0:T(8,128)(2,1)S(1)}, bf16[48,3072]{1,0:T(8,128)(2,1)S(1)}, u32[]{:S(2)}, u32[]{:S(2)}) %collective-permute-start.6) | collective-permute-done | bytes 294944 | tf_op jit(solution)/shard_map/ppermute | solution.py:26
  71.0 3.8 %collective-permute-done.5 = bf16[48,3072]{1,0:T(8,128)(2,1)S(1)} collective-permute-done((bf16[48,3072]{1,0:T(8,128)(2,1)S(1)}, bf16[48,3072]{1,0:T(8,128)(2,1)S(1)}, u32[]{:S(2)}, u32[]{:S(2)}) %collective-permute-start.5) | collective-permute-done | bytes 294944 | tf_op jit(solution)/shard_map/ppermute | solution.py:26
  75.8 7.3 %shard_map.76 = (bf16[4,4,2,96,384]{4,3,2,1,0:T(8,128)(2,1)S(1)}, bf16[4,4,2,96,384]{4,3,2,1,0:T(8,128)(2,1)}) custom-call(s32[17]{0:T(128)S(1)} %concatenate.25.where, bf16[192,3072]{1,0:T(8,128)(2,1)S(1)} %pad_maximum_fusion.grad, bf16[192,384]{1,0:T(8,128)(2,1)S(1)} %get-tuple-element.21.hidden, bf16[192,3072]{1,0:T(8,128)(2,1)S(1)} %pad_maximum_fusion.1.normed, ...), custom_call_target="tpu_custom_call" | custom-call | flops 905969664 | bytes 9437184 | tf_op jit(solution)/shard_map/pallas_call | solution.py:99
  83.1 1.4 copy-done.1
  84.5 1.9 collective-permute-start.12
  87.5 1.9 collective-permute-start.7
  89.5 9.8 %collective-permute-done.7 = bf16[2,48,3072]{2,1,0:T(8,128)(2,1)S(1)} collective-permute-done((bf16[2,48,3072]{2,1,0:T(8,128)(2,1)S(1)}, bf16[2,48,3072]{2,1,0:T(8,128)(2,1)S(1)}, u32[]{:S(2)}, u32[]{:S(2)}) %collective-permute-start.7) | collective-permute-done | bytes 589856 | tf_op jit(solution)/shard_map/ppermute | solution.py:42
  99.4 2.4 %collective-permute-start.8 = (bf16[48,3072]{1,0:T(8,128)(2,1)S(1)}, bf16[48,3072]{1,0:T(8,128)(2,1)S(1)}, u32[]{:S(2)}, u32[]{:S(2)}) collective-permute-start(bf16[48,3072]{1,0:T(8,128)(2,1)S(1)} %fusion.8), channel_id=1, source_target_pairs={{0,24},{8,16},{16,8},{24,0},{32,40},{40,32},{48,56},{56,48},{1,25}... | collective-permute-start | bytes 884744 | tf_op jit(solution)/shard_map/ppermute | solution.py:42
  101.8 1.6 add_convert_fusion
  103.4 3.7 %collective-permute-start.13 = (bf16[2,4,2,96,384]{4,3,2,1,0:T(8,128)(2,1)S(1)}, bf16[2,4,2,96,384]{4,3,2,1,0:T(8,128)(2,1)S(1)}, u32[]{:S(2)}, u32[]{:S(2)}) collective-permute-start(bf16[2,4,2,96,384]{4,3,2,1,0:T(8,128)(2,1)S(1)} %add_convert_fusion), channel_id=1, source_target_pairs={{0,64},{64,0},{128,192},{192,128},{32,224},{96,160},{160,96},{224,... | collective-permute-start | bytes 3538952 | tf_op jit(solution)/shard_map/ppermute | solution.py:42
  107.1 2.1 %collective-permute-done.8 = bf16[48,3072]{1,0:T(8,128)(2,1)S(1)} collective-permute-done((bf16[48,3072]{1,0:T(8,128)(2,1)S(1)}, bf16[48,3072]{1,0:T(8,128)(2,1)S(1)}, u32[]{:S(2)}, u32[]{:S(2)}) %collective-permute-start.8) | collective-permute-done | bytes 294944 | tf_op jit(solution)/shard_map/ppermute | solution.py:42
  109.3 4.4 %collective-permute-start.9 = (bf16[24,3072]{1,0:T(8,128)(2,1)S(1)}, bf16[24,3072]{1,0:T(8,128)(2,1)S(1)}, u32[]{:S(2)}, u32[]{:S(2)}) collective-permute-start(bf16[24,3072]{1,0:T(8,128)(2,1)S(1)} %slice.257), channel_id=1, source_target_pairs={{0,1},{1,0},{2,3},{3,2},{4,5},{5,4},{6,7},{7,6},{8,9},{9,8},{10,11... | collective-permute-start | bytes 442376 | tf_op jit(solution)/shard_map/ppermute | solution.py:22
  113.7 3.1 %collective-permute-done.9 = bf16[24,3072]{1,0:T(8,128)(2,1)S(1)} collective-permute-done((bf16[24,3072]{1,0:T(8,128)(2,1)S(1)}, bf16[24,3072]{1,0:T(8,128)(2,1)S(1)}, u32[]{:S(2)}, u32[]{:S(2)}) %collective-permute-start.9) | collective-permute-done | bytes 147488 | tf_op jit(solution)/shard_map/ppermute | solution.py:22
  117.0 7.0 %collective-permute-start.10 = (bf16[12,3072]{1,0:T(8,128)(2,1)S(1)}, bf16[12,3072]{1,0:T(8,128)(2,1)S(1)}, u32[]{:S(2)}, u32[]{:S(2)}) collective-permute-start(bf16[12,3072]{1,0:T(8,128)(2,1)S(1)} %slice.258), channel_id=1, source_target_pairs={{0,2},{1,3},{2,0},{3,1},{4,6},{5,7},{6,4},{7,5},{8,10},{9,11},{10,... | collective-permute-start | bytes 221192 | tf_op jit(solution)/shard_map/ppermute | solution.py:22
  124.0 1.3 fusion.2
  125.3 4.8 %collective-permute-start.14 = (bf16[4,2,96,384]{3,2,1,0:T(8,128)(2,1)S(1)}, bf16[4,2,96,384]{3,2,1,0:T(8,128)(2,1)S(1)}, u32[]{:S(2)}, u32[]{:S(2)}) collective-permute-start(bf16[4,2,96,384]{3,2,1,0:T(8,128)(2,1)S(1)} %fusion.2), channel_id=1, source_target_pairs={{0,192},{64,128},{128,64},{192,0},{32,96},{96,32},{160,224},{224,1... | collective-permute-start | bytes 1769480 | tf_op jit(solution)/shard_map/ppermute | solution.py:42
  130.1 8.3 %collective-permute-start.11 = (bf16[6,3072]{1,0:T(8,128)(2,1)S(1)}, bf16[6,3072]{1,0:T(8,128)(2,1)S(1)}, u32[]{:S(2)}, u32[]{:S(2)}) collective-permute-start(bf16[6,3072]{1,0:T(8,128)(2,1)S(1)} %slice.259), channel_id=1, source_target_pairs={{0,4},{1,5},{2,6},{3,7},{4,0},{5,1},{6,2},{7,3},{8,12},{9,13},{10,... | collective-permute-start | bytes 110600 | tf_op jit(solution)/shard_map/ppermute | solution.py:22
  139.5 15.7 %collective-permute-start.15 = (bf16[2,2,96,384]{3,2,1,0:T(8,128)(2,1)S(1)}, bf16[2,2,96,384]{3,2,1,0:T(8,128)(2,1)S(1)}, u32[]{:S(2)}, u32[]{:S(2)}) collective-permute-start(bf16[2,2,96,384]{3,2,1,0:T(8,128)(2,1)S(1)} %fusion.3), channel_id=1, source_target_pairs={{0,256},{256,0},{512,768},{768,512},{32,800},{288,544},{544,288},{... | collective-permute-start | bytes 884744 | tf_op jit(solution)/shard_map/ppermute | solution.py:42
  155.5 26.6 %collective-permute-done.15 = bf16[2,2,96,384]{3,2,1,0:T(8,128)(2,1)S(1)} collective-permute-done((bf16[2,2,96,384]{3,2,1,0:T(8,128)(2,1)S(1)}, bf16[2,2,96,384]{3,2,1,0:T(8,128)(2,1)S(1)}, u32[]{:S(2)}, u32[]{:S(2)}) %collective-permute-start.15) | collective-permute-done | bytes 294944 | tf_op jit(solution)/shard_map/ppermute | solution.py:42
  183.1 13.9 %collective-permute-start.16 = (bf16[2,96,384]{2,1,0:T(8,128)(2,1)S(1)}, bf16[2,96,384]{2,1,0:T(8,128)(2,1)S(1)}, u32[]{:S(2)}, u32[]{:S(2)}) collective-permute-start(bf16[2,96,384]{2,1,0:T(8,128)(2,1)S(1)} %fusion.9), channel_id=1, source_target_pairs={{0,768},{256,512},{512,256},{768,0},{32,288},{288,32},{544,800},{8... | collective-permute-start | bytes 442376 | tf_op jit(solution)/shard_map/ppermute | solution.py:42
  197.7 8.9 %collective-permute-done.16 = bf16[2,96,384]{2,1,0:T(8,128)(2,1)S(1)} collective-permute-done((bf16[2,96,384]{2,1,0:T(8,128)(2,1)S(1)}, bf16[2,96,384]{2,1,0:T(8,128)(2,1)S(1)}, u32[]{:S(2)}, u32[]{:S(2)}) %collective-permute-start.16) | collective-permute-done | bytes 147488 | tf_op jit(solution)/shard_map/ppermute | solution.py:42
  (56 shorter events, 14.9 us)
Async XLA Ops:
  0.6 69.5 %copy-start = (bf16[3072,384]{1,0:T(8,128)(2,1)S(1)}, bf16[3072,384]{1,0:T(8,128)(2,1)}, u32[]{:S(2)}) copy-start(bf16[3072,384]{1,0:T(8,128)(2,1)} %param.8) | copy-start | bytes 7077892
  4.5 18.2 %collective-permute-start = (bf16[2,6,3072]{2,1,0:T(8,128)(2,1)S(1)}, bf16[2,6,3072]{2,1,0:T(8,128)(2,1)S(1)}, u32[]{:S(2)}, u32[]{:S(2)}) collective-permute-start(bf16[2,6,3072]{2,1,0:T(8,128)(2,1)S(1)} %pad_maximum_fusion.5), channel_id=1, source_target_pairs={{0,4},{1,5},{2,6},{3,7},{4,0},{5,1},{6,2},{7,3},{8,12},{9,13},{10,... | collective-permute-start | bytes 221192 | tf_op jit(solution)/shard_map/ppermute | solution.py:22
  23.5 11.6 %collective-permute-start.1 = (bf16[2,12,3072]{2,1,0:T(8,128)(2,1)S(1)}, bf16[2,12,3072]{2,1,0:T(8,128)(2,1)S(1)}, u32[]{:S(2)}, u32[]{:S(2)}) collective-permute-start(bf16[2,12,3072]{2,1,0:T(8,128)(2,1)S(1)} %pad_maximum_fusion.4), channel_id=1, source_target_pairs={{0,2},{1,3},{2,0},{3,1},{4,6},{5,7},{6,4},{7,5},{8,10},{9,11},{10,... | collective-permute-start | bytes 442376 | tf_op jit(solution)/shard_map/ppermute | solution.py:22
  36.1 9.0 %collective-permute-start.2 = (bf16[2,24,3072]{2,1,0:T(8,128)(2,1)S(1)}, bf16[2,24,3072]{2,1,0:T(8,128)(2,1)S(1)}, u32[]{:S(2)}, u32[]{:S(2)}) collective-permute-start(bf16[2,24,3072]{2,1,0:T(8,128)(2,1)S(1)} %pad_maximum_fusion.3), channel_id=1, source_target_pairs={{0,1},{1,0},{2,3},{3,2},{4,5},{5,4},{6,7},{7,6},{8,9},{9,8},{10,11... | collective-permute-start | bytes 884744 | tf_op jit(solution)/shard_map/ppermute | solution.py:22
  46.0 15.4 %collective-permute-start.3 = (bf16[96,3072]{1,0:T(8,128)(2,1)S(1)}, bf16[96,3072]{1,0:T(8,128)(2,1)S(1)}, u32[]{:S(2)}, u32[]{:S(2)}) collective-permute-start(bf16[96,3072]{1,0:T(8,128)(2,1)S(1)} %bitcast.56), channel_id=1, source_target_pairs={{0,8},{8,16},{16,24},{24,0},{1,9},{9,17},{17,25},{25,1},{2,10},{10... | collective-permute-start | bytes 1769480 | tf_op jit(solution)/shard_map/ppermute | solution.py:26
  49.9 14.9 %collective-permute-start.4 = (bf16[96,3072]{1,0:T(8,128)(2,1)S(1)}, bf16[96,3072]{1,0:T(8,128)(2,1)S(1)}, u32[]{:S(2)}, u32[]{:S(2)}) collective-permute-start(bf16[96,3072]{1,0:T(8,128)(2,1)S(1)} %bitcast.57), channel_id=1, source_target_pairs={{0,24},{8,0},{16,8},{24,16},{1,25},{9,1},{17,9},{25,17},{2,26},{10... | collective-permute-start | bytes 1769480 | tf_op jit(solution)/shard_map/ppermute | solution.py:26
  61.4 8.6 %collective-permute-start.6 = (bf16[48,3072]{1,0:T(8,128)(2,1)S(1)}, bf16[48,3072]{1,0:T(8,128)(2,1)S(1)}, u32[]{:S(2)}, u32[]{:S(2)}) collective-permute-start(bf16[48,3072]{1,0:T(8,128)(2,1)S(1)} %get-tuple-element.12), channel_id=1, source_target_pairs={{0,8},{8,16},{16,24},{24,0},{1,9},{9,17},{17,25},{25,1},{2,10},{10... | collective-permute-start | bytes 884744 | tf_op jit(solution)/shard_map/ppermute | solution.py:26
  64.9 9.8 %collective-permute-start.5 = (bf16[48,3072]{1,0:T(8,128)(2,1)S(1)}, bf16[48,3072]{1,0:T(8,128)(2,1)S(1)}, u32[]{:S(2)}, u32[]{:S(2)}) collective-permute-start(bf16[48,3072]{1,0:T(8,128)(2,1)S(1)} %get-tuple-element.13), channel_id=1, source_target_pairs={{0,24},{8,0},{16,8},{24,16},{1,25},{9,1},{17,9},{25,17},{2,26},{10... | collective-permute-start | bytes 884744 | tf_op jit(solution)/shard_map/ppermute | solution.py:26
  71.0 3.8 %copy-start.6 = (bf16[384,3072]{1,0:T(8,128)(2,1)S(1)}, bf16[384,3072]{1,0:T(8,128)(2,1)}, u32[]{:S(2)}) copy-start(bf16[384,3072]{1,0:T(8,128)(2,1)} %param.9) | copy-start | bytes 7077892
  83.1 1.4 copy-start.1
  84.5 17.3 %collective-permute-start.12 = (bf16[4,4,2,96,384]{4,3,2,1,0:T(8,128)(2,1)}, bf16[4,4,2,96,384]{4,3,2,1,0:T(8,128)(2,1)}, u32[]{:S(2)}, u32[]{:S(2)}) collective-permute-start(bf16[4,4,2,96,384]{4,3,2,1,0:T(8,128)(2,1)} %get-tuple-element.6), channel_id=1, source_target_pairs={{0,32},{32,0},{1,33},{33,1},{2,34},{34,2},{3,35},{35,3},{4,36},{36... | collective-permute-start | bytes 7077896 | tf_op jit(solution)/shard_map/ppermute | solution.py:161
  86.5 15.3 %copy-start.2 = (bf16[4,4,2,96,384]{4,3,2,1,0:T(8,128)(2,1)S(1)}, bf16[4,4,2,96,384]{4,3,2,1,0:T(8,128)(2,1)}, u32[]{:S(2)}) copy-start(bf16[4,4,2,96,384]{4,3,2,1,0:T(8,128)(2,1)} %copy-done.1) | copy-start | bytes 7077892
  87.5 11.8 %collective-permute-start.7 = (bf16[2,48,3072]{2,1,0:T(8,128)(2,1)S(1)}, bf16[2,48,3072]{2,1,0:T(8,128)(2,1)S(1)}, u32[]{:S(2)}, u32[]{:S(2)}) collective-permute-start(bf16[2,48,3072]{2,1,0:T(8,128)(2,1)S(1)} %slice.182), channel_id=1, source_target_pairs={{0,8},{8,0},{16,24},{24,16},{32,56},{40,48},{48,40},{56,32},{1,9},... | collective-permute-start | bytes 1769480 | tf_op jit(solution)/shard_map/ppermute | solution.py:42
  99.4 9.8 %collective-permute-start.8 = (bf16[48,3072]{1,0:T(8,128)(2,1)S(1)}, bf16[48,3072]{1,0:T(8,128)(2,1)S(1)}, u32[]{:S(2)}, u32[]{:S(2)}) collective-permute-start(bf16[48,3072]{1,0:T(8,128)(2,1)S(1)} %fusion.8), channel_id=1, source_target_pairs={{0,24},{8,16},{16,8},{24,0},{32,40},{40,32},{48,56},{56,48},{1,25}... | collective-permute-start | bytes 884744 | tf_op jit(solution)/shard_map/ppermute | solution.py:42
  103.4 20.5 %collective-permute-start.13 = (bf16[2,4,2,96,384]{4,3,2,1,0:T(8,128)(2,1)S(1)}, bf16[2,4,2,96,384]{4,3,2,1,0:T(8,128)(2,1)S(1)}, u32[]{:S(2)}, u32[]{:S(2)}) collective-permute-start(bf16[2,4,2,96,384]{4,3,2,1,0:T(8,128)(2,1)S(1)} %add_convert_fusion), channel_id=1, source_target_pairs={{0,64},{64,0},{128,192},{192,128},{32,224},{96,160},{160,96},{224,... | collective-permute-start | bytes 3538952 | tf_op jit(solution)/shard_map/ppermute | solution.py:42
  109.3 7.5 %collective-permute-start.9 = (bf16[24,3072]{1,0:T(8,128)(2,1)S(1)}, bf16[24,3072]{1,0:T(8,128)(2,1)S(1)}, u32[]{:S(2)}, u32[]{:S(2)}) collective-permute-start(bf16[24,3072]{1,0:T(8,128)(2,1)S(1)} %slice.257), channel_id=1, source_target_pairs={{0,1},{1,0},{2,3},{3,2},{4,5},{5,4},{6,7},{7,6},{8,9},{9,8},{10,11... | collective-permute-start | bytes 442376 | tf_op jit(solution)/shard_map/ppermute | solution.py:22
  116.9 38.4 %copy-start.4 = (bf16[6,3072]{1,0:T(8,128)(2,1)S(1)}, bf16[6,3072]{1,0:T(8,128)(2,1)}, u32[]{:S(2)}) copy-start(bf16[6,3072]{1,0:T(8,128)(2,1)} %param.5) | copy-start | bytes 110596
  116.9 38.4 %copy-start.5 = (f32[3072]{0:T(1024)S(1)}, f32[3072]{0:T(1024)}, u32[]{:S(2)}) copy-start(f32[3072]{0:T(1024)} %param.7) | copy-start | bytes 36868
  116.9 80.1 %copy-start.3 = (bf16[6,3072]{1,0:T(8,128)(2,1)S(1)}, bf16[6,3072]{1,0:T(8,128)(2,1)}, u32[]{:S(2)}) copy-start(bf16[6,3072]{1,0:T(8,128)(2,1)} %param.6) | copy-start | bytes 110596
  117.0 13.1 %collective-permute-start.10 = (bf16[12,3072]{1,0:T(8,128)(2,1)S(1)}, bf16[12,3072]{1,0:T(8,128)(2,1)S(1)}, u32[]{:S(2)}, u32[]{:S(2)}) collective-permute-start(bf16[12,3072]{1,0:T(8,128)(2,1)S(1)} %slice.258), channel_id=1, source_target_pairs={{0,2},{1,3},{2,0},{3,1},{4,6},{5,7},{6,4},{7,5},{8,10},{9,11},{10,... | collective-permute-start | bytes 221192 | tf_op jit(solution)/shard_map/ppermute | solution.py:22
  125.3 13.2 %collective-permute-start.14 = (bf16[4,2,96,384]{3,2,1,0:T(8,128)(2,1)S(1)}, bf16[4,2,96,384]{3,2,1,0:T(8,128)(2,1)S(1)}, u32[]{:S(2)}, u32[]{:S(2)}) collective-permute-start(bf16[4,2,96,384]{3,2,1,0:T(8,128)(2,1)S(1)} %fusion.2), channel_id=1, source_target_pairs={{0,192},{64,128},{128,64},{192,0},{32,96},{96,32},{160,224},{224,1... | collective-permute-start | bytes 1769480 | tf_op jit(solution)/shard_map/ppermute | solution.py:42
  130.1 25.2 %collective-permute-start.11 = (bf16[6,3072]{1,0:T(8,128)(2,1)S(1)}, bf16[6,3072]{1,0:T(8,128)(2,1)S(1)}, u32[]{:S(2)}, u32[]{:S(2)}) collective-permute-start(bf16[6,3072]{1,0:T(8,128)(2,1)S(1)} %slice.259), channel_id=1, source_target_pairs={{0,4},{1,5},{2,6},{3,7},{4,0},{5,1},{6,2},{7,3},{8,12},{9,13},{10,... | collective-permute-start | bytes 110600 | tf_op jit(solution)/shard_map/ppermute | solution.py:22
  139.5 42.6 %collective-permute-start.15 = (bf16[2,2,96,384]{3,2,1,0:T(8,128)(2,1)S(1)}, bf16[2,2,96,384]{3,2,1,0:T(8,128)(2,1)S(1)}, u32[]{:S(2)}, u32[]{:S(2)}) collective-permute-start(bf16[2,2,96,384]{3,2,1,0:T(8,128)(2,1)S(1)} %fusion.3), channel_id=1, source_target_pairs={{0,256},{256,0},{512,768},{768,512},{32,800},{288,544},{544,288},{... | collective-permute-start | bytes 884744 | tf_op jit(solution)/shard_map/ppermute | solution.py:42
  183.1 23.5 %collective-permute-start.16 = (bf16[2,96,384]{2,1,0:T(8,128)(2,1)S(1)}, bf16[2,96,384]{2,1,0:T(8,128)(2,1)S(1)}, u32[]{:S(2)}, u32[]{:S(2)}) collective-permute-start(bf16[2,96,384]{2,1,0:T(8,128)(2,1)S(1)} %fusion.9), channel_id=1, source_target_pairs={{0,768},{256,512},{512,256},{768,0},{32,288},{288,32},{544,800},{8... | collective-permute-start | bytes 442376 | tf_op jit(solution)/shard_map/ppermute | solution.py:42

commit v5 on v4

--- a/solution.py
+++ b/solution.py
@@ -59,55 +59,40 @@
     return lax.dynamic_index_in_dim(array, index, axis, keepdims=False)
 
 
-def terms_kernel(where, grad, hidden, normed, pre_grad, keep, send):
-    part = keep.shape[3]
+def term_kernel(where, left, right, keep, send):
+    part = keep.shape[2]
     c = where[16]
-
-    def block(g, _):
-        columns = pl.ds(pl.multiple_of(g * 4 * part, 4 * part), 4 * part)
-        at_z, there_z = where[4 + g // 2], where[12 + g // 2]
-        for k, (left, right) in enumerate(((grad, hidden), (normed, pre_grad))):
-            term = lax.dot_general(
-                left[:, columns], right[...], (((0,), (0,)), ((), ())), preferred_element_type=F32
-            ).astype(BF16)
-            for pair in range(2):
-                at_y = where[2 * (g % 2) + pair]
-                there_y = where[8 + 2 * (g % 2) + pair]
-                low = term[2 * pair * part : (2 * pair + 1) * part]
-                high = term[(2 * pair + 1) * part : (2 * pair + 2) * part]
-
-                @pl.when(c == 0)
-                def _():
-                    keep[at_y, at_z, k] = low
-                    send[there_y, there_z, k] = high
-
-                @pl.when(c == 1)
-                def _():
-                    keep[at_y, at_z, k] = high
-                    send[there_y, there_z, k] = low
-
-        return 0
-
-    lax.fori_loop(0, 8, block, 0)
-
-
-def term_halves(where, grad, hidden, normed, pre_grad):
-    tokens, width = grad.shape
-    hidden_width = hidden.shape[1]
-    half = jax.ShapeDtypeStruct((4, 4, 2, width // 32, hidden_width), BF16)
+    for g in range(8):
+        columns = slice(4 * part * g, 4 * part * (g + 1))
+        term = lax.dot_general(
+            left[:, columns], right[...], (((0,), (0,)), ((), ())), preferred_element_type=F32
+        ).astype(BF16)
+        for pair in range(2):
+            at_y, there_y = (where[at + 2 * (g % 2) + pair] for at in (0, 8))
+            at_z, there_z = (where[at + g // 2] for at in (4, 12))
+            low = term[2 * pair * part : (2 * pair + 1) * part]
+            high = term[(2 * pair + 1) * part : (2 * pair + 2) * part]
+            keep[at_y, at_z] = jnp.where(c == 0, low, high)
+            send[there_y, there_z] = jnp.where(c == 0, high, low)
+
+
+def term_halves(where, left, right):
+    tokens, width = left.shape
+    hidden_width = right.shape[1]
+    half = jax.ShapeDtypeStruct((4, 4, width // 32, hidden_width), BF16)
     vmem = pl.BlockSpec(memory_space=pltpu.VMEM)
     return pl.pallas_call(
-        terms_kernel,
+        term_kernel,
         out_shape=(half, half),
-        in_specs=[pl.BlockSpec(memory_space=pltpu.SMEM)] + [vmem] * 4,
+        in_specs=[pl.BlockSpec(memory_space=pltpu.SMEM), vmem, vmem],
         out_specs=(vmem, vmem),
-        compiler_params=pltpu.CompilerParams(vmem_limit_bytes=32 * 1024 * 1024),
+        compiler_params=pltpu.CompilerParams(vmem_limit_bytes=12 * 1024 * 1024),
         cost_estimate=pl.CostEstimate(
-            flops=4 * tokens * width * hidden_width,
-            bytes_accessed=8 * width * hidden_width,
+            flops=2 * tokens * width * hidden_width,
+            bytes_accessed=4 * width * hidden_width,
             transcendentals=0,
         ),
-    )(where, grad, hidden, normed, pre_grad)
+    )(where, left, right)
 
 
 def shards(layer_input, out_grad, norm_gain_vector, up_weight, down_weight):
@@ -139,37 +124,59 @@
     hidden_grad = jnp.einsum("td,fd->tf", grad_all, down_weight, preferred_element_type=F32)
     pre_grad = (hidden_grad * slope).astype(BF16)
 
+    four = jnp.arange(4)
+    where = [place(own, four, core) for core in (c, 1 - c) for own in (y, zh)]
+    where = jnp.concatenate(where + [c[None]]).astype(jnp.int32)
+
     blocks = pre_grad.reshape(nx, middle, hidden_width)
     near, far = jnp.where(x % 2 == 0, 2, 1), jnp.where(x % 2 == 0, 1, 2)
     first, second = jnp.where(c == 0, near, far), jnp.where(c == 0, far, near)
     blocks = jnp.stack([blocks[0], pick(blocks, second, 0), pick(blocks, first, 0), blocks[3]])
+
+    fence = lax.optimization_barrier
+    down, up = term_halves(where, grad_all, hidden), term_halves(where, normed_all, pre_grad)
+
+    def to_core(term):
+        return lax.ppermute(term[1], "c", [(0, 1), (1, 0)])
+
+    def to_y(term, core):
+        return paired(added(term[0][2:], core[2:]).astype(BF16), "y", 0)
+
+    def to_second_y(term, core, got):
+        return paired(added(term[0][1], core[1], got[1]).astype(BF16), "y", 1)
+
+    def summed(term, at):
+        keep, core, got, second = term
+        return added(keep[0, at], core[0, at], got[0, at], second[at])
+
+    def to_z(*term):
+        return paired(summed(term, slice(2, 4)).astype(BF16), "zh", 0)
+
+    def to_second_z(term, got):
+        return paired(added(summed(term, 1), got[1]).astype(BF16), "zh", 1)
+
+    down_core, up_core = to_core(down), to_core(up)
+    down_core, blocks = fence((down_core, blocks))
     full_term = jnp.einsum("xtf,df->xtd", blocks, up_weight, preferred_element_type=F32)
     full_term = full_term.astype(BF16)
     x_first = paired(full_term[2:], "x", 0)
+    down_y, up_y = to_y(down, down_core), to_y(up, up_core)
+    down_y, x_first = fence((down_y, x_first))
     x_second = paired(added(full_term[1], x_first[1]).astype(BF16), "x", 1)
     own = added(full_term[0], x_first[0], x_second)
-    for distance in (1, 2, 4):
-        half = own.shape[0] // 2
-        own = added(own[:half], swap(own[half:].astype(BF16), distance))
-    normed_grad = own
-
-
-    four = jnp.arange(4)
-    where = [place(own, four, core) for core in (c, 1 - c) for own in (y, zh)]
-    where = jnp.concatenate(where + [c[None]]).astype(jnp.int32)
-    keep, send = term_halves(where, grad_all, hidden, normed_all, pre_grad)
-    core = lax.ppermute(send, "c", [(0, 1), (1, 0)])
-
-    y_first = paired(added(keep[2:], core[2:]).astype(BF16), "y", 0)
-    y_second = paired(added(keep[1], core[1], y_first[1]).astype(BF16), "y", 1)
-
-    def summed(at):
-        return added(keep[0, at], core[0, at], y_first[0, at], y_second[at])
-
-    z_first = paired(summed(slice(2, 4)).astype(BF16), "zh", 0)
-    z_second = paired(added(summed(1), z_first[1]).astype(BF16), "zh", 1)
-    total = added(summed(0), z_first[0], z_second)
-    down_grad, up_grad = total[0].T, total[1]
+    down_y2, up_y2 = to_second_y(down, down_core, down_y), to_second_y(up, up_core, up_y)
+    down_y2, own = fence((down_y2, own))
+    half = own.shape[0] // 2
+    own = added(own[:half], swap(own[half:].astype(BF16), 1))
+    down, up = (down[0], down_core, down_y, down_y2), (up[0], up_core, up_y, up_y2)
+    down_z, up_z = to_z(*down), to_z(*up)
+    down_z, own = fence((down_z, own))
+    half = own.shape[0] // 2
+    own = added(own[:half], swap(own[half:].astype(BF16), 2))
+    down_z2, up_z2 = to_second_z(down, down_z), to_second_z(up, up_z)
+    normed_grad = added(own[:rows], swap(own[rows:].astype(BF16), 4))
+    down_grad = added(summed(down, 0), down_z[0], down_z2).T
+    up_grad = added(summed(up, 0), up_z[0], up_z2)
 
     g = normed_grad * norm_gain_vector
     back = rstd * (

time: 211 us -> 200 us (0.948)
  the two profiles are of different devices: /device:TPU:6 before, /device:TPU:52 now
where the time goes in v5:
time: 200 us; the launch traced here: 199 us
  starting transfers between devices  120 us (60%)
  waiting for transfers between devices  61.8 us (31%)
  other arithmetic  9.39 us (5%)
  Pallas kernels  3.17 us (2%)
  matrix products  2.77 us (1%)
    ppermute x10, starting transfers between devices, paired(): return lax.ppermute(block, names, moves)  79.9 us
    ppermute x6, waiting for transfers between devices, swap(): return lax.ppermute(block, 'zl', [(i, i ^ distance) for i in range(8)])  24.5 us
    ppermute x6, starting transfers between devices, swap(): return lax.ppermute(block, 'zl', [(i, i ^ distance) for i in range(8)])  24 us
    ppermute x10, waiting for transfers between devices, paired(): return lax.ppermute(block, names, moves)  18.8 us
    ppermute x4, waiting for transfers between devices, shift(): return lax.ppermute(block, 'x', [(i, (i + distance) % 4) for i in range(4)])  18.5 us
    ppermute x4, starting transfers between devices, shift(): return lax.ppermute(block, 'x', [(i, (i + distance) % 4) for i in range(4)])  11.7 us
    ppermute x2, starting transfers between devices, to_core(): return lax.ppermute(term[1], 'c', [(0, 1), (1, 0)])  4.46 us
  transfers between devices with their start and end apart: 22, of which 13 were waited for; matrix products, arithmetic and copies ran while one was open for 2% of the time, Pallas kernels for 1%

profile of v5, /device:TPU:52, one launch (start us, length us, event | category | flops | bytes accessed | tf_op | source)
XLA Modules:
  0.0 198.8 jit_solution(10065861453835604081)
XLA Ops:
  4.5 9.1 %collective-permute-start = (bf16[2,6,3072]{2,1,0:T(8,128)(2,1)S(1)}, bf16[2,6,3072]{2,1,0:T(8,128)(2,1)S(1)}, u32[]{:S(2)}, u32[]{:S(2)}) collective-permute-start(bf16[2,6,3072]{2,1,0:T(8,128)(2,1)S(1)} %pad_maximum_fusion.6), channel_id=1, source_target_pairs={{0,4},{1,5},{2,6},{3,7},{4,0},{5,1},{6,2},{7,3},{8,12},{9,13},{10,... | collective-permute-start | bytes 221192 | tf_op jit(solution)/shard_map/ppermute | solution.py:22
  13.6 7.1 %collective-permute-done = bf16[2,6,3072]{2,1,0:T(8,128)(2,1)S(1)} collective-permute-done((bf16[2,6,3072]{2,1,0:T(8,128)(2,1)S(1)}, bf16[2,6,3072]{2,1,0:T(8,128)(2,1)S(1)}, u32[]{:S(2)}, u32[]{:S(2)}) %collective-permute-start) | collective-permute-done | bytes 73760 | tf_op jit(solution)/shard_map/ppermute | solution.py:22
  21.6 5.1 %collective-permute-start.1 = (bf16[2,12,3072]{2,1,0:T(8,128)(2,1)S(1)}, bf16[2,12,3072]{2,1,0:T(8,128)(2,1)S(1)}, u32[]{:S(2)}, u32[]{:S(2)}) collective-permute-start(bf16[2,12,3072]{2,1,0:T(8,128)(2,1)S(1)} %pad_maximum_fusion.4), channel_id=1, source_target_pairs={{0,2},{1,3},{2,0},{3,1},{4,6},{5,7},{6,4},{7,5},{8,10},{9,11},{10,... | collective-permute-start | bytes 442376 | tf_op jit(solution)/shard_map/ppermute | solution.py:22
  26.6 6.5 %collective-permute-done.1 = bf16[2,12,3072]{2,1,0:T(8,128)(2,1)S(1)} collective-permute-done((bf16[2,12,3072]{2,1,0:T(8,128)(2,1)S(1)}, bf16[2,12,3072]{2,1,0:T(8,128)(2,1)S(1)}, u32[]{:S(2)}, u32[]{:S(2)}) %collective-permute-start.1) | collective-permute-done | bytes 147488 | tf_op jit(solution)/shard_map/ppermute | solution.py:22
  34.0 4.1 %collective-permute-start.2 = (bf16[2,24,3072]{2,1,0:T(8,128)(2,1)S(1)}, bf16[2,24,3072]{2,1,0:T(8,128)(2,1)S(1)}, u32[]{:S(2)}, u32[]{:S(2)}) collective-permute-start(bf16[2,24,3072]{2,1,0:T(8,128)(2,1)S(1)} %pad_maximum_fusion.3), channel_id=1, source_target_pairs={{0,1},{1,0},{2,3},{3,2},{4,5},{5,4},{6,7},{7,6},{8,9},{9,8},{10,11... | collective-permute-start | bytes 884744 | tf_op jit(solution)/shard_map/ppermute | solution.py:22
  38.3 6.6 %collective-permute-done.2 = bf16[2,24,3072]{2,1,0:T(8,128)(2,1)S(1)} collective-permute-done((bf16[2,24,3072]{2,1,0:T(8,128)(2,1)S(1)}, bf16[2,24,3072]{2,1,0:T(8,128)(2,1)S(1)}, u32[]{:S(2)}, u32[]{:S(2)}) %collective-permute-start.2) | collective-permute-done | bytes 294944 | tf_op jit(solution)/shard_map/ppermute | solution.py:22
  45.0 3.1 %collective-permute-start.3 = (bf16[96,3072]{1,0:T(8,128)(2,1)S(1)}, bf16[96,3072]{1,0:T(8,128)(2,1)S(1)}, u32[]{:S(2)}, u32[]{:S(2)}) collective-permute-start(bf16[96,3072]{1,0:T(8,128)(2,1)S(1)} %bitcast.75), channel_id=1, source_target_pairs={{0,8},{8,16},{16,24},{24,0},{1,9},{9,17},{17,25},{25,1},{2,10},{10... | collective-permute-start | bytes 1769480 | tf_op jit(solution)/shard_map/ppermute | solution.py:26
  48.1 2.7 %collective-permute-start.4 = (bf16[96,3072]{1,0:T(8,128)(2,1)S(1)}, bf16[96,3072]{1,0:T(8,128)(2,1)S(1)}, u32[]{:S(2)}, u32[]{:S(2)}) collective-permute-start(bf16[96,3072]{1,0:T(8,128)(2,1)S(1)} %bitcast.76), channel_id=1, source_target_pairs={{0,24},{8,0},{16,8},{24,16},{1,25},{9,1},{17,9},{25,17},{2,26},{10... | collective-permute-start | bytes 1769480 | tf_op jit(solution)/shard_map/ppermute | solution.py:26
  50.9 13.1 %collective-permute-done.4 = bf16[96,3072]{1,0:T(8,128)(2,1)S(1)} collective-permute-done((bf16[96,3072]{1,0:T(8,128)(2,1)S(1)}, bf16[96,3072]{1,0:T(8,128)(2,1)S(1)}, u32[]{:S(2)}, u32[]{:S(2)}) %collective-permute-start.4) | collective-permute-done | bytes 589856 | tf_op jit(solution)/shard_map/ppermute | solution.py:26
  64.0 2.7 %collective-permute-start.5 = (bf16[48,3072]{1,0:T(8,128)(2,1)S(1)}, bf16[48,3072]{1,0:T(8,128)(2,1)S(1)}, u32[]{:S(2)}, u32[]{:S(2)}) collective-permute-start(bf16[48,3072]{1,0:T(8,128)(2,1)S(1)} %get-tuple-element.32), channel_id=1, source_target_pairs={{0,24},{8,0},{16,8},{24,16},{1,25},{9,1},{17,9},{25,17},{2,26},{10... | collective-permute-start | bytes 884744 | tf_op jit(solution)/shard_map/ppermute | solution.py:26
  66.8 3.1 %collective-permute-start.6 = (bf16[48,3072]{1,0:T(8,128)(2,1)S(1)}, bf16[48,3072]{1,0:T(8,128)(2,1)S(1)}, u32[]{:S(2)}, u32[]{:S(2)}) collective-permute-start(bf16[48,3072]{1,0:T(8,128)(2,1)S(1)} %get-tuple-element.33), channel_id=1, source_target_pairs={{0,8},{8,16},{16,24},{24,0},{1,9},{9,17},{17,25},{25,1},{2,10},{10... | collective-permute-start | bytes 884744 | tf_op jit(solution)/shard_map/ppermute | solution.py:26
  69.9 2.7 %collective-permute-done.5 = bf16[48,3072]{1,0:T(8,128)(2,1)S(1)} collective-permute-done((bf16[48,3072]{1,0:T(8,128)(2,1)S(1)}, bf16[48,3072]{1,0:T(8,128)(2,1)S(1)}, u32[]{:S(2)}, u32[]{:S(2)}) %collective-permute-start.5) | collective-permute-done | bytes 294944 | tf_op jit(solution)/shard_map/ppermute | solution.py:26
  72.7 2.7 %collective-permute-done.6 = bf16[48,3072]{1,0:T(8,128)(2,1)S(1)} collective-permute-done((bf16[48,3072]{1,0:T(8,128)(2,1)S(1)}, bf16[48,3072]{1,0:T(8,128)(2,1)S(1)}, u32[]{:S(2)}, u32[]{:S(2)}) %collective-permute-start.6) | collective-permute-done | bytes 294944 | tf_op jit(solution)/shard_map/ppermute | solution.py:26
  77.9 2.1 %collective-permute-start.7 = (bf16[4,4,96,384]{3,2,1,0:T(8,128)(2,1)S(1)}, bf16[4,4,96,384]{3,2,1,0:T(8,128)(2,1)S(1)}, u32[]{:S(2)}, u32[]{:S(2)}) collective-permute-start(bf16[4,4,96,384]{3,2,1,0:T(8,128)(2,1)S(1)} %get-tuple-element.16), channel_id=1, source_target_pairs={{0,32},{32,0},{1,33},{33,1},{2,34},{34,2},{3,35},{35,3},{4,36},{36... | collective-permute-start | bytes 3538952 | tf_op jit(solution)/shard_map/ppermute | solution.py:140
  82.6 2.4 %collective-permute-start.16 = (bf16[4,4,96,384]{3,2,1,0:T(8,128)(2,1)S(1)}, bf16[4,4,96,384]{3,2,1,0:T(8,128)(2,1)S(1)}, u32[]{:S(2)}, u32[]{:S(2)}) collective-permute-start(bf16[4,4,96,384]{3,2,1,0:T(8,128)(2,1)S(1)} %get-tuple-element.25), channel_id=1, source_target_pairs={{0,32},{32,0},{1,33},{33,1},{2,34},{34,2},{3,35},{35,3},{4,36},{36... | collective-permute-start | bytes 3538952 | tf_op jit(solution)/shard_map/ppermute | solution.py:140
  86.2 3.5 %collective-permute-start.9 = (bf16[2,48,3072]{2,1,0:T(8,128)(2,1)S(1)}, bf16[2,48,3072]{2,1,0:T(8,128)(2,1)S(1)}, u32[]{:S(2)}, u32[]{:S(2)}) collective-permute-start(bf16[2,48,3072]{2,1,0:T(8,128)(2,1)S(1)} %slice.249), channel_id=1, source_target_pairs={{0,8},{8,0},{16,24},{24,16},{32,56},{40,48},{48,40},{56,32},{1,9},... | collective-permute-start | bytes 1769480 | tf_op jit(solution)/shard_map/ppermute | solution.py:42
  89.8 3.2 %collective-permute-start.8 = (bf16[2,4,96,384]{3,2,1,0:T(8,128)(2,1)S(1)}, bf16[2,4,96,384]{3,2,1,0:T(8,128)(2,1)S(1)}, u32[]{:S(2)}, u32[]{:S(2)}) collective-permute-start(bf16[2,4,96,384]{3,2,1,0:T(8,128)(2,1)S(1)} %add_convert_fusion.1), channel_id=1, source_target_pairs={{0,64},{64,0},{128,192},{192,128},{32,224},{96,160},{160,96},{224,... | collective-permute-start | bytes 1769480 | tf_op jit(solution)/shard_map/ppermute | solution.py:42
  93.2 2.7 %collective-permute-start.17 = (bf16[2,4,96,384]{3,2,1,0:T(8,128)(2,1)S(1)}, bf16[2,4,96,384]{3,2,1,0:T(8,128)(2,1)S(1)}, u32[]{:S(2)}, u32[]{:S(2)}) collective-permute-start(bf16[2,4,96,384]{3,2,1,0:T(8,128)(2,1)S(1)} %add_convert_fusion), channel_id=1, source_target_pairs={{0,64},{64,0},{128,192},{192,128},{32,224},{96,160},{160,96},{224,... | collective-permute-start | bytes 1769480 | tf_op jit(solution)/shard_map/ppermute | solution.py:42
  95.9 2.1 %collective-permute-done.9 = bf16[2,48,3072]{2,1,0:T(8,128)(2,1)S(1)} collective-permute-done((bf16[2,48,3072]{2,1,0:T(8,128)(2,1)S(1)}, bf16[2,48,3072]{2,1,0:T(8,128)(2,1)S(1)}, u32[]{:S(2)}, u32[]{:S(2)}) %collective-permute-start.9) | collective-permute-done | bytes 589856 | tf_op jit(solution)/shard_map/ppermute | solution.py:42
  97.9 3.7 %collective-permute-done.8 = bf16[2,4,96,384]{3,2,1,0:T(8,128)(2,1)S(1)} collective-permute-done((bf16[2,4,96,384]{3,2,1,0:T(8,128)(2,1)S(1)}, bf16[2,4,96,384]{3,2,1,0:T(8,128)(2,1)S(1)}, u32[]{:S(2)}, u32[]{:S(2)}) %collective-permute-start.8) | collective-permute-done | bytes 589856 | tf_op jit(solution)/shard_map/ppermute | solution.py:42
  101.7 5.0 %collective-permute-start.11 = (bf16[48,3072]{1,0:T(8,128)(2,1)S(1)}, bf16[48,3072]{1,0:T(8,128)(2,1)S(1)}, u32[]{:S(2)}, u32[]{:S(2)}) collective-permute-start(bf16[48,3072]{1,0:T(8,128)(2,1)S(1)} %fusion.7), channel_id=1, source_target_pairs={{0,24},{8,16},{16,8},{24,0},{32,40},{40,32},{48,56},{56,48},{1,25}... | collective-permute-start | bytes 884744 | tf_op jit(solution)/shard_map/ppermute | solution.py:42
  106.8 2.4 %collective-permute-start.10 = (bf16[4,96,384]{2,1,0:T(8,128)(2,1)S(1)}, bf16[4,96,384]{2,1,0:T(8,128)(2,1)S(1)}, u32[]{:S(2)}, u32[]{:S(2)}) collective-permute-start(bf16[4,96,384]{2,1,0:T(8,128)(2,1)S(1)} %fusion.6), channel_id=1, source_target_pairs={{0,192},{64,128},{128,64},{192,0},{32,96},{96,32},{160,224},{224,1... | collective-permute-start | bytes 884744 | tf_op jit(solution)/shard_map/ppermute | solution.py:42
  109.3 3.5 %collective-permute-start.18 = (bf16[4,96,384]{2,1,0:T(8,128)(2,1)S(1)}, bf16[4,96,384]{2,1,0:T(8,128)(2,1)S(1)}, u32[]{:S(2)}, u32[]{:S(2)}) collective-permute-start(bf16[4,96,384]{2,1,0:T(8,128)(2,1)S(1)} %fusion.8), channel_id=1, source_target_pairs={{0,192},{64,128},{128,64},{192,0},{32,96},{96,32},{160,224},{224,1... | collective-permute-start | bytes 884744 | tf_op jit(solution)/shard_map/ppermute | solution.py:42
  112.9 2.5 %collective-permute-done.10 = bf16[4,96,384]{2,1,0:T(8,128)(2,1)S(1)} collective-permute-done((bf16[4,96,384]{2,1,0:T(8,128)(2,1)S(1)}, bf16[4,96,384]{2,1,0:T(8,128)(2,1)S(1)}, u32[]{:S(2)}, u32[]{:S(2)}) %collective-permute-start.10) | collective-permute-done | bytes 294944 | tf_op jit(solution)/shard_map/ppermute | solution.py:42
  115.4 1.9 collective-permute-start.13
  117.5 15.7 %collective-permute-start.12 = (bf16[2,96,384]{2,1,0:T(8,128)(2,1)S(1)}, bf16[2,96,384]{2,1,0:T(8,128)(2,1)S(1)}, u32[]{:S(2)}, u32[]{:S(2)}) collective-permute-start(bf16[2,96,384]{2,1,0:T(8,128)(2,1)S(1)} %fusion.10), channel_id=1, source_target_pairs={{0,256},{256,0},{512,768},{768,512},{32,800},{288,544},{544,288},{... | collective-permute-start | bytes 442376 | tf_op jit(solution)/shard_map/ppermute | solution.py:42
  135.3 7.3 %collective-permute-done.12 = bf16[2,96,384]{2,1,0:T(8,128)(2,1)S(1)} collective-permute-done((bf16[2,96,384]{2,1,0:T(8,128)(2,1)S(1)}, bf16[2,96,384]{2,1,0:T(8,128)(2,1)S(1)}, u32[]{:S(2)}, u32[]{:S(2)}) %collective-permute-start.12) | collective-permute-done | bytes 147488 | tf_op jit(solution)/shard_map/ppermute | solution.py:42
  142.7 32.8 %collective-permute-start.21 = (bf16[96,384]{1,0:T(8,128)(2,1)S(1)}, bf16[96,384]{1,0:T(8,128)(2,1)S(1)}, u32[]{:S(2)}, u32[]{:S(2)}) collective-permute-start(bf16[96,384]{1,0:T(8,128)(2,1)S(1)} %fusion.11), channel_id=1, source_target_pairs={{0,768},{256,512},{512,256},{768,0},{32,288},{288,32},{544,800},{8... | collective-permute-start | bytes 221192 | tf_op jit(solution)/shard_map/ppermute | solution.py:42
  177.5 9.3 %collective-permute-start.20 = (bf16[96,384]{1,0:T(8,128)(2,1)S(1)}, bf16[96,384]{1,0:T(8,128)(2,1)S(1)}, u32[]{:S(2)}, u32[]{:S(2)}) collective-permute-start(bf16[96,384]{1,0:T(8,128)(2,1)S(1)} %fusion.14), channel_id=1, source_target_pairs={{0,768},{256,512},{512,256},{768,0},{32,288},{288,32},{544,800},{8... | collective-permute-start | bytes 221192 | tf_op jit(solution)/shard_map/ppermute | solution.py:42
  187.9 1.9 collective-permute-start.15
  190.6 3.2 %collective-permute-done.20 = bf16[96,384]{1,0:T(8,128)(2,1)S(1)} collective-permute-done((bf16[96,384]{1,0:T(8,128)(2,1)S(1)}, bf16[96,384]{1,0:T(8,128)(2,1)S(1)}, u32[]{:S(2)}, u32[]{:S(2)}) %collective-permute-start.20) | collective-permute-done | bytes 73760 | tf_op jit(solution)/shard_map/ppermute | solution.py:42
  194.5 3.3 %collective-permute-done.15 = bf16[6,3072]{1,0:T(8,128)(2,1)S(1)} collective-permute-done((bf16[6,3072]{1,0:T(8,128)(2,1)S(1)}, bf16[6,3072]{1,0:T(8,128)(2,1)S(1)}, u32[]{:S(2)}, u32[]{:S(2)}) %collective-permute-start.15) | collective-permute-done | bytes 36896 | tf_op jit(solution)/shard_map/ppermute | solution.py:22
  (69 shorter events, 20.6 us)
Async XLA Ops:
  0.6 74.8 %copy-start = (bf16[3072,384]{1,0:T(8,128)(2,1)S(1)}, bf16[3072,384]{1,0:T(8,128)(2,1)}, u32[]{:S(2)}) copy-start(bf16[3072,384]{1,0:T(8,128)(2,1)} %param.8) | copy-start | bytes 7077892
  0.6 44.2 %copy-start.1 = (bf16[6,3072]{1,0:T(8,128)(2,1)S(1)}, bf16[6,3072]{1,0:T(8,128)(2,1)}, u32[]{:S(2)}) copy-start(bf16[6,3072]{1,0:T(8,128)(2,1)} %param.6) | copy-start | bytes 110596
  4.5 16.2 %collective-permute-start = (bf16[2,6,3072]{2,1,0:T(8,128)(2,1)S(1)}, bf16[2,6,3072]{2,1,0:T(8,128)(2,1)S(1)}, u32[]{:S(2)}, u32[]{:S(2)}) collective-permute-start(bf16[2,6,3072]{2,1,0:T(8,128)(2,1)S(1)} %pad_maximum_fusion.6), channel_id=1, source_target_pairs={{0,4},{1,5},{2,6},{3,7},{4,0},{5,1},{6,2},{7,3},{8,12},{9,13},{10,... | collective-permute-start | bytes 221192 | tf_op jit(solution)/shard_map/ppermute | solution.py:22
  21.6 11.6 %collective-permute-start.1 = (bf16[2,12,3072]{2,1,0:T(8,128)(2,1)S(1)}, bf16[2,12,3072]{2,1,0:T(8,128)(2,1)S(1)}, u32[]{:S(2)}, u32[]{:S(2)}) collective-permute-start(bf16[2,12,3072]{2,1,0:T(8,128)(2,1)S(1)} %pad_maximum_fusion.4), channel_id=1, source_target_pairs={{0,2},{1,3},{2,0},{3,1},{4,6},{5,7},{6,4},{7,5},{8,10},{9,11},{10,... | collective-permute-start | bytes 442376 | tf_op jit(solution)/shard_map/ppermute | solution.py:22
  34.0 10.8 %collective-permute-start.2 = (bf16[2,24,3072]{2,1,0:T(8,128)(2,1)S(1)}, bf16[2,24,3072]{2,1,0:T(8,128)(2,1)S(1)}, u32[]{:S(2)}, u32[]{:S(2)}) collective-permute-start(bf16[2,24,3072]{2,1,0:T(8,128)(2,1)S(1)} %pad_maximum_fusion.3), channel_id=1, source_target_pairs={{0,1},{1,0},{2,3},{3,2},{4,5},{5,4},{6,7},{7,6},{8,9},{9,8},{10,11... | collective-permute-start | bytes 884744 | tf_op jit(solution)/shard_map/ppermute | solution.py:22
  45.0 21.8 %collective-permute-start.3 = (bf16[96,3072]{1,0:T(8,128)(2,1)S(1)}, bf16[96,3072]{1,0:T(8,128)(2,1)S(1)}, u32[]{:S(2)}, u32[]{:S(2)}) collective-permute-start(bf16[96,3072]{1,0:T(8,128)(2,1)S(1)} %bitcast.75), channel_id=1, source_target_pairs={{0,8},{8,16},{16,24},{24,0},{1,9},{9,17},{17,25},{25,1},{2,10},{10... | collective-permute-start | bytes 1769480 | tf_op jit(solution)/shard_map/ppermute | solution.py:26
  48.1 15.8 %collective-permute-start.4 = (bf16[96,3072]{1,0:T(8,128)(2,1)S(1)}, bf16[96,3072]{1,0:T(8,128)(2,1)S(1)}, u32[]{:S(2)}, u32[]{:S(2)}) collective-permute-start(bf16[96,3072]{1,0:T(8,128)(2,1)S(1)} %bitcast.76), channel_id=1, source_target_pairs={{0,24},{8,0},{16,8},{24,16},{1,25},{9,1},{17,9},{25,17},{2,26},{10... | collective-permute-start | bytes 1769480 | tf_op jit(solution)/shard_map/ppermute | solution.py:26
  64.0 8.6 %collective-permute-start.5 = (bf16[48,3072]{1,0:T(8,128)(2,1)S(1)}, bf16[48,3072]{1,0:T(8,128)(2,1)S(1)}, u32[]{:S(2)}, u32[]{:S(2)}) collective-permute-start(bf16[48,3072]{1,0:T(8,128)(2,1)S(1)} %get-tuple-element.32), channel_id=1, source_target_pairs={{0,24},{8,0},{16,8},{24,16},{1,25},{9,1},{17,9},{25,17},{2,26},{10... | collective-permute-start | bytes 884744 | tf_op jit(solution)/shard_map/ppermute | solution.py:26
  66.8 8.6 %collective-permute-start.6 = (bf16[48,3072]{1,0:T(8,128)(2,1)S(1)}, bf16[48,3072]{1,0:T(8,128)(2,1)S(1)}, u32[]{:S(2)}, u32[]{:S(2)}) collective-permute-start(bf16[48,3072]{1,0:T(8,128)(2,1)S(1)} %get-tuple-element.33), channel_id=1, source_target_pairs={{0,8},{8,16},{16,24},{24,0},{1,9},{9,17},{17,25},{25,1},{2,10},{10... | collective-permute-start | bytes 884744 | tf_op jit(solution)/shard_map/ppermute | solution.py:26
  77.9 2.2 %copy-start.4 = (bf16[384,3072]{1,0:T(8,128)(2,1)S(1)}, bf16[384,3072]{1,0:T(8,128)(2,1)}, u32[]{:S(2)}) copy-start(bf16[384,3072]{1,0:T(8,128)(2,1)} %param.9) | copy-start | bytes 7077892
  77.9 7.2 %collective-permute-start.7 = (bf16[4,4,96,384]{3,2,1,0:T(8,128)(2,1)S(1)}, bf16[4,4,96,384]{3,2,1,0:T(8,128)(2,1)S(1)}, u32[]{:S(2)}, u32[]{:S(2)}) collective-permute-start(bf16[4,4,96,384]{3,2,1,0:T(8,128)(2,1)S(1)} %get-tuple-element.16), channel_id=1, source_target_pairs={{0,32},{32,0},{1,33},{33,1},{2,34},{34,2},{3,35},{35,3},{4,36},{36... | collective-permute-start | bytes 3538952 | tf_op jit(solution)/shard_map/ppermute | solution.py:140
  82.6 10.4 %collective-permute-start.16 = (bf16[4,4,96,384]{3,2,1,0:T(8,128)(2,1)S(1)}, bf16[4,4,96,384]{3,2,1,0:T(8,128)(2,1)S(1)}, u32[]{:S(2)}, u32[]{:S(2)}) collective-permute-start(bf16[4,4,96,384]{3,2,1,0:T(8,128)(2,1)S(1)} %get-tuple-element.25), channel_id=1, source_target_pairs={{0,32},{32,0},{1,33},{33,1},{2,34},{34,2},{3,35},{35,3},{4,36},{36... | collective-permute-start | bytes 3538952 | tf_op jit(solution)/shard_map/ppermute | solution.py:140
  86.2 11.8 %collective-permute-start.9 = (bf16[2,48,3072]{2,1,0:T(8,128)(2,1)S(1)}, bf16[2,48,3072]{2,1,0:T(8,128)(2,1)S(1)}, u32[]{:S(2)}, u32[]{:S(2)}) collective-permute-start(bf16[2,48,3072]{2,1,0:T(8,128)(2,1)S(1)} %slice.249), channel_id=1, source_target_pairs={{0,8},{8,0},{16,24},{24,16},{32,56},{40,48},{48,40},{56,32},{1,9},... | collective-permute-start | bytes 1769480 | tf_op jit(solution)/shard_map/ppermute | solution.py:42
  89.8 11.8 %collective-permute-start.8 = (bf16[2,4,96,384]{3,2,1,0:T(8,128)(2,1)S(1)}, bf16[2,4,96,384]{3,2,1,0:T(8,128)(2,1)S(1)}, u32[]{:S(2)}, u32[]{:S(2)}) collective-permute-start(bf16[2,4,96,384]{3,2,1,0:T(8,128)(2,1)S(1)} %add_convert_fusion.1), channel_id=1, source_target_pairs={{0,64},{64,0},{128,192},{192,128},{32,224},{96,160},{160,96},{224,... | collective-permute-start | bytes 1769480 | tf_op jit(solution)/shard_map/ppermute | solution.py:42
  93.2 16.0 %collective-permute-start.17 = (bf16[2,4,96,384]{3,2,1,0:T(8,128)(2,1)S(1)}, bf16[2,4,96,384]{3,2,1,0:T(8,128)(2,1)S(1)}, u32[]{:S(2)}, u32[]{:S(2)}) collective-permute-start(bf16[2,4,96,384]{3,2,1,0:T(8,128)(2,1)S(1)} %add_convert_fusion), channel_id=1, source_target_pairs={{0,64},{64,0},{128,192},{192,128},{32,224},{96,160},{160,96},{224,... | collective-permute-start | bytes 1769480 | tf_op jit(solution)/shard_map/ppermute | solution.py:42
  101.7 11.1 %collective-permute-start.11 = (bf16[48,3072]{1,0:T(8,128)(2,1)S(1)}, bf16[48,3072]{1,0:T(8,128)(2,1)S(1)}, u32[]{:S(2)}, u32[]{:S(2)}) collective-permute-start(bf16[48,3072]{1,0:T(8,128)(2,1)S(1)} %fusion.7), channel_id=1, source_target_pairs={{0,24},{8,16},{16,8},{24,0},{32,40},{40,32},{48,56},{56,48},{1,25}... | collective-permute-start | bytes 884744 | tf_op jit(solution)/shard_map/ppermute | solution.py:42
  106.8 8.6 %collective-permute-start.10 = (bf16[4,96,384]{2,1,0:T(8,128)(2,1)S(1)}, bf16[4,96,384]{2,1,0:T(8,128)(2,1)S(1)}, u32[]{:S(2)}, u32[]{:S(2)}) collective-permute-start(bf16[4,96,384]{2,1,0:T(8,128)(2,1)S(1)} %fusion.6), channel_id=1, source_target_pairs={{0,192},{64,128},{128,64},{192,0},{32,96},{96,32},{160,224},{224,1... | collective-permute-start | bytes 884744 | tf_op jit(solution)/shard_map/ppermute | solution.py:42
  109.3 23.9 %collective-permute-start.18 = (bf16[4,96,384]{2,1,0:T(8,128)(2,1)S(1)}, bf16[4,96,384]{2,1,0:T(8,128)(2,1)S(1)}, u32[]{:S(2)}, u32[]{:S(2)}) collective-permute-start(bf16[4,96,384]{2,1,0:T(8,128)(2,1)S(1)} %fusion.8), channel_id=1, source_target_pairs={{0,192},{64,128},{128,64},{192,0},{32,96},{96,32},{160,224},{224,1... | collective-permute-start | bytes 884744 | tf_op jit(solution)/shard_map/ppermute | solution.py:42
  115.4 19.8 %collective-permute-start.13 = (bf16[24,3072]{1,0:T(8,128)(2,1)S(1)}, bf16[24,3072]{1,0:T(8,128)(2,1)S(1)}, u32[]{:S(2)}, u32[]{:S(2)}) collective-permute-start(bf16[24,3072]{1,0:T(8,128)(2,1)S(1)} %slice.336), channel_id=1, source_target_pairs={{0,1},{1,0},{2,3},{3,2},{4,5},{5,4},{6,7},{7,6},{8,9},{9,8},{10,11... | collective-permute-start | bytes 442376 | tf_op jit(solution)/shard_map/ppermute | solution.py:22
  117.5 25.1 %collective-permute-start.12 = (bf16[2,96,384]{2,1,0:T(8,128)(2,1)S(1)}, bf16[2,96,384]{2,1,0:T(8,128)(2,1)S(1)}, u32[]{:S(2)}, u32[]{:S(2)}) collective-permute-start(bf16[2,96,384]{2,1,0:T(8,128)(2,1)S(1)} %fusion.10), channel_id=1, source_target_pairs={{0,256},{256,0},{512,768},{768,512},{32,800},{288,544},{544,288},{... | collective-permute-start | bytes 442376 | tf_op jit(solution)/shard_map/ppermute | solution.py:42
  133.3 44.1 %collective-permute-start.19 = (bf16[2,96,384]{2,1,0:T(8,128)(2,1)S(1)}, bf16[2,96,384]{2,1,0:T(8,128)(2,1)S(1)}, u32[]{:S(2)}, u32[]{:S(2)}) collective-permute-start(bf16[2,96,384]{2,1,0:T(8,128)(2,1)S(1)} %fusion.9), channel_id=1, source_target_pairs={{0,256},{256,0},{512,768},{768,512},{32,800},{288,544},{544,288},{... | collective-permute-start | bytes 442376 | tf_op jit(solution)/shard_map/ppermute | solution.py:42
  142.6 55.2 %copy-start.2 = (bf16[6,3072]{1,0:T(8,128)(2,1)S(1)}, bf16[6,3072]{1,0:T(8,128)(2,1)}, u32[]{:S(2)}) copy-start(bf16[6,3072]{1,0:T(8,128)(2,1)} %param.5) | copy-start | bytes 110596
  142.7 55.2 %copy-start.3 = (f32[3072]{0:T(1024)S(1)}, f32[3072]{0:T(1024)}, u32[]{:S(2)}) copy-start(f32[3072]{0:T(1024)} %param.7) | copy-start | bytes 36868
  142.7 47.2 %collective-permute-start.21 = (bf16[96,384]{1,0:T(8,128)(2,1)S(1)}, bf16[96,384]{1,0:T(8,128)(2,1)S(1)}, u32[]{:S(2)}, u32[]{:S(2)}) collective-permute-start(bf16[96,384]{1,0:T(8,128)(2,1)S(1)} %fusion.11), channel_id=1, source_target_pairs={{0,768},{256,512},{512,256},{768,0},{32,288},{288,32},{544,800},{8... | collective-permute-start | bytes 221192 | tf_op jit(solution)/shard_map/ppermute | solution.py:42
  175.5 12.4 %collective-permute-start.14 = (bf16[12,3072]{1,0:T(8,128)(2,1)S(1)}, bf16[12,3072]{1,0:T(8,128)(2,1)S(1)}, u32[]{:S(2)}, u32[]{:S(2)}) collective-permute-start(bf16[12,3072]{1,0:T(8,128)(2,1)S(1)} %slice.337), channel_id=1, source_target_pairs={{0,2},{1,3},{2,0},{3,1},{4,6},{5,7},{6,4},{7,5},{8,10},{9,11},{10,... | collective-permute-start | bytes 221192 | tf_op jit(solution)/shard_map/ppermute | solution.py:22
  177.5 16.4 %collective-permute-start.20 = (bf16[96,384]{1,0:T(8,128)(2,1)S(1)}, bf16[96,384]{1,0:T(8,128)(2,1)S(1)}, u32[]{:S(2)}, u32[]{:S(2)}) collective-permute-start(bf16[96,384]{1,0:T(8,128)(2,1)S(1)} %fusion.14), channel_id=1, source_target_pairs={{0,768},{256,512},{512,256},{768,0},{32,288},{288,32},{544,800},{8... | collective-permute-start | bytes 221192 | tf_op jit(solution)/shard_map/ppermute | solution.py:42
  187.9 9.9 %collective-permute-start.15 = (bf16[6,3072]{1,0:T(8,128)(2,1)S(1)}, bf16[6,3072]{1,0:T(8,128)(2,1)S(1)}, u32[]{:S(2)}, u32[]{:S(2)}) collective-permute-start(bf16[6,3072]{1,0:T(8,128)(2,1)S(1)} %slice.338), channel_id=1, source_target_pairs={{0,4},{1,5},{2,6},{3,7},{4,0},{5,1},{6,2},{7,3},{8,12},{9,13},{10,... | collective-permute-start | bytes 110600 | tf_op jit(solution)/shard_map/ppermute | solution.py:22

commit v6 on v5

--- a/solution.py
+++ b/solution.py
@@ -57,6 +57,48 @@
 
 def pick(array, index, axis):
     return lax.dynamic_index_in_dim(array, index, axis, keepdims=False)
+
+
+def pack_kernel(layer_input, out_grad, gain, packed, stats):
+    rows, width = layer_input.shape
+    xf = layer_input[...].astype(F32)
+    mean = jnp.mean(xf, axis=1, keepdims=True)
+    centered = xf - mean
+    rstd = 1.0 / jnp.sqrt(jnp.mean(centered * centered, axis=1, keepdims=True) + 1e-06)
+    normed = (centered * rstd * gain[...]).astype(BF16)
+    half = width // 2
+    for at, block in enumerate((normed, out_grad[...])):
+        packed[2 * at * rows : (2 * at + 1) * rows] = block[:, :half]
+        packed[(2 * at + 1) * rows : (2 * at + 2) * rows] = block[:, half:]
+    stats[:, 0:1] = mean
+    stats[:, 1:2] = rstd
+
+
+def unpack_kernel(own, far, block):
+    rows, half = own.shape[0] // 4, own.shape[1]
+    for at in range(2):
+        for k, source in enumerate((own, far)):
+            to = slice((2 * at + k) * rows, (2 * at + k + 1) * rows)
+            block[to, :half] = source[2 * at * rows : (2 * at + 1) * rows]
+            block[to, half:] = source[(2 * at + 1) * rows : (2 * at + 2) * rows]
+
+
+def join_kernel(*refs):
+    pieces, outs = refs[:4], refs[4:]
+    rows = pieces[0].shape[0] // 2
+    for k, piece in enumerate(pieces):
+        for at, out in enumerate(outs):
+            out[k * rows : (k + 1) * rows] = piece[at * rows : (at + 1) * rows]
+
+
+def in_vmem(kernel, outs, *operands):
+    return pl.pallas_call(
+        kernel,
+        out_shape=[jax.ShapeDtypeStruct(*out) for out in outs],
+        in_specs=[pl.BlockSpec(memory_space=pltpu.VMEM)] * len(operands),
+        out_specs=[pl.BlockSpec(memory_space=pltpu.VMEM)] * len(outs),
+        compiler_params=pltpu.CompilerParams(vmem_limit_bytes=8 * 1024 * 1024),
+    )(*operands)
 
 
 def term_kernel(where, left, right, keep, send):
@@ -102,21 +144,22 @@
     zh, y, c = lax.axis_index("zh"), lax.axis_index("y"), lax.axis_index("c")
     x, zl = lax.axis_index("x"), lax.axis_index("zl")
 
-    xf = layer_input.astype(F32)
-    centered = xf - jnp.mean(xf, axis=1, keepdims=True)
-    rstd = 1.0 / jnp.sqrt(jnp.mean(centered * centered, axis=1, keepdims=True) + 1e-06)
-    xhat = centered * rstd
-    normed = (xhat * norm_gain_vector).astype(BF16)
-
-    pair = jnp.stack([normed, out_grad])
-    for distance in (4, 2, 1):
-        pair = jnp.concatenate([pair, swap(pair, distance)], axis=1)
+    packed, stats = in_vmem(
+        pack_kernel,
+        [((4 * rows, width // 2), BF16), ((rows, 2), F32)],
+        layer_input,
+        out_grad,
+        norm_gain_vector[None],
+    )
+    (block,) = in_vmem(unpack_kernel, [((4 * rows, width), BF16)], packed, swap(packed, 4))
     middle = nzl * rows
-    pair = lax.optimization_barrier(pair.reshape(2 * middle, width))
-    left, right = shift(pair, 1), shift(pair, -1)
-    across_normed, across_grad = shift(left[:middle], 1), shift(right[middle:], -1)
-    normed_all = jnp.concatenate([pair[:middle], left[:middle], right[:middle], across_normed])
-    grad_all = jnp.concatenate([pair[middle:], left[middle:], right[middle:], across_grad])
+    normed, grad = in_vmem(
+        join_kernel, [((middle, width), BF16)] * 2, block, *[swap(block, k) for k in (1, 2, 3)]
+    )
+    normed_left, grad_right = shift(normed, 1), shift(grad, -1)
+    grad_left, normed_right = shift(grad, 1), shift(normed, -1)
+    normed_all = jnp.concatenate([normed, normed_left, normed_right, shift(normed_left, 1)])
+    grad_all = jnp.concatenate([grad, grad_left, grad_right, shift(grad_right, -1)])
 
     pre = jnp.dot(normed_all, up_weight, preferred_element_type=F32)
     value, slope = gelu_parts(pre)
@@ -167,17 +210,19 @@
     down_y2, up_y2 = to_second_y(down, down_core, down_y), to_second_y(up, up_core, up_y)
     down_y2, own = fence((down_y2, own))
     half = own.shape[0] // 2
-    own = added(own[:half], swap(own[half:].astype(BF16), 1))
+    own = added(own[:half], swap(own[half:].astype(BF16), 2))
     down, up = (down[0], down_core, down_y, down_y2), (up[0], up_core, up_y, up_y2)
     down_z, up_z = to_z(*down), to_z(*up)
     down_z, own = fence((down_z, own))
     half = own.shape[0] // 2
-    own = added(own[:half], swap(own[half:].astype(BF16), 2))
+    own = added(own[:half], swap(own[half:].astype(BF16), 1))
     down_z2, up_z2 = to_second_z(down, down_z), to_second_z(up, up_z)
     normed_grad = added(own[:rows], swap(own[rows:].astype(BF16), 4))
     down_grad = added(summed(down, 0), down_z[0], down_z2).T
     up_grad = added(summed(up, 0), up_z[0], up_z2)
 
+    rstd = stats[:, 1:2]
+    xhat = (layer_input.astype(F32) - stats[:, 0:1]) * rstd
     g = normed_grad * norm_gain_vector
     back = rstd * (
         g

time: 200 us -> 193 us (0.965)
  the two profiles are of different devices: /device:TPU:52 before, /device:TPU:24 now
where the time goes in v6:
time: 193 us; the launch traced here: 192 us
  starting transfers between devices  131 us (68%)
  waiting for transfers between devices  37.8 us (20%)
  other arithmetic  8.27 us (4%)
  matrix products  5.58 us (3%)
  Pallas kernels  4.54 us (2%)
  local copies, waits for them, and re-layouts  4.07 us (2%)
    ppermute x10, starting transfers between devices, paired(): return lax.ppermute(block, names, moves)  73.4 us
    ppermute x7, starting transfers between devices, swap(): return lax.ppermute(block, 'zl', [(i, i ^ distance) for i in range(8)])  31.7 us
    ppermute x6, starting transfers between devices, shift(): return lax.ppermute(block, 'x', [(i, (i + distance) % 4) for i in range(4)])  21.2 us
    ppermute x7, waiting for transfers between devices, swap(): return lax.ppermute(block, 'zl', [(i, i ^ distance) for i in range(8)])  17.6 us
    ppermute x10, waiting for transfers between devices, paired(): return lax.ppermute(block, names, moves)  15.1 us
    ppermute x6, waiting for transfers between devices, shift(): return lax.ppermute(block, 'x', [(i, (i + distance) % 4) for i in range(4)])  5.1 us
    ppermute x2, starting transfers between devices, to_core(): return lax.ppermute(term[1], 'c', [(0, 1), (1, 0)])  4.31 us
    pallas_call x2, Pallas kernels, term_halves(): pl.pallas_call(term_kernel, out_shape=(half, half), in_specs=[pl.BlockSpe...  4.2 us
  transfers between devices with their start and end apart: 25, of which 9 were waited for; matrix products, arithmetic and copies ran while one was open for 7% of the time, Pallas kernels for 1%

profile of v6, /device:TPU:24, one launch (start us, length us, event | category | flops | bytes accessed | tf_op | source)
XLA Modules:
  0.0 192.1 jit_solution(10499839992084691964)
XLA Ops:
  3.3 9.1 %collective-permute-start = (bf16[24,1536]{1,0:T(8,128)(2,1)S(1)}, bf16[24,1536]{1,0:T(8,128)(2,1)S(1)}, u32[]{:S(2)}, u32[]{:S(2)}) collective-permute-start(bf16[24,1536]{1,0:T(8,128)(2,1)S(1)} %get-tuple-element.20.own), channel_id=1, source_target_pairs={{0,4},{1,5},{2,6},{3,7},{4,0},{5,1},{6,2},{7,3},{8,12},{9,13},{10,... | collective-permute-start | bytes 221192 | tf_op jit(solution)/shard_map/ppermute | solution.py:22
  12.5 7.0 %collective-permute-done.far = bf16[24,1536]{1,0:T(8,128)(2,1)S(1)} collective-permute-done((bf16[24,1536]{1,0:T(8,128)(2,1)S(1)}, bf16[24,1536]{1,0:T(8,128)(2,1)S(1)}, u32[]{:S(2)}, u32[]{:S(2)}) %collective-permute-start) | collective-permute-done | bytes 73760 | tf_op jit(solution)/shard_map/ppermute | solution.py:22
  19.5 2.3 %collective-permute-start.1 = (bf16[24,3072]{1,0:T(8,128)(2,1)S(1)}, bf16[24,3072]{1,0:T(8,128)(2,1)S(1)}, u32[]{:S(2)}, u32[]{:S(2)}) collective-permute-start(bf16[24,3072]{1,0:T(8,128)(2,1)S(1)} %shard_map.77.refs_0_), channel_id=1, source_target_pairs={{0,1},{1,0},{2,3},{3,2},{4,5},{5,4},{6,7},{7,6},{8,9},{9,8},{10,11... | collective-permute-start | bytes 442376 | tf_op jit(solution)/shard_map/ppermute | solution.py:22
  21.8 4.5 %collective-permute-start.2 = (bf16[24,3072]{1,0:T(8,128)(2,1)S(1)}, bf16[24,3072]{1,0:T(8,128)(2,1)S(1)}, u32[]{:S(2)}, u32[]{:S(2)}) collective-permute-start(bf16[24,3072]{1,0:T(8,128)(2,1)S(1)} %shard_map.77.refs_0_), channel_id=1, source_target_pairs={{0,2},{1,3},{2,0},{3,1},{4,6},{5,7},{6,4},{7,5},{8,10},{9,11},{10,... | collective-permute-start | bytes 442376 | tf_op jit(solution)/shard_map/ppermute | solution.py:22
  26.4 3.3 %collective-permute-start.3 = (bf16[24,3072]{1,0:T(8,128)(2,1)S(1)}, bf16[24,3072]{1,0:T(8,128)(2,1)S(1)}, u32[]{:S(2)}, u32[]{:S(2)}) collective-permute-start(bf16[24,3072]{1,0:T(8,128)(2,1)S(1)} %shard_map.77.refs_0_), channel_id=1, source_target_pairs={{0,3},{1,2},{2,1},{3,0},{4,7},{5,6},{6,5},{7,4},{8,11},{9,10},{10,... | collective-permute-start | bytes 442376 | tf_op jit(solution)/shard_map/ppermute | solution.py:22
  29.8 7.3 %collective-permute-done.2.refs_2_ = bf16[24,3072]{1,0:T(8,128)(2,1)S(1)} collective-permute-done((bf16[24,3072]{1,0:T(8,128)(2,1)S(1)}, bf16[24,3072]{1,0:T(8,128)(2,1)S(1)}, u32[]{:S(2)}, u32[]{:S(2)}) %collective-permute-start.2) | collective-permute-done | bytes 147488 | tf_op jit(solution)/shard_map/ppermute | solution.py:22
  37.2 3.4 %collective-permute-start.7 = (bf16[48,3072]{1,0:T(8,128)(2,1)S(1)}, bf16[48,3072]{1,0:T(8,128)(2,1)S(1)}, u32[]{:S(2)}, u32[]{:S(2)}) collective-permute-start(bf16[48,3072]{1,0:T(8,128)(2,1)S(1)} %get-tuple-element.22), channel_id=1, source_target_pairs={{0,8},{8,16},{16,24},{24,0},{1,9},{9,17},{17,25},{25,1},{2,10},{10... | collective-permute-start | bytes 884744 | tf_op jit(solution)/shard_map/ppermute | solution.py:26
  40.6 3.7 %collective-permute-start.8 = (bf16[48,3072]{1,0:T(8,128)(2,1)S(1)}, bf16[48,3072]{1,0:T(8,128)(2,1)S(1)}, u32[]{:S(2)}, u32[]{:S(2)}) collective-permute-start(bf16[48,3072]{1,0:T(8,128)(2,1)S(1)} %get-tuple-element.22), channel_id=1, source_target_pairs={{0,24},{8,0},{16,8},{24,16},{1,25},{9,1},{17,9},{25,17},{2,26},{10... | collective-permute-start | bytes 884744 | tf_op jit(solution)/shard_map/ppermute | solution.py:26
  44.3 2.2 %collective-permute-start.4 = (bf16[48,3072]{1,0:T(8,128)(2,1)S(1)}, bf16[48,3072]{1,0:T(8,128)(2,1)S(1)}, u32[]{:S(2)}, u32[]{:S(2)}) collective-permute-start(bf16[48,3072]{1,0:T(8,128)(2,1)S(1)} %get-tuple-element.21), channel_id=1, source_target_pairs={{0,8},{8,16},{16,24},{24,0},{1,9},{9,17},{17,25},{25,1},{2,10},{10... | collective-permute-start | bytes 884744 | tf_op jit(solution)/shard_map/ppermute | solution.py:26
  46.5 4.9 %collective-permute-start.5 = (bf16[48,3072]{1,0:T(8,128)(2,1)S(1)}, bf16[48,3072]{1,0:T(8,128)(2,1)S(1)}, u32[]{:S(2)}, u32[]{:S(2)}) collective-permute-start(bf16[48,3072]{1,0:T(8,128)(2,1)S(1)} %get-tuple-element.21), channel_id=1, source_target_pairs={{0,24},{8,0},{16,8},{24,16},{1,25},{9,1},{17,9},{25,17},{2,26},{10... | collective-permute-start | bytes 884744 | tf_op jit(solution)/shard_map/ppermute | solution.py:26
  53.3 2.6 %collective-permute-done.5 = bf16[48,3072]{1,0:T(8,128)(2,1)S(1)} collective-permute-done((bf16[48,3072]{1,0:T(8,128)(2,1)S(1)}, bf16[48,3072]{1,0:T(8,128)(2,1)S(1)}, u32[]{:S(2)}, u32[]{:S(2)}) %collective-permute-start.5) | collective-permute-done | bytes 294944 | tf_op jit(solution)/shard_map/ppermute | solution.py:26
  55.9 5.2 %collective-permute-start.6 = (bf16[48,3072]{1,0:T(8,128)(2,1)S(1)}, bf16[48,3072]{1,0:T(8,128)(2,1)S(1)}, u32[]{:S(2)}, u32[]{:S(2)}) collective-permute-start(bf16[48,3072]{1,0:T(8,128)(2,1)S(1)} %collective-permute-done.5), channel_id=1, source_target_pairs={{0,24},{8,0},{16,8},{24,16},{1,25},{9,1},{17,9},{25,17},{2,26},{10... | collective-permute-start | bytes 884744 | tf_op jit(solution)/shard_map/ppermute | solution.py:26
  62.9 2.5 %collective-permute-done.6 = bf16[48,3072]{1,0:T(8,128)(2,1)S(1)} collective-permute-done((bf16[48,3072]{1,0:T(8,128)(2,1)S(1)}, bf16[48,3072]{1,0:T(8,128)(2,1)S(1)}, u32[]{:S(2)}, u32[]{:S(2)}) %collective-permute-start.6) | collective-permute-done | bytes 294944 | tf_op jit(solution)/shard_map/ppermute | solution.py:26
  65.4 2.6 %shard_map.79 = (bf16[4,4,96,384]{3,2,1,0:T(8,128)(2,1)S(1)}, bf16[4,4,96,384]{3,2,1,0:T(8,128)(2,1)}) custom-call(s32[17]{0:T(128)S(1)} %concatenate.9.where, bf16[192,3072]{1,0:T(8,128)(2,1)S(1)} %constant_dynamic-update-slice_fusion.left, bf16[192,384]{1,0:T(8,128)(2,1)S(1)} %get-tuple-element.43.right), custom_call_target="tpu_custom_call" | custom-call | flops 452984832 | bytes 4718592 | tf_op jit(solution)/shard_map/pallas_call | solution.py:126
  71.0 3.1 %fusion.1.right = bf16[192,384]{1,0:T(8,128)(2,1)S(1)} fusion(bf16[192,3072]{1,0:T(8,128)(2,1)} %copy-done.7, bf16[384,3072]{1,0:T(8,128)(2,1)} %param.9, f32[192,384]{1,0:T(8,128)} %get-tuple-element.44), kind=kOutput, calls=%fused_computation.5 | convolution fusion | flops 453722112 | bytes 3981312 | tf_op jit(solution)/shard_map/td,fd->tf/dot_general | solution.py:167
  75.7 2.4 %collective-permute-start.19 = (bf16[4,4,96,384]{3,2,1,0:T(8,128)(2,1)S(1)}, bf16[4,4,96,384]{3,2,1,0:T(8,128)(2,1)S(1)}, u32[]{:S(2)}, u32[]{:S(2)}) collective-permute-start(bf16[4,4,96,384]{3,2,1,0:T(8,128)(2,1)S(1)} %get-tuple-element.33), channel_id=1, source_target_pairs={{0,32},{32,0},{1,33},{33,1},{2,34},{34,2},{3,35},{35,3},{4,36},{36... | collective-permute-start | bytes 3538952 | tf_op jit(solution)/shard_map/ppermute | solution.py:183
  79.2 2.6 %collective-permute-start.12 = (bf16[2,48,3072]{2,1,0:T(8,128)(2,1)S(1)}, bf16[2,48,3072]{2,1,0:T(8,128)(2,1)S(1)}, u32[]{:S(2)}, u32[]{:S(2)}) collective-permute-start(bf16[2,48,3072]{2,1,0:T(8,128)(2,1)S(1)} %slice.225), channel_id=1, source_target_pairs={{0,8},{8,0},{16,24},{24,16},{32,56},{40,48},{48,40},{56,32},{1,9},... | collective-permute-start | bytes 1769480 | tf_op jit(solution)/shard_map/ppermute | solution.py:42
  83.0 2.7 %collective-permute-start.11 = (bf16[2,4,96,384]{3,2,1,0:T(8,128)(2,1)S(1)}, bf16[2,4,96,384]{3,2,1,0:T(8,128)(2,1)S(1)}, u32[]{:S(2)}, u32[]{:S(2)}) collective-permute-start(bf16[2,4,96,384]{3,2,1,0:T(8,128)(2,1)S(1)} %add_convert_fusion.1), channel_id=1, source_target_pairs={{0,64},{64,0},{128,192},{192,128},{32,224},{96,160},{160,96},{224,... | collective-permute-start | bytes 1769480 | tf_op jit(solution)/shard_map/ppermute | solution.py:42
  86.0 3.2 %collective-permute-start.20 = (bf16[2,4,96,384]{3,2,1,0:T(8,128)(2,1)S(1)}, bf16[2,4,96,384]{3,2,1,0:T(8,128)(2,1)S(1)}, u32[]{:S(2)}, u32[]{:S(2)}) collective-permute-start(bf16[2,4,96,384]{3,2,1,0:T(8,128)(2,1)S(1)} %add_convert_fusion), channel_id=1, source_target_pairs={{0,64},{64,0},{128,192},{192,128},{32,224},{96,160},{160,96},{224,... | collective-permute-start | bytes 1769480 | tf_op jit(solution)/shard_map/ppermute | solution.py:42
  91.0 3.8 %collective-permute-done.11 = bf16[2,4,96,384]{3,2,1,0:T(8,128)(2,1)S(1)} collective-permute-done((bf16[2,4,96,384]{3,2,1,0:T(8,128)(2,1)S(1)}, bf16[2,4,96,384]{3,2,1,0:T(8,128)(2,1)S(1)}, u32[]{:S(2)}, u32[]{:S(2)}) %collective-permute-start.11) | collective-permute-done | bytes 589856 | tf_op jit(solution)/shard_map/ppermute | solution.py:42
  94.9 5.0 %collective-permute-start.14 = (bf16[48,3072]{1,0:T(8,128)(2,1)S(1)}, bf16[48,3072]{1,0:T(8,128)(2,1)S(1)}, u32[]{:S(2)}, u32[]{:S(2)}) collective-permute-start(bf16[48,3072]{1,0:T(8,128)(2,1)S(1)} %fusion.7), channel_id=1, source_target_pairs={{0,24},{8,16},{16,8},{24,0},{32,40},{40,32},{48,56},{56,48},{1,25}... | collective-permute-start | bytes 884744 | tf_op jit(solution)/shard_map/ppermute | solution.py:42
  100.9 4.6 %collective-permute-start.13 = (bf16[4,96,384]{2,1,0:T(8,128)(2,1)S(1)}, bf16[4,96,384]{2,1,0:T(8,128)(2,1)S(1)}, u32[]{:S(2)}, u32[]{:S(2)}) collective-permute-start(bf16[4,96,384]{2,1,0:T(8,128)(2,1)S(1)} %fusion.6), channel_id=1, source_target_pairs={{0,192},{64,128},{128,64},{192,0},{32,96},{96,32},{160,224},{224,1... | collective-permute-start | bytes 884744 | tf_op jit(solution)/shard_map/ppermute | solution.py:42
  105.7 2.4 %collective-permute-start.21 = (bf16[4,96,384]{2,1,0:T(8,128)(2,1)S(1)}, bf16[4,96,384]{2,1,0:T(8,128)(2,1)S(1)}, u32[]{:S(2)}, u32[]{:S(2)}) collective-permute-start(bf16[4,96,384]{2,1,0:T(8,128)(2,1)S(1)} %fusion.8), channel_id=1, source_target_pairs={{0,192},{64,128},{128,64},{192,0},{32,96},{96,32},{160,224},{224,1... | collective-permute-start | bytes 884744 | tf_op jit(solution)/shard_map/ppermute | solution.py:42
  108.3 2.5 %collective-permute-done.13 = bf16[4,96,384]{2,1,0:T(8,128)(2,1)S(1)} collective-permute-done((bf16[4,96,384]{2,1,0:T(8,128)(2,1)S(1)}, bf16[4,96,384]{2,1,0:T(8,128)(2,1)S(1)}, u32[]{:S(2)}, u32[]{:S(2)}) %collective-permute-start.13) | collective-permute-done | bytes 294944 | tf_op jit(solution)/shard_map/ppermute | solution.py:42
  110.8 6.2 %collective-permute-start.16 = (bf16[24,3072]{1,0:T(8,128)(2,1)S(1)}, bf16[24,3072]{1,0:T(8,128)(2,1)S(1)}, u32[]{:S(2)}, u32[]{:S(2)}) collective-permute-start(bf16[24,3072]{1,0:T(8,128)(2,1)S(1)} %slice.314), channel_id=1, source_target_pairs={{0,2},{1,3},{2,0},{3,1},{4,6},{5,7},{6,4},{7,5},{8,10},{9,11},{10,... | collective-permute-start | bytes 442376 | tf_op jit(solution)/shard_map/ppermute | solution.py:22
  118.0 15.7 %collective-permute-start.15 = (bf16[2,96,384]{2,1,0:T(8,128)(2,1)S(1)}, bf16[2,96,384]{2,1,0:T(8,128)(2,1)S(1)}, u32[]{:S(2)}, u32[]{:S(2)}) collective-permute-start(bf16[2,96,384]{2,1,0:T(8,128)(2,1)S(1)} %fusion.10), channel_id=1, source_target_pairs={{0,256},{256,0},{512,768},{768,512},{32,800},{288,544},{544,288},{... | collective-permute-start | bytes 442376 | tf_op jit(solution)/shard_map/ppermute | solution.py:42
  135.8 7.0 %collective-permute-done.15 = bf16[2,96,384]{2,1,0:T(8,128)(2,1)S(1)} collective-permute-done((bf16[2,96,384]{2,1,0:T(8,128)(2,1)S(1)}, bf16[2,96,384]{2,1,0:T(8,128)(2,1)S(1)}, u32[]{:S(2)}, u32[]{:S(2)}) %collective-permute-start.15) | collective-permute-done | bytes 147488 | tf_op jit(solution)/shard_map/ppermute | solution.py:42
  143.7 16.6 %collective-permute-start.24 = (bf16[96,384]{1,0:T(8,128)(2,1)S(1)}, bf16[96,384]{1,0:T(8,128)(2,1)S(1)}, u32[]{:S(2)}, u32[]{:S(2)}) collective-permute-start(bf16[96,384]{1,0:T(8,128)(2,1)S(1)} %fusion.11), channel_id=1, source_target_pairs={{0,768},{256,512},{512,256},{768,0},{32,288},{288,32},{544,800},{8... | collective-permute-start | bytes 221192 | tf_op jit(solution)/shard_map/ppermute | solution.py:42
  160.4 2.1 %collective-permute-start.17 = (bf16[12,3072]{1,0:T(8,128)(2,1)S(1)}, bf16[12,3072]{1,0:T(8,128)(2,1)S(1)}, u32[]{:S(2)}, u32[]{:S(2)}) collective-permute-start(bf16[12,3072]{1,0:T(8,128)(2,1)S(1)} %slice.315), channel_id=1, source_target_pairs={{0,1},{1,0},{2,3},{3,2},{4,5},{5,4},{6,7},{7,6},{8,9},{9,8},{10,11... | collective-permute-start | bytes 221192 | tf_op jit(solution)/shard_map/ppermute | solution.py:22
  162.5 18.7 %collective-permute-start.23 = (bf16[96,384]{1,0:T(8,128)(2,1)S(1)}, bf16[96,384]{1,0:T(8,128)(2,1)S(1)}, u32[]{:S(2)}, u32[]{:S(2)}) collective-permute-start(bf16[96,384]{1,0:T(8,128)(2,1)S(1)} %fusion.14), channel_id=1, source_target_pairs={{0,768},{256,512},{512,256},{768,0},{32,288},{288,32},{544,800},{8... | collective-permute-start | bytes 221192 | tf_op jit(solution)/shard_map/ppermute | solution.py:42
  181.3 4.3 %collective-permute-start.18 = (bf16[6,3072]{1,0:T(8,128)(2,1)S(1)}, bf16[6,3072]{1,0:T(8,128)(2,1)S(1)}, u32[]{:S(2)}, u32[]{:S(2)}) collective-permute-start(bf16[6,3072]{1,0:T(8,128)(2,1)S(1)} %slice.316), channel_id=1, source_target_pairs={{0,4},{1,5},{2,6},{3,7},{4,0},{5,1},{6,2},{7,3},{8,12},{9,13},{10,... | collective-permute-start | bytes 110600 | tf_op jit(solution)/shard_map/ppermute | solution.py:22
  187.9 3.2 %collective-permute-done.18 = bf16[6,3072]{1,0:T(8,128)(2,1)S(1)} collective-permute-done((bf16[6,3072]{1,0:T(8,128)(2,1)S(1)}, bf16[6,3072]{1,0:T(8,128)(2,1)S(1)}, u32[]{:S(2)}, u32[]{:S(2)}) %collective-permute-start.18) | collective-permute-done | bytes 36896 | tf_op jit(solution)/shard_map/ppermute | solution.py:22
  (82 shorter events, 24.3 us)
Async XLA Ops:
  0.6 60.7 %copy-start = (bf16[3072,384]{1,0:T(8,128)(2,1)S(1)}, bf16[3072,384]{1,0:T(8,128)(2,1)}, u32[]{:S(2)}) copy-start(bf16[3072,384]{1,0:T(8,128)(2,1)} %param.8) | copy-start | bytes 7077892
  3.3 16.2 %collective-permute-start = (bf16[24,1536]{1,0:T(8,128)(2,1)S(1)}, bf16[24,1536]{1,0:T(8,128)(2,1)S(1)}, u32[]{:S(2)}, u32[]{:S(2)}) collective-permute-start(bf16[24,1536]{1,0:T(8,128)(2,1)S(1)} %get-tuple-element.20.own), channel_id=1, source_target_pairs={{0,4},{1,5},{2,6},{3,7},{4,0},{5,1},{6,2},{7,3},{8,12},{9,13},{10,... | collective-permute-start | bytes 221192 | tf_op jit(solution)/shard_map/ppermute | solution.py:22
  19.5 10.3 %collective-permute-start.1 = (bf16[24,3072]{1,0:T(8,128)(2,1)S(1)}, bf16[24,3072]{1,0:T(8,128)(2,1)S(1)}, u32[]{:S(2)}, u32[]{:S(2)}) collective-permute-start(bf16[24,3072]{1,0:T(8,128)(2,1)S(1)} %shard_map.77.refs_0_), channel_id=1, source_target_pairs={{0,1},{1,0},{2,3},{3,2},{4,5},{5,4},{6,7},{7,6},{8,9},{9,8},{10,11... | collective-permute-start | bytes 442376 | tf_op jit(solution)/shard_map/ppermute | solution.py:22
  21.8 15.3 %collective-permute-start.2 = (bf16[24,3072]{1,0:T(8,128)(2,1)S(1)}, bf16[24,3072]{1,0:T(8,128)(2,1)S(1)}, u32[]{:S(2)}, u32[]{:S(2)}) collective-permute-start(bf16[24,3072]{1,0:T(8,128)(2,1)S(1)} %shard_map.77.refs_0_), channel_id=1, source_target_pairs={{0,2},{1,3},{2,0},{3,1},{4,6},{5,7},{6,4},{7,5},{8,10},{9,11},{10,... | collective-permute-start | bytes 442376 | tf_op jit(solution)/shard_map/ppermute | solution.py:22
  26.4 10.7 %collective-permute-start.3 = (bf16[24,3072]{1,0:T(8,128)(2,1)S(1)}, bf16[24,3072]{1,0:T(8,128)(2,1)S(1)}, u32[]{:S(2)}, u32[]{:S(2)}) collective-permute-start(bf16[24,3072]{1,0:T(8,128)(2,1)S(1)} %shard_map.77.refs_0_), channel_id=1, source_target_pairs={{0,3},{1,2},{2,1},{3,0},{4,7},{5,6},{6,5},{7,4},{8,11},{9,10},{10,... | collective-permute-start | bytes 442376 | tf_op jit(solution)/shard_map/ppermute | solution.py:22
  37.2 14.2 %collective-permute-start.7 = (bf16[48,3072]{1,0:T(8,128)(2,1)S(1)}, bf16[48,3072]{1,0:T(8,128)(2,1)S(1)}, u32[]{:S(2)}, u32[]{:S(2)}) collective-permute-start(bf16[48,3072]{1,0:T(8,128)(2,1)S(1)} %get-tuple-element.22), channel_id=1, source_target_pairs={{0,8},{8,16},{16,24},{24,0},{1,9},{9,17},{17,25},{25,1},{2,10},{10... | collective-permute-start | bytes 884744 | tf_op jit(solution)/shard_map/ppermute | solution.py:26
  40.6 20.6 %collective-permute-start.8 = (bf16[48,3072]{1,0:T(8,128)(2,1)S(1)}, bf16[48,3072]{1,0:T(8,128)(2,1)S(1)}, u32[]{:S(2)}, u32[]{:S(2)}) collective-permute-start(bf16[48,3072]{1,0:T(8,128)(2,1)S(1)} %get-tuple-element.22), channel_id=1, source_target_pairs={{0,24},{8,0},{16,8},{24,16},{1,25},{9,1},{17,9},{25,17},{2,26},{10... | collective-permute-start | bytes 884744 | tf_op jit(solution)/shard_map/ppermute | solution.py:26
  44.3 16.9 %collective-permute-start.4 = (bf16[48,3072]{1,0:T(8,128)(2,1)S(1)}, bf16[48,3072]{1,0:T(8,128)(2,1)S(1)}, u32[]{:S(2)}, u32[]{:S(2)}) collective-permute-start(bf16[48,3072]{1,0:T(8,128)(2,1)S(1)} %get-tuple-element.21), channel_id=1, source_target_pairs={{0,8},{8,16},{16,24},{24,0},{1,9},{9,17},{17,25},{25,1},{2,10},{10... | collective-permute-start | bytes 884744 | tf_op jit(solution)/shard_map/ppermute | solution.py:26
  46.5 9.5 %collective-permute-start.5 = (bf16[48,3072]{1,0:T(8,128)(2,1)S(1)}, bf16[48,3072]{1,0:T(8,128)(2,1)S(1)}, u32[]{:S(2)}, u32[]{:S(2)}) collective-permute-start(bf16[48,3072]{1,0:T(8,128)(2,1)S(1)} %get-tuple-element.21), channel_id=1, source_target_pairs={{0,24},{8,0},{16,8},{24,16},{1,25},{9,1},{17,9},{25,17},{2,26},{10... | collective-permute-start | bytes 884744 | tf_op jit(solution)/shard_map/ppermute | solution.py:26
  51.4 9.9 %collective-permute-start.9 = (bf16[48,3072]{1,0:T(8,128)(2,1)S(1)}, bf16[48,3072]{1,0:T(8,128)(2,1)S(1)}, u32[]{:S(2)}, u32[]{:S(2)}) collective-permute-start(bf16[48,3072]{1,0:T(8,128)(2,1)S(1)} %collective-permute-done.7), channel_id=1, source_target_pairs={{0,8},{8,16},{16,24},{24,0},{1,9},{9,17},{17,25},{25,1},{2,10},{10... | collective-permute-start | bytes 884744 | tf_op jit(solution)/shard_map/ppermute | solution.py:26
  55.9 9.4 %collective-permute-start.6 = (bf16[48,3072]{1,0:T(8,128)(2,1)S(1)}, bf16[48,3072]{1,0:T(8,128)(2,1)S(1)}, u32[]{:S(2)}, u32[]{:S(2)}) collective-permute-start(bf16[48,3072]{1,0:T(8,128)(2,1)S(1)} %collective-permute-done.5), channel_id=1, source_target_pairs={{0,24},{8,0},{16,8},{24,16},{1,25},{9,1},{17,9},{25,17},{2,26},{10... | collective-permute-start | bytes 884744 | tf_op jit(solution)/shard_map/ppermute | solution.py:26
  61.3 1.5 copy-start.8
  68.0 1.0 copy-start.7
  69.0 9.1 %collective-permute-start.10 = (bf16[4,4,96,384]{3,2,1,0:T(8,128)(2,1)}, bf16[4,4,96,384]{3,2,1,0:T(8,128)(2,1)}, u32[]{:S(2)}, u32[]{:S(2)}) collective-permute-start(bf16[4,4,96,384]{3,2,1,0:T(8,128)(2,1)} %get-tuple-element.24), channel_id=1, source_target_pairs={{0,32},{32,0},{1,33},{33,1},{2,34},{34,2},{3,35},{35,3},{4,36},{36... | collective-permute-start | bytes 3538952 | tf_op jit(solution)/shard_map/ppermute | solution.py:183
  71.0 3.1 %copy-start.9 = (bf16[192,3072]{1,0:T(8,128)(2,1)S(1)}, bf16[192,3072]{1,0:T(8,128)(2,1)}, u32[]{:S(2)}) copy-start(bf16[192,3072]{1,0:T(8,128)(2,1)} %copy-done.8) | copy-start | bytes 3538948
  75.7 10.2 %collective-permute-start.19 = (bf16[4,4,96,384]{3,2,1,0:T(8,128)(2,1)S(1)}, bf16[4,4,96,384]{3,2,1,0:T(8,128)(2,1)S(1)}, u32[]{:S(2)}, u32[]{:S(2)}) collective-permute-start(bf16[4,4,96,384]{3,2,1,0:T(8,128)(2,1)S(1)} %get-tuple-element.33), channel_id=1, source_target_pairs={{0,32},{32,0},{1,33},{33,1},{2,34},{34,2},{3,35},{35,3},{4,36},{36... | collective-permute-start | bytes 3538952 | tf_op jit(solution)/shard_map/ppermute | solution.py:183
  79.2 11.8 %collective-permute-start.12 = (bf16[2,48,3072]{2,1,0:T(8,128)(2,1)S(1)}, bf16[2,48,3072]{2,1,0:T(8,128)(2,1)S(1)}, u32[]{:S(2)}, u32[]{:S(2)}) collective-permute-start(bf16[2,48,3072]{2,1,0:T(8,128)(2,1)S(1)} %slice.225), channel_id=1, source_target_pairs={{0,8},{8,0},{16,24},{24,16},{32,56},{40,48},{48,40},{56,32},{1,9},... | collective-permute-start | bytes 1769480 | tf_op jit(solution)/shard_map/ppermute | solution.py:42
  83.0 11.8 %collective-permute-start.11 = (bf16[2,4,96,384]{3,2,1,0:T(8,128)(2,1)S(1)}, bf16[2,4,96,384]{3,2,1,0:T(8,128)(2,1)S(1)}, u32[]{:S(2)}, u32[]{:S(2)}) collective-permute-start(bf16[2,4,96,384]{3,2,1,0:T(8,128)(2,1)S(1)} %add_convert_fusion.1), channel_id=1, source_target_pairs={{0,64},{64,0},{128,192},{192,128},{32,224},{96,160},{160,96},{224,... | collective-permute-start | bytes 1769480 | tf_op jit(solution)/shard_map/ppermute | solution.py:42
  86.0 19.6 %collective-permute-start.20 = (bf16[2,4,96,384]{3,2,1,0:T(8,128)(2,1)S(1)}, bf16[2,4,96,384]{3,2,1,0:T(8,128)(2,1)S(1)}, u32[]{:S(2)}, u32[]{:S(2)}) collective-permute-start(bf16[2,4,96,384]{3,2,1,0:T(8,128)(2,1)S(1)} %add_convert_fusion), channel_id=1, source_target_pairs={{0,64},{64,0},{128,192},{192,128},{32,224},{96,160},{160,96},{224,... | collective-permute-start | bytes 1769480 | tf_op jit(solution)/shard_map/ppermute | solution.py:42
  94.9 13.3 %collective-permute-start.14 = (bf16[48,3072]{1,0:T(8,128)(2,1)S(1)}, bf16[48,3072]{1,0:T(8,128)(2,1)S(1)}, u32[]{:S(2)}, u32[]{:S(2)}) collective-permute-start(bf16[48,3072]{1,0:T(8,128)(2,1)S(1)} %fusion.7), channel_id=1, source_target_pairs={{0,24},{8,16},{16,8},{24,0},{32,40},{40,32},{48,56},{56,48},{1,25}... | collective-permute-start | bytes 884744 | tf_op jit(solution)/shard_map/ppermute | solution.py:42
  100.9 9.8 %collective-permute-start.13 = (bf16[4,96,384]{2,1,0:T(8,128)(2,1)S(1)}, bf16[4,96,384]{2,1,0:T(8,128)(2,1)S(1)}, u32[]{:S(2)}, u32[]{:S(2)}) collective-permute-start(bf16[4,96,384]{2,1,0:T(8,128)(2,1)S(1)} %fusion.6), channel_id=1, source_target_pairs={{0,192},{64,128},{128,64},{192,0},{32,96},{96,32},{160,224},{224,1... | collective-permute-start | bytes 884744 | tf_op jit(solution)/shard_map/ppermute | solution.py:42
  105.7 28.0 %collective-permute-start.21 = (bf16[4,96,384]{2,1,0:T(8,128)(2,1)S(1)}, bf16[4,96,384]{2,1,0:T(8,128)(2,1)S(1)}, u32[]{:S(2)}, u32[]{:S(2)}) collective-permute-start(bf16[4,96,384]{2,1,0:T(8,128)(2,1)S(1)} %fusion.8), channel_id=1, source_target_pairs={{0,192},{64,128},{128,64},{192,0},{32,96},{96,32},{160,224},{224,1... | collective-permute-start | bytes 884744 | tf_op jit(solution)/shard_map/ppermute | solution.py:42
  110.8 24.9 %collective-permute-start.16 = (bf16[24,3072]{1,0:T(8,128)(2,1)S(1)}, bf16[24,3072]{1,0:T(8,128)(2,1)S(1)}, u32[]{:S(2)}, u32[]{:S(2)}) collective-permute-start(bf16[24,3072]{1,0:T(8,128)(2,1)S(1)} %slice.314), channel_id=1, source_target_pairs={{0,2},{1,3},{2,0},{3,1},{4,6},{5,7},{6,4},{7,5},{8,10},{9,11},{10,... | collective-permute-start | bytes 442376 | tf_op jit(solution)/shard_map/ppermute | solution.py:22
  118.0 24.8 %collective-permute-start.15 = (bf16[2,96,384]{2,1,0:T(8,128)(2,1)S(1)}, bf16[2,96,384]{2,1,0:T(8,128)(2,1)S(1)}, u32[]{:S(2)}, u32[]{:S(2)}) collective-permute-start(bf16[2,96,384]{2,1,0:T(8,128)(2,1)S(1)} %fusion.10), channel_id=1, source_target_pairs={{0,256},{256,0},{512,768},{768,512},{32,800},{288,544},{544,288},{... | collective-permute-start | bytes 442376 | tf_op jit(solution)/shard_map/ppermute | solution.py:42
  133.8 28.7 %collective-permute-start.22 = (bf16[2,96,384]{2,1,0:T(8,128)(2,1)S(1)}, bf16[2,96,384]{2,1,0:T(8,128)(2,1)S(1)}, u32[]{:S(2)}, u32[]{:S(2)}) collective-permute-start(bf16[2,96,384]{2,1,0:T(8,128)(2,1)S(1)} %fusion.9), channel_id=1, source_target_pairs={{0,256},{256,0},{512,768},{768,512},{32,800},{288,544},{544,288},{... | collective-permute-start | bytes 442376 | tf_op jit(solution)/shard_map/ppermute | solution.py:42
  143.7 47.5 %copy-start.2 = (bf16[6,3072]{1,0:T(8,128)(2,1)S(1)}, bf16[6,3072]{1,0:T(8,128)(2,1)}, u32[]{:S(2)}) copy-start(bf16[6,3072]{1,0:T(8,128)(2,1)} %layer_input.1) | copy-start | bytes 110596
  143.7 47.5 %copy-start.6 = (f32[3072]{0:T(1024)S(1)}, f32[3072]{0:T(1024)}, u32[]{:S(2)}) copy-start(f32[3072]{0:T(1024)} %param.7) | copy-start | bytes 36868
  143.7 41.9 %collective-permute-start.24 = (bf16[96,384]{1,0:T(8,128)(2,1)S(1)}, bf16[96,384]{1,0:T(8,128)(2,1)S(1)}, u32[]{:S(2)}, u32[]{:S(2)}) collective-permute-start(bf16[96,384]{1,0:T(8,128)(2,1)S(1)} %fusion.11), channel_id=1, source_target_pairs={{0,768},{256,512},{512,256},{768,0},{32,288},{288,32},{544,800},{8... | collective-permute-start | bytes 221192 | tf_op jit(solution)/shard_map/ppermute | solution.py:42
  160.4 31.0 %copy-start.4 = (bf16[6,3072]{1,0:T(8,128)(2,1)S(1)}, bf16[6,3072]{1,0:T(8,128)(2,1)}, u32[]{:S(2)}) copy-start(bf16[6,3072]{1,0:T(8,128)(2,1)} %out_grad.1) | copy-start | bytes 110596
  160.4 20.8 %collective-permute-start.17 = (bf16[12,3072]{1,0:T(8,128)(2,1)S(1)}, bf16[12,3072]{1,0:T(8,128)(2,1)S(1)}, u32[]{:S(2)}, u32[]{:S(2)}) collective-permute-start(bf16[12,3072]{1,0:T(8,128)(2,1)S(1)} %slice.315), channel_id=1, source_target_pairs={{0,1},{1,0},{2,3},{3,2},{4,5},{5,4},{6,7},{7,6},{8,9},{9,8},{10,11... | collective-permute-start | bytes 221192 | tf_op jit(solution)/shard_map/ppermute | solution.py:22
  162.5 24.7 %collective-permute-start.23 = (bf16[96,384]{1,0:T(8,128)(2,1)S(1)}, bf16[96,384]{1,0:T(8,128)(2,1)S(1)}, u32[]{:S(2)}, u32[]{:S(2)}) collective-permute-start(bf16[96,384]{1,0:T(8,128)(2,1)S(1)} %fusion.14), channel_id=1, source_target_pairs={{0,768},{256,512},{512,256},{768,0},{32,288},{288,32},{544,800},{8... | collective-permute-start | bytes 221192 | tf_op jit(solution)/shard_map/ppermute | solution.py:42
  181.3 9.9 %collective-permute-start.18 = (bf16[6,3072]{1,0:T(8,128)(2,1)S(1)}, bf16[6,3072]{1,0:T(8,128)(2,1)S(1)}, u32[]{:S(2)}, u32[]{:S(2)}) collective-permute-start(bf16[6,3072]{1,0:T(8,128)(2,1)S(1)} %slice.316), channel_id=1, source_target_pairs={{0,4},{1,5},{2,6},{3,7},{4,0},{5,1},{6,2},{7,3},{8,12},{9,13},{10,... | collective-permute-start | bytes 110600 | tf_op jit(solution)/shard_map/ppermute | solution.py:22
  (3 other events, 2.5 us)

commit v7 on v6

--- a/solution.py
+++ b/solution.py
@@ -22,8 +22,9 @@
     return lax.ppermute(block, "zl", [(i, i ^ distance) for i in range(8)])
 
 
-def shift(block, distance):
-    return lax.ppermute(block, "x", [(i, (i + distance) % 4) for i in range(4)])
+def x_moves(way):
+    moves = [(4 * c + i, 4 * c + (i + way * (1 - 2 * c)) % 4) for c in range(2) for i in range(4)]
+    return lambda block: lax.ppermute(block, ("c", "x"), moves)
 
 
 def pairs(axis, step):
@@ -59,19 +60,51 @@
     return lax.dynamic_index_in_dim(array, index, axis, keepdims=False)
 
 
-def pack_kernel(layer_input, out_grad, gain, packed, stats):
-    rows, width = layer_input.shape
-    xf = layer_input[...].astype(F32)
+def pack_kernel(layer_input, out_grad, gain, packed, stats, rows_in, grad_in, gain_in, sems):
+    loads = [
+        pltpu.make_async_copy(source, target, sems.at[k])
+        for k, (source, target) in enumerate(
+            ((layer_input, rows_in), (gain, gain_in), (out_grad, grad_in))
+        )
+    ]
+    for load in loads:
+        load.start()
+    rows, width = rows_in.shape
+    half = width // 2
+    loads[0].wait()
+    xf = rows_in[...].astype(F32)
     mean = jnp.mean(xf, axis=1, keepdims=True)
     centered = xf - mean
     rstd = 1.0 / jnp.sqrt(jnp.mean(centered * centered, axis=1, keepdims=True) + 1e-06)
-    normed = (centered * rstd * gain[...]).astype(BF16)
-    half = width // 2
-    for at, block in enumerate((normed, out_grad[...])):
+    loads[1].wait()
+    normed = (centered * rstd * gain_in[...]).astype(BF16)
+    loads[2].wait()
+    for at, block in enumerate((normed, grad_in[...])):
         packed[2 * at * rows : (2 * at + 1) * rows] = block[:, :half]
         packed[(2 * at + 1) * rows : (2 * at + 2) * rows] = block[:, half:]
     stats[:, 0:1] = mean
     stats[:, 1:2] = rstd
+
+
+def pack(layer_input, out_grad, gain):
+    rows, width = layer_input.shape
+    vmem = pl.BlockSpec(memory_space=pltpu.VMEM)
+    return pl.pallas_call(
+        pack_kernel,
+        out_shape=(
+            jax.ShapeDtypeStruct((4 * rows, width // 2), BF16),
+            jax.ShapeDtypeStruct((rows, 2), F32),
+        ),
+        in_specs=[pl.BlockSpec(memory_space=pl.ANY)] * 3,
+        out_specs=(vmem, vmem),
+        scratch_shapes=[
+            pltpu.VMEM((rows, width), BF16),
+            pltpu.VMEM((rows, width), BF16),
+            pltpu.VMEM((1, width), F32),
+            pltpu.SemaphoreType.DMA((3,)),
+        ],
+        compiler_params=pltpu.CompilerParams(vmem_limit_bytes=4 * 1024 * 1024),
+    )(layer_input, out_grad, gain[None])
 
 
 def unpack_kernel(own, far, block):
@@ -101,13 +134,23 @@
     )(*operands)
 
 
-def term_kernel(where, left, right, keep, send):
+def pre_kernel(*refs):
+    pieces, (weight, rows, hidden, slope) = refs[:4], refs[4:]
+    count = pieces[0].shape[0]
+    for k, piece in enumerate(pieces):
+        rows[k * count : (k + 1) * count] = piece[...]
+    pre = jnp.dot(rows[...], weight[...], preferred_element_type=F32)
+    value, slope[...] = gelu_parts(pre)
+    hidden[...] = value.astype(BF16)
+
+
+def write_halves(where, left, right, keep, send):
     part = keep.shape[2]
     c = where[16]
     for g in range(8):
         columns = slice(4 * part * g, 4 * part * (g + 1))
         term = lax.dot_general(
-            left[:, columns], right[...], (((0,), (0,)), ((), ())), preferred_element_type=F32
+            left[:, columns], right, (((0,), (0,)), ((), ())), preferred_element_type=F32
         ).astype(BF16)
         for pair in range(2):
             at_y, there_y = (where[at + 2 * (g % 2) + pair] for at in (0, 8))
@@ -118,23 +161,36 @@
             send[there_y, there_z] = jnp.where(c == 0, high, low)
 
 
-def term_halves(where, left, right):
-    tokens, width = left.shape
-    hidden_width = right.shape[1]
-    half = jax.ShapeDtypeStruct((4, 4, width // 32, hidden_width), BF16)
+def down_kernel(where, *refs):
+    pieces, (hidden, rows, keep, send) = refs[:4], refs[4:]
+    count = pieces[0].shape[0]
+    for k, piece in enumerate(pieces):
+        rows[k * count : (k + 1) * count] = piece[...]
+    write_halves(where, rows, hidden[...], keep, send)
+
+
+def up_kernel(where, grad, normed, slope, weight, pre_grad, keep, send):
+    hidden_grad = lax.dot_general(
+        grad[...], weight[...], (((1,), (1,)), ((), ())), preferred_element_type=F32
+    )
+    product = (hidden_grad * slope[...]).astype(BF16)
+    pre_grad[...] = product
+    write_halves(where, normed, product, keep, send)
+
+
+def computed(kernel, flops, outs, *operands):
     vmem = pl.BlockSpec(memory_space=pltpu.VMEM)
+    scalars = [operand.dtype == jnp.int32 for operand in operands]
     return pl.pallas_call(
-        term_kernel,
-        out_shape=(half, half),
-        in_specs=[pl.BlockSpec(memory_space=pltpu.SMEM), vmem, vmem],
-        out_specs=(vmem, vmem),
+        kernel,
+        out_shape=[jax.ShapeDtypeStruct(*out) for out in outs],
+        in_specs=[pl.BlockSpec(memory_space=pltpu.SMEM) if scalar else vmem for scalar in scalars],
+        out_specs=[vmem] * len(outs),
         compiler_params=pltpu.CompilerParams(vmem_limit_bytes=12 * 1024 * 1024),
         cost_estimate=pl.CostEstimate(
-            flops=2 * tokens * width * hidden_width,
-            bytes_accessed=4 * width * hidden_width,
-            transcendentals=0,
+            flops=flops, bytes_accessed=8 * 1024 * 1024, transcendentals=0
         ),
-    )(where, left, right)
+    )(*operands)
 
 
 def shards(layer_input, out_grad, norm_gain_vector, up_weight, down_weight):
@@ -144,40 +200,39 @@
     zh, y, c = lax.axis_index("zh"), lax.axis_index("y"), lax.axis_index("c")
     x, zl = lax.axis_index("x"), lax.axis_index("zl")
 
-    packed, stats = in_vmem(
-        pack_kernel,
-        [((4 * rows, width // 2), BF16), ((rows, 2), F32)],
-        layer_input,
-        out_grad,
-        norm_gain_vector[None],
-    )
+    packed, stats = pack(layer_input, out_grad, norm_gain_vector)
     (block,) = in_vmem(unpack_kernel, [((4 * rows, width), BF16)], packed, swap(packed, 4))
     middle = nzl * rows
     normed, grad = in_vmem(
         join_kernel, [((middle, width), BF16)] * 2, block, *[swap(block, k) for k in (1, 2, 3)]
     )
-    normed_left, grad_right = shift(normed, 1), shift(grad, -1)
-    grad_left, normed_right = shift(grad, 1), shift(normed, -1)
-    normed_all = jnp.concatenate([normed, normed_left, normed_right, shift(normed_left, 1)])
-    grad_all = jnp.concatenate([grad, grad_left, grad_right, shift(grad_right, -1)])
-
-    pre = jnp.dot(normed_all, up_weight, preferred_element_type=F32)
-    value, slope = gelu_parts(pre)
-    hidden = value.astype(BF16)
-    hidden_grad = jnp.einsum("td,fd->tf", grad_all, down_weight, preferred_element_type=F32)
-    pre_grad = (hidden_grad * slope).astype(BF16)
+    ahead, back = x_moves(1), x_moves(-1)
+    normed_ahead, grad_ahead = ahead(normed), ahead(grad)
+    normed_pieces = normed, normed_ahead, back(normed), ahead(normed_ahead)
+    grad_pieces = grad, grad_ahead, back(grad), ahead(grad_ahead)
 
     four = jnp.arange(4)
     where = [place(own, four, core) for core in (c, 1 - c) for own in (y, zh)]
     where = jnp.concatenate(where + [c[None]]).astype(jnp.int32)
 
+    tokens = nx * middle
+    shape = (tokens, hidden_width)
+    flops = 2 * tokens * width * hidden_width
+    halves = [((4, 4, width // 32, hidden_width), BF16)] * 2
+    rows_of = ((tokens, width), BF16)
+    normed_all, hidden, slope = computed(
+        pre_kernel, flops, [rows_of, (shape, BF16), (shape, F32)], *normed_pieces, up_weight
+    )
+    grad_all, *down = computed(down_kernel, flops, [rows_of] + halves, where, *grad_pieces, hidden)
+    pre_grad, *up = computed(
+        up_kernel, 2 * flops, [(shape, BF16)] + halves, where, grad_all, normed_all, slope, down_weight
+    )
+
     blocks = pre_grad.reshape(nx, middle, hidden_width)
-    near, far = jnp.where(x % 2 == 0, 2, 1), jnp.where(x % 2 == 0, 1, 2)
-    first, second = jnp.where(c == 0, near, far), jnp.where(c == 0, far, near)
+    first, second = jnp.where(x % 2 == 0, 2, 1), jnp.where(x % 2 == 0, 1, 2)
     blocks = jnp.stack([blocks[0], pick(blocks, second, 0), pick(blocks, first, 0), blocks[3]])
 
     fence = lax.optimization_barrier
-    down, up = term_halves(where, grad_all, hidden), term_halves(where, normed_all, pre_grad)
 
     def to_core(term):
         return lax.ppermute(term[1], "c", [(0, 1), (1, 0)])
@@ -198,25 +253,25 @@
     def to_second_z(term, got):
         return paired(added(summed(term, 1), got[1]).astype(BF16), "zh", 1)
 
-    down_core, up_core = to_core(down), to_core(up)
-    down_core, blocks = fence((down_core, blocks))
+    up_core, down_core = to_core(up), to_core(down)
+    up_core, blocks = fence((up_core, blocks))
     full_term = jnp.einsum("xtf,df->xtd", blocks, up_weight, preferred_element_type=F32)
     full_term = full_term.astype(BF16)
     x_first = paired(full_term[2:], "x", 0)
-    down_y, up_y = to_y(down, down_core), to_y(up, up_core)
-    down_y, x_first = fence((down_y, x_first))
+    up_y, down_y = to_y(up, up_core), to_y(down, down_core)
+    up_y, x_first = fence((up_y, x_first))
     x_second = paired(added(full_term[1], x_first[1]).astype(BF16), "x", 1)
     own = added(full_term[0], x_first[0], x_second)
-    down_y2, up_y2 = to_second_y(down, down_core, down_y), to_second_y(up, up_core, up_y)
-    down_y2, own = fence((down_y2, own))
+    up_y2, down_y2 = to_second_y(up, up_core, up_y), to_second_y(down, down_core, down_y)
+    up_y2, own = fence((up_y2, own))
     half = own.shape[0] // 2
     own = added(own[:half], swap(own[half:].astype(BF16), 2))
-    down, up = (down[0], down_core, down_y, down_y2), (up[0], up_core, up_y, up_y2)
-    down_z, up_z = to_z(*down), to_z(*up)
-    down_z, own = fence((down_z, own))
+    up, down = (up[0], up_core, up_y, up_y2), (down[0], down_core, down_y, down_y2)
+    up_z, down_z = to_z(*up), to_z(*down)
+    up_z, own = fence((up_z, own))
     half = own.shape[0] // 2
     own = added(own[:half], swap(own[half:].astype(BF16), 1))
-    down_z2, up_z2 = to_second_z(down, down_z), to_second_z(up, up_z)
+    up_z2, down_z2 = to_second_z(up, up_z), to_second_z(down, down_z)
     normed_grad = added(own[:rows], swap(own[rows:].astype(BF16), 4))
     down_grad = added(summed(down, 0), down_z[0], down_z2).T
     up_grad = added(summed(up, 0), up_z[0], up_z2)

time: 193 us -> 197 us (1.021)
  the two profiles are of different devices: /device:TPU:24 before, /device:TPU:34 now
where the time goes in v7:
time: 197 us; the launch traced here: 196 us
  starting transfers between devices  131 us (66%)
  waiting for transfers between devices  37.6 us (19%)
  other arithmetic  13 us (7%)
  Pallas kernels  7.65 us (4%)
  local copies, waits for them, and re-layouts  4.38 us (2%)
    ppermute x10, starting transfers between devices, paired(): return lax.ppermute(block, names, moves)  80.2 us
    ppermute x7, starting transfers between devices, swap(): return lax.ppermute(block, 'zl', [(i, i ^ distance) for i in range(8)])  28.3 us
    ppermute x6, starting transfers between devices, x_moves(): return lambda block: lax.ppermute(block, ('c', 'x'), moves)  18.2 us
    ppermute x10, waiting for transfers between devices, paired(): return lax.ppermute(block, names, moves)  16.7 us
    ppermute x7, waiting for transfers between devices, swap(): return lax.ppermute(block, 'zl', [(i, i ^ distance) for i in range(8)])  16.4 us
    pallas_call x3, Pallas kernels, computed(): pl.pallas_call(kernel, out_shape=[jax.ShapeDtypeStruct(*out) for out in o...  7.18 us
    ppermute x6, waiting for transfers between devices, x_moves(): return lambda block: lax.ppermute(block, ('c', 'x'), moves)  4.57 us
    ppermute x2, starting transfers between devices, to_core(): return lax.ppermute(term[1], 'c', [(0, 1), (1, 0)])  4.31 us
  transfers between devices with their start and end apart: 25, of which 9 were waited for; matrix products, arithmetic and copies ran while one was open for 7% of the time, Pallas kernels for 2%

profile of v7, /device:TPU:34, one launch (start us, length us, event | category | flops | bytes accessed | tf_op | source)
XLA Modules:
  0.0 195.9 jit_solution(8368358153645966118)
XLA Ops:
  3.3 9.1 %collective-permute-start = (bf16[24,1536]{1,0:T(8,128)(2,1)S(1)}, bf16[24,1536]{1,0:T(8,128)(2,1)S(1)}, u32[]{:S(2)}, u32[]{:S(2)}) collective-permute-start(bf16[24,1536]{1,0:T(8,128)(2,1)S(1)} %get-tuple-element.25.own), channel_id=1, source_target_pairs={{0,4},{1,5},{2,6},{3,7},{4,0},{5,1},{6,2},{7,3},{8,12},{9,13},{10,... | collective-permute-start | bytes 221192 | tf_op jit(solution)/shard_map/ppermute | solution.py:22
  12.4 5.5 %collective-permute-done.far = bf16[24,1536]{1,0:T(8,128)(2,1)S(1)} collective-permute-done((bf16[24,1536]{1,0:T(8,128)(2,1)S(1)}, bf16[24,1536]{1,0:T(8,128)(2,1)S(1)}, u32[]{:S(2)}, u32[]{:S(2)}) %collective-permute-start) | collective-permute-done | bytes 73760 | tf_op jit(solution)/shard_map/ppermute | solution.py:22
  18.0 3.6 %collective-permute-start.1 = (bf16[24,3072]{1,0:T(8,128)(2,1)S(1)}, bf16[24,3072]{1,0:T(8,128)(2,1)S(1)}, u32[]{:S(2)}, u32[]{:S(2)}) collective-permute-start(bf16[24,3072]{1,0:T(8,128)(2,1)S(1)} %shard_map.77.refs_0_), channel_id=1, source_target_pairs={{0,1},{1,0},{2,3},{3,2},{4,5},{5,4},{6,7},{7,6},{8,9},{9,8},{10,11... | collective-permute-start | bytes 442376 | tf_op jit(solution)/shard_map/ppermute | solution.py:22
  21.5 2.9 %collective-permute-start.2 = (bf16[24,3072]{1,0:T(8,128)(2,1)S(1)}, bf16[24,3072]{1,0:T(8,128)(2,1)S(1)}, u32[]{:S(2)}, u32[]{:S(2)}) collective-permute-start(bf16[24,3072]{1,0:T(8,128)(2,1)S(1)} %shard_map.77.refs_0_), channel_id=1, source_target_pairs={{0,2},{1,3},{2,0},{3,1},{4,6},{5,7},{6,4},{7,5},{8,10},{9,11},{10,... | collective-permute-start | bytes 442376 | tf_op jit(solution)/shard_map/ppermute | solution.py:22
  24.5 2.7 %collective-permute-start.3 = (bf16[24,3072]{1,0:T(8,128)(2,1)S(1)}, bf16[24,3072]{1,0:T(8,128)(2,1)S(1)}, u32[]{:S(2)}, u32[]{:S(2)}) collective-permute-start(bf16[24,3072]{1,0:T(8,128)(2,1)S(1)} %shard_map.77.refs_0_), channel_id=1, source_target_pairs={{0,3},{1,2},{2,1},{3,0},{4,7},{5,6},{6,5},{7,4},{8,11},{9,10},{10,... | collective-permute-start | bytes 442376 | tf_op jit(solution)/shard_map/ppermute | solution.py:22
  27.2 7.8 %collective-permute-done.2.refs_2_ = bf16[24,3072]{1,0:T(8,128)(2,1)S(1)} collective-permute-done((bf16[24,3072]{1,0:T(8,128)(2,1)S(1)}, bf16[24,3072]{1,0:T(8,128)(2,1)S(1)}, u32[]{:S(2)}, u32[]{:S(2)}) %collective-permute-start.2) | collective-permute-done | bytes 147488 | tf_op jit(solution)/shard_map/ppermute | solution.py:22
  35.0 3.1 %collective-permute-done.3.refs_3_ = bf16[24,3072]{1,0:T(8,128)(2,1)S(1)} collective-permute-done((bf16[24,3072]{1,0:T(8,128)(2,1)S(1)}, bf16[24,3072]{1,0:T(8,128)(2,1)S(1)}, u32[]{:S(2)}, u32[]{:S(2)}) %collective-permute-start.3) | collective-permute-done | bytes 147488 | tf_op jit(solution)/shard_map/ppermute | solution.py:22
  38.2 3.4 %collective-permute-start.7 = (bf16[48,3072]{1,0:T(8,128)(2,1)S(1)}, bf16[48,3072]{1,0:T(8,128)(2,1)S(1)}, u32[]{:S(2)}, u32[]{:S(2)}) collective-permute-start(bf16[48,3072]{1,0:T(8,128)(2,1)S(1)} %get-tuple-element.27.refs_0_), channel_id=1, source_target_pairs={{0,8},{8,16},{16,24},{24,0},{32,56},{40,32},{48,40},{56,48},{1,9},... | collective-permute-start | bytes 884744 | tf_op jit(solution)/shard_map/ppermute | solution.py:27
  41.6 3.1 %collective-permute-start.4 = (bf16[48,3072]{1,0:T(8,128)(2,1)S(1)}, bf16[48,3072]{1,0:T(8,128)(2,1)S(1)}, u32[]{:S(2)}, u32[]{:S(2)}) collective-permute-start(bf16[48,3072]{1,0:T(8,128)(2,1)S(1)} %get-tuple-element.26.refs_0_), channel_id=1, source_target_pairs={{0,8},{8,16},{16,24},{24,0},{32,56},{40,32},{48,40},{56,48},{1,9},... | collective-permute-start | bytes 884744 | tf_op jit(solution)/shard_map/ppermute | solution.py:27
  44.7 2.7 %collective-permute-start.8 = (bf16[48,3072]{1,0:T(8,128)(2,1)S(1)}, bf16[48,3072]{1,0:T(8,128)(2,1)S(1)}, u32[]{:S(2)}, u32[]{:S(2)}) collective-permute-start(bf16[48,3072]{1,0:T(8,128)(2,1)S(1)} %get-tuple-element.27.refs_0_), channel_id=1, source_target_pairs={{0,24},{8,0},{16,8},{24,16},{32,40},{40,48},{48,56},{56,32},{1,25}... | collective-permute-start | bytes 884744 | tf_op jit(solution)/shard_map/ppermute | solution.py:27
  47.4 3.1 %collective-permute-start.9 = (bf16[48,3072]{1,0:T(8,128)(2,1)S(1)}, bf16[48,3072]{1,0:T(8,128)(2,1)S(1)}, u32[]{:S(2)}, u32[]{:S(2)}) collective-permute-start(bf16[48,3072]{1,0:T(8,128)(2,1)S(1)} %collective-permute-done.7.refs_1_), channel_id=1, source_target_pairs={{0,8},{8,16},{16,24},{24,0},{32,56},{40,32},{48,40},{56,48},{1,9},... | collective-permute-start | bytes 884744 | tf_op jit(solution)/shard_map/ppermute | solution.py:27
  50.5 3.3 %collective-permute-start.5 = (bf16[48,3072]{1,0:T(8,128)(2,1)S(1)}, bf16[48,3072]{1,0:T(8,128)(2,1)S(1)}, u32[]{:S(2)}, u32[]{:S(2)}) collective-permute-start(bf16[48,3072]{1,0:T(8,128)(2,1)S(1)} %get-tuple-element.26.refs_0_), channel_id=1, source_target_pairs={{0,24},{8,0},{16,8},{24,16},{32,40},{40,48},{48,56},{56,32},{1,25}... | collective-permute-start | bytes 884744 | tf_op jit(solution)/shard_map/ppermute | solution.py:27
  53.8 2.6 %collective-permute-start.6 = (bf16[48,3072]{1,0:T(8,128)(2,1)S(1)}, bf16[48,3072]{1,0:T(8,128)(2,1)S(1)}, u32[]{:S(2)}, u32[]{:S(2)}) collective-permute-start(bf16[48,3072]{1,0:T(8,128)(2,1)S(1)} %collective-permute-done.4.refs_1_), channel_id=1, source_target_pairs={{0,8},{8,16},{16,24},{24,0},{32,56},{40,32},{48,40},{56,48},{1,9},... | collective-permute-start | bytes 884744 | tf_op jit(solution)/shard_map/ppermute | solution.py:27
  56.6 2.5 %collective-permute-done.9.refs_3_ = bf16[48,3072]{1,0:T(8,128)(2,1)S(1)} collective-permute-done((bf16[48,3072]{1,0:T(8,128)(2,1)S(1)}, bf16[48,3072]{1,0:T(8,128)(2,1)S(1)}, u32[]{:S(2)}, u32[]{:S(2)}) %collective-permute-start.9) | collective-permute-done | bytes 294944 | tf_op jit(solution)/shard_map/ppermute | solution.py:27
  63.6 2.7 %shard_map.80 = (bf16[192,3072]{1,0:T(8,128)(2,1)S(1)}, bf16[4,4,96,384]{3,2,1,0:T(8,128)(2,1)S(1)}, bf16[4,4,96,384]{3,2,1,0:T(8,128)(2,1)}) custom-call(s32[17]{0:T(128)S(1)} %concatenate.3.where, bf16[48,3072]{1,0:T(8,128)(2,1)S(1)} %get-tuple-element.26.refs_0_, bf16[48,3072]{1,0:T(8,128)(2,1)S(1)} %collective-permute-done.4.refs_1_, ...), custom_call_target="tpu_custom_call" | custom-call | flops 452984832 | bytes 8388608 | tf_op jit(solution)/shard_map/pallas_call | solution.py:184
  68.3 3.7 %shard_map.81 = (bf16[192,384]{1,0:T(8,128)(2,1)S(1)}, bf16[4,4,96,384]{3,2,1,0:T(8,128)(2,1)S(1)}, bf16[4,4,96,384]{3,2,1,0:T(8,128)(2,1)}) custom-call(s32[17]{0:T(128)S(1)} %concatenate.3.where, bf16[192,3072]{1,0:T(8,128)(2,1)S(1)} %get-tuple-element.29.grad, bf16[192,3072]{1,0:T(8,128)(2,1)S(1)} %get-tuple-element.30.normed, ...), custom_call_target="tpu_custom_call" | custom-call | flops 905969664 | bytes 8388608 | tf_op jit(solution)/shard_map/pallas_call | solution.py:184
  71.9 2.4 %collective-permute-start.10 = (bf16[4,4,96,384]{3,2,1,0:T(8,128)(2,1)}, bf16[4,4,96,384]{3,2,1,0:T(8,128)(2,1)}, u32[]{:S(2)}, u32[]{:S(2)}) collective-permute-start(bf16[4,4,96,384]{3,2,1,0:T(8,128)(2,1)} %get-tuple-element.33), channel_id=1, source_target_pairs={{0,32},{32,0},{1,33},{33,1},{2,34},{34,2},{3,35},{35,3},{4,36},{36... | collective-permute-start | bytes 3538952 | tf_op jit(solution)/shard_map/ppermute | solution.py:238
  75.8 2.7 %collective-permute-start.21 = (bf16[2,4,96,384]{3,2,1,0:T(8,128)(2,1)S(1)}, bf16[2,4,96,384]{3,2,1,0:T(8,128)(2,1)S(1)}, u32[]{:S(2)}, u32[]{:S(2)}) collective-permute-start(bf16[2,4,96,384]{3,2,1,0:T(8,128)(2,1)S(1)} %add_convert_fusion), channel_id=1, source_target_pairs={{0,64},{64,0},{128,192},{192,128},{32,224},{96,160},{160,96},{224,... | collective-permute-start | bytes 1769480 | tf_op jit(solution)/shard_map/ppermute | solution.py:43
  79.6 5.1 %collective-permute-start.12 = (bf16[2,48,3072]{2,1,0:T(8,128)(2,1)S(1)}, bf16[2,48,3072]{2,1,0:T(8,128)(2,1)S(1)}, u32[]{:S(2)}, u32[]{:S(2)}) collective-permute-start(bf16[2,48,3072]{2,1,0:T(8,128)(2,1)S(1)} %slice.223), channel_id=1, source_target_pairs={{0,8},{8,0},{16,24},{24,16},{32,56},{40,48},{48,40},{56,32},{1,9},... | collective-permute-start | bytes 1769480 | tf_op jit(solution)/shard_map/ppermute | solution.py:43
  85.9 3.1 %collective-permute-start.11 = (bf16[2,4,96,384]{3,2,1,0:T(8,128)(2,1)S(1)}, bf16[2,4,96,384]{3,2,1,0:T(8,128)(2,1)S(1)}, u32[]{:S(2)}, u32[]{:S(2)}) collective-permute-start(bf16[2,4,96,384]{3,2,1,0:T(8,128)(2,1)S(1)} %add_convert_fusion.1), channel_id=1, source_target_pairs={{0,64},{64,0},{128,192},{192,128},{32,224},{96,160},{160,96},{224,... | collective-permute-start | bytes 1769480 | tf_op jit(solution)/shard_map/ppermute | solution.py:43
  90.3 4.1 %collective-permute-start.22 = (bf16[4,96,384]{2,1,0:T(8,128)(2,1)S(1)}, bf16[4,96,384]{2,1,0:T(8,128)(2,1)S(1)}, u32[]{:S(2)}, u32[]{:S(2)}) collective-permute-start(bf16[4,96,384]{2,1,0:T(8,128)(2,1)S(1)} %fusion.3), channel_id=1, source_target_pairs={{0,192},{64,128},{128,64},{192,0},{32,96},{96,32},{160,224},{224,1... | collective-permute-start | bytes 884744 | tf_op jit(solution)/shard_map/ppermute | solution.py:43
  94.5 6.4 %collective-permute-done.11 = bf16[2,4,96,384]{3,2,1,0:T(8,128)(2,1)S(1)} collective-permute-done((bf16[2,4,96,384]{3,2,1,0:T(8,128)(2,1)S(1)}, bf16[2,4,96,384]{3,2,1,0:T(8,128)(2,1)S(1)}, u32[]{:S(2)}, u32[]{:S(2)}) %collective-permute-start.11) | collective-permute-done | bytes 589856 | tf_op jit(solution)/shard_map/ppermute | solution.py:43
  103.9 4.1 %collective-permute-start.13 = (bf16[4,96,384]{2,1,0:T(8,128)(2,1)S(1)}, bf16[4,96,384]{2,1,0:T(8,128)(2,1)S(1)}, u32[]{:S(2)}, u32[]{:S(2)}) collective-permute-start(bf16[4,96,384]{2,1,0:T(8,128)(2,1)S(1)} %fusion.1), channel_id=1, source_target_pairs={{0,192},{64,128},{128,64},{192,0},{32,96},{96,32},{160,224},{224,1... | collective-permute-start | bytes 884744 | tf_op jit(solution)/shard_map/ppermute | solution.py:43
  109.0 15.7 %collective-permute-start.23 = (bf16[2,96,384]{2,1,0:T(8,128)(2,1)S(1)}, bf16[2,96,384]{2,1,0:T(8,128)(2,1)S(1)}, u32[]{:S(2)}, u32[]{:S(2)}) collective-permute-start(bf16[2,96,384]{2,1,0:T(8,128)(2,1)S(1)} %fusion.4), channel_id=1, source_target_pairs={{0,256},{256,0},{512,768},{768,512},{32,800},{288,544},{544,288},{... | collective-permute-start | bytes 442376 | tf_op jit(solution)/shard_map/ppermute | solution.py:43
  124.9 2.5 %collective-permute-start.16 = (bf16[24,3072]{1,0:T(8,128)(2,1)S(1)}, bf16[24,3072]{1,0:T(8,128)(2,1)S(1)}, u32[]{:S(2)}, u32[]{:S(2)}) collective-permute-start(bf16[24,3072]{1,0:T(8,128)(2,1)S(1)} %slice.312), channel_id=1, source_target_pairs={{0,2},{1,3},{2,0},{3,1},{4,6},{5,7},{6,4},{7,5},{8,10},{9,11},{10,... | collective-permute-start | bytes 442376 | tf_op jit(solution)/shard_map/ppermute | solution.py:22
  128.4 4.6 %collective-permute-start.15 = (bf16[2,96,384]{2,1,0:T(8,128)(2,1)S(1)}, bf16[2,96,384]{2,1,0:T(8,128)(2,1)S(1)}, u32[]{:S(2)}, u32[]{:S(2)}) collective-permute-start(bf16[2,96,384]{2,1,0:T(8,128)(2,1)S(1)} %fusion.5), channel_id=1, source_target_pairs={{0,256},{256,0},{512,768},{768,512},{32,800},{288,544},{544,288},{... | collective-permute-start | bytes 442376 | tf_op jit(solution)/shard_map/ppermute | solution.py:43
  133.0 2.9 %collective-permute-done.23 = bf16[2,96,384]{2,1,0:T(8,128)(2,1)S(1)} collective-permute-done((bf16[2,96,384]{2,1,0:T(8,128)(2,1)S(1)}, bf16[2,96,384]{2,1,0:T(8,128)(2,1)S(1)}, u32[]{:S(2)}, u32[]{:S(2)}) %collective-permute-start.23) | collective-permute-done | bytes 147488 | tf_op jit(solution)/shard_map/ppermute | solution.py:43
  136.8 33.6 %collective-permute-start.24 = (bf16[96,384]{1,0:T(8,128)(2,1)S(1)}, bf16[96,384]{1,0:T(8,128)(2,1)S(1)}, u32[]{:S(2)}, u32[]{:S(2)}) collective-permute-start(bf16[96,384]{1,0:T(8,128)(2,1)S(1)} %fusion.6), channel_id=1, source_target_pairs={{0,768},{256,512},{512,256},{768,0},{32,288},{288,32},{544,800},{8... | collective-permute-start | bytes 221192 | tf_op jit(solution)/shard_map/ppermute | solution.py:43
  170.5 2.1 %collective-permute-start.17 = (bf16[12,3072]{1,0:T(8,128)(2,1)S(1)}, bf16[12,3072]{1,0:T(8,128)(2,1)S(1)}, u32[]{:S(2)}, u32[]{:S(2)}) collective-permute-start(bf16[12,3072]{1,0:T(8,128)(2,1)S(1)} %slice.313), channel_id=1, source_target_pairs={{0,1},{1,0},{2,3},{3,2},{4,5},{5,4},{6,7},{7,6},{8,9},{9,8},{10,11... | collective-permute-start | bytes 221192 | tf_op jit(solution)/shard_map/ppermute | solution.py:22
  173.5 5.2 %collective-permute-start.19 = (bf16[96,384]{1,0:T(8,128)(2,1)S(1)}, bf16[96,384]{1,0:T(8,128)(2,1)S(1)}, u32[]{:S(2)}, u32[]{:S(2)}) collective-permute-start(bf16[96,384]{1,0:T(8,128)(2,1)S(1)} %fusion.9), channel_id=1, source_target_pairs={{0,768},{256,512},{512,256},{768,0},{32,288},{288,32},{544,800},{8... | collective-permute-start | bytes 221192 | tf_op jit(solution)/shard_map/ppermute | solution.py:43
  178.8 5.5 %collective-permute-start.18 = (bf16[6,3072]{1,0:T(8,128)(2,1)S(1)}, bf16[6,3072]{1,0:T(8,128)(2,1)S(1)}, u32[]{:S(2)}, u32[]{:S(2)}) collective-permute-start(bf16[6,3072]{1,0:T(8,128)(2,1)S(1)} %slice.314), channel_id=1, source_target_pairs={{0,4},{1,5},{2,6},{3,7},{4,0},{5,1},{6,2},{7,3},{8,12},{9,13},{10,... | collective-permute-start | bytes 110600 | tf_op jit(solution)/shard_map/ppermute | solution.py:22
  185.9 7.4 %collective-permute-done.19 = bf16[96,384]{1,0:T(8,128)(2,1)S(1)} collective-permute-done((bf16[96,384]{1,0:T(8,128)(2,1)S(1)}, bf16[96,384]{1,0:T(8,128)(2,1)S(1)}, u32[]{:S(2)}, u32[]{:S(2)}) %collective-permute-start.19) | collective-permute-done | bytes 73760 | tf_op jit(solution)/shard_map/ppermute | solution.py:43
  (72 shorter events, 25.7 us)
Async XLA Ops:
  0.6 0.8 copy-start.3
  3.3 14.6 %collective-permute-start = (bf16[24,1536]{1,0:T(8,128)(2,1)S(1)}, bf16[24,1536]{1,0:T(8,128)(2,1)S(1)}, u32[]{:S(2)}, u32[]{:S(2)}) collective-permute-start(bf16[24,1536]{1,0:T(8,128)(2,1)S(1)} %get-tuple-element.25.own), channel_id=1, source_target_pairs={{0,4},{1,5},{2,6},{3,7},{4,0},{5,1},{6,2},{7,3},{8,12},{9,13},{10,... | collective-permute-start | bytes 221192 | tf_op jit(solution)/shard_map/ppermute | solution.py:22
  18.0 9.2 %collective-permute-start.1 = (bf16[24,3072]{1,0:T(8,128)(2,1)S(1)}, bf16[24,3072]{1,0:T(8,128)(2,1)S(1)}, u32[]{:S(2)}, u32[]{:S(2)}) collective-permute-start(bf16[24,3072]{1,0:T(8,128)(2,1)S(1)} %shard_map.77.refs_0_), channel_id=1, source_target_pairs={{0,1},{1,0},{2,3},{3,2},{4,5},{5,4},{6,7},{7,6},{8,9},{9,8},{10,11... | collective-permute-start | bytes 442376 | tf_op jit(solution)/shard_map/ppermute | solution.py:22
  21.5 13.5 %collective-permute-start.2 = (bf16[24,3072]{1,0:T(8,128)(2,1)S(1)}, bf16[24,3072]{1,0:T(8,128)(2,1)S(1)}, u32[]{:S(2)}, u32[]{:S(2)}) collective-permute-start(bf16[24,3072]{1,0:T(8,128)(2,1)S(1)} %shard_map.77.refs_0_), channel_id=1, source_target_pairs={{0,2},{1,3},{2,0},{3,1},{4,6},{5,7},{6,4},{7,5},{8,10},{9,11},{10,... | collective-permute-start | bytes 442376 | tf_op jit(solution)/shard_map/ppermute | solution.py:22
  24.5 13.6 %collective-permute-start.3 = (bf16[24,3072]{1,0:T(8,128)(2,1)S(1)}, bf16[24,3072]{1,0:T(8,128)(2,1)S(1)}, u32[]{:S(2)}, u32[]{:S(2)}) collective-permute-start(bf16[24,3072]{1,0:T(8,128)(2,1)S(1)} %shard_map.77.refs_0_), channel_id=1, source_target_pairs={{0,3},{1,2},{2,1},{3,0},{4,7},{5,6},{6,5},{7,4},{8,11},{9,10},{10,... | collective-permute-start | bytes 442376 | tf_op jit(solution)/shard_map/ppermute | solution.py:22
  38.2 9.3 %collective-permute-start.7 = (bf16[48,3072]{1,0:T(8,128)(2,1)S(1)}, bf16[48,3072]{1,0:T(8,128)(2,1)S(1)}, u32[]{:S(2)}, u32[]{:S(2)}) collective-permute-start(bf16[48,3072]{1,0:T(8,128)(2,1)S(1)} %get-tuple-element.27.refs_0_), channel_id=1, source_target_pairs={{0,8},{8,16},{16,24},{24,0},{32,56},{40,32},{48,40},{56,48},{1,9},... | collective-permute-start | bytes 884744 | tf_op jit(solution)/shard_map/ppermute | solution.py:27
  41.6 12.2 %collective-permute-start.4 = (bf16[48,3072]{1,0:T(8,128)(2,1)S(1)}, bf16[48,3072]{1,0:T(8,128)(2,1)S(1)}, u32[]{:S(2)}, u32[]{:S(2)}) collective-permute-start(bf16[48,3072]{1,0:T(8,128)(2,1)S(1)} %get-tuple-element.26.refs_0_), channel_id=1, source_target_pairs={{0,8},{8,16},{16,24},{24,0},{32,56},{40,32},{48,40},{56,48},{1,9},... | collective-permute-start | bytes 884744 | tf_op jit(solution)/shard_map/ppermute | solution.py:27
  44.7 11.9 %collective-permute-start.8 = (bf16[48,3072]{1,0:T(8,128)(2,1)S(1)}, bf16[48,3072]{1,0:T(8,128)(2,1)S(1)}, u32[]{:S(2)}, u32[]{:S(2)}) collective-permute-start(bf16[48,3072]{1,0:T(8,128)(2,1)S(1)} %get-tuple-element.27.refs_0_), channel_id=1, source_target_pairs={{0,24},{8,0},{16,8},{24,16},{32,40},{40,48},{48,56},{56,32},{1,25}... | collective-permute-start | bytes 884744 | tf_op jit(solution)/shard_map/ppermute | solution.py:27
  47.4 11.6 %collective-permute-start.9 = (bf16[48,3072]{1,0:T(8,128)(2,1)S(1)}, bf16[48,3072]{1,0:T(8,128)(2,1)S(1)}, u32[]{:S(2)}, u32[]{:S(2)}) collective-permute-start(bf16[48,3072]{1,0:T(8,128)(2,1)S(1)} %collective-permute-done.7.refs_1_), channel_id=1, source_target_pairs={{0,8},{8,16},{16,24},{24,0},{32,56},{40,32},{48,40},{56,48},{1,9},... | collective-permute-start | bytes 884744 | tf_op jit(solution)/shard_map/ppermute | solution.py:27
  50.5 11.9 %collective-permute-start.5 = (bf16[48,3072]{1,0:T(8,128)(2,1)S(1)}, bf16[48,3072]{1,0:T(8,128)(2,1)S(1)}, u32[]{:S(2)}, u32[]{:S(2)}) collective-permute-start(bf16[48,3072]{1,0:T(8,128)(2,1)S(1)} %get-tuple-element.26.refs_0_), channel_id=1, source_target_pairs={{0,24},{8,0},{16,8},{24,16},{32,40},{40,48},{48,56},{56,32},{1,25}... | collective-permute-start | bytes 884744 | tf_op jit(solution)/shard_map/ppermute | solution.py:27
  53.8 9.8 %collective-permute-start.6 = (bf16[48,3072]{1,0:T(8,128)(2,1)S(1)}, bf16[48,3072]{1,0:T(8,128)(2,1)S(1)}, u32[]{:S(2)}, u32[]{:S(2)}) collective-permute-start(bf16[48,3072]{1,0:T(8,128)(2,1)S(1)} %collective-permute-done.4.refs_1_), channel_id=1, source_target_pairs={{0,8},{8,16},{16,24},{24,0},{32,56},{40,32},{48,40},{56,48},{1,9},... | collective-permute-start | bytes 884744 | tf_op jit(solution)/shard_map/ppermute | solution.py:27
  59.1 1.7 copy-start
  60.7 7.5 %copy-start.2 = (bf16[384,3072]{1,0:T(8,128)(2,1)S(1)}, bf16[384,3072]{1,0:T(8,128)(2,1)}, u32[]{:S(2)}) copy-start(bf16[384,3072]{1,0:T(8,128)(2,1)} %weight.1) | copy-start | bytes 7077892
  66.3 8.1 %collective-permute-start.20 = (bf16[4,4,96,384]{3,2,1,0:T(8,128)(2,1)}, bf16[4,4,96,384]{3,2,1,0:T(8,128)(2,1)}, u32[]{:S(2)}, u32[]{:S(2)}) collective-permute-start(bf16[4,4,96,384]{3,2,1,0:T(8,128)(2,1)} %get-tuple-element.44), channel_id=1, source_target_pairs={{0,32},{32,0},{1,33},{33,1},{2,34},{34,2},{3,35},{35,3},{4,36},{36... | collective-permute-start | bytes 3538952 | tf_op jit(solution)/shard_map/ppermute | solution.py:238
  71.9 6.6 %collective-permute-start.10 = (bf16[4,4,96,384]{3,2,1,0:T(8,128)(2,1)}, bf16[4,4,96,384]{3,2,1,0:T(8,128)(2,1)}, u32[]{:S(2)}, u32[]{:S(2)}) collective-permute-start(bf16[4,4,96,384]{3,2,1,0:T(8,128)(2,1)} %get-tuple-element.33), channel_id=1, source_target_pairs={{0,32},{32,0},{1,33},{33,1},{2,34},{34,2},{3,35},{35,3},{4,36},{36... | collective-permute-start | bytes 3538952 | tf_op jit(solution)/shard_map/ppermute | solution.py:238
  74.3 4.2 %copy-start.1 = (bf16[3072,384]{1,0:T(8,128)(2,1)S(1)}, bf16[3072,384]{1,0:T(8,128)(2,1)}, u32[]{:S(2)}) copy-start(bf16[3072,384]{1,0:T(8,128)(2,1)} %refs_4_.1) | copy-start | bytes 7077892
  75.8 13.5 %collective-permute-start.21 = (bf16[2,4,96,384]{3,2,1,0:T(8,128)(2,1)S(1)}, bf16[2,4,96,384]{3,2,1,0:T(8,128)(2,1)S(1)}, u32[]{:S(2)}, u32[]{:S(2)}) collective-permute-start(bf16[2,4,96,384]{3,2,1,0:T(8,128)(2,1)S(1)} %add_convert_fusion), channel_id=1, source_target_pairs={{0,64},{64,0},{128,192},{192,128},{32,224},{96,160},{160,96},{224,... | collective-permute-start | bytes 1769480 | tf_op jit(solution)/shard_map/ppermute | solution.py:43
  79.6 14.9 %collective-permute-start.12 = (bf16[2,48,3072]{2,1,0:T(8,128)(2,1)S(1)}, bf16[2,48,3072]{2,1,0:T(8,128)(2,1)S(1)}, u32[]{:S(2)}, u32[]{:S(2)}) collective-permute-start(bf16[2,48,3072]{2,1,0:T(8,128)(2,1)S(1)} %slice.223), channel_id=1, source_target_pairs={{0,8},{8,0},{16,24},{24,16},{32,56},{40,48},{48,40},{56,32},{1,9},... | collective-permute-start | bytes 1769480 | tf_op jit(solution)/shard_map/ppermute | solution.py:43
  85.9 14.9 %collective-permute-start.11 = (bf16[2,4,96,384]{3,2,1,0:T(8,128)(2,1)S(1)}, bf16[2,4,96,384]{3,2,1,0:T(8,128)(2,1)S(1)}, u32[]{:S(2)}, u32[]{:S(2)}) collective-permute-start(bf16[2,4,96,384]{3,2,1,0:T(8,128)(2,1)S(1)} %add_convert_fusion.1), channel_id=1, source_target_pairs={{0,64},{64,0},{128,192},{192,128},{32,224},{96,160},{160,96},{224,... | collective-permute-start | bytes 1769480 | tf_op jit(solution)/shard_map/ppermute | solution.py:43
  90.3 17.7 %collective-permute-start.22 = (bf16[4,96,384]{2,1,0:T(8,128)(2,1)S(1)}, bf16[4,96,384]{2,1,0:T(8,128)(2,1)S(1)}, u32[]{:S(2)}, u32[]{:S(2)}) collective-permute-start(bf16[4,96,384]{2,1,0:T(8,128)(2,1)S(1)} %fusion.3), channel_id=1, source_target_pairs={{0,192},{64,128},{128,64},{192,0},{32,96},{96,32},{160,224},{224,1... | collective-permute-start | bytes 884744 | tf_op jit(solution)/shard_map/ppermute | solution.py:43
  100.9 23.8 %collective-permute-start.14 = (bf16[48,3072]{1,0:T(8,128)(2,1)S(1)}, bf16[48,3072]{1,0:T(8,128)(2,1)S(1)}, u32[]{:S(2)}, u32[]{:S(2)}) collective-permute-start(bf16[48,3072]{1,0:T(8,128)(2,1)S(1)} %fusion.2), channel_id=1, source_target_pairs={{0,24},{8,16},{16,8},{24,0},{32,40},{40,32},{48,56},{56,48},{1,25}... | collective-permute-start | bytes 884744 | tf_op jit(solution)/shard_map/ppermute | solution.py:43
  103.9 20.9 %collective-permute-start.13 = (bf16[4,96,384]{2,1,0:T(8,128)(2,1)S(1)}, bf16[4,96,384]{2,1,0:T(8,128)(2,1)S(1)}, u32[]{:S(2)}, u32[]{:S(2)}) collective-permute-start(bf16[4,96,384]{2,1,0:T(8,128)(2,1)S(1)} %fusion.1), channel_id=1, source_target_pairs={{0,192},{64,128},{128,64},{192,0},{32,96},{96,32},{160,224},{224,1... | collective-permute-start | bytes 884744 | tf_op jit(solution)/shard_map/ppermute | solution.py:43
  109.0 26.8 %collective-permute-start.23 = (bf16[2,96,384]{2,1,0:T(8,128)(2,1)S(1)}, bf16[2,96,384]{2,1,0:T(8,128)(2,1)S(1)}, u32[]{:S(2)}, u32[]{:S(2)}) collective-permute-start(bf16[2,96,384]{2,1,0:T(8,128)(2,1)S(1)} %fusion.4), channel_id=1, source_target_pairs={{0,256},{256,0},{512,768},{768,512},{32,800},{288,544},{544,288},{... | collective-permute-start | bytes 442376 | tf_op jit(solution)/shard_map/ppermute | solution.py:43
  124.9 45.5 %collective-permute-start.16 = (bf16[24,3072]{1,0:T(8,128)(2,1)S(1)}, bf16[24,3072]{1,0:T(8,128)(2,1)S(1)}, u32[]{:S(2)}, u32[]{:S(2)}) collective-permute-start(bf16[24,3072]{1,0:T(8,128)(2,1)S(1)} %slice.312), channel_id=1, source_target_pairs={{0,2},{1,3},{2,0},{3,1},{4,6},{5,7},{6,4},{7,5},{8,10},{9,11},{10,... | collective-permute-start | bytes 442376 | tf_op jit(solution)/shard_map/ppermute | solution.py:22
  128.4 42.0 %collective-permute-start.15 = (bf16[2,96,384]{2,1,0:T(8,128)(2,1)S(1)}, bf16[2,96,384]{2,1,0:T(8,128)(2,1)S(1)}, u32[]{:S(2)}, u32[]{:S(2)}) collective-permute-start(bf16[2,96,384]{2,1,0:T(8,128)(2,1)S(1)} %fusion.5), channel_id=1, source_target_pairs={{0,256},{256,0},{512,768},{768,512},{32,800},{288,544},{544,288},{... | collective-permute-start | bytes 442376 | tf_op jit(solution)/shard_map/ppermute | solution.py:43
  136.8 47.5 %collective-permute-start.24 = (bf16[96,384]{1,0:T(8,128)(2,1)S(1)}, bf16[96,384]{1,0:T(8,128)(2,1)S(1)}, u32[]{:S(2)}, u32[]{:S(2)}) collective-permute-start(bf16[96,384]{1,0:T(8,128)(2,1)S(1)} %fusion.6), channel_id=1, source_target_pairs={{0,768},{256,512},{512,256},{768,0},{32,288},{288,32},{544,800},{8... | collective-permute-start | bytes 221192 | tf_op jit(solution)/shard_map/ppermute | solution.py:43
  170.4 24.5 %copy-start.4 = (bf16[6,3072]{1,0:T(8,128)(2,1)S(1)}, bf16[6,3072]{1,0:T(8,128)(2,1)}, u32[]{:S(2)}) copy-start(bf16[6,3072]{1,0:T(8,128)(2,1)} %layer_input.1) | copy-start | bytes 110596
  170.4 24.5 %copy-start.8 = (f32[3072]{0:T(1024)S(1)}, f32[3072]{0:T(1024)}, u32[]{:S(2)}) copy-start(f32[3072]{0:T(1024)} %param.7) | copy-start | bytes 36868
  170.5 24.7 %copy-start.6 = (bf16[6,3072]{1,0:T(8,128)(2,1)S(1)}, bf16[6,3072]{1,0:T(8,128)(2,1)}, u32[]{:S(2)}) copy-start(bf16[6,3072]{1,0:T(8,128)(2,1)} %out_grad.1) | copy-start | bytes 110596
  170.5 8.2 %collective-permute-start.17 = (bf16[12,3072]{1,0:T(8,128)(2,1)S(1)}, bf16[12,3072]{1,0:T(8,128)(2,1)S(1)}, u32[]{:S(2)}, u32[]{:S(2)}) collective-permute-start(bf16[12,3072]{1,0:T(8,128)(2,1)S(1)} %slice.313), channel_id=1, source_target_pairs={{0,1},{1,0},{2,3},{3,2},{4,5},{5,4},{6,7},{7,6},{8,9},{9,8},{10,11... | collective-permute-start | bytes 221192 | tf_op jit(solution)/shard_map/ppermute | solution.py:22
  173.5 19.8 %collective-permute-start.19 = (bf16[96,384]{1,0:T(8,128)(2,1)S(1)}, bf16[96,384]{1,0:T(8,128)(2,1)S(1)}, u32[]{:S(2)}, u32[]{:S(2)}) collective-permute-start(bf16[96,384]{1,0:T(8,128)(2,1)S(1)} %fusion.9), channel_id=1, source_target_pairs={{0,768},{256,512},{512,256},{768,0},{32,288},{288,32},{544,800},{8... | collective-permute-start | bytes 221192 | tf_op jit(solution)/shard_map/ppermute | solution.py:43
  178.8 16.2 %collective-permute-start.18 = (bf16[6,3072]{1,0:T(8,128)(2,1)S(1)}, bf16[6,3072]{1,0:T(8,128)(2,1)S(1)}, u32[]{:S(2)}, u32[]{:S(2)}) collective-permute-start(bf16[6,3072]{1,0:T(8,128)(2,1)S(1)} %slice.314), channel_id=1, source_target_pairs={{0,4},{1,5},{2,6},{3,7},{4,0},{5,1},{6,2},{7,3},{8,12},{9,13},{10,... | collective-permute-start | bytes 110600 | tf_op jit(solution)/shard_map/ppermute | solution.py:22
  (2 other events, 1.5 us)

commit v8 on v7

--- a/solution.py
+++ b/solution.py
@@ -204,7 +204,7 @@
     (block,) = in_vmem(unpack_kernel, [((4 * rows, width), BF16)], packed, swap(packed, 4))
     middle = nzl * rows
     normed, grad = in_vmem(
-        join_kernel, [((middle, width), BF16)] * 2, block, *[swap(block, k) for k in (1, 2, 3)]
+        join_kernel, [((middle, width), BF16)] * 2, block, *[swap(block, k) for k in (2, 1, 3)]
     )
     ahead, back = x_moves(1), x_moves(-1)
     normed_ahead, grad_ahead = ahead(normed), ahead(grad)
@@ -253,26 +253,34 @@
     def to_second_z(term, got):
         return paired(added(summed(term, 1), got[1]).astype(BF16), "zh", 1)
 
-    up_core, down_core = to_core(up), to_core(down)
+    down_core, up_core = to_core(down), to_core(up)
+    down_y, up_y = to_y(down, down_core), to_y(up, up_core)
     up_core, blocks = fence((up_core, blocks))
     full_term = jnp.einsum("xtf,df->xtd", blocks, up_weight, preferred_element_type=F32)
     full_term = full_term.astype(BF16)
     x_first = paired(full_term[2:], "x", 0)
-    up_y, down_y = to_y(up, up_core), to_y(down, down_core)
-    up_y, x_first = fence((up_y, x_first))
+
+    down_y2 = to_second_y(down, down_core, down_y)
+    down_z = to_z(down[0], down_core, down_y, down_y2)
+    down_y2, x_first = fence((down_y2, x_first))
     x_second = paired(added(full_term[1], x_first[1]).astype(BF16), "x", 1)
+    up_y, x_second = fence((up_y, x_second))
+    up_y2 = to_second_y(up, up_core, up_y)
+    up_z = to_z(up[0], up_core, up_y, up_y2)
     own = added(full_term[0], x_first[0], x_second)
-    up_y2, down_y2 = to_second_y(up, up_core, up_y), to_second_y(down, down_core, down_y)
+
+    def halved(own, distance):
+        half = own.shape[0] // 2
+        return added(own[:half], swap(own[half:].astype(BF16), distance))
+
     up_y2, own = fence((up_y2, own))
-    half = own.shape[0] // 2
-    own = added(own[:half], swap(own[half:].astype(BF16), 2))
-    up, down = (up[0], up_core, up_y, up_y2), (down[0], down_core, down_y, down_y2)
-    up_z, down_z = to_z(*up), to_z(*down)
+    own = halved(own, 1)
+    down, up = (down[0], down_core, down_y, down_y2), (up[0], up_core, up_y, up_y2)
+    down_z, own = fence((down_z, own))
+    down_z2, up_z2 = to_second_z(down, down_z), to_second_z(up, up_z)
+    own = halved(own, 2)
     up_z, own = fence((up_z, own))
-    half = own.shape[0] // 2
-    own = added(own[:half], swap(own[half:].astype(BF16), 1))
-    up_z2, down_z2 = to_second_z(up, up_z), to_second_z(down, down_z)
-    normed_grad = added(own[:rows], swap(own[rows:].astype(BF16), 4))
+    normed_grad = halved(own, 4)
     down_grad = added(summed(down, 0), down_z[0], down_z2).T
     up_grad = added(summed(up, 0), up_z[0], up_z2)
 

time: 197 us -> 196 us (level)
  the two profiles are of different devices: /device:TPU:34 before, /device:TPU:56 now
where the time goes in v8:
time: 196 us; the launch traced here: 195 us
  starting transfers between devices  130 us (66%)
  waiting for transfers between devices  37.3 us (19%)
  other arithmetic  13 us (7%)
  Pallas kernels  7.67 us (4%)
  local copies, waits for them, and re-layouts  4.38 us (2%)
    ppermute x10, starting transfers between devices, paired(): return lax.ppermute(block, names, moves)  66.5 us
    ppermute x7, starting transfers between devices, swap(): return lax.ppermute(block, 'zl', [(i, i ^ distance) for i in range(8)])  40 us
    ppermute x6, starting transfers between devices, x_moves(): return lambda block: lax.ppermute(block, ('c', 'x'), moves)  19.4 us
    ppermute x10, waiting for transfers between devices, paired(): return lax.ppermute(block, names, moves)  18.9 us
    ppermute x7, waiting for transfers between devices, swap(): return lax.ppermute(block, 'zl', [(i, i ^ distance) for i in range(8)])  13.2 us
    pallas_call x3, Pallas kernels, computed(): pl.pallas_call(kernel, out_shape=[jax.ShapeDtypeStruct(*out) for out in o...  7.19 us
    ppermute x6, waiting for transfers between devices, x_moves(): return lambda block: lax.ppermute(block, ('c', 'x'), moves)  5.24 us
    ppermute x2, starting transfers between devices, to_core(): return lax.ppermute(term[1], 'c', [(0, 1), (1, 0)])  4.3 us
  transfers between devices with their start and end apart: 25, of which 10 were waited for; matrix products, arithmetic and copies ran while one was open for 7% of the time, Pallas kernels for 2%

profile of v8, /device:TPU:56, one launch (start us, length us, event | category | flops | bytes accessed | tf_op | source)
XLA Modules:
  0.0 194.8 jit_solution(14628049266889134210)
XLA Ops:
  3.3 9.1 %collective-permute-start = (bf16[24,1536]{1,0:T(8,128)(2,1)S(1)}, bf16[24,1536]{1,0:T(8,128)(2,1)S(1)}, u32[]{:S(2)}, u32[]{:S(2)}) collective-permute-start(bf16[24,1536]{1,0:T(8,128)(2,1)S(1)} %get-tuple-element.29.own), channel_id=1, source_target_pairs={{0,4},{1,5},{2,6},{3,7},{4,0},{5,1},{6,2},{7,3},{8,12},{9,13},{10,... | collective-permute-start | bytes 221192 | tf_op jit(solution)/shard_map/ppermute | solution.py:22
  12.4 5.5 %collective-permute-done.far = bf16[24,1536]{1,0:T(8,128)(2,1)S(1)} collective-permute-done((bf16[24,1536]{1,0:T(8,128)(2,1)S(1)}, bf16[24,1536]{1,0:T(8,128)(2,1)S(1)}, u32[]{:S(2)}, u32[]{:S(2)}) %collective-permute-start) | collective-permute-done | bytes 73760 | tf_op jit(solution)/shard_map/ppermute | solution.py:22
  18.0 4.5 %collective-permute-start.1 = (bf16[24,3072]{1,0:T(8,128)(2,1)S(1)}, bf16[24,3072]{1,0:T(8,128)(2,1)S(1)}, u32[]{:S(2)}, u32[]{:S(2)}) collective-permute-start(bf16[24,3072]{1,0:T(8,128)(2,1)S(1)} %shard_map.77.refs_0_), channel_id=1, source_target_pairs={{0,2},{1,3},{2,0},{3,1},{4,6},{5,7},{6,4},{7,5},{8,10},{9,11},{10,... | collective-permute-start | bytes 442376 | tf_op jit(solution)/shard_map/ppermute | solution.py:22
  22.5 1.9 collective-permute-start.2
  24.5 2.7 %collective-permute-start.3 = (bf16[24,3072]{1,0:T(8,128)(2,1)S(1)}, bf16[24,3072]{1,0:T(8,128)(2,1)S(1)}, u32[]{:S(2)}, u32[]{:S(2)}) collective-permute-start(bf16[24,3072]{1,0:T(8,128)(2,1)S(1)} %shard_map.77.refs_0_), channel_id=1, source_target_pairs={{0,3},{1,2},{2,1},{3,0},{4,7},{5,6},{6,5},{7,4},{8,11},{9,10},{10,... | collective-permute-start | bytes 442376 | tf_op jit(solution)/shard_map/ppermute | solution.py:22
  27.6 3.5 %collective-permute-done.2.refs_2_ = bf16[24,3072]{1,0:T(8,128)(2,1)S(1)} collective-permute-done((bf16[24,3072]{1,0:T(8,128)(2,1)S(1)}, bf16[24,3072]{1,0:T(8,128)(2,1)S(1)}, u32[]{:S(2)}, u32[]{:S(2)}) %collective-permute-start.2) | collective-permute-done | bytes 147488 | tf_op jit(solution)/shard_map/ppermute | solution.py:22
  31.1 3.8 %collective-permute-done.3.refs_3_ = bf16[24,3072]{1,0:T(8,128)(2,1)S(1)} collective-permute-done((bf16[24,3072]{1,0:T(8,128)(2,1)S(1)}, bf16[24,3072]{1,0:T(8,128)(2,1)S(1)}, u32[]{:S(2)}, u32[]{:S(2)}) %collective-permute-start.3) | collective-permute-done | bytes 147488 | tf_op jit(solution)/shard_map/ppermute | solution.py:22
  34.9 3.4 %collective-permute-start.7 = (bf16[48,3072]{1,0:T(8,128)(2,1)S(1)}, bf16[48,3072]{1,0:T(8,128)(2,1)S(1)}, u32[]{:S(2)}, u32[]{:S(2)}) collective-permute-start(bf16[48,3072]{1,0:T(8,128)(2,1)S(1)} %get-tuple-element.31.refs_0_), channel_id=1, source_target_pairs={{0,8},{8,16},{16,24},{24,0},{32,56},{40,32},{48,40},{56,48},{1,9},... | collective-permute-start | bytes 884744 | tf_op jit(solution)/shard_map/ppermute | solution.py:27
  38.3 3.4 %collective-permute-start.4 = (bf16[48,3072]{1,0:T(8,128)(2,1)S(1)}, bf16[48,3072]{1,0:T(8,128)(2,1)S(1)}, u32[]{:S(2)}, u32[]{:S(2)}) collective-permute-start(bf16[48,3072]{1,0:T(8,128)(2,1)S(1)} %get-tuple-element.30.refs_0_), channel_id=1, source_target_pairs={{0,8},{8,16},{16,24},{24,0},{32,56},{40,32},{48,40},{56,48},{1,9},... | collective-permute-start | bytes 884744 | tf_op jit(solution)/shard_map/ppermute | solution.py:27
  41.8 3.7 %collective-permute-start.8 = (bf16[48,3072]{1,0:T(8,128)(2,1)S(1)}, bf16[48,3072]{1,0:T(8,128)(2,1)S(1)}, u32[]{:S(2)}, u32[]{:S(2)}) collective-permute-start(bf16[48,3072]{1,0:T(8,128)(2,1)S(1)} %get-tuple-element.31.refs_0_), channel_id=1, source_target_pairs={{0,24},{8,0},{16,8},{24,16},{32,40},{40,48},{48,56},{56,32},{1,25}... | collective-permute-start | bytes 884744 | tf_op jit(solution)/shard_map/ppermute | solution.py:27
  45.4 2.2 %collective-permute-start.9 = (bf16[48,3072]{1,0:T(8,128)(2,1)S(1)}, bf16[48,3072]{1,0:T(8,128)(2,1)S(1)}, u32[]{:S(2)}, u32[]{:S(2)}) collective-permute-start(bf16[48,3072]{1,0:T(8,128)(2,1)S(1)} %collective-permute-done.7.refs_1_), channel_id=1, source_target_pairs={{0,8},{8,16},{16,24},{24,0},{32,56},{40,32},{48,40},{56,48},{1,9},... | collective-permute-start | bytes 884744 | tf_op jit(solution)/shard_map/ppermute | solution.py:27
  47.6 4.9 %collective-permute-start.5 = (bf16[48,3072]{1,0:T(8,128)(2,1)S(1)}, bf16[48,3072]{1,0:T(8,128)(2,1)S(1)}, u32[]{:S(2)}, u32[]{:S(2)}) collective-permute-start(bf16[48,3072]{1,0:T(8,128)(2,1)S(1)} %get-tuple-element.30.refs_0_), channel_id=1, source_target_pairs={{0,24},{8,0},{16,8},{24,16},{32,40},{40,48},{48,56},{56,32},{1,25}... | collective-permute-start | bytes 884744 | tf_op jit(solution)/shard_map/ppermute | solution.py:27
  52.5 1.9 collective-permute-start.6
  54.6 3.4 %collective-permute-done.9.refs_3_ = bf16[48,3072]{1,0:T(8,128)(2,1)S(1)} collective-permute-done((bf16[48,3072]{1,0:T(8,128)(2,1)S(1)}, bf16[48,3072]{1,0:T(8,128)(2,1)S(1)}, u32[]{:S(2)}, u32[]{:S(2)}) %collective-permute-start.9) | collective-permute-done | bytes 294944 | tf_op jit(solution)/shard_map/ppermute | solution.py:27
  62.3 2.7 %shard_map.80 = (bf16[192,3072]{1,0:T(8,128)(2,1)S(1)}, bf16[4,4,96,384]{3,2,1,0:T(8,128)(2,1)S(1)}, bf16[4,4,96,384]{3,2,1,0:T(8,128)(2,1)}) custom-call(s32[17]{0:T(128)S(1)} %concatenate.3.where, bf16[48,3072]{1,0:T(8,128)(2,1)S(1)} %get-tuple-element.30.refs_0_, bf16[48,3072]{1,0:T(8,128)(2,1)S(1)} %collective-permute-done.4.refs_1_, ...), custom_call_target="tpu_custom_call" | custom-call | flops 452984832 | bytes 8388608 | tf_op jit(solution)/shard_map/pallas_call | solution.py:184
  66.9 3.7 %shard_map.81 = (bf16[192,384]{1,0:T(8,128)(2,1)S(1)}, bf16[4,4,96,384]{3,2,1,0:T(8,128)(2,1)S(1)}, bf16[4,4,96,384]{3,2,1,0:T(8,128)(2,1)}) custom-call(s32[17]{0:T(128)S(1)} %concatenate.3.where, bf16[192,3072]{1,0:T(8,128)(2,1)S(1)} %get-tuple-element.33.grad, bf16[192,3072]{1,0:T(8,128)(2,1)S(1)} %get-tuple-element.34.normed, ...), custom_call_target="tpu_custom_call" | custom-call | flops 905969664 | bytes 8388608 | tf_op jit(solution)/shard_map/pallas_call | solution.py:184
  70.6 2.4 %collective-permute-start.10 = (bf16[4,4,96,384]{3,2,1,0:T(8,128)(2,1)}, bf16[4,4,96,384]{3,2,1,0:T(8,128)(2,1)}, u32[]{:S(2)}, u32[]{:S(2)}) collective-permute-start(bf16[4,4,96,384]{3,2,1,0:T(8,128)(2,1)} %get-tuple-element.37), channel_id=1, source_target_pairs={{0,32},{32,0},{1,33},{33,1},{2,34},{34,2},{3,35},{35,3},{4,36},{36... | collective-permute-start | bytes 3538952 | tf_op jit(solution)/shard_map/ppermute | solution.py:238
  74.4 2.7 %collective-permute-start.13 = (bf16[2,4,96,384]{3,2,1,0:T(8,128)(2,1)S(1)}, bf16[2,4,96,384]{3,2,1,0:T(8,128)(2,1)S(1)}, u32[]{:S(2)}, u32[]{:S(2)}) collective-permute-start(bf16[2,4,96,384]{3,2,1,0:T(8,128)(2,1)S(1)} %add_convert_fusion), channel_id=1, source_target_pairs={{0,64},{64,0},{128,192},{192,128},{32,224},{96,160},{160,96},{224,... | collective-permute-start | bytes 1769480 | tf_op jit(solution)/shard_map/ppermute | solution.py:43
  78.2 1.9 collective-permute-start.15
  80.1 6.0 %collective-permute-done.13 = bf16[2,4,96,384]{3,2,1,0:T(8,128)(2,1)S(1)} collective-permute-done((bf16[2,4,96,384]{3,2,1,0:T(8,128)(2,1)S(1)}, bf16[2,4,96,384]{3,2,1,0:T(8,128)(2,1)S(1)}, u32[]{:S(2)}, u32[]{:S(2)}) %collective-permute-start.13) | collective-permute-done | bytes 589856 | tf_op jit(solution)/shard_map/ppermute | solution.py:43
  87.3 8.2 %collective-permute-start.14 = (bf16[4,96,384]{2,1,0:T(8,128)(2,1)S(1)}, bf16[4,96,384]{2,1,0:T(8,128)(2,1)S(1)}, u32[]{:S(2)}, u32[]{:S(2)}) collective-permute-start(bf16[4,96,384]{2,1,0:T(8,128)(2,1)S(1)} %fusion.1), channel_id=1, source_target_pairs={{0,192},{64,128},{128,64},{192,0},{32,96},{96,32},{160,224},{224,1... | collective-permute-start | bytes 884744 | tf_op jit(solution)/shard_map/ppermute | solution.py:43
  98.6 2.1 %collective-permute-done.14 = bf16[4,96,384]{2,1,0:T(8,128)(2,1)S(1)} collective-permute-done((bf16[4,96,384]{2,1,0:T(8,128)(2,1)S(1)}, bf16[4,96,384]{2,1,0:T(8,128)(2,1)S(1)}, u32[]{:S(2)}, u32[]{:S(2)}) %collective-permute-start.14) | collective-permute-done | bytes 294944 | tf_op jit(solution)/shard_map/ppermute | solution.py:43
  103.9 13.9 %collective-permute-start.19 = (bf16[2,96,384]{2,1,0:T(8,128)(2,1)S(1)}, bf16[2,96,384]{2,1,0:T(8,128)(2,1)S(1)}, u32[]{:S(2)}, u32[]{:S(2)}) collective-permute-start(bf16[2,96,384]{2,1,0:T(8,128)(2,1)S(1)} %fusion.4), channel_id=1, source_target_pairs={{0,256},{256,0},{512,768},{768,512},{32,800},{288,544},{544,288},{... | collective-permute-start | bytes 442376 | tf_op jit(solution)/shard_map/ppermute | solution.py:43
  118.8 1.9 collective-permute-start.17
  120.9 7.8 %collective-permute-done.17 = bf16[4,96,384]{2,1,0:T(8,128)(2,1)S(1)} collective-permute-done((bf16[4,96,384]{2,1,0:T(8,128)(2,1)S(1)}, bf16[4,96,384]{2,1,0:T(8,128)(2,1)S(1)}, u32[]{:S(2)}, u32[]{:S(2)}) %collective-permute-start.17) | collective-permute-done | bytes 294944 | tf_op jit(solution)/shard_map/ppermute | solution.py:43
  128.7 2.6 %collective-permute-start.20 = (bf16[24,3072]{1,0:T(8,128)(2,1)S(1)}, bf16[24,3072]{1,0:T(8,128)(2,1)S(1)}, u32[]{:S(2)}, u32[]{:S(2)}) collective-permute-start(bf16[24,3072]{1,0:T(8,128)(2,1)S(1)} %slice.302), channel_id=1, source_target_pairs={{0,1},{1,0},{2,3},{3,2},{4,5},{5,4},{6,7},{7,6},{8,9},{9,8},{10,11... | collective-permute-start | bytes 442376 | tf_op jit(solution)/shard_map/ppermute | solution.py:22
  132.3 5.6 %collective-permute-start.18 = (bf16[2,96,384]{2,1,0:T(8,128)(2,1)S(1)}, bf16[2,96,384]{2,1,0:T(8,128)(2,1)S(1)}, u32[]{:S(2)}, u32[]{:S(2)}) collective-permute-start(bf16[2,96,384]{2,1,0:T(8,128)(2,1)S(1)} %fusion.5), channel_id=1, source_target_pairs={{0,256},{256,0},{512,768},{768,512},{32,800},{288,544},{544,288},{... | collective-permute-start | bytes 442376 | tf_op jit(solution)/shard_map/ppermute | solution.py:43
  138.9 14.0 %collective-permute-start.24 = (bf16[96,384]{1,0:T(8,128)(2,1)S(1)}, bf16[96,384]{1,0:T(8,128)(2,1)S(1)}, u32[]{:S(2)}, u32[]{:S(2)}) collective-permute-start(bf16[96,384]{1,0:T(8,128)(2,1)S(1)} %fusion.6), channel_id=1, source_target_pairs={{0,768},{256,512},{512,256},{768,0},{32,288},{288,32},{544,800},{8... | collective-permute-start | bytes 221192 | tf_op jit(solution)/shard_map/ppermute | solution.py:43
  153.0 5.3 %collective-permute-start.21 = (bf16[12,3072]{1,0:T(8,128)(2,1)S(1)}, bf16[12,3072]{1,0:T(8,128)(2,1)S(1)}, u32[]{:S(2)}, u32[]{:S(2)}) collective-permute-start(bf16[12,3072]{1,0:T(8,128)(2,1)S(1)} %slice.303), channel_id=1, source_target_pairs={{0,2},{1,3},{2,0},{3,1},{4,6},{5,7},{6,4},{7,5},{8,10},{9,11},{10,... | collective-permute-start | bytes 221192 | tf_op jit(solution)/shard_map/ppermute | solution.py:22
  158.3 2.9 %collective-permute-done.18 = bf16[2,96,384]{2,1,0:T(8,128)(2,1)S(1)} collective-permute-done((bf16[2,96,384]{2,1,0:T(8,128)(2,1)S(1)}, bf16[2,96,384]{2,1,0:T(8,128)(2,1)S(1)}, u32[]{:S(2)}, u32[]{:S(2)}) %collective-permute-start.18) | collective-permute-done | bytes 147488 | tf_op jit(solution)/shard_map/ppermute | solution.py:43
  162.2 14.5 %collective-permute-start.23 = (bf16[96,384]{1,0:T(8,128)(2,1)S(1)}, bf16[96,384]{1,0:T(8,128)(2,1)S(1)}, u32[]{:S(2)}, u32[]{:S(2)}) collective-permute-start(bf16[96,384]{1,0:T(8,128)(2,1)S(1)} %fusion.9), channel_id=1, source_target_pairs={{0,768},{256,512},{512,256},{768,0},{32,288},{288,32},{544,800},{8... | collective-permute-start | bytes 221192 | tf_op jit(solution)/shard_map/ppermute | solution.py:43
  176.7 13.8 %collective-permute-start.22 = (bf16[6,3072]{1,0:T(8,128)(2,1)S(1)}, bf16[6,3072]{1,0:T(8,128)(2,1)S(1)}, u32[]{:S(2)}, u32[]{:S(2)}) collective-permute-start(bf16[6,3072]{1,0:T(8,128)(2,1)S(1)} %slice.304), channel_id=1, source_target_pairs={{0,4},{1,5},{2,6},{3,7},{4,0},{5,1},{6,2},{7,3},{8,12},{9,13},{10,... | collective-permute-start | bytes 110600 | tf_op jit(solution)/shard_map/ppermute | solution.py:22
  (72 shorter events, 27.7 us)
Async XLA Ops:
  0.6 0.8 copy-start.3
  3.3 14.6 %collective-permute-start = (bf16[24,1536]{1,0:T(8,128)(2,1)S(1)}, bf16[24,1536]{1,0:T(8,128)(2,1)S(1)}, u32[]{:S(2)}, u32[]{:S(2)}) collective-permute-start(bf16[24,1536]{1,0:T(8,128)(2,1)S(1)} %get-tuple-element.29.own), channel_id=1, source_target_pairs={{0,4},{1,5},{2,6},{3,7},{4,0},{5,1},{6,2},{7,3},{8,12},{9,13},{10,... | collective-permute-start | bytes 221192 | tf_op jit(solution)/shard_map/ppermute | solution.py:22
  18.0 9.6 %collective-permute-start.1 = (bf16[24,3072]{1,0:T(8,128)(2,1)S(1)}, bf16[24,3072]{1,0:T(8,128)(2,1)S(1)}, u32[]{:S(2)}, u32[]{:S(2)}) collective-permute-start(bf16[24,3072]{1,0:T(8,128)(2,1)S(1)} %shard_map.77.refs_0_), channel_id=1, source_target_pairs={{0,2},{1,3},{2,0},{3,1},{4,6},{5,7},{6,4},{7,5},{8,10},{9,11},{10,... | collective-permute-start | bytes 442376 | tf_op jit(solution)/shard_map/ppermute | solution.py:22
  22.5 8.5 %collective-permute-start.2 = (bf16[24,3072]{1,0:T(8,128)(2,1)S(1)}, bf16[24,3072]{1,0:T(8,128)(2,1)S(1)}, u32[]{:S(2)}, u32[]{:S(2)}) collective-permute-start(bf16[24,3072]{1,0:T(8,128)(2,1)S(1)} %shard_map.77.refs_0_), channel_id=1, source_target_pairs={{0,1},{1,0},{2,3},{3,2},{4,5},{5,4},{6,7},{7,6},{8,9},{9,8},{10,11... | collective-permute-start | bytes 442376 | tf_op jit(solution)/shard_map/ppermute | solution.py:22
  24.5 10.4 %collective-permute-start.3 = (bf16[24,3072]{1,0:T(8,128)(2,1)S(1)}, bf16[24,3072]{1,0:T(8,128)(2,1)S(1)}, u32[]{:S(2)}, u32[]{:S(2)}) collective-permute-start(bf16[24,3072]{1,0:T(8,128)(2,1)S(1)} %shard_map.77.refs_0_), channel_id=1, source_target_pairs={{0,3},{1,2},{2,1},{3,0},{4,7},{5,6},{6,5},{7,4},{8,11},{9,10},{10,... | collective-permute-start | bytes 442376 | tf_op jit(solution)/shard_map/ppermute | solution.py:22
  34.9 10.5 %collective-permute-start.7 = (bf16[48,3072]{1,0:T(8,128)(2,1)S(1)}, bf16[48,3072]{1,0:T(8,128)(2,1)S(1)}, u32[]{:S(2)}, u32[]{:S(2)}) collective-permute-start(bf16[48,3072]{1,0:T(8,128)(2,1)S(1)} %get-tuple-element.31.refs_0_), channel_id=1, source_target_pairs={{0,8},{8,16},{16,24},{24,0},{32,56},{40,32},{48,40},{56,48},{1,9},... | collective-permute-start | bytes 884744 | tf_op jit(solution)/shard_map/ppermute | solution.py:27
  38.3 14.2 %collective-permute-start.4 = (bf16[48,3072]{1,0:T(8,128)(2,1)S(1)}, bf16[48,3072]{1,0:T(8,128)(2,1)S(1)}, u32[]{:S(2)}, u32[]{:S(2)}) collective-permute-start(bf16[48,3072]{1,0:T(8,128)(2,1)S(1)} %get-tuple-element.30.refs_0_), channel_id=1, source_target_pairs={{0,8},{8,16},{16,24},{24,0},{32,56},{40,32},{48,40},{56,48},{1,9},... | collective-permute-start | bytes 884744 | tf_op jit(solution)/shard_map/ppermute | solution.py:27
  41.8 12.8 %collective-permute-start.8 = (bf16[48,3072]{1,0:T(8,128)(2,1)S(1)}, bf16[48,3072]{1,0:T(8,128)(2,1)S(1)}, u32[]{:S(2)}, u32[]{:S(2)}) collective-permute-start(bf16[48,3072]{1,0:T(8,128)(2,1)S(1)} %get-tuple-element.31.refs_0_), channel_id=1, source_target_pairs={{0,24},{8,0},{16,8},{24,16},{32,40},{40,48},{48,56},{56,32},{1,25}... | collective-permute-start | bytes 884744 | tf_op jit(solution)/shard_map/ppermute | solution.py:27
  45.4 12.6 %collective-permute-start.9 = (bf16[48,3072]{1,0:T(8,128)(2,1)S(1)}, bf16[48,3072]{1,0:T(8,128)(2,1)S(1)}, u32[]{:S(2)}, u32[]{:S(2)}) collective-permute-start(bf16[48,3072]{1,0:T(8,128)(2,1)S(1)} %collective-permute-done.7.refs_1_), channel_id=1, source_target_pairs={{0,8},{8,16},{16,24},{24,0},{32,56},{40,32},{48,40},{56,48},{1,9},... | collective-permute-start | bytes 884744 | tf_op jit(solution)/shard_map/ppermute | solution.py:27
  47.6 12.9 %collective-permute-start.5 = (bf16[48,3072]{1,0:T(8,128)(2,1)S(1)}, bf16[48,3072]{1,0:T(8,128)(2,1)S(1)}, u32[]{:S(2)}, u32[]{:S(2)}) collective-permute-start(bf16[48,3072]{1,0:T(8,128)(2,1)S(1)} %get-tuple-element.30.refs_0_), channel_id=1, source_target_pairs={{0,24},{8,0},{16,8},{24,16},{32,40},{40,48},{48,56},{56,32},{1,25}... | collective-permute-start | bytes 884744 | tf_op jit(solution)/shard_map/ppermute | solution.py:27
  52.5 9.8 %collective-permute-start.6 = (bf16[48,3072]{1,0:T(8,128)(2,1)S(1)}, bf16[48,3072]{1,0:T(8,128)(2,1)S(1)}, u32[]{:S(2)}, u32[]{:S(2)}) collective-permute-start(bf16[48,3072]{1,0:T(8,128)(2,1)S(1)} %collective-permute-done.4.refs_1_), channel_id=1, source_target_pairs={{0,8},{8,16},{16,24},{24,0},{32,56},{40,32},{48,40},{56,48},{1,9},... | collective-permute-start | bytes 884744 | tf_op jit(solution)/shard_map/ppermute | solution.py:27
  58.0 1.7 copy-start
  59.6 7.3 %copy-start.2 = (bf16[384,3072]{1,0:T(8,128)(2,1)S(1)}, bf16[384,3072]{1,0:T(8,128)(2,1)}, u32[]{:S(2)}) copy-start(bf16[384,3072]{1,0:T(8,128)(2,1)} %weight.1) | copy-start | bytes 7077892
  65.0 8.0 %collective-permute-start.12 = (bf16[4,4,96,384]{3,2,1,0:T(8,128)(2,1)}, bf16[4,4,96,384]{3,2,1,0:T(8,128)(2,1)}, u32[]{:S(2)}, u32[]{:S(2)}) collective-permute-start(bf16[4,4,96,384]{3,2,1,0:T(8,128)(2,1)} %get-tuple-element.42), channel_id=1, source_target_pairs={{0,32},{32,0},{1,33},{33,1},{2,34},{34,2},{3,35},{35,3},{4,36},{36... | collective-permute-start | bytes 3538952 | tf_op jit(solution)/shard_map/ppermute | solution.py:238
  70.6 6.5 %collective-permute-start.10 = (bf16[4,4,96,384]{3,2,1,0:T(8,128)(2,1)}, bf16[4,4,96,384]{3,2,1,0:T(8,128)(2,1)}, u32[]{:S(2)}, u32[]{:S(2)}) collective-permute-start(bf16[4,4,96,384]{3,2,1,0:T(8,128)(2,1)} %get-tuple-element.37), channel_id=1, source_target_pairs={{0,32},{32,0},{1,33},{33,1},{2,34},{34,2},{3,35},{35,3},{4,36},{36... | collective-permute-start | bytes 3538952 | tf_op jit(solution)/shard_map/ppermute | solution.py:238
  73.0 4.1 %copy-start.1 = (bf16[3072,384]{1,0:T(8,128)(2,1)S(1)}, bf16[3072,384]{1,0:T(8,128)(2,1)}, u32[]{:S(2)}) copy-start(bf16[3072,384]{1,0:T(8,128)(2,1)} %refs_4_.1) | copy-start | bytes 7077892
  74.4 11.8 %collective-permute-start.13 = (bf16[2,4,96,384]{3,2,1,0:T(8,128)(2,1)S(1)}, bf16[2,4,96,384]{3,2,1,0:T(8,128)(2,1)S(1)}, u32[]{:S(2)}, u32[]{:S(2)}) collective-permute-start(bf16[2,4,96,384]{3,2,1,0:T(8,128)(2,1)S(1)} %add_convert_fusion), channel_id=1, source_target_pairs={{0,64},{64,0},{128,192},{192,128},{32,224},{96,160},{160,96},{224,... | collective-permute-start | bytes 1769480 | tf_op jit(solution)/shard_map/ppermute | solution.py:43
  78.2 20.4 %collective-permute-start.15 = (bf16[2,48,3072]{2,1,0:T(8,128)(2,1)S(1)}, bf16[2,48,3072]{2,1,0:T(8,128)(2,1)S(1)}, u32[]{:S(2)}, u32[]{:S(2)}) collective-permute-start(bf16[2,48,3072]{2,1,0:T(8,128)(2,1)S(1)} %slice.228), channel_id=1, source_target_pairs={{0,8},{8,0},{16,24},{24,16},{32,56},{40,48},{48,40},{56,32},{1,9},... | collective-permute-start | bytes 1769480 | tf_op jit(solution)/shard_map/ppermute | solution.py:43
  87.3 13.4 %collective-permute-start.14 = (bf16[4,96,384]{2,1,0:T(8,128)(2,1)S(1)}, bf16[4,96,384]{2,1,0:T(8,128)(2,1)S(1)}, u32[]{:S(2)}, u32[]{:S(2)}) collective-permute-start(bf16[4,96,384]{2,1,0:T(8,128)(2,1)S(1)} %fusion.1), channel_id=1, source_target_pairs={{0,192},{64,128},{128,64},{192,0},{32,96},{96,32},{160,224},{224,1... | collective-permute-start | bytes 884744 | tf_op jit(solution)/shard_map/ppermute | solution.py:43
  96.6 21.1 %collective-permute-start.11 = (bf16[2,4,96,384]{3,2,1,0:T(8,128)(2,1)S(1)}, bf16[2,4,96,384]{3,2,1,0:T(8,128)(2,1)S(1)}, u32[]{:S(2)}, u32[]{:S(2)}) collective-permute-start(bf16[2,4,96,384]{3,2,1,0:T(8,128)(2,1)S(1)} %add_convert_fusion.1), channel_id=1, source_target_pairs={{0,64},{64,0},{128,192},{192,128},{32,224},{96,160},{160,96},{224,... | collective-permute-start | bytes 1769480 | tf_op jit(solution)/shard_map/ppermute | solution.py:43
  100.8 17.0 %collective-permute-start.16 = (bf16[48,3072]{1,0:T(8,128)(2,1)S(1)}, bf16[48,3072]{1,0:T(8,128)(2,1)S(1)}, u32[]{:S(2)}, u32[]{:S(2)}) collective-permute-start(bf16[48,3072]{1,0:T(8,128)(2,1)S(1)} %fusion.2), channel_id=1, source_target_pairs={{0,24},{8,16},{16,8},{24,0},{32,40},{40,32},{48,56},{56,48},{1,25}... | collective-permute-start | bytes 884744 | tf_op jit(solution)/shard_map/ppermute | solution.py:43
  103.9 34.1 %collective-permute-start.19 = (bf16[2,96,384]{2,1,0:T(8,128)(2,1)S(1)}, bf16[2,96,384]{2,1,0:T(8,128)(2,1)S(1)}, u32[]{:S(2)}, u32[]{:S(2)}) collective-permute-start(bf16[2,96,384]{2,1,0:T(8,128)(2,1)S(1)} %fusion.4), channel_id=1, source_target_pairs={{0,256},{256,0},{512,768},{768,512},{32,800},{288,544},{544,288},{... | collective-permute-start | bytes 442376 | tf_op jit(solution)/shard_map/ppermute | solution.py:43
  118.8 9.8 %collective-permute-start.17 = (bf16[4,96,384]{2,1,0:T(8,128)(2,1)S(1)}, bf16[4,96,384]{2,1,0:T(8,128)(2,1)S(1)}, u32[]{:S(2)}, u32[]{:S(2)}) collective-permute-start(bf16[4,96,384]{2,1,0:T(8,128)(2,1)S(1)} %fusion.3), channel_id=1, source_target_pairs={{0,192},{64,128},{128,64},{192,0},{32,96},{96,32},{160,224},{224,1... | collective-permute-start | bytes 884744 | tf_op jit(solution)/shard_map/ppermute | solution.py:43
  128.7 9.2 %collective-permute-start.20 = (bf16[24,3072]{1,0:T(8,128)(2,1)S(1)}, bf16[24,3072]{1,0:T(8,128)(2,1)S(1)}, u32[]{:S(2)}, u32[]{:S(2)}) collective-permute-start(bf16[24,3072]{1,0:T(8,128)(2,1)S(1)} %slice.302), channel_id=1, source_target_pairs={{0,1},{1,0},{2,3},{3,2},{4,5},{5,4},{6,7},{7,6},{8,9},{9,8},{10,11... | collective-permute-start | bytes 442376 | tf_op jit(solution)/shard_map/ppermute | solution.py:22
  132.3 28.9 %collective-permute-start.18 = (bf16[2,96,384]{2,1,0:T(8,128)(2,1)S(1)}, bf16[2,96,384]{2,1,0:T(8,128)(2,1)S(1)}, u32[]{:S(2)}, u32[]{:S(2)}) collective-permute-start(bf16[2,96,384]{2,1,0:T(8,128)(2,1)S(1)} %fusion.5), channel_id=1, source_target_pairs={{0,256},{256,0},{512,768},{768,512},{32,800},{288,544},{544,288},{... | collective-permute-start | bytes 442376 | tf_op jit(solution)/shard_map/ppermute | solution.py:43
  138.9 54.9 %copy-start.4 = (bf16[6,3072]{1,0:T(8,128)(2,1)S(1)}, bf16[6,3072]{1,0:T(8,128)(2,1)}, u32[]{:S(2)}) copy-start(bf16[6,3072]{1,0:T(8,128)(2,1)} %layer_input.1) | copy-start | bytes 110596
  138.9 54.9 %copy-start.8 = (f32[3072]{0:T(1024)S(1)}, f32[3072]{0:T(1024)}, u32[]{:S(2)}) copy-start(f32[3072]{0:T(1024)} %param.7) | copy-start | bytes 36868
  138.9 51.7 %collective-permute-start.24 = (bf16[96,384]{1,0:T(8,128)(2,1)S(1)}, bf16[96,384]{1,0:T(8,128)(2,1)S(1)}, u32[]{:S(2)}, u32[]{:S(2)}) collective-permute-start(bf16[96,384]{1,0:T(8,128)(2,1)S(1)} %fusion.6), channel_id=1, source_target_pairs={{0,768},{256,512},{512,256},{768,0},{32,288},{288,32},{544,800},{8... | collective-permute-start | bytes 221192 | tf_op jit(solution)/shard_map/ppermute | solution.py:43
  153.0 41.1 %copy-start.6 = (bf16[6,3072]{1,0:T(8,128)(2,1)S(1)}, bf16[6,3072]{1,0:T(8,128)(2,1)}, u32[]{:S(2)}) copy-start(bf16[6,3072]{1,0:T(8,128)(2,1)} %out_grad.1) | copy-start | bytes 110596
  153.0 23.7 %collective-permute-start.21 = (bf16[12,3072]{1,0:T(8,128)(2,1)S(1)}, bf16[12,3072]{1,0:T(8,128)(2,1)S(1)}, u32[]{:S(2)}, u32[]{:S(2)}) collective-permute-start(bf16[12,3072]{1,0:T(8,128)(2,1)S(1)} %slice.303), channel_id=1, source_target_pairs={{0,2},{1,3},{2,0},{3,1},{4,6},{5,7},{6,4},{7,5},{8,10},{9,11},{10,... | collective-permute-start | bytes 221192 | tf_op jit(solution)/shard_map/ppermute | solution.py:22
  162.2 30.1 %collective-permute-start.23 = (bf16[96,384]{1,0:T(8,128)(2,1)S(1)}, bf16[96,384]{1,0:T(8,128)(2,1)S(1)}, u32[]{:S(2)}, u32[]{:S(2)}) collective-permute-start(bf16[96,384]{1,0:T(8,128)(2,1)S(1)} %fusion.9), channel_id=1, source_target_pairs={{0,768},{256,512},{512,256},{768,0},{32,288},{288,32},{544,800},{8... | collective-permute-start | bytes 221192 | tf_op jit(solution)/shard_map/ppermute | solution.py:43
  176.7 17.1 %collective-permute-start.22 = (bf16[6,3072]{1,0:T(8,128)(2,1)S(1)}, bf16[6,3072]{1,0:T(8,128)(2,1)S(1)}, u32[]{:S(2)}, u32[]{:S(2)}) collective-permute-start(bf16[6,3072]{1,0:T(8,128)(2,1)S(1)} %slice.304), channel_id=1, source_target_pairs={{0,4},{1,5},{2,6},{3,7},{4,0},{5,1},{6,2},{7,3},{8,12},{9,13},{10,... | collective-permute-start | bytes 110600 | tf_op jit(solution)/shard_map/ppermute | solution.py:22
  (2 other events, 1.5 us)

commit v9 on v8

--- a/solution.py
+++ b/solution.py
@@ -254,19 +254,18 @@
         return paired(added(summed(term, 1), got[1]).astype(BF16), "zh", 1)
 
     down_core, up_core = to_core(down), to_core(up)
-    down_y, up_y = to_y(down, down_core), to_y(up, up_core)
-    up_core, blocks = fence((up_core, blocks))
+    up_core_now, blocks = fence((up_core, blocks))
     full_term = jnp.einsum("xtf,df->xtd", blocks, up_weight, preferred_element_type=F32)
     full_term = full_term.astype(BF16)
     x_first = paired(full_term[2:], "x", 0)
-
+    down_y, up_y = to_y(down, down_core), to_y(up, up_core)
+    up_core = up_core_now
     down_y2 = to_second_y(down, down_core, down_y)
     down_z = to_z(down[0], down_core, down_y, down_y2)
-    down_y2, x_first = fence((down_y2, x_first))
-    x_second = paired(added(full_term[1], x_first[1]).astype(BF16), "x", 1)
-    up_y, x_second = fence((up_y, x_second))
+    down_y2, x_first, up_y = fence((down_y2, x_first, up_y))
     up_y2 = to_second_y(up, up_core, up_y)
     up_z = to_z(up[0], up_core, up_y, up_y2)
+    x_second = paired(added(full_term[1], x_first[1]).astype(BF16), "x", 1)
     own = added(full_term[0], x_first[0], x_second)
 
     def halved(own, distance):

time: 196 us -> 193 us (0.985)
  the two profiles are of different devices: /device:TPU:56 before, /device:TPU:6 now
where the time goes in v9:
time: 193 us; the launch traced here: 192 us
  starting transfers between devices  112 us (58%)
  waiting for transfers between devices  52.3 us (27%)
  other arithmetic  13 us (7%)
  Pallas kernels  7.65 us (4%)
  local copies, waits for them, and re-layouts  4.37 us (2%)
    ppermute x10, starting transfers between devices, paired(): return lax.ppermute(block, names, moves)  56.3 us
    ppermute x7, waiting for transfers between devices, swap(): return lax.ppermute(block, 'zl', [(i, i ^ distance) for i in range(8)])  36.4 us
    ppermute x7, starting transfers between devices, swap(): return lax.ppermute(block, 'zl', [(i, i ^ distance) for i in range(8)])  26.6 us
    ppermute x6, starting transfers between devices, x_moves(): return lambda block: lax.ppermute(block, ('c', 'x'), moves)  25.2 us
    ppermute x10, waiting for transfers between devices, paired(): return lax.ppermute(block, names, moves)  13 us
    pallas_call x3, Pallas kernels, computed(): pl.pallas_call(kernel, out_shape=[jax.ShapeDtypeStruct(*out) for out in o...  7.17 us
    ppermute x2, starting transfers between devices, to_core(): return lax.ppermute(term[1], 'c', [(0, 1), (1, 0)])  4.31 us
    unnamed x18, local copies, waits for them, and re-layouts  3.99 us
  transfers between devices with their start and end apart: 25, of which 14 were waited for; matrix products, arithmetic and copies ran while one was open for 7% of the time, Pallas kernels for 2%

profile of v9, /device:TPU:6, one launch (start us, length us, event | category | flops | bytes accessed | tf_op | source)
XLA Modules:
  0.0 191.9 jit_solution(4797406795656407439)
XLA Ops:
  3.3 9.1 %collective-permute-start = (bf16[24,1536]{1,0:T(8,128)(2,1)S(1)}, bf16[24,1536]{1,0:T(8,128)(2,1)S(1)}, u32[]{:S(2)}, u32[]{:S(2)}) collective-permute-start(bf16[24,1536]{1,0:T(8,128)(2,1)S(1)} %get-tuple-element.28.own), channel_id=1, source_target_pairs={{0,4},{1,5},{2,6},{3,7},{4,0},{5,1},{6,2},{7,3},{8,12},{9,13},{10,... | collective-permute-start | bytes 221192 | tf_op jit(solution)/shard_map/ppermute | solution.py:22
  12.4 7.1 %collective-permute-done.far = bf16[24,1536]{1,0:T(8,128)(2,1)S(1)} collective-permute-done((bf16[24,1536]{1,0:T(8,128)(2,1)S(1)}, bf16[24,1536]{1,0:T(8,128)(2,1)S(1)}, u32[]{:S(2)}, u32[]{:S(2)}) %collective-permute-start) | collective-permute-done | bytes 73760 | tf_op jit(solution)/shard_map/ppermute | solution.py:22
  19.5 2.1 %collective-permute-start.1 = (bf16[24,3072]{1,0:T(8,128)(2,1)S(1)}, bf16[24,3072]{1,0:T(8,128)(2,1)S(1)}, u32[]{:S(2)}, u32[]{:S(2)}) collective-permute-start(bf16[24,3072]{1,0:T(8,128)(2,1)S(1)} %shard_map.77.refs_0_), channel_id=1, source_target_pairs={{0,2},{1,3},{2,0},{3,1},{4,6},{5,7},{6,4},{7,5},{8,10},{9,11},{10,... | collective-permute-start | bytes 442376 | tf_op jit(solution)/shard_map/ppermute | solution.py:22
  21.6 4.7 %collective-permute-start.2 = (bf16[24,3072]{1,0:T(8,128)(2,1)S(1)}, bf16[24,3072]{1,0:T(8,128)(2,1)S(1)}, u32[]{:S(2)}, u32[]{:S(2)}) collective-permute-start(bf16[24,3072]{1,0:T(8,128)(2,1)S(1)} %shard_map.77.refs_0_), channel_id=1, source_target_pairs={{0,1},{1,0},{2,3},{3,2},{4,5},{5,4},{6,7},{7,6},{8,9},{9,8},{10,11... | collective-permute-start | bytes 442376 | tf_op jit(solution)/shard_map/ppermute | solution.py:22
  26.4 3.3 %collective-permute-start.3 = (bf16[24,3072]{1,0:T(8,128)(2,1)S(1)}, bf16[24,3072]{1,0:T(8,128)(2,1)S(1)}, u32[]{:S(2)}, u32[]{:S(2)}) collective-permute-start(bf16[24,3072]{1,0:T(8,128)(2,1)S(1)} %shard_map.77.refs_0_), channel_id=1, source_target_pairs={{0,3},{1,2},{2,1},{3,0},{4,7},{5,6},{6,5},{7,4},{8,11},{9,10},{10,... | collective-permute-start | bytes 442376 | tf_op jit(solution)/shard_map/ppermute | solution.py:22
  31.4 3.8 %collective-permute-done.3.refs_3_ = bf16[24,3072]{1,0:T(8,128)(2,1)S(1)} collective-permute-done((bf16[24,3072]{1,0:T(8,128)(2,1)S(1)}, bf16[24,3072]{1,0:T(8,128)(2,1)S(1)}, u32[]{:S(2)}, u32[]{:S(2)}) %collective-permute-start.3) | collective-permute-done | bytes 147488 | tf_op jit(solution)/shard_map/ppermute | solution.py:22
  35.3 6.7 %collective-permute-start.7 = (bf16[48,3072]{1,0:T(8,128)(2,1)S(1)}, bf16[48,3072]{1,0:T(8,128)(2,1)S(1)}, u32[]{:S(2)}, u32[]{:S(2)}) collective-permute-start(bf16[48,3072]{1,0:T(8,128)(2,1)S(1)} %get-tuple-element.30.refs_0_), channel_id=1, source_target_pairs={{0,8},{8,16},{16,24},{24,0},{32,56},{40,32},{48,40},{56,48},{1,9},... | collective-permute-start | bytes 884744 | tf_op jit(solution)/shard_map/ppermute | solution.py:27
  42.1 1.9 %collective-permute-start.4 = (bf16[48,3072]{1,0:T(8,128)(2,1)S(1)}, bf16[48,3072]{1,0:T(8,128)(2,1)S(1)}, u32[]{:S(2)}, u32[]{:S(2)}) collective-permute-start(bf16[48,3072]{1,0:T(8,128)(2,1)S(1)} %get-tuple-element.29.refs_0_), channel_id=1, source_target_pairs={{0,8},{8,16},{16,24},{24,0},{32,56},{40,32},{48,40},{56,48},{1,9},... | collective-permute-start | bytes 884744 | tf_op jit(solution)/shard_map/ppermute | solution.py:27
  44.0 3.9 %collective-permute-start.8 = (bf16[48,3072]{1,0:T(8,128)(2,1)S(1)}, bf16[48,3072]{1,0:T(8,128)(2,1)S(1)}, u32[]{:S(2)}, u32[]{:S(2)}) collective-permute-start(bf16[48,3072]{1,0:T(8,128)(2,1)S(1)} %get-tuple-element.30.refs_0_), channel_id=1, source_target_pairs={{0,24},{8,0},{16,8},{24,16},{32,40},{40,48},{48,56},{56,32},{1,25}... | collective-permute-start | bytes 884744 | tf_op jit(solution)/shard_map/ppermute | solution.py:27
  49.2 5.6 %collective-permute-start.9 = (bf16[48,3072]{1,0:T(8,128)(2,1)S(1)}, bf16[48,3072]{1,0:T(8,128)(2,1)S(1)}, u32[]{:S(2)}, u32[]{:S(2)}) collective-permute-start(bf16[48,3072]{1,0:T(8,128)(2,1)S(1)} %collective-permute-done.7.refs_1_), channel_id=1, source_target_pairs={{0,8},{8,16},{16,24},{24,0},{32,56},{40,32},{48,40},{56,48},{1,9},... | collective-permute-start | bytes 884744 | tf_op jit(solution)/shard_map/ppermute | solution.py:27
  54.8 1.9 %collective-permute-start.5 = (bf16[48,3072]{1,0:T(8,128)(2,1)S(1)}, bf16[48,3072]{1,0:T(8,128)(2,1)S(1)}, u32[]{:S(2)}, u32[]{:S(2)}) collective-permute-start(bf16[48,3072]{1,0:T(8,128)(2,1)S(1)} %get-tuple-element.29.refs_0_), channel_id=1, source_target_pairs={{0,24},{8,0},{16,8},{24,16},{32,40},{40,48},{48,56},{56,32},{1,25}... | collective-permute-start | bytes 884744 | tf_op jit(solution)/shard_map/ppermute | solution.py:27
  56.7 5.1 %collective-permute-start.6 = (bf16[48,3072]{1,0:T(8,128)(2,1)S(1)}, bf16[48,3072]{1,0:T(8,128)(2,1)S(1)}, u32[]{:S(2)}, u32[]{:S(2)}) collective-permute-start(bf16[48,3072]{1,0:T(8,128)(2,1)S(1)} %collective-permute-done.4.refs_1_), channel_id=1, source_target_pairs={{0,8},{8,16},{16,24},{24,0},{32,56},{40,32},{48,40},{56,48},{1,9},... | collective-permute-start | bytes 884744 | tf_op jit(solution)/shard_map/ppermute | solution.py:27
  66.1 2.7 %shard_map.80 = (bf16[192,3072]{1,0:T(8,128)(2,1)S(1)}, bf16[4,4,96,384]{3,2,1,0:T(8,128)(2,1)S(1)}, bf16[4,4,96,384]{3,2,1,0:T(8,128)(2,1)}) custom-call(s32[17]{0:T(128)S(1)} %concatenate.3.where, bf16[48,3072]{1,0:T(8,128)(2,1)S(1)} %get-tuple-element.29.refs_0_, bf16[48,3072]{1,0:T(8,128)(2,1)S(1)} %collective-permute-done.4.refs_1_, ...), custom_call_target="tpu_custom_call" | custom-call | flops 452984832 | bytes 8388608 | tf_op jit(solution)/shard_map/pallas_call | solution.py:184
  70.7 3.7 %shard_map.81 = (bf16[192,384]{1,0:T(8,128)(2,1)S(1)}, bf16[4,4,96,384]{3,2,1,0:T(8,128)(2,1)S(1)}, bf16[4,4,96,384]{3,2,1,0:T(8,128)(2,1)}) custom-call(s32[17]{0:T(128)S(1)} %concatenate.3.where, bf16[192,3072]{1,0:T(8,128)(2,1)S(1)} %get-tuple-element.32.grad, bf16[192,3072]{1,0:T(8,128)(2,1)S(1)} %get-tuple-element.33.normed, ...), custom_call_target="tpu_custom_call" | custom-call | flops 905969664 | bytes 8388608 | tf_op jit(solution)/shard_map/pallas_call | solution.py:184
  74.4 2.4 %collective-permute-start.10 = (bf16[4,4,96,384]{3,2,1,0:T(8,128)(2,1)}, bf16[4,4,96,384]{3,2,1,0:T(8,128)(2,1)}, u32[]{:S(2)}, u32[]{:S(2)}) collective-permute-start(bf16[4,4,96,384]{3,2,1,0:T(8,128)(2,1)} %get-tuple-element.36), channel_id=1, source_target_pairs={{0,32},{32,0},{1,33},{33,1},{2,34},{34,2},{3,35},{35,3},{4,36},{36... | collective-permute-start | bytes 3538952 | tf_op jit(solution)/shard_map/ppermute | solution.py:238
  78.2 1.9 %collective-permute-start.12 = (bf16[2,4,96,384]{3,2,1,0:T(8,128)(2,1)S(1)}, bf16[2,4,96,384]{3,2,1,0:T(8,128)(2,1)S(1)}, u32[]{:S(2)}, u32[]{:S(2)}) collective-permute-start(bf16[2,4,96,384]{3,2,1,0:T(8,128)(2,1)S(1)} %add_convert_fusion.1), channel_id=1, source_target_pairs={{0,64},{64,0},{128,192},{192,128},{32,224},{96,160},{160,96},{224,... | collective-permute-start | bytes 1769480 | tf_op jit(solution)/shard_map/ppermute | solution.py:43
  81.4 3.9 %collective-permute-start.15 = (bf16[2,4,96,384]{3,2,1,0:T(8,128)(2,1)S(1)}, bf16[2,4,96,384]{3,2,1,0:T(8,128)(2,1)S(1)}, u32[]{:S(2)}, u32[]{:S(2)}) collective-permute-start(bf16[2,4,96,384]{3,2,1,0:T(8,128)(2,1)S(1)} %add_convert_fusion), channel_id=1, source_target_pairs={{0,64},{64,0},{128,192},{192,128},{32,224},{96,160},{160,96},{224,... | collective-permute-start | bytes 1769480 | tf_op jit(solution)/shard_map/ppermute | solution.py:43
  86.4 1.9 %collective-permute-start.14 = (bf16[2,48,3072]{2,1,0:T(8,128)(2,1)S(1)}, bf16[2,48,3072]{2,1,0:T(8,128)(2,1)S(1)}, u32[]{:S(2)}, u32[]{:S(2)}) collective-permute-start(bf16[2,48,3072]{2,1,0:T(8,128)(2,1)S(1)} %slice.226), channel_id=1, source_target_pairs={{0,8},{8,0},{16,24},{24,16},{32,56},{40,48},{48,40},{56,32},{1,9},... | collective-permute-start | bytes 1769480 | tf_op jit(solution)/shard_map/ppermute | solution.py:43
  91.1 1.9 %collective-permute-start.13 = (bf16[4,96,384]{2,1,0:T(8,128)(2,1)S(1)}, bf16[4,96,384]{2,1,0:T(8,128)(2,1)S(1)}, u32[]{:S(2)}, u32[]{:S(2)}) collective-permute-start(bf16[4,96,384]{2,1,0:T(8,128)(2,1)S(1)} %fusion.1), channel_id=1, source_target_pairs={{0,192},{64,128},{128,64},{192,0},{32,96},{96,32},{160,224},{224,1... | collective-permute-start | bytes 884744 | tf_op jit(solution)/shard_map/ppermute | solution.py:43
  93.2 3.1 %collective-permute-done.15 = bf16[2,4,96,384]{3,2,1,0:T(8,128)(2,1)S(1)} collective-permute-done((bf16[2,4,96,384]{3,2,1,0:T(8,128)(2,1)S(1)}, bf16[2,4,96,384]{3,2,1,0:T(8,128)(2,1)S(1)}, u32[]{:S(2)}, u32[]{:S(2)}) %collective-permute-start.15) | collective-permute-done | bytes 589856 | tf_op jit(solution)/shard_map/ppermute | solution.py:43
  98.2 2.8 %collective-permute-done.13 = bf16[4,96,384]{2,1,0:T(8,128)(2,1)S(1)} collective-permute-done((bf16[4,96,384]{2,1,0:T(8,128)(2,1)S(1)}, bf16[4,96,384]{2,1,0:T(8,128)(2,1)S(1)}, u32[]{:S(2)}, u32[]{:S(2)}) %collective-permute-start.13) | collective-permute-done | bytes 294944 | tf_op jit(solution)/shard_map/ppermute | solution.py:43
  101.0 5.6 %collective-permute-start.19 = (bf16[48,3072]{1,0:T(8,128)(2,1)S(1)}, bf16[48,3072]{1,0:T(8,128)(2,1)S(1)}, u32[]{:S(2)}, u32[]{:S(2)}) collective-permute-start(bf16[48,3072]{1,0:T(8,128)(2,1)S(1)} %fusion.3), channel_id=1, source_target_pairs={{0,24},{8,16},{16,8},{24,0},{32,40},{40,32},{48,56},{56,48},{1,25}... | collective-permute-start | bytes 884744 | tf_op jit(solution)/shard_map/ppermute | solution.py:43
  107.7 1.9 %collective-permute-start.16 = (bf16[4,96,384]{2,1,0:T(8,128)(2,1)S(1)}, bf16[4,96,384]{2,1,0:T(8,128)(2,1)S(1)}, u32[]{:S(2)}, u32[]{:S(2)}) collective-permute-start(bf16[4,96,384]{2,1,0:T(8,128)(2,1)S(1)} %fusion.2), channel_id=1, source_target_pairs={{0,192},{64,128},{128,64},{192,0},{32,96},{96,32},{160,224},{224,1... | collective-permute-start | bytes 884744 | tf_op jit(solution)/shard_map/ppermute | solution.py:43
  110.6 12.1 %collective-permute-start.18 = (bf16[2,96,384]{2,1,0:T(8,128)(2,1)S(1)}, bf16[2,96,384]{2,1,0:T(8,128)(2,1)S(1)}, u32[]{:S(2)}, u32[]{:S(2)}) collective-permute-start(bf16[2,96,384]{2,1,0:T(8,128)(2,1)S(1)} %fusion.4), channel_id=1, source_target_pairs={{0,256},{256,0},{512,768},{768,512},{32,800},{288,544},{544,288},{... | collective-permute-start | bytes 442376 | tf_op jit(solution)/shard_map/ppermute | solution.py:43
  122.9 3.4 %collective-permute-start.20 = (bf16[24,3072]{1,0:T(8,128)(2,1)S(1)}, bf16[24,3072]{1,0:T(8,128)(2,1)S(1)}, u32[]{:S(2)}, u32[]{:S(2)}) collective-permute-start(bf16[24,3072]{1,0:T(8,128)(2,1)S(1)} %slice.302), channel_id=1, source_target_pairs={{0,1},{1,0},{2,3},{3,2},{4,5},{5,4},{6,7},{7,6},{8,9},{9,8},{10,11... | collective-permute-start | bytes 442376 | tf_op jit(solution)/shard_map/ppermute | solution.py:22
  127.3 3.8 %collective-permute-start.17 = (bf16[2,96,384]{2,1,0:T(8,128)(2,1)S(1)}, bf16[2,96,384]{2,1,0:T(8,128)(2,1)S(1)}, u32[]{:S(2)}, u32[]{:S(2)}) collective-permute-start(bf16[2,96,384]{2,1,0:T(8,128)(2,1)S(1)} %fusion.5), channel_id=1, source_target_pairs={{0,256},{256,0},{512,768},{768,512},{32,800},{288,544},{544,288},{... | collective-permute-start | bytes 442376 | tf_op jit(solution)/shard_map/ppermute | solution.py:43
  131.1 16.6 %collective-permute-done.20 = bf16[24,3072]{1,0:T(8,128)(2,1)S(1)} collective-permute-done((bf16[24,3072]{1,0:T(8,128)(2,1)S(1)}, bf16[24,3072]{1,0:T(8,128)(2,1)S(1)}, u32[]{:S(2)}, u32[]{:S(2)}) %collective-permute-start.20) | collective-permute-done | bytes 147488 | tf_op jit(solution)/shard_map/ppermute | solution.py:22
  148.7 21.3 %collective-permute-start.24 = (bf16[96,384]{1,0:T(8,128)(2,1)S(1)}, bf16[96,384]{1,0:T(8,128)(2,1)S(1)}, u32[]{:S(2)}, u32[]{:S(2)}) collective-permute-start(bf16[96,384]{1,0:T(8,128)(2,1)S(1)} %fusion.6), channel_id=1, source_target_pairs={{0,768},{256,512},{512,256},{768,0},{32,288},{288,32},{544,800},{8... | collective-permute-start | bytes 221192 | tf_op jit(solution)/shard_map/ppermute | solution.py:43
  170.0 2.1 %collective-permute-start.21 = (bf16[12,3072]{1,0:T(8,128)(2,1)S(1)}, bf16[12,3072]{1,0:T(8,128)(2,1)S(1)}, u32[]{:S(2)}, u32[]{:S(2)}) collective-permute-start(bf16[12,3072]{1,0:T(8,128)(2,1)S(1)} %slice.303), channel_id=1, source_target_pairs={{0,2},{1,3},{2,0},{3,1},{4,6},{5,7},{6,4},{7,5},{8,10},{9,11},{10,... | collective-permute-start | bytes 221192 | tf_op jit(solution)/shard_map/ppermute | solution.py:22
  173.0 1.9 %collective-permute-start.23 = (bf16[96,384]{1,0:T(8,128)(2,1)S(1)}, bf16[96,384]{1,0:T(8,128)(2,1)S(1)}, u32[]{:S(2)}, u32[]{:S(2)}) collective-permute-start(bf16[96,384]{1,0:T(8,128)(2,1)S(1)} %fusion.9), channel_id=1, source_target_pairs={{0,768},{256,512},{512,256},{768,0},{32,288},{288,32},{544,800},{8... | collective-permute-start | bytes 221192 | tf_op jit(solution)/shard_map/ppermute | solution.py:43
  175.0 6.0 %collective-permute-done.21 = bf16[12,3072]{1,0:T(8,128)(2,1)S(1)} collective-permute-done((bf16[12,3072]{1,0:T(8,128)(2,1)S(1)}, bf16[12,3072]{1,0:T(8,128)(2,1)S(1)}, u32[]{:S(2)}, u32[]{:S(2)}) %collective-permute-start.21) | collective-permute-done | bytes 73760 | tf_op jit(solution)/shard_map/ppermute | solution.py:22
  184.6 3.5 %collective-permute-done.23 = bf16[96,384]{1,0:T(8,128)(2,1)S(1)} collective-permute-done((bf16[96,384]{1,0:T(8,128)(2,1)S(1)}, bf16[96,384]{1,0:T(8,128)(2,1)S(1)}, u32[]{:S(2)}, u32[]{:S(2)}) %collective-permute-start.23) | collective-permute-done | bytes 73760 | tf_op jit(solution)/shard_map/ppermute | solution.py:43
  (72 shorter events, 32.9 us)
Async XLA Ops:
  0.6 0.8 copy-start.3
  3.3 16.2 %collective-permute-start = (bf16[24,1536]{1,0:T(8,128)(2,1)S(1)}, bf16[24,1536]{1,0:T(8,128)(2,1)S(1)}, u32[]{:S(2)}, u32[]{:S(2)}) collective-permute-start(bf16[24,1536]{1,0:T(8,128)(2,1)S(1)} %get-tuple-element.28.own), channel_id=1, source_target_pairs={{0,4},{1,5},{2,6},{3,7},{4,0},{5,1},{6,2},{7,3},{8,12},{9,13},{10,... | collective-permute-start | bytes 221192 | tf_op jit(solution)/shard_map/ppermute | solution.py:22
  19.5 10.1 %collective-permute-start.1 = (bf16[24,3072]{1,0:T(8,128)(2,1)S(1)}, bf16[24,3072]{1,0:T(8,128)(2,1)S(1)}, u32[]{:S(2)}, u32[]{:S(2)}) collective-permute-start(bf16[24,3072]{1,0:T(8,128)(2,1)S(1)} %shard_map.77.refs_0_), channel_id=1, source_target_pairs={{0,2},{1,3},{2,0},{3,1},{4,6},{5,7},{6,4},{7,5},{8,10},{9,11},{10,... | collective-permute-start | bytes 442376 | tf_op jit(solution)/shard_map/ppermute | solution.py:22
  21.6 9.8 %collective-permute-start.2 = (bf16[24,3072]{1,0:T(8,128)(2,1)S(1)}, bf16[24,3072]{1,0:T(8,128)(2,1)S(1)}, u32[]{:S(2)}, u32[]{:S(2)}) collective-permute-start(bf16[24,3072]{1,0:T(8,128)(2,1)S(1)} %shard_map.77.refs_0_), channel_id=1, source_target_pairs={{0,1},{1,0},{2,3},{3,2},{4,5},{5,4},{6,7},{7,6},{8,9},{9,8},{10,11... | collective-permute-start | bytes 442376 | tf_op jit(solution)/shard_map/ppermute | solution.py:22
  26.4 8.9 %collective-permute-start.3 = (bf16[24,3072]{1,0:T(8,128)(2,1)S(1)}, bf16[24,3072]{1,0:T(8,128)(2,1)S(1)}, u32[]{:S(2)}, u32[]{:S(2)}) collective-permute-start(bf16[24,3072]{1,0:T(8,128)(2,1)S(1)} %shard_map.77.refs_0_), channel_id=1, source_target_pairs={{0,3},{1,2},{2,1},{3,0},{4,7},{5,6},{6,5},{7,4},{8,11},{9,10},{10,... | collective-permute-start | bytes 442376 | tf_op jit(solution)/shard_map/ppermute | solution.py:22
  35.3 13.9 %collective-permute-start.7 = (bf16[48,3072]{1,0:T(8,128)(2,1)S(1)}, bf16[48,3072]{1,0:T(8,128)(2,1)S(1)}, u32[]{:S(2)}, u32[]{:S(2)}) collective-permute-start(bf16[48,3072]{1,0:T(8,128)(2,1)S(1)} %get-tuple-element.30.refs_0_), channel_id=1, source_target_pairs={{0,8},{8,16},{16,24},{24,0},{32,56},{40,32},{48,40},{56,48},{1,9},... | collective-permute-start | bytes 884744 | tf_op jit(solution)/shard_map/ppermute | solution.py:27
  42.1 14.7 %collective-permute-start.4 = (bf16[48,3072]{1,0:T(8,128)(2,1)S(1)}, bf16[48,3072]{1,0:T(8,128)(2,1)S(1)}, u32[]{:S(2)}, u32[]{:S(2)}) collective-permute-start(bf16[48,3072]{1,0:T(8,128)(2,1)S(1)} %get-tuple-element.29.refs_0_), channel_id=1, source_target_pairs={{0,8},{8,16},{16,24},{24,0},{32,56},{40,32},{48,40},{56,48},{1,9},... | collective-permute-start | bytes 884744 | tf_op jit(solution)/shard_map/ppermute | solution.py:27
  44.0 18.0 %collective-permute-start.8 = (bf16[48,3072]{1,0:T(8,128)(2,1)S(1)}, bf16[48,3072]{1,0:T(8,128)(2,1)S(1)}, u32[]{:S(2)}, u32[]{:S(2)}) collective-permute-start(bf16[48,3072]{1,0:T(8,128)(2,1)S(1)} %get-tuple-element.30.refs_0_), channel_id=1, source_target_pairs={{0,24},{8,0},{16,8},{24,16},{32,40},{40,48},{48,56},{56,32},{1,25}... | collective-permute-start | bytes 884744 | tf_op jit(solution)/shard_map/ppermute | solution.py:27
  49.2 12.8 %collective-permute-start.9 = (bf16[48,3072]{1,0:T(8,128)(2,1)S(1)}, bf16[48,3072]{1,0:T(8,128)(2,1)S(1)}, u32[]{:S(2)}, u32[]{:S(2)}) collective-permute-start(bf16[48,3072]{1,0:T(8,128)(2,1)S(1)} %collective-permute-done.7.refs_1_), channel_id=1, source_target_pairs={{0,8},{8,16},{16,24},{24,0},{32,56},{40,32},{48,40},{56,48},{1,9},... | collective-permute-start | bytes 884744 | tf_op jit(solution)/shard_map/ppermute | solution.py:27
  54.8 9.8 %collective-permute-start.5 = (bf16[48,3072]{1,0:T(8,128)(2,1)S(1)}, bf16[48,3072]{1,0:T(8,128)(2,1)S(1)}, u32[]{:S(2)}, u32[]{:S(2)}) collective-permute-start(bf16[48,3072]{1,0:T(8,128)(2,1)S(1)} %get-tuple-element.29.refs_0_), channel_id=1, source_target_pairs={{0,24},{8,0},{16,8},{24,16},{32,40},{40,48},{48,56},{56,32},{1,25}... | collective-permute-start | bytes 884744 | tf_op jit(solution)/shard_map/ppermute | solution.py:27
  56.7 9.4 %collective-permute-start.6 = (bf16[48,3072]{1,0:T(8,128)(2,1)S(1)}, bf16[48,3072]{1,0:T(8,128)(2,1)S(1)}, u32[]{:S(2)}, u32[]{:S(2)}) collective-permute-start(bf16[48,3072]{1,0:T(8,128)(2,1)S(1)} %collective-permute-done.4.refs_1_), channel_id=1, source_target_pairs={{0,8},{8,16},{16,24},{24,0},{32,56},{40,32},{48,40},{56,48},{1,9},... | collective-permute-start | bytes 884744 | tf_op jit(solution)/shard_map/ppermute | solution.py:27
  62.0 1.7 copy-start
  63.7 7.0 %copy-start.2 = (bf16[384,3072]{1,0:T(8,128)(2,1)S(1)}, bf16[384,3072]{1,0:T(8,128)(2,1)}, u32[]{:S(2)}) copy-start(bf16[384,3072]{1,0:T(8,128)(2,1)} %weight.1) | copy-start | bytes 7077892
  68.8 8.1 %collective-permute-start.11 = (bf16[4,4,96,384]{3,2,1,0:T(8,128)(2,1)}, bf16[4,4,96,384]{3,2,1,0:T(8,128)(2,1)}, u32[]{:S(2)}, u32[]{:S(2)}) collective-permute-start(bf16[4,4,96,384]{3,2,1,0:T(8,128)(2,1)} %get-tuple-element.40), channel_id=1, source_target_pairs={{0,32},{32,0},{1,33},{33,1},{2,34},{34,2},{3,35},{35,3},{4,36},{36... | collective-permute-start | bytes 3538952 | tf_op jit(solution)/shard_map/ppermute | solution.py:238
  74.4 5.8 %collective-permute-start.10 = (bf16[4,4,96,384]{3,2,1,0:T(8,128)(2,1)}, bf16[4,4,96,384]{3,2,1,0:T(8,128)(2,1)}, u32[]{:S(2)}, u32[]{:S(2)}) collective-permute-start(bf16[4,4,96,384]{3,2,1,0:T(8,128)(2,1)} %get-tuple-element.36), channel_id=1, source_target_pairs={{0,32},{32,0},{1,33},{33,1},{2,34},{34,2},{3,35},{35,3},{4,36},{36... | collective-permute-start | bytes 3538952 | tf_op jit(solution)/shard_map/ppermute | solution.py:238
  76.9 8.5 %copy-start.1 = (bf16[3072,384]{1,0:T(8,128)(2,1)S(1)}, bf16[3072,384]{1,0:T(8,128)(2,1)}, u32[]{:S(2)}) copy-start(bf16[3072,384]{1,0:T(8,128)(2,1)} %refs_4_.1) | copy-start | bytes 7077892
  78.2 11.8 %collective-permute-start.12 = (bf16[2,4,96,384]{3,2,1,0:T(8,128)(2,1)S(1)}, bf16[2,4,96,384]{3,2,1,0:T(8,128)(2,1)S(1)}, u32[]{:S(2)}, u32[]{:S(2)}) collective-permute-start(bf16[2,4,96,384]{3,2,1,0:T(8,128)(2,1)S(1)} %add_convert_fusion.1), channel_id=1, source_target_pairs={{0,64},{64,0},{128,192},{192,128},{32,224},{96,160},{160,96},{224,... | collective-permute-start | bytes 1769480 | tf_op jit(solution)/shard_map/ppermute | solution.py:43
  81.4 14.9 %collective-permute-start.15 = (bf16[2,4,96,384]{3,2,1,0:T(8,128)(2,1)S(1)}, bf16[2,4,96,384]{3,2,1,0:T(8,128)(2,1)S(1)}, u32[]{:S(2)}, u32[]{:S(2)}) collective-permute-start(bf16[2,4,96,384]{3,2,1,0:T(8,128)(2,1)S(1)} %add_convert_fusion), channel_id=1, source_target_pairs={{0,64},{64,0},{128,192},{192,128},{32,224},{96,160},{160,96},{224,... | collective-permute-start | bytes 1769480 | tf_op jit(solution)/shard_map/ppermute | solution.py:43
  86.4 11.8 %collective-permute-start.14 = (bf16[2,48,3072]{2,1,0:T(8,128)(2,1)S(1)}, bf16[2,48,3072]{2,1,0:T(8,128)(2,1)S(1)}, u32[]{:S(2)}, u32[]{:S(2)}) collective-permute-start(bf16[2,48,3072]{2,1,0:T(8,128)(2,1)S(1)} %slice.226), channel_id=1, source_target_pairs={{0,8},{8,0},{16,24},{24,16},{32,56},{40,48},{48,40},{56,32},{1,9},... | collective-permute-start | bytes 1769480 | tf_op jit(solution)/shard_map/ppermute | solution.py:43
  91.1 9.8 %collective-permute-start.13 = (bf16[4,96,384]{2,1,0:T(8,128)(2,1)S(1)}, bf16[4,96,384]{2,1,0:T(8,128)(2,1)S(1)}, u32[]{:S(2)}, u32[]{:S(2)}) collective-permute-start(bf16[4,96,384]{2,1,0:T(8,128)(2,1)S(1)} %fusion.1), channel_id=1, source_target_pairs={{0,192},{64,128},{128,64},{192,0},{32,96},{96,32},{160,224},{224,1... | collective-permute-start | bytes 884744 | tf_op jit(solution)/shard_map/ppermute | solution.py:43
  101.0 21.7 %collective-permute-start.19 = (bf16[48,3072]{1,0:T(8,128)(2,1)S(1)}, bf16[48,3072]{1,0:T(8,128)(2,1)S(1)}, u32[]{:S(2)}, u32[]{:S(2)}) collective-permute-start(bf16[48,3072]{1,0:T(8,128)(2,1)S(1)} %fusion.3), channel_id=1, source_target_pairs={{0,24},{8,16},{16,8},{24,0},{32,40},{40,32},{48,56},{56,48},{1,25}... | collective-permute-start | bytes 884744 | tf_op jit(solution)/shard_map/ppermute | solution.py:43
  107.7 15.2 %collective-permute-start.16 = (bf16[4,96,384]{2,1,0:T(8,128)(2,1)S(1)}, bf16[4,96,384]{2,1,0:T(8,128)(2,1)S(1)}, u32[]{:S(2)}, u32[]{:S(2)}) collective-permute-start(bf16[4,96,384]{2,1,0:T(8,128)(2,1)S(1)} %fusion.2), channel_id=1, source_target_pairs={{0,192},{64,128},{128,64},{192,0},{32,96},{96,32},{160,224},{224,1... | collective-permute-start | bytes 884744 | tf_op jit(solution)/shard_map/ppermute | solution.py:43
  110.6 37.1 %collective-permute-start.18 = (bf16[2,96,384]{2,1,0:T(8,128)(2,1)S(1)}, bf16[2,96,384]{2,1,0:T(8,128)(2,1)S(1)}, u32[]{:S(2)}, u32[]{:S(2)}) collective-permute-start(bf16[2,96,384]{2,1,0:T(8,128)(2,1)S(1)} %fusion.4), channel_id=1, source_target_pairs={{0,256},{256,0},{512,768},{768,512},{32,800},{288,544},{544,288},{... | collective-permute-start | bytes 442376 | tf_op jit(solution)/shard_map/ppermute | solution.py:43
  122.9 24.8 %collective-permute-start.20 = (bf16[24,3072]{1,0:T(8,128)(2,1)S(1)}, bf16[24,3072]{1,0:T(8,128)(2,1)S(1)}, u32[]{:S(2)}, u32[]{:S(2)}) collective-permute-start(bf16[24,3072]{1,0:T(8,128)(2,1)S(1)} %slice.302), channel_id=1, source_target_pairs={{0,1},{1,0},{2,3},{3,2},{4,5},{5,4},{6,7},{7,6},{8,9},{9,8},{10,11... | collective-permute-start | bytes 442376 | tf_op jit(solution)/shard_map/ppermute | solution.py:22
  127.3 44.8 %collective-permute-start.17 = (bf16[2,96,384]{2,1,0:T(8,128)(2,1)S(1)}, bf16[2,96,384]{2,1,0:T(8,128)(2,1)S(1)}, u32[]{:S(2)}, u32[]{:S(2)}) collective-permute-start(bf16[2,96,384]{2,1,0:T(8,128)(2,1)S(1)} %fusion.5), channel_id=1, source_target_pairs={{0,256},{256,0},{512,768},{768,512},{32,800},{288,544},{544,288},{... | collective-permute-start | bytes 442376 | tf_op jit(solution)/shard_map/ppermute | solution.py:43
  148.7 42.3 %copy-start.4 = (bf16[6,3072]{1,0:T(8,128)(2,1)S(1)}, bf16[6,3072]{1,0:T(8,128)(2,1)}, u32[]{:S(2)}) copy-start(bf16[6,3072]{1,0:T(8,128)(2,1)} %layer_input.1) | copy-start | bytes 110596
  148.7 42.3 %copy-start.8 = (f32[3072]{0:T(1024)S(1)}, f32[3072]{0:T(1024)}, u32[]{:S(2)}) copy-start(f32[3072]{0:T(1024)} %param.7) | copy-start | bytes 36868
  148.7 34.3 %collective-permute-start.24 = (bf16[96,384]{1,0:T(8,128)(2,1)S(1)}, bf16[96,384]{1,0:T(8,128)(2,1)S(1)}, u32[]{:S(2)}, u32[]{:S(2)}) collective-permute-start(bf16[96,384]{1,0:T(8,128)(2,1)S(1)} %fusion.6), channel_id=1, source_target_pairs={{0,768},{256,512},{512,256},{768,0},{32,288},{288,32},{544,800},{8... | collective-permute-start | bytes 221192 | tf_op jit(solution)/shard_map/ppermute | solution.py:43
  170.0 21.2 %copy-start.6 = (bf16[6,3072]{1,0:T(8,128)(2,1)S(1)}, bf16[6,3072]{1,0:T(8,128)(2,1)}, u32[]{:S(2)}) copy-start(bf16[6,3072]{1,0:T(8,128)(2,1)} %out_grad.1) | copy-start | bytes 110596
  170.0 11.0 %collective-permute-start.21 = (bf16[12,3072]{1,0:T(8,128)(2,1)S(1)}, bf16[12,3072]{1,0:T(8,128)(2,1)S(1)}, u32[]{:S(2)}, u32[]{:S(2)}) collective-permute-start(bf16[12,3072]{1,0:T(8,128)(2,1)S(1)} %slice.303), channel_id=1, source_target_pairs={{0,2},{1,3},{2,0},{3,1},{4,6},{5,7},{6,4},{7,5},{8,10},{9,11},{10,... | collective-permute-start | bytes 221192 | tf_op jit(solution)/shard_map/ppermute | solution.py:22
  173.0 15.1 %collective-permute-start.23 = (bf16[96,384]{1,0:T(8,128)(2,1)S(1)}, bf16[96,384]{1,0:T(8,128)(2,1)S(1)}, u32[]{:S(2)}, u32[]{:S(2)}) collective-permute-start(bf16[96,384]{1,0:T(8,128)(2,1)S(1)} %fusion.9), channel_id=1, source_target_pairs={{0,768},{256,512},{512,256},{768,0},{32,288},{288,32},{544,800},{8... | collective-permute-start | bytes 221192 | tf_op jit(solution)/shard_map/ppermute | solution.py:43
  181.1 9.9 %collective-permute-start.22 = (bf16[6,3072]{1,0:T(8,128)(2,1)S(1)}, bf16[6,3072]{1,0:T(8,128)(2,1)S(1)}, u32[]{:S(2)}, u32[]{:S(2)}) collective-permute-start(bf16[6,3072]{1,0:T(8,128)(2,1)S(1)} %slice.304), channel_id=1, source_target_pairs={{0,4},{1,5},{2,6},{3,7},{4,0},{5,1},{6,2},{7,3},{8,12},{9,13},{10,... | collective-permute-start | bytes 110600 | tf_op jit(solution)/shard_map/ppermute | solution.py:22
  (2 other events, 1.5 us)

commit v10 on v9

--- a/solution.py
+++ b/solution.py
@@ -272,7 +272,6 @@
         half = own.shape[0] // 2
         return added(own[:half], swap(own[half:].astype(BF16), distance))
 
-    up_y2, own = fence((up_y2, own))
     own = halved(own, 1)
     down, up = (down[0], down_core, down_y, down_y2), (up[0], up_core, up_y, up_y2)
     down_z, own = fence((down_z, own))

time: 193 us -> 190 us (0.984)
  the two profiles are of different devices: /device:TPU:6 before, /device:TPU:56 now
where the time goes in v10:
time: 190 us; the launch traced here: 189 us
  starting transfers between devices  118 us (62%)
  waiting for transfers between devices  43.8 us (23%)
  other arithmetic  13 us (7%)
  Pallas kernels  7.67 us (4%)
  local copies, waits for them, and re-layouts  4.38 us (2%)
    ppermute x10, starting transfers between devices, paired(): return lax.ppermute(block, names, moves)  59.3 us
    ppermute x7, starting transfers between devices, swap(): return lax.ppermute(block, 'zl', [(i, i ^ distance) for i in range(8)])  34.8 us
    ppermute x7, waiting for transfers between devices, swap(): return lax.ppermute(block, 'zl', [(i, i ^ distance) for i in range(8)])  27.3 us
    ppermute x6, starting transfers between devices, x_moves(): return lambda block: lax.ppermute(block, ('c', 'x'), moves)  19.4 us
    ppermute x10, waiting for transfers between devices, paired(): return lax.ppermute(block, names, moves)  11.3 us
    pallas_call x3, Pallas kernels, computed(): pl.pallas_call(kernel, out_shape=[jax.ShapeDtypeStruct(*out) for out in o...  7.19 us
    ppermute x6, waiting for transfers between devices, x_moves(): return lambda block: lax.ppermute(block, ('c', 'x'), moves)  5.24 us
    ppermute x2, starting transfers between devices, to_core(): return lax.ppermute(term[1], 'c', [(0, 1), (1, 0)])  4.3 us
  transfers between devices with their start and end apart: 25, of which 10 were waited for; matrix products, arithmetic and copies ran while one was open for 7% of the time, Pallas kernels for 2%

profile of v10, /device:TPU:56, one launch (start us, length us, event | category | flops | bytes accessed | tf_op | source)
XLA Modules:
  0.0 189.0 jit_solution(14111060575278261904)
XLA Ops:
  3.3 9.1 %collective-permute-start = (bf16[24,1536]{1,0:T(8,128)(2,1)S(1)}, bf16[24,1536]{1,0:T(8,128)(2,1)S(1)}, u32[]{:S(2)}, u32[]{:S(2)}) collective-permute-start(bf16[24,1536]{1,0:T(8,128)(2,1)S(1)} %get-tuple-element.26.own), channel_id=1, source_target_pairs={{0,4},{1,5},{2,6},{3,7},{4,0},{5,1},{6,2},{7,3},{8,12},{9,13},{10,... | collective-permute-start | bytes 221192 | tf_op jit(solution)/shard_map/ppermute | solution.py:22
  12.4 5.5 %collective-permute-done.far = bf16[24,1536]{1,0:T(8,128)(2,1)S(1)} collective-permute-done((bf16[24,1536]{1,0:T(8,128)(2,1)S(1)}, bf16[24,1536]{1,0:T(8,128)(2,1)S(1)}, u32[]{:S(2)}, u32[]{:S(2)}) %collective-permute-start) | collective-permute-done | bytes 73760 | tf_op jit(solution)/shard_map/ppermute | solution.py:22
  18.0 4.5 %collective-permute-start.1 = (bf16[24,3072]{1,0:T(8,128)(2,1)S(1)}, bf16[24,3072]{1,0:T(8,128)(2,1)S(1)}, u32[]{:S(2)}, u32[]{:S(2)}) collective-permute-start(bf16[24,3072]{1,0:T(8,128)(2,1)S(1)} %shard_map.77.refs_0_), channel_id=1, source_target_pairs={{0,2},{1,3},{2,0},{3,1},{4,6},{5,7},{6,4},{7,5},{8,10},{9,11},{10,... | collective-permute-start | bytes 442376 | tf_op jit(solution)/shard_map/ppermute | solution.py:22
  22.5 1.9 %collective-permute-start.2 = (bf16[24,3072]{1,0:T(8,128)(2,1)S(1)}, bf16[24,3072]{1,0:T(8,128)(2,1)S(1)}, u32[]{:S(2)}, u32[]{:S(2)}) collective-permute-start(bf16[24,3072]{1,0:T(8,128)(2,1)S(1)} %shard_map.77.refs_0_), channel_id=1, source_target_pairs={{0,1},{1,0},{2,3},{3,2},{4,5},{5,4},{6,7},{7,6},{8,9},{9,8},{10,11... | collective-permute-start | bytes 442376 | tf_op jit(solution)/shard_map/ppermute | solution.py:22
  24.5 2.7 %collective-permute-start.3 = (bf16[24,3072]{1,0:T(8,128)(2,1)S(1)}, bf16[24,3072]{1,0:T(8,128)(2,1)S(1)}, u32[]{:S(2)}, u32[]{:S(2)}) collective-permute-start(bf16[24,3072]{1,0:T(8,128)(2,1)S(1)} %shard_map.77.refs_0_), channel_id=1, source_target_pairs={{0,3},{1,2},{2,1},{3,0},{4,7},{5,6},{6,5},{7,4},{8,11},{9,10},{10,... | collective-permute-start | bytes 442376 | tf_op jit(solution)/shard_map/ppermute | solution.py:22
  27.6 3.5 %collective-permute-done.2.refs_2_ = bf16[24,3072]{1,0:T(8,128)(2,1)S(1)} collective-permute-done((bf16[24,3072]{1,0:T(8,128)(2,1)S(1)}, bf16[24,3072]{1,0:T(8,128)(2,1)S(1)}, u32[]{:S(2)}, u32[]{:S(2)}) %collective-permute-start.2) | collective-permute-done | bytes 147488 | tf_op jit(solution)/shard_map/ppermute | solution.py:22
  31.1 3.8 %collective-permute-done.3.refs_3_ = bf16[24,3072]{1,0:T(8,128)(2,1)S(1)} collective-permute-done((bf16[24,3072]{1,0:T(8,128)(2,1)S(1)}, bf16[24,3072]{1,0:T(8,128)(2,1)S(1)}, u32[]{:S(2)}, u32[]{:S(2)}) %collective-permute-start.3) | collective-permute-done | bytes 147488 | tf_op jit(solution)/shard_map/ppermute | solution.py:22
  34.9 3.4 %collective-permute-start.7 = (bf16[48,3072]{1,0:T(8,128)(2,1)S(1)}, bf16[48,3072]{1,0:T(8,128)(2,1)S(1)}, u32[]{:S(2)}, u32[]{:S(2)}) collective-permute-start(bf16[48,3072]{1,0:T(8,128)(2,1)S(1)} %get-tuple-element.28.refs_0_), channel_id=1, source_target_pairs={{0,8},{8,16},{16,24},{24,0},{32,56},{40,32},{48,40},{56,48},{1,9},... | collective-permute-start | bytes 884744 | tf_op jit(solution)/shard_map/ppermute | solution.py:27
  38.3 3.4 %collective-permute-start.4 = (bf16[48,3072]{1,0:T(8,128)(2,1)S(1)}, bf16[48,3072]{1,0:T(8,128)(2,1)S(1)}, u32[]{:S(2)}, u32[]{:S(2)}) collective-permute-start(bf16[48,3072]{1,0:T(8,128)(2,1)S(1)} %get-tuple-element.27.refs_0_), channel_id=1, source_target_pairs={{0,8},{8,16},{16,24},{24,0},{32,56},{40,32},{48,40},{56,48},{1,9},... | collective-permute-start | bytes 884744 | tf_op jit(solution)/shard_map/ppermute | solution.py:27
  41.8 3.7 %collective-permute-start.8 = (bf16[48,3072]{1,0:T(8,128)(2,1)S(1)}, bf16[48,3072]{1,0:T(8,128)(2,1)S(1)}, u32[]{:S(2)}, u32[]{:S(2)}) collective-permute-start(bf16[48,3072]{1,0:T(8,128)(2,1)S(1)} %get-tuple-element.28.refs_0_), channel_id=1, source_target_pairs={{0,24},{8,0},{16,8},{24,16},{32,40},{40,48},{48,56},{56,32},{1,25}... | collective-permute-start | bytes 884744 | tf_op jit(solution)/shard_map/ppermute | solution.py:27
  45.4 2.2 %collective-permute-start.9 = (bf16[48,3072]{1,0:T(8,128)(2,1)S(1)}, bf16[48,3072]{1,0:T(8,128)(2,1)S(1)}, u32[]{:S(2)}, u32[]{:S(2)}) collective-permute-start(bf16[48,3072]{1,0:T(8,128)(2,1)S(1)} %collective-permute-done.7.refs_1_), channel_id=1, source_target_pairs={{0,8},{8,16},{16,24},{24,0},{32,56},{40,32},{48,40},{56,48},{1,9},... | collective-permute-start | bytes 884744 | tf_op jit(solution)/shard_map/ppermute | solution.py:27
  47.6 4.9 %collective-permute-start.5 = (bf16[48,3072]{1,0:T(8,128)(2,1)S(1)}, bf16[48,3072]{1,0:T(8,128)(2,1)S(1)}, u32[]{:S(2)}, u32[]{:S(2)}) collective-permute-start(bf16[48,3072]{1,0:T(8,128)(2,1)S(1)} %get-tuple-element.27.refs_0_), channel_id=1, source_target_pairs={{0,24},{8,0},{16,8},{24,16},{32,40},{40,48},{48,56},{56,32},{1,25}... | collective-permute-start | bytes 884744 | tf_op jit(solution)/shard_map/ppermute | solution.py:27
  52.5 1.9 %collective-permute-start.6 = (bf16[48,3072]{1,0:T(8,128)(2,1)S(1)}, bf16[48,3072]{1,0:T(8,128)(2,1)S(1)}, u32[]{:S(2)}, u32[]{:S(2)}) collective-permute-start(bf16[48,3072]{1,0:T(8,128)(2,1)S(1)} %collective-permute-done.4.refs_1_), channel_id=1, source_target_pairs={{0,8},{8,16},{16,24},{24,0},{32,56},{40,32},{48,40},{56,48},{1,9},... | collective-permute-start | bytes 884744 | tf_op jit(solution)/shard_map/ppermute | solution.py:27
  54.6 3.4 %collective-permute-done.9.refs_3_ = bf16[48,3072]{1,0:T(8,128)(2,1)S(1)} collective-permute-done((bf16[48,3072]{1,0:T(8,128)(2,1)S(1)}, bf16[48,3072]{1,0:T(8,128)(2,1)S(1)}, u32[]{:S(2)}, u32[]{:S(2)}) %collective-permute-start.9) | collective-permute-done | bytes 294944 | tf_op jit(solution)/shard_map/ppermute | solution.py:27
  62.3 2.7 %shard_map.80 = (bf16[192,3072]{1,0:T(8,128)(2,1)S(1)}, bf16[4,4,96,384]{3,2,1,0:T(8,128)(2,1)S(1)}, bf16[4,4,96,384]{3,2,1,0:T(8,128)(2,1)}) custom-call(s32[17]{0:T(128)S(1)} %concatenate.3.where, bf16[48,3072]{1,0:T(8,128)(2,1)S(1)} %get-tuple-element.27.refs_0_, bf16[48,3072]{1,0:T(8,128)(2,1)S(1)} %collective-permute-done.4.refs_1_, ...), custom_call_target="tpu_custom_call" | custom-call | flops 452984832 | bytes 8388608 | tf_op jit(solution)/shard_map/pallas_call | solution.py:184
  66.9 3.7 %shard_map.81 = (bf16[192,384]{1,0:T(8,128)(2,1)S(1)}, bf16[4,4,96,384]{3,2,1,0:T(8,128)(2,1)S(1)}, bf16[4,4,96,384]{3,2,1,0:T(8,128)(2,1)}) custom-call(s32[17]{0:T(128)S(1)} %concatenate.3.where, bf16[192,3072]{1,0:T(8,128)(2,1)S(1)} %get-tuple-element.30.grad, bf16[192,3072]{1,0:T(8,128)(2,1)S(1)} %get-tuple-element.31.normed, ...), custom_call_target="tpu_custom_call" | custom-call | flops 905969664 | bytes 8388608 | tf_op jit(solution)/shard_map/pallas_call | solution.py:184
  70.6 2.4 %collective-permute-start.10 = (bf16[4,4,96,384]{3,2,1,0:T(8,128)(2,1)}, bf16[4,4,96,384]{3,2,1,0:T(8,128)(2,1)}, u32[]{:S(2)}, u32[]{:S(2)}) collective-permute-start(bf16[4,4,96,384]{3,2,1,0:T(8,128)(2,1)} %get-tuple-element.34), channel_id=1, source_target_pairs={{0,32},{32,0},{1,33},{33,1},{2,34},{34,2},{3,35},{35,3},{4,36},{36... | collective-permute-start | bytes 3538952 | tf_op jit(solution)/shard_map/ppermute | solution.py:238
  74.5 2.7 %collective-permute-start.12 = (bf16[2,4,96,384]{3,2,1,0:T(8,128)(2,1)S(1)}, bf16[2,4,96,384]{3,2,1,0:T(8,128)(2,1)S(1)}, u32[]{:S(2)}, u32[]{:S(2)}) collective-permute-start(bf16[2,4,96,384]{3,2,1,0:T(8,128)(2,1)S(1)} %add_convert_fusion.1), channel_id=1, source_target_pairs={{0,64},{64,0},{128,192},{192,128},{32,224},{96,160},{160,96},{224,... | collective-permute-start | bytes 1769480 | tf_op jit(solution)/shard_map/ppermute | solution.py:43
  78.4 3.2 %collective-permute-start.15 = (bf16[2,4,96,384]{3,2,1,0:T(8,128)(2,1)S(1)}, bf16[2,4,96,384]{3,2,1,0:T(8,128)(2,1)S(1)}, u32[]{:S(2)}, u32[]{:S(2)}) collective-permute-start(bf16[2,4,96,384]{3,2,1,0:T(8,128)(2,1)S(1)} %add_convert_fusion), channel_id=1, source_target_pairs={{0,64},{64,0},{128,192},{192,128},{32,224},{96,160},{160,96},{224,... | collective-permute-start | bytes 1769480 | tf_op jit(solution)/shard_map/ppermute | solution.py:43
  87.3 8.2 %collective-permute-start.13 = (bf16[4,96,384]{2,1,0:T(8,128)(2,1)S(1)}, bf16[4,96,384]{2,1,0:T(8,128)(2,1)S(1)}, u32[]{:S(2)}, u32[]{:S(2)}) collective-permute-start(bf16[4,96,384]{2,1,0:T(8,128)(2,1)S(1)} %fusion.1), channel_id=1, source_target_pairs={{0,192},{64,128},{128,64},{192,0},{32,96},{96,32},{160,224},{224,1... | collective-permute-start | bytes 884744 | tf_op jit(solution)/shard_map/ppermute | solution.py:43
  95.7 4.5 %collective-permute-done.13 = bf16[4,96,384]{2,1,0:T(8,128)(2,1)S(1)} collective-permute-done((bf16[4,96,384]{2,1,0:T(8,128)(2,1)S(1)}, bf16[4,96,384]{2,1,0:T(8,128)(2,1)S(1)}, u32[]{:S(2)}, u32[]{:S(2)}) %collective-permute-start.13) | collective-permute-done | bytes 294944 | tf_op jit(solution)/shard_map/ppermute | solution.py:43
  100.3 1.9 %collective-permute-start.19 = (bf16[48,3072]{1,0:T(8,128)(2,1)S(1)}, bf16[48,3072]{1,0:T(8,128)(2,1)S(1)}, u32[]{:S(2)}, u32[]{:S(2)}) collective-permute-start(bf16[48,3072]{1,0:T(8,128)(2,1)S(1)} %fusion.3), channel_id=1, source_target_pairs={{0,24},{8,16},{16,8},{24,0},{32,40},{40,32},{48,56},{56,48},{1,25}... | collective-permute-start | bytes 884744 | tf_op jit(solution)/shard_map/ppermute | solution.py:43
  103.2 13.7 %collective-permute-start.18 = (bf16[2,96,384]{2,1,0:T(8,128)(2,1)S(1)}, bf16[2,96,384]{2,1,0:T(8,128)(2,1)S(1)}, u32[]{:S(2)}, u32[]{:S(2)}) collective-permute-start(bf16[2,96,384]{2,1,0:T(8,128)(2,1)S(1)} %fusion.4), channel_id=1, source_target_pairs={{0,256},{256,0},{512,768},{768,512},{32,800},{288,544},{544,288},{... | collective-permute-start | bytes 442376 | tf_op jit(solution)/shard_map/ppermute | solution.py:43
  118.0 2.1 %collective-permute-start.16 = (bf16[4,96,384]{2,1,0:T(8,128)(2,1)S(1)}, bf16[4,96,384]{2,1,0:T(8,128)(2,1)S(1)}, u32[]{:S(2)}, u32[]{:S(2)}) collective-permute-start(bf16[4,96,384]{2,1,0:T(8,128)(2,1)S(1)} %fusion.2), channel_id=1, source_target_pairs={{0,192},{64,128},{128,64},{192,0},{32,96},{96,32},{160,224},{224,1... | collective-permute-start | bytes 884744 | tf_op jit(solution)/shard_map/ppermute | solution.py:43
  120.2 2.5 %collective-permute-start.20 = (bf16[24,3072]{1,0:T(8,128)(2,1)S(1)}, bf16[24,3072]{1,0:T(8,128)(2,1)S(1)}, u32[]{:S(2)}, u32[]{:S(2)}) collective-permute-start(bf16[24,3072]{1,0:T(8,128)(2,1)S(1)} %slice.309), channel_id=1, source_target_pairs={{0,1},{1,0},{2,3},{3,2},{4,5},{5,4},{6,7},{7,6},{8,9},{9,8},{10,11... | collective-permute-start | bytes 442376 | tf_op jit(solution)/shard_map/ppermute | solution.py:22
  122.7 5.0 %collective-permute-done.16 = bf16[4,96,384]{2,1,0:T(8,128)(2,1)S(1)} collective-permute-done((bf16[4,96,384]{2,1,0:T(8,128)(2,1)S(1)}, bf16[4,96,384]{2,1,0:T(8,128)(2,1)S(1)}, u32[]{:S(2)}, u32[]{:S(2)}) %collective-permute-start.16) | collective-permute-done | bytes 294944 | tf_op jit(solution)/shard_map/ppermute | solution.py:43
  128.8 1.9 %collective-permute-start.17 = (bf16[2,96,384]{2,1,0:T(8,128)(2,1)S(1)}, bf16[2,96,384]{2,1,0:T(8,128)(2,1)S(1)}, u32[]{:S(2)}, u32[]{:S(2)}) collective-permute-start(bf16[2,96,384]{2,1,0:T(8,128)(2,1)S(1)} %fusion.5), channel_id=1, source_target_pairs={{0,256},{256,0},{512,768},{768,512},{32,800},{288,544},{544,288},{... | collective-permute-start | bytes 442376 | tf_op jit(solution)/shard_map/ppermute | solution.py:43
  130.7 14.2 %collective-permute-done.20 = bf16[24,3072]{1,0:T(8,128)(2,1)S(1)} collective-permute-done((bf16[24,3072]{1,0:T(8,128)(2,1)S(1)}, bf16[24,3072]{1,0:T(8,128)(2,1)S(1)}, u32[]{:S(2)}, u32[]{:S(2)}) %collective-permute-start.20) | collective-permute-done | bytes 147488 | tf_op jit(solution)/shard_map/ppermute | solution.py:22
  145.9 3.7 %collective-permute-start.24 = (bf16[96,384]{1,0:T(8,128)(2,1)S(1)}, bf16[96,384]{1,0:T(8,128)(2,1)S(1)}, u32[]{:S(2)}, u32[]{:S(2)}) collective-permute-start(bf16[96,384]{1,0:T(8,128)(2,1)S(1)} %fusion.6), channel_id=1, source_target_pairs={{0,768},{256,512},{512,256},{768,0},{32,288},{288,32},{544,800},{8... | collective-permute-start | bytes 221192 | tf_op jit(solution)/shard_map/ppermute | solution.py:43
  149.6 2.8 %collective-permute-start.21 = (bf16[12,3072]{1,0:T(8,128)(2,1)S(1)}, bf16[12,3072]{1,0:T(8,128)(2,1)S(1)}, u32[]{:S(2)}, u32[]{:S(2)}) collective-permute-start(bf16[12,3072]{1,0:T(8,128)(2,1)S(1)} %slice.310), channel_id=1, source_target_pairs={{0,2},{1,3},{2,0},{3,1},{4,6},{5,7},{6,4},{7,5},{8,10},{9,11},{10,... | collective-permute-start | bytes 221192 | tf_op jit(solution)/shard_map/ppermute | solution.py:22
  153.4 20.1 %collective-permute-start.23 = (bf16[96,384]{1,0:T(8,128)(2,1)S(1)}, bf16[96,384]{1,0:T(8,128)(2,1)S(1)}, u32[]{:S(2)}, u32[]{:S(2)}) collective-permute-start(bf16[96,384]{1,0:T(8,128)(2,1)S(1)} %fusion.9), channel_id=1, source_target_pairs={{0,768},{256,512},{512,256},{768,0},{32,288},{288,32},{544,800},{8... | collective-permute-start | bytes 221192 | tf_op jit(solution)/shard_map/ppermute | solution.py:43
  173.6 11.2 %collective-permute-start.22 = (bf16[6,3072]{1,0:T(8,128)(2,1)S(1)}, bf16[6,3072]{1,0:T(8,128)(2,1)S(1)}, u32[]{:S(2)}, u32[]{:S(2)}) collective-permute-start(bf16[6,3072]{1,0:T(8,128)(2,1)S(1)} %slice.311), channel_id=1, source_target_pairs={{0,4},{1,5},{2,6},{3,7},{4,0},{5,1},{6,2},{7,3},{8,12},{9,13},{10,... | collective-permute-start | bytes 110600 | tf_op jit(solution)/shard_map/ppermute | solution.py:22
  (72 shorter events, 27.5 us)
Async XLA Ops:
  0.6 0.8 copy-start.3
  3.3 14.6 %collective-permute-start = (bf16[24,1536]{1,0:T(8,128)(2,1)S(1)}, bf16[24,1536]{1,0:T(8,128)(2,1)S(1)}, u32[]{:S(2)}, u32[]{:S(2)}) collective-permute-start(bf16[24,1536]{1,0:T(8,128)(2,1)S(1)} %get-tuple-element.26.own), channel_id=1, source_target_pairs={{0,4},{1,5},{2,6},{3,7},{4,0},{5,1},{6,2},{7,3},{8,12},{9,13},{10,... | collective-permute-start | bytes 221192 | tf_op jit(solution)/shard_map/ppermute | solution.py:22
  18.0 9.6 %collective-permute-start.1 = (bf16[24,3072]{1,0:T(8,128)(2,1)S(1)}, bf16[24,3072]{1,0:T(8,128)(2,1)S(1)}, u32[]{:S(2)}, u32[]{:S(2)}) collective-permute-start(bf16[24,3072]{1,0:T(8,128)(2,1)S(1)} %shard_map.77.refs_0_), channel_id=1, source_target_pairs={{0,2},{1,3},{2,0},{3,1},{4,6},{5,7},{6,4},{7,5},{8,10},{9,11},{10,... | collective-permute-start | bytes 442376 | tf_op jit(solution)/shard_map/ppermute | solution.py:22
  22.5 8.5 %collective-permute-start.2 = (bf16[24,3072]{1,0:T(8,128)(2,1)S(1)}, bf16[24,3072]{1,0:T(8,128)(2,1)S(1)}, u32[]{:S(2)}, u32[]{:S(2)}) collective-permute-start(bf16[24,3072]{1,0:T(8,128)(2,1)S(1)} %shard_map.77.refs_0_), channel_id=1, source_target_pairs={{0,1},{1,0},{2,3},{3,2},{4,5},{5,4},{6,7},{7,6},{8,9},{9,8},{10,11... | collective-permute-start | bytes 442376 | tf_op jit(solution)/shard_map/ppermute | solution.py:22
  24.5 10.4 %collective-permute-start.3 = (bf16[24,3072]{1,0:T(8,128)(2,1)S(1)}, bf16[24,3072]{1,0:T(8,128)(2,1)S(1)}, u32[]{:S(2)}, u32[]{:S(2)}) collective-permute-start(bf16[24,3072]{1,0:T(8,128)(2,1)S(1)} %shard_map.77.refs_0_), channel_id=1, source_target_pairs={{0,3},{1,2},{2,1},{3,0},{4,7},{5,6},{6,5},{7,4},{8,11},{9,10},{10,... | collective-permute-start | bytes 442376 | tf_op jit(solution)/shard_map/ppermute | solution.py:22
  34.9 10.5 %collective-permute-start.7 = (bf16[48,3072]{1,0:T(8,128)(2,1)S(1)}, bf16[48,3072]{1,0:T(8,128)(2,1)S(1)}, u32[]{:S(2)}, u32[]{:S(2)}) collective-permute-start(bf16[48,3072]{1,0:T(8,128)(2,1)S(1)} %get-tuple-element.28.refs_0_), channel_id=1, source_target_pairs={{0,8},{8,16},{16,24},{24,0},{32,56},{40,32},{48,40},{56,48},{1,9},... | collective-permute-start | bytes 884744 | tf_op jit(solution)/shard_map/ppermute | solution.py:27
  38.3 14.2 %collective-permute-start.4 = (bf16[48,3072]{1,0:T(8,128)(2,1)S(1)}, bf16[48,3072]{1,0:T(8,128)(2,1)S(1)}, u32[]{:S(2)}, u32[]{:S(2)}) collective-permute-start(bf16[48,3072]{1,0:T(8,128)(2,1)S(1)} %get-tuple-element.27.refs_0_), channel_id=1, source_target_pairs={{0,8},{8,16},{16,24},{24,0},{32,56},{40,32},{48,40},{56,48},{1,9},... | collective-permute-start | bytes 884744 | tf_op jit(solution)/shard_map/ppermute | solution.py:27
  41.8 12.8 %collective-permute-start.8 = (bf16[48,3072]{1,0:T(8,128)(2,1)S(1)}, bf16[48,3072]{1,0:T(8,128)(2,1)S(1)}, u32[]{:S(2)}, u32[]{:S(2)}) collective-permute-start(bf16[48,3072]{1,0:T(8,128)(2,1)S(1)} %get-tuple-element.28.refs_0_), channel_id=1, source_target_pairs={{0,24},{8,0},{16,8},{24,16},{32,40},{40,48},{48,56},{56,32},{1,25}... | collective-permute-start | bytes 884744 | tf_op jit(solution)/shard_map/ppermute | solution.py:27
  45.4 12.6 %collective-permute-start.9 = (bf16[48,3072]{1,0:T(8,128)(2,1)S(1)}, bf16[48,3072]{1,0:T(8,128)(2,1)S(1)}, u32[]{:S(2)}, u32[]{:S(2)}) collective-permute-start(bf16[48,3072]{1,0:T(8,128)(2,1)S(1)} %collective-permute-done.7.refs_1_), channel_id=1, source_target_pairs={{0,8},{8,16},{16,24},{24,0},{32,56},{40,32},{48,40},{56,48},{1,9},... | collective-permute-start | bytes 884744 | tf_op jit(solution)/shard_map/ppermute | solution.py:27
  47.6 12.9 %collective-permute-start.5 = (bf16[48,3072]{1,0:T(8,128)(2,1)S(1)}, bf16[48,3072]{1,0:T(8,128)(2,1)S(1)}, u32[]{:S(2)}, u32[]{:S(2)}) collective-permute-start(bf16[48,3072]{1,0:T(8,128)(2,1)S(1)} %get-tuple-element.27.refs_0_), channel_id=1, source_target_pairs={{0,24},{8,0},{16,8},{24,16},{32,40},{40,48},{48,56},{56,32},{1,25}... | collective-permute-start | bytes 884744 | tf_op jit(solution)/shard_map/ppermute | solution.py:27
  52.5 9.8 %collective-permute-start.6 = (bf16[48,3072]{1,0:T(8,128)(2,1)S(1)}, bf16[48,3072]{1,0:T(8,128)(2,1)S(1)}, u32[]{:S(2)}, u32[]{:S(2)}) collective-permute-start(bf16[48,3072]{1,0:T(8,128)(2,1)S(1)} %collective-permute-done.4.refs_1_), channel_id=1, source_target_pairs={{0,8},{8,16},{16,24},{24,0},{32,56},{40,32},{48,40},{56,48},{1,9},... | collective-permute-start | bytes 884744 | tf_op jit(solution)/shard_map/ppermute | solution.py:27
  58.0 1.7 copy-start
  59.6 7.3 %copy-start.2 = (bf16[384,3072]{1,0:T(8,128)(2,1)S(1)}, bf16[384,3072]{1,0:T(8,128)(2,1)}, u32[]{:S(2)}) copy-start(bf16[384,3072]{1,0:T(8,128)(2,1)} %weight.1) | copy-start | bytes 7077892
  65.0 8.1 %collective-permute-start.11 = (bf16[4,4,96,384]{3,2,1,0:T(8,128)(2,1)}, bf16[4,4,96,384]{3,2,1,0:T(8,128)(2,1)}, u32[]{:S(2)}, u32[]{:S(2)}) collective-permute-start(bf16[4,4,96,384]{3,2,1,0:T(8,128)(2,1)} %get-tuple-element.38), channel_id=1, source_target_pairs={{0,32},{32,0},{1,33},{33,1},{2,34},{34,2},{3,35},{35,3},{4,36},{36... | collective-permute-start | bytes 3538952 | tf_op jit(solution)/shard_map/ppermute | solution.py:238
  70.6 6.5 %collective-permute-start.10 = (bf16[4,4,96,384]{3,2,1,0:T(8,128)(2,1)}, bf16[4,4,96,384]{3,2,1,0:T(8,128)(2,1)}, u32[]{:S(2)}, u32[]{:S(2)}) collective-permute-start(bf16[4,4,96,384]{3,2,1,0:T(8,128)(2,1)} %get-tuple-element.34), channel_id=1, source_target_pairs={{0,32},{32,0},{1,33},{33,1},{2,34},{34,2},{3,35},{35,3},{4,36},{36... | collective-permute-start | bytes 3538952 | tf_op jit(solution)/shard_map/ppermute | solution.py:238
  73.1 8.5 %copy-start.1 = (bf16[3072,384]{1,0:T(8,128)(2,1)S(1)}, bf16[3072,384]{1,0:T(8,128)(2,1)}, u32[]{:S(2)}) copy-start(bf16[3072,384]{1,0:T(8,128)(2,1)} %refs_4_.1) | copy-start | bytes 7077892
  74.5 11.8 %collective-permute-start.12 = (bf16[2,4,96,384]{3,2,1,0:T(8,128)(2,1)S(1)}, bf16[2,4,96,384]{3,2,1,0:T(8,128)(2,1)S(1)}, u32[]{:S(2)}, u32[]{:S(2)}) collective-permute-start(bf16[2,4,96,384]{3,2,1,0:T(8,128)(2,1)S(1)} %add_convert_fusion.1), channel_id=1, source_target_pairs={{0,64},{64,0},{128,192},{192,128},{32,224},{96,160},{160,96},{224,... | collective-permute-start | bytes 1769480 | tf_op jit(solution)/shard_map/ppermute | solution.py:43
  78.4 17.3 %collective-permute-start.15 = (bf16[2,4,96,384]{3,2,1,0:T(8,128)(2,1)S(1)}, bf16[2,4,96,384]{3,2,1,0:T(8,128)(2,1)S(1)}, u32[]{:S(2)}, u32[]{:S(2)}) collective-permute-start(bf16[2,4,96,384]{3,2,1,0:T(8,128)(2,1)S(1)} %add_convert_fusion), channel_id=1, source_target_pairs={{0,64},{64,0},{128,192},{192,128},{32,224},{96,160},{160,96},{224,... | collective-permute-start | bytes 1769480 | tf_op jit(solution)/shard_map/ppermute | solution.py:43
  82.6 13.1 %collective-permute-start.14 = (bf16[2,48,3072]{2,1,0:T(8,128)(2,1)S(1)}, bf16[2,48,3072]{2,1,0:T(8,128)(2,1)S(1)}, u32[]{:S(2)}, u32[]{:S(2)}) collective-permute-start(bf16[2,48,3072]{2,1,0:T(8,128)(2,1)S(1)} %slice.226), channel_id=1, source_target_pairs={{0,8},{8,0},{16,24},{24,16},{32,56},{40,48},{48,40},{56,32},{1,9},... | collective-permute-start | bytes 1769480 | tf_op jit(solution)/shard_map/ppermute | solution.py:43
  87.3 12.9 %collective-permute-start.13 = (bf16[4,96,384]{2,1,0:T(8,128)(2,1)S(1)}, bf16[4,96,384]{2,1,0:T(8,128)(2,1)S(1)}, u32[]{:S(2)}, u32[]{:S(2)}) collective-permute-start(bf16[4,96,384]{2,1,0:T(8,128)(2,1)S(1)} %fusion.1), channel_id=1, source_target_pairs={{0,192},{64,128},{128,64},{192,0},{32,96},{96,32},{160,224},{224,1... | collective-permute-start | bytes 884744 | tf_op jit(solution)/shard_map/ppermute | solution.py:43
  100.3 19.8 %collective-permute-start.19 = (bf16[48,3072]{1,0:T(8,128)(2,1)S(1)}, bf16[48,3072]{1,0:T(8,128)(2,1)S(1)}, u32[]{:S(2)}, u32[]{:S(2)}) collective-permute-start(bf16[48,3072]{1,0:T(8,128)(2,1)S(1)} %fusion.3), channel_id=1, source_target_pairs={{0,24},{8,16},{16,8},{24,0},{32,40},{40,32},{48,56},{56,48},{1,25}... | collective-permute-start | bytes 884744 | tf_op jit(solution)/shard_map/ppermute | solution.py:43
  103.2 41.7 %collective-permute-start.18 = (bf16[2,96,384]{2,1,0:T(8,128)(2,1)S(1)}, bf16[2,96,384]{2,1,0:T(8,128)(2,1)S(1)}, u32[]{:S(2)}, u32[]{:S(2)}) collective-permute-start(bf16[2,96,384]{2,1,0:T(8,128)(2,1)S(1)} %fusion.4), channel_id=1, source_target_pairs={{0,256},{256,0},{512,768},{768,512},{32,800},{288,544},{544,288},{... | collective-permute-start | bytes 442376 | tf_op jit(solution)/shard_map/ppermute | solution.py:43
  118.0 9.8 %collective-permute-start.16 = (bf16[4,96,384]{2,1,0:T(8,128)(2,1)S(1)}, bf16[4,96,384]{2,1,0:T(8,128)(2,1)S(1)}, u32[]{:S(2)}, u32[]{:S(2)}) collective-permute-start(bf16[4,96,384]{2,1,0:T(8,128)(2,1)S(1)} %fusion.2), channel_id=1, source_target_pairs={{0,192},{64,128},{128,64},{192,0},{32,96},{96,32},{160,224},{224,1... | collective-permute-start | bytes 884744 | tf_op jit(solution)/shard_map/ppermute | solution.py:43
  120.2 24.6 %collective-permute-start.20 = (bf16[24,3072]{1,0:T(8,128)(2,1)S(1)}, bf16[24,3072]{1,0:T(8,128)(2,1)S(1)}, u32[]{:S(2)}, u32[]{:S(2)}) collective-permute-start(bf16[24,3072]{1,0:T(8,128)(2,1)S(1)} %slice.309), channel_id=1, source_target_pairs={{0,1},{1,0},{2,3},{3,2},{4,5},{5,4},{6,7},{7,6},{8,9},{9,8},{10,11... | collective-permute-start | bytes 442376 | tf_op jit(solution)/shard_map/ppermute | solution.py:22
  128.8 23.7 %collective-permute-start.17 = (bf16[2,96,384]{2,1,0:T(8,128)(2,1)S(1)}, bf16[2,96,384]{2,1,0:T(8,128)(2,1)S(1)}, u32[]{:S(2)}, u32[]{:S(2)}) collective-permute-start(bf16[2,96,384]{2,1,0:T(8,128)(2,1)S(1)} %fusion.5), channel_id=1, source_target_pairs={{0,256},{256,0},{512,768},{768,512},{32,800},{288,544},{544,288},{... | collective-permute-start | bytes 442376 | tf_op jit(solution)/shard_map/ppermute | solution.py:43
  145.9 42.1 %copy-start.4 = (bf16[6,3072]{1,0:T(8,128)(2,1)S(1)}, bf16[6,3072]{1,0:T(8,128)(2,1)}, u32[]{:S(2)}) copy-start(bf16[6,3072]{1,0:T(8,128)(2,1)} %layer_input.1) | copy-start | bytes 110596
  145.9 42.1 %copy-start.8 = (f32[3072]{0:T(1024)S(1)}, f32[3072]{0:T(1024)}, u32[]{:S(2)}) copy-start(f32[3072]{0:T(1024)} %param.7) | copy-start | bytes 36868
  145.9 38.9 %collective-permute-start.24 = (bf16[96,384]{1,0:T(8,128)(2,1)S(1)}, bf16[96,384]{1,0:T(8,128)(2,1)S(1)}, u32[]{:S(2)}, u32[]{:S(2)}) collective-permute-start(bf16[96,384]{1,0:T(8,128)(2,1)S(1)} %fusion.6), channel_id=1, source_target_pairs={{0,768},{256,512},{512,256},{768,0},{32,288},{288,32},{544,800},{8... | collective-permute-start | bytes 221192 | tf_op jit(solution)/shard_map/ppermute | solution.py:43
  149.6 38.7 %copy-start.6 = (bf16[6,3072]{1,0:T(8,128)(2,1)S(1)}, bf16[6,3072]{1,0:T(8,128)(2,1)}, u32[]{:S(2)}) copy-start(bf16[6,3072]{1,0:T(8,128)(2,1)} %out_grad.1) | copy-start | bytes 110596
  149.6 23.9 %collective-permute-start.21 = (bf16[12,3072]{1,0:T(8,128)(2,1)S(1)}, bf16[12,3072]{1,0:T(8,128)(2,1)S(1)}, u32[]{:S(2)}, u32[]{:S(2)}) collective-permute-start(bf16[12,3072]{1,0:T(8,128)(2,1)S(1)} %slice.310), channel_id=1, source_target_pairs={{0,2},{1,3},{2,0},{3,1},{4,6},{5,7},{6,4},{7,5},{8,10},{9,11},{10,... | collective-permute-start | bytes 221192 | tf_op jit(solution)/shard_map/ppermute | solution.py:22
  153.4 33.0 %collective-permute-start.23 = (bf16[96,384]{1,0:T(8,128)(2,1)S(1)}, bf16[96,384]{1,0:T(8,128)(2,1)S(1)}, u32[]{:S(2)}, u32[]{:S(2)}) collective-permute-start(bf16[96,384]{1,0:T(8,128)(2,1)S(1)} %fusion.9), channel_id=1, source_target_pairs={{0,768},{256,512},{512,256},{768,0},{32,288},{288,32},{544,800},{8... | collective-permute-start | bytes 221192 | tf_op jit(solution)/shard_map/ppermute | solution.py:43
  173.6 14.4 %collective-permute-start.22 = (bf16[6,3072]{1,0:T(8,128)(2,1)S(1)}, bf16[6,3072]{1,0:T(8,128)(2,1)S(1)}, u32[]{:S(2)}, u32[]{:S(2)}) collective-permute-start(bf16[6,3072]{1,0:T(8,128)(2,1)S(1)} %slice.311), channel_id=1, source_target_pairs={{0,4},{1,5},{2,6},{3,7},{4,0},{5,1},{6,2},{7,3},{8,12},{9,13},{10,... | collective-permute-start | bytes 110600 | tf_op jit(solution)/shard_map/ppermute | solution.py:22
  (2 other events, 1.5 us)

commit v11 on v10

--- a/solution.py
+++ b/solution.py
@@ -275,9 +275,9 @@
     own = halved(own, 1)
     down, up = (down[0], down_core, down_y, down_y2), (up[0], up_core, up_y, up_y2)
     down_z, own = fence((down_z, own))
-    down_z2, up_z2 = to_second_z(down, down_z), to_second_z(up, up_z)
     own = halved(own, 2)
     up_z, own = fence((up_z, own))
+    down_z2, up_z2 = to_second_z(down, down_z), to_second_z(up, up_z)
     normed_grad = halved(own, 4)
     down_grad = added(summed(down, 0), down_z[0], down_z2).T
     up_grad = added(summed(up, 0), up_z[0], up_z2)

time: 190 us -> 192 us (1.011)
  the two profiles are of different devices: /device:TPU:56 before, /device:TPU:6 now
where the time goes in v11:
time: 192 us; the launch traced here: 191 us
  starting transfers between devices  113 us (59%)
  waiting for transfers between devices  49.1 us (26%)
  other arithmetic  13 us (7%)
  Pallas kernels  7.65 us (4%)
  local copies, waits for them, and re-layouts  6.04 us (3%)
    ppermute x10, starting transfers between devices, paired(): return lax.ppermute(block, names, moves)  56.9 us
    ppermute x7, waiting for transfers between devices, swap(): return lax.ppermute(block, 'zl', [(i, i ^ distance) for i in range(8)])  35.5 us
    ppermute x7, starting transfers between devices, swap(): return lax.ppermute(block, 'zl', [(i, i ^ distance) for i in range(8)])  26.6 us
    ppermute x6, starting transfers between devices, x_moves(): return lambda block: lax.ppermute(block, ('c', 'x'), moves)  25.2 us
    ppermute x10, waiting for transfers between devices, paired(): return lax.ppermute(block, names, moves)  10.8 us
    pallas_call x3, Pallas kernels, computed(): pl.pallas_call(kernel, out_shape=[jax.ShapeDtypeStruct(*out) for out in o...  7.17 us
    unnamed x22, local copies, waits for them, and re-layouts  5.66 us
    ppermute x2, starting transfers between devices, to_core(): return lax.ppermute(term[1], 'c', [(0, 1), (1, 0)])  4.3 us
  transfers between devices with their start and end apart: 25, of which 14 were waited for; matrix products, arithmetic and copies ran while one was open for 7% of the time, Pallas kernels for 2%

profile of v11, /device:TPU:6, one launch (start us, length us, event | category | flops | bytes accessed | tf_op | source)
XLA Modules:
  0.0 191.0 jit_solution(14445056806939325834)
XLA Ops:
  3.3 9.1 %collective-permute-start = (bf16[24,1536]{1,0:T(8,128)(2,1)S(1)}, bf16[24,1536]{1,0:T(8,128)(2,1)S(1)}, u32[]{:S(2)}, u32[]{:S(2)}) collective-permute-start(bf16[24,1536]{1,0:T(8,128)(2,1)S(1)} %get-tuple-element.26.own), channel_id=1, source_target_pairs={{0,4},{1,5},{2,6},{3,7},{4,0},{5,1},{6,2},{7,3},{8,12},{9,13},{10,... | collective-permute-start | bytes 221192 | tf_op jit(solution)/shard_map/ppermute | solution.py:22
  12.4 7.1 %collective-permute-done.far = bf16[24,1536]{1,0:T(8,128)(2,1)S(1)} collective-permute-done((bf16[24,1536]{1,0:T(8,128)(2,1)S(1)}, bf16[24,1536]{1,0:T(8,128)(2,1)S(1)}, u32[]{:S(2)}, u32[]{:S(2)}) %collective-permute-start) | collective-permute-done | bytes 73760 | tf_op jit(solution)/shard_map/ppermute | solution.py:22
  19.5 2.1 %collective-permute-start.1 = (bf16[24,3072]{1,0:T(8,128)(2,1)S(1)}, bf16[24,3072]{1,0:T(8,128)(2,1)S(1)}, u32[]{:S(2)}, u32[]{:S(2)}) collective-permute-start(bf16[24,3072]{1,0:T(8,128)(2,1)S(1)} %shard_map.77.refs_0_), channel_id=1, source_target_pairs={{0,2},{1,3},{2,0},{3,1},{4,6},{5,7},{6,4},{7,5},{8,10},{9,11},{10,... | collective-permute-start | bytes 442376 | tf_op jit(solution)/shard_map/ppermute | solution.py:22
  21.6 4.7 %collective-permute-start.2 = (bf16[24,3072]{1,0:T(8,128)(2,1)S(1)}, bf16[24,3072]{1,0:T(8,128)(2,1)S(1)}, u32[]{:S(2)}, u32[]{:S(2)}) collective-permute-start(bf16[24,3072]{1,0:T(8,128)(2,1)S(1)} %shard_map.77.refs_0_), channel_id=1, source_target_pairs={{0,1},{1,0},{2,3},{3,2},{4,5},{5,4},{6,7},{7,6},{8,9},{9,8},{10,11... | collective-permute-start | bytes 442376 | tf_op jit(solution)/shard_map/ppermute | solution.py:22
  26.4 3.3 %collective-permute-start.3 = (bf16[24,3072]{1,0:T(8,128)(2,1)S(1)}, bf16[24,3072]{1,0:T(8,128)(2,1)S(1)}, u32[]{:S(2)}, u32[]{:S(2)}) collective-permute-start(bf16[24,3072]{1,0:T(8,128)(2,1)S(1)} %shard_map.77.refs_0_), channel_id=1, source_target_pairs={{0,3},{1,2},{2,1},{3,0},{4,7},{5,6},{6,5},{7,4},{8,11},{9,10},{10,... | collective-permute-start | bytes 442376 | tf_op jit(solution)/shard_map/ppermute | solution.py:22
  31.4 3.8 %collective-permute-done.3.refs_3_ = bf16[24,3072]{1,0:T(8,128)(2,1)S(1)} collective-permute-done((bf16[24,3072]{1,0:T(8,128)(2,1)S(1)}, bf16[24,3072]{1,0:T(8,128)(2,1)S(1)}, u32[]{:S(2)}, u32[]{:S(2)}) %collective-permute-start.3) | collective-permute-done | bytes 147488 | tf_op jit(solution)/shard_map/ppermute | solution.py:22
  35.3 6.7 %collective-permute-start.7 = (bf16[48,3072]{1,0:T(8,128)(2,1)S(1)}, bf16[48,3072]{1,0:T(8,128)(2,1)S(1)}, u32[]{:S(2)}, u32[]{:S(2)}) collective-permute-start(bf16[48,3072]{1,0:T(8,128)(2,1)S(1)} %get-tuple-element.28.refs_0_), channel_id=1, source_target_pairs={{0,8},{8,16},{16,24},{24,0},{32,56},{40,32},{48,40},{56,48},{1,9},... | collective-permute-start | bytes 884744 | tf_op jit(solution)/shard_map/ppermute | solution.py:27
  42.1 1.9 %collective-permute-start.4 = (bf16[48,3072]{1,0:T(8,128)(2,1)S(1)}, bf16[48,3072]{1,0:T(8,128)(2,1)S(1)}, u32[]{:S(2)}, u32[]{:S(2)}) collective-permute-start(bf16[48,3072]{1,0:T(8,128)(2,1)S(1)} %get-tuple-element.27.refs_0_), channel_id=1, source_target_pairs={{0,8},{8,16},{16,24},{24,0},{32,56},{40,32},{48,40},{56,48},{1,9},... | collective-permute-start | bytes 884744 | tf_op jit(solution)/shard_map/ppermute | solution.py:27
  44.0 3.9 %collective-permute-start.8 = (bf16[48,3072]{1,0:T(8,128)(2,1)S(1)}, bf16[48,3072]{1,0:T(8,128)(2,1)S(1)}, u32[]{:S(2)}, u32[]{:S(2)}) collective-permute-start(bf16[48,3072]{1,0:T(8,128)(2,1)S(1)} %get-tuple-element.28.refs_0_), channel_id=1, source_target_pairs={{0,24},{8,0},{16,8},{24,16},{32,40},{40,48},{48,56},{56,32},{1,25}... | collective-permute-start | bytes 884744 | tf_op jit(solution)/shard_map/ppermute | solution.py:27
  49.2 5.6 %collective-permute-start.9 = (bf16[48,3072]{1,0:T(8,128)(2,1)S(1)}, bf16[48,3072]{1,0:T(8,128)(2,1)S(1)}, u32[]{:S(2)}, u32[]{:S(2)}) collective-permute-start(bf16[48,3072]{1,0:T(8,128)(2,1)S(1)} %collective-permute-done.7.refs_1_), channel_id=1, source_target_pairs={{0,8},{8,16},{16,24},{24,0},{32,56},{40,32},{48,40},{56,48},{1,9},... | collective-permute-start | bytes 884744 | tf_op jit(solution)/shard_map/ppermute | solution.py:27
  54.8 1.9 %collective-permute-start.5 = (bf16[48,3072]{1,0:T(8,128)(2,1)S(1)}, bf16[48,3072]{1,0:T(8,128)(2,1)S(1)}, u32[]{:S(2)}, u32[]{:S(2)}) collective-permute-start(bf16[48,3072]{1,0:T(8,128)(2,1)S(1)} %get-tuple-element.27.refs_0_), channel_id=1, source_target_pairs={{0,24},{8,0},{16,8},{24,16},{32,40},{40,48},{48,56},{56,32},{1,25}... | collective-permute-start | bytes 884744 | tf_op jit(solution)/shard_map/ppermute | solution.py:27
  56.7 5.1 %collective-permute-start.6 = (bf16[48,3072]{1,0:T(8,128)(2,1)S(1)}, bf16[48,3072]{1,0:T(8,128)(2,1)S(1)}, u32[]{:S(2)}, u32[]{:S(2)}) collective-permute-start(bf16[48,3072]{1,0:T(8,128)(2,1)S(1)} %collective-permute-done.4.refs_1_), channel_id=1, source_target_pairs={{0,8},{8,16},{16,24},{24,0},{32,56},{40,32},{48,40},{56,48},{1,9},... | collective-permute-start | bytes 884744 | tf_op jit(solution)/shard_map/ppermute | solution.py:27
  67.8 2.7 %shard_map.80 = (bf16[192,3072]{1,0:T(8,128)(2,1)S(1)}, bf16[4,4,96,384]{3,2,1,0:T(8,128)(2,1)S(1)}, bf16[4,4,96,384]{3,2,1,0:T(8,128)(2,1)}) custom-call(s32[17]{0:T(128)S(1)} %concatenate.3.where, bf16[48,3072]{1,0:T(8,128)(2,1)S(1)} %get-tuple-element.27.refs_0_, bf16[48,3072]{1,0:T(8,128)(2,1)S(1)} %collective-permute-done.4.refs_1_, ...), custom_call_target="tpu_custom_call" | custom-call | flops 452984832 | bytes 8388608 | tf_op jit(solution)/shard_map/pallas_call | solution.py:184
  72.4 3.7 %shard_map.81 = (bf16[192,384]{1,0:T(8,128)(2,1)S(1)}, bf16[4,4,96,384]{3,2,1,0:T(8,128)(2,1)S(1)}, bf16[4,4,96,384]{3,2,1,0:T(8,128)(2,1)}) custom-call(s32[17]{0:T(128)S(1)} %concatenate.3.where, bf16[192,3072]{1,0:T(8,128)(2,1)S(1)} %get-tuple-element.30.grad, bf16[192,3072]{1,0:T(8,128)(2,1)S(1)} %get-tuple-element.31.normed, ...), custom_call_target="tpu_custom_call" | custom-call | flops 905969664 | bytes 8388608 | tf_op jit(solution)/shard_map/pallas_call | solution.py:184
  76.0 2.4 %collective-permute-start.10 = (bf16[4,4,96,384]{3,2,1,0:T(8,128)(2,1)}, bf16[4,4,96,384]{3,2,1,0:T(8,128)(2,1)}, u32[]{:S(2)}, u32[]{:S(2)}) collective-permute-start(bf16[4,4,96,384]{3,2,1,0:T(8,128)(2,1)} %get-tuple-element.34), channel_id=1, source_target_pairs={{0,32},{32,0},{1,33},{33,1},{2,34},{34,2},{3,35},{35,3},{4,36},{36... | collective-permute-start | bytes 3538952 | tf_op jit(solution)/shard_map/ppermute | solution.py:238
  79.9 1.9 %collective-permute-start.12 = (bf16[2,4,96,384]{3,2,1,0:T(8,128)(2,1)S(1)}, bf16[2,4,96,384]{3,2,1,0:T(8,128)(2,1)S(1)}, u32[]{:S(2)}, u32[]{:S(2)}) collective-permute-start(bf16[2,4,96,384]{3,2,1,0:T(8,128)(2,1)S(1)} %add_convert_fusion.1), channel_id=1, source_target_pairs={{0,64},{64,0},{128,192},{192,128},{32,224},{96,160},{160,96},{224,... | collective-permute-start | bytes 1769480 | tf_op jit(solution)/shard_map/ppermute | solution.py:43
  83.1 3.9 %collective-permute-start.15 = (bf16[2,4,96,384]{3,2,1,0:T(8,128)(2,1)S(1)}, bf16[2,4,96,384]{3,2,1,0:T(8,128)(2,1)S(1)}, u32[]{:S(2)}, u32[]{:S(2)}) collective-permute-start(bf16[2,4,96,384]{3,2,1,0:T(8,128)(2,1)S(1)} %add_convert_fusion), channel_id=1, source_target_pairs={{0,64},{64,0},{128,192},{192,128},{32,224},{96,160},{160,96},{224,... | collective-permute-start | bytes 1769480 | tf_op jit(solution)/shard_map/ppermute | solution.py:43
  88.0 1.9 %collective-permute-start.14 = (bf16[2,48,3072]{2,1,0:T(8,128)(2,1)S(1)}, bf16[2,48,3072]{2,1,0:T(8,128)(2,1)S(1)}, u32[]{:S(2)}, u32[]{:S(2)}) collective-permute-start(bf16[2,48,3072]{2,1,0:T(8,128)(2,1)S(1)} %slice.226), channel_id=1, source_target_pairs={{0,8},{8,0},{16,24},{24,16},{32,56},{40,48},{48,40},{56,32},{1,9},... | collective-permute-start | bytes 1769480 | tf_op jit(solution)/shard_map/ppermute | solution.py:43
  92.8 1.9 %collective-permute-start.13 = (bf16[4,96,384]{2,1,0:T(8,128)(2,1)S(1)}, bf16[4,96,384]{2,1,0:T(8,128)(2,1)S(1)}, u32[]{:S(2)}, u32[]{:S(2)}) collective-permute-start(bf16[4,96,384]{2,1,0:T(8,128)(2,1)S(1)} %fusion.1), channel_id=1, source_target_pairs={{0,192},{64,128},{128,64},{192,0},{32,96},{96,32},{160,224},{224,1... | collective-permute-start | bytes 884744 | tf_op jit(solution)/shard_map/ppermute | solution.py:43
  94.9 3.1 %collective-permute-done.15 = bf16[2,4,96,384]{3,2,1,0:T(8,128)(2,1)S(1)} collective-permute-done((bf16[2,4,96,384]{3,2,1,0:T(8,128)(2,1)S(1)}, bf16[2,4,96,384]{3,2,1,0:T(8,128)(2,1)S(1)}, u32[]{:S(2)}, u32[]{:S(2)}) %collective-permute-start.15) | collective-permute-done | bytes 589856 | tf_op jit(solution)/shard_map/ppermute | solution.py:43
  99.8 2.8 %collective-permute-done.13 = bf16[4,96,384]{2,1,0:T(8,128)(2,1)S(1)} collective-permute-done((bf16[4,96,384]{2,1,0:T(8,128)(2,1)S(1)}, bf16[4,96,384]{2,1,0:T(8,128)(2,1)S(1)}, u32[]{:S(2)}, u32[]{:S(2)}) %collective-permute-start.13) | collective-permute-done | bytes 294944 | tf_op jit(solution)/shard_map/ppermute | solution.py:43
  102.7 5.6 %collective-permute-start.19 = (bf16[48,3072]{1,0:T(8,128)(2,1)S(1)}, bf16[48,3072]{1,0:T(8,128)(2,1)S(1)}, u32[]{:S(2)}, u32[]{:S(2)}) collective-permute-start(bf16[48,3072]{1,0:T(8,128)(2,1)S(1)} %fusion.3), channel_id=1, source_target_pairs={{0,24},{8,16},{16,8},{24,0},{32,40},{40,32},{48,56},{56,48},{1,25}... | collective-permute-start | bytes 884744 | tf_op jit(solution)/shard_map/ppermute | solution.py:43
  109.3 9.1 %collective-permute-start.18 = (bf16[2,96,384]{2,1,0:T(8,128)(2,1)S(1)}, bf16[2,96,384]{2,1,0:T(8,128)(2,1)S(1)}, u32[]{:S(2)}, u32[]{:S(2)}) collective-permute-start(bf16[2,96,384]{2,1,0:T(8,128)(2,1)S(1)} %fusion.4), channel_id=1, source_target_pairs={{0,256},{256,0},{512,768},{768,512},{32,800},{288,544},{544,288},{... | collective-permute-start | bytes 442376 | tf_op jit(solution)/shard_map/ppermute | solution.py:43
  119.5 4.9 %collective-permute-start.16 = (bf16[4,96,384]{2,1,0:T(8,128)(2,1)S(1)}, bf16[4,96,384]{2,1,0:T(8,128)(2,1)S(1)}, u32[]{:S(2)}, u32[]{:S(2)}) collective-permute-start(bf16[4,96,384]{2,1,0:T(8,128)(2,1)S(1)} %fusion.2), channel_id=1, source_target_pairs={{0,192},{64,128},{128,64},{192,0},{32,96},{96,32},{160,224},{224,1... | collective-permute-start | bytes 884744 | tf_op jit(solution)/shard_map/ppermute | solution.py:43
  124.5 3.4 %collective-permute-start.20 = (bf16[24,3072]{1,0:T(8,128)(2,1)S(1)}, bf16[24,3072]{1,0:T(8,128)(2,1)S(1)}, u32[]{:S(2)}, u32[]{:S(2)}) collective-permute-start(bf16[24,3072]{1,0:T(8,128)(2,1)S(1)} %slice.306), channel_id=1, source_target_pairs={{0,1},{1,0},{2,3},{3,2},{4,5},{5,4},{6,7},{7,6},{8,9},{9,8},{10,11... | collective-permute-start | bytes 442376 | tf_op jit(solution)/shard_map/ppermute | solution.py:22
  130.3 5.4 %collective-permute-start.17 = (bf16[2,96,384]{2,1,0:T(8,128)(2,1)S(1)}, bf16[2,96,384]{2,1,0:T(8,128)(2,1)S(1)}, u32[]{:S(2)}, u32[]{:S(2)}) collective-permute-start(bf16[2,96,384]{2,1,0:T(8,128)(2,1)S(1)} %fusion.5), channel_id=1, source_target_pairs={{0,256},{256,0},{512,768},{768,512},{32,800},{288,544},{544,288},{... | collective-permute-start | bytes 442376 | tf_op jit(solution)/shard_map/ppermute | solution.py:43
  135.7 13.1 %collective-permute-done.20 = bf16[24,3072]{1,0:T(8,128)(2,1)S(1)} collective-permute-done((bf16[24,3072]{1,0:T(8,128)(2,1)S(1)}, bf16[24,3072]{1,0:T(8,128)(2,1)S(1)}, u32[]{:S(2)}, u32[]{:S(2)}) %collective-permute-start.20) | collective-permute-done | bytes 147488 | tf_op jit(solution)/shard_map/ppermute | solution.py:22
  148.9 2.1 %collective-permute-start.21 = (bf16[12,3072]{1,0:T(8,128)(2,1)S(1)}, bf16[12,3072]{1,0:T(8,128)(2,1)S(1)}, u32[]{:S(2)}, u32[]{:S(2)}) collective-permute-start(bf16[12,3072]{1,0:T(8,128)(2,1)S(1)} %slice.307), channel_id=1, source_target_pairs={{0,2},{1,3},{2,0},{3,1},{4,6},{5,7},{6,4},{7,5},{8,10},{9,11},{10,... | collective-permute-start | bytes 221192 | tf_op jit(solution)/shard_map/ppermute | solution.py:22
  151.9 2.9 %collective-permute-start.24 = (bf16[96,384]{1,0:T(8,128)(2,1)S(1)}, bf16[96,384]{1,0:T(8,128)(2,1)S(1)}, u32[]{:S(2)}, u32[]{:S(2)}) collective-permute-start(bf16[96,384]{1,0:T(8,128)(2,1)S(1)} %fusion.6), channel_id=1, source_target_pairs={{0,768},{256,512},{512,256},{768,0},{32,288},{288,32},{544,800},{8... | collective-permute-start | bytes 221192 | tf_op jit(solution)/shard_map/ppermute | solution.py:43
  154.9 3.5 %collective-permute-done.21 = bf16[12,3072]{1,0:T(8,128)(2,1)S(1)} collective-permute-done((bf16[12,3072]{1,0:T(8,128)(2,1)S(1)}, bf16[12,3072]{1,0:T(8,128)(2,1)S(1)}, u32[]{:S(2)}, u32[]{:S(2)}) %collective-permute-start.21) | collective-permute-done | bytes 73760 | tf_op jit(solution)/shard_map/ppermute | solution.py:22
  159.3 19.2 %collective-permute-start.23 = (bf16[96,384]{1,0:T(8,128)(2,1)S(1)}, bf16[96,384]{1,0:T(8,128)(2,1)S(1)}, u32[]{:S(2)}, u32[]{:S(2)}) collective-permute-start(bf16[96,384]{1,0:T(8,128)(2,1)S(1)} %fusion.9), channel_id=1, source_target_pairs={{0,768},{256,512},{512,256},{768,0},{32,288},{288,32},{544,800},{8... | collective-permute-start | bytes 221192 | tf_op jit(solution)/shard_map/ppermute | solution.py:43
  182.1 6.3 %collective-permute-done.22 = bf16[6,3072]{1,0:T(8,128)(2,1)S(1)} collective-permute-done((bf16[6,3072]{1,0:T(8,128)(2,1)S(1)}, bf16[6,3072]{1,0:T(8,128)(2,1)S(1)}, u32[]{:S(2)}, u32[]{:S(2)}) %collective-permute-start.22) | collective-permute-done | bytes 36896 | tf_op jit(solution)/shard_map/ppermute | solution.py:22
  (76 shorter events, 34.7 us)
Async XLA Ops:
  3.3 16.2 %collective-permute-start = (bf16[24,1536]{1,0:T(8,128)(2,1)S(1)}, bf16[24,1536]{1,0:T(8,128)(2,1)S(1)}, u32[]{:S(2)}, u32[]{:S(2)}) collective-permute-start(bf16[24,1536]{1,0:T(8,128)(2,1)S(1)} %get-tuple-element.26.own), channel_id=1, source_target_pairs={{0,4},{1,5},{2,6},{3,7},{4,0},{5,1},{6,2},{7,3},{8,12},{9,13},{10,... | collective-permute-start | bytes 221192 | tf_op jit(solution)/shard_map/ppermute | solution.py:22
  19.5 10.1 %collective-permute-start.1 = (bf16[24,3072]{1,0:T(8,128)(2,1)S(1)}, bf16[24,3072]{1,0:T(8,128)(2,1)S(1)}, u32[]{:S(2)}, u32[]{:S(2)}) collective-permute-start(bf16[24,3072]{1,0:T(8,128)(2,1)S(1)} %shard_map.77.refs_0_), channel_id=1, source_target_pairs={{0,2},{1,3},{2,0},{3,1},{4,6},{5,7},{6,4},{7,5},{8,10},{9,11},{10,... | collective-permute-start | bytes 442376 | tf_op jit(solution)/shard_map/ppermute | solution.py:22
  21.6 9.8 %collective-permute-start.2 = (bf16[24,3072]{1,0:T(8,128)(2,1)S(1)}, bf16[24,3072]{1,0:T(8,128)(2,1)S(1)}, u32[]{:S(2)}, u32[]{:S(2)}) collective-permute-start(bf16[24,3072]{1,0:T(8,128)(2,1)S(1)} %shard_map.77.refs_0_), channel_id=1, source_target_pairs={{0,1},{1,0},{2,3},{3,2},{4,5},{5,4},{6,7},{7,6},{8,9},{9,8},{10,11... | collective-permute-start | bytes 442376 | tf_op jit(solution)/shard_map/ppermute | solution.py:22
  26.4 8.9 %collective-permute-start.3 = (bf16[24,3072]{1,0:T(8,128)(2,1)S(1)}, bf16[24,3072]{1,0:T(8,128)(2,1)S(1)}, u32[]{:S(2)}, u32[]{:S(2)}) collective-permute-start(bf16[24,3072]{1,0:T(8,128)(2,1)S(1)} %shard_map.77.refs_0_), channel_id=1, source_target_pairs={{0,3},{1,2},{2,1},{3,0},{4,7},{5,6},{6,5},{7,4},{8,11},{9,10},{10,... | collective-permute-start | bytes 442376 | tf_op jit(solution)/shard_map/ppermute | solution.py:22
  35.3 13.9 %collective-permute-start.7 = (bf16[48,3072]{1,0:T(8,128)(2,1)S(1)}, bf16[48,3072]{1,0:T(8,128)(2,1)S(1)}, u32[]{:S(2)}, u32[]{:S(2)}) collective-permute-start(bf16[48,3072]{1,0:T(8,128)(2,1)S(1)} %get-tuple-element.28.refs_0_), channel_id=1, source_target_pairs={{0,8},{8,16},{16,24},{24,0},{32,56},{40,32},{48,40},{56,48},{1,9},... | collective-permute-start | bytes 884744 | tf_op jit(solution)/shard_map/ppermute | solution.py:27
  42.1 14.7 %collective-permute-start.4 = (bf16[48,3072]{1,0:T(8,128)(2,1)S(1)}, bf16[48,3072]{1,0:T(8,128)(2,1)S(1)}, u32[]{:S(2)}, u32[]{:S(2)}) collective-permute-start(bf16[48,3072]{1,0:T(8,128)(2,1)S(1)} %get-tuple-element.27.refs_0_), channel_id=1, source_target_pairs={{0,8},{8,16},{16,24},{24,0},{32,56},{40,32},{48,40},{56,48},{1,9},... | collective-permute-start | bytes 884744 | tf_op jit(solution)/shard_map/ppermute | solution.py:27
  44.0 18.0 %collective-permute-start.8 = (bf16[48,3072]{1,0:T(8,128)(2,1)S(1)}, bf16[48,3072]{1,0:T(8,128)(2,1)S(1)}, u32[]{:S(2)}, u32[]{:S(2)}) collective-permute-start(bf16[48,3072]{1,0:T(8,128)(2,1)S(1)} %get-tuple-element.28.refs_0_), channel_id=1, source_target_pairs={{0,24},{8,0},{16,8},{24,16},{32,40},{40,48},{48,56},{56,32},{1,25}... | collective-permute-start | bytes 884744 | tf_op jit(solution)/shard_map/ppermute | solution.py:27
  49.2 12.8 %collective-permute-start.9 = (bf16[48,3072]{1,0:T(8,128)(2,1)S(1)}, bf16[48,3072]{1,0:T(8,128)(2,1)S(1)}, u32[]{:S(2)}, u32[]{:S(2)}) collective-permute-start(bf16[48,3072]{1,0:T(8,128)(2,1)S(1)} %collective-permute-done.7.refs_1_), channel_id=1, source_target_pairs={{0,8},{8,16},{16,24},{24,0},{32,56},{40,32},{48,40},{56,48},{1,9},... | collective-permute-start | bytes 884744 | tf_op jit(solution)/shard_map/ppermute | solution.py:27
  54.8 9.8 %collective-permute-start.5 = (bf16[48,3072]{1,0:T(8,128)(2,1)S(1)}, bf16[48,3072]{1,0:T(8,128)(2,1)S(1)}, u32[]{:S(2)}, u32[]{:S(2)}) collective-permute-start(bf16[48,3072]{1,0:T(8,128)(2,1)S(1)} %get-tuple-element.27.refs_0_), channel_id=1, source_target_pairs={{0,24},{8,0},{16,8},{24,16},{32,40},{40,48},{48,56},{56,32},{1,25}... | collective-permute-start | bytes 884744 | tf_op jit(solution)/shard_map/ppermute | solution.py:27
  56.7 9.4 %collective-permute-start.6 = (bf16[48,3072]{1,0:T(8,128)(2,1)S(1)}, bf16[48,3072]{1,0:T(8,128)(2,1)S(1)}, u32[]{:S(2)}, u32[]{:S(2)}) collective-permute-start(bf16[48,3072]{1,0:T(8,128)(2,1)S(1)} %collective-permute-done.4.refs_1_), channel_id=1, source_target_pairs={{0,8},{8,16},{16,24},{24,0},{32,56},{40,32},{48,40},{56,48},{1,9},... | collective-permute-start | bytes 884744 | tf_op jit(solution)/shard_map/ppermute | solution.py:27
  62.0 1.7 copy-start
  63.7 8.7 %copy-start.2 = (bf16[384,3072]{1,0:T(8,128)(2,1)S(1)}, bf16[384,3072]{1,0:T(8,128)(2,1)}, u32[]{:S(2)}) copy-start(bf16[384,3072]{1,0:T(8,128)(2,1)} %weight.1) | copy-start | bytes 7077892
  66.8 1.0 copy-start.10
  70.5 8.1 %collective-permute-start.11 = (bf16[4,4,96,384]{3,2,1,0:T(8,128)(2,1)}, bf16[4,4,96,384]{3,2,1,0:T(8,128)(2,1)}, u32[]{:S(2)}, u32[]{:S(2)}) collective-permute-start(bf16[4,4,96,384]{3,2,1,0:T(8,128)(2,1)} %get-tuple-element.38), channel_id=1, source_target_pairs={{0,32},{32,0},{1,33},{33,1},{2,34},{34,2},{3,35},{35,3},{4,36},{36... | collective-permute-start | bytes 3538952 | tf_op jit(solution)/shard_map/ppermute | solution.py:238
  76.0 5.8 %collective-permute-start.10 = (bf16[4,4,96,384]{3,2,1,0:T(8,128)(2,1)}, bf16[4,4,96,384]{3,2,1,0:T(8,128)(2,1)}, u32[]{:S(2)}, u32[]{:S(2)}) collective-permute-start(bf16[4,4,96,384]{3,2,1,0:T(8,128)(2,1)} %get-tuple-element.34), channel_id=1, source_target_pairs={{0,32},{32,0},{1,33},{33,1},{2,34},{34,2},{3,35},{35,3},{4,36},{36... | collective-permute-start | bytes 3538952 | tf_op jit(solution)/shard_map/ppermute | solution.py:238
  78.5 8.5 %copy-start.1 = (bf16[3072,384]{1,0:T(8,128)(2,1)S(1)}, bf16[3072,384]{1,0:T(8,128)(2,1)}, u32[]{:S(2)}) copy-start(bf16[3072,384]{1,0:T(8,128)(2,1)} %refs_4_.1) | copy-start | bytes 7077892
  79.9 11.8 %collective-permute-start.12 = (bf16[2,4,96,384]{3,2,1,0:T(8,128)(2,1)S(1)}, bf16[2,4,96,384]{3,2,1,0:T(8,128)(2,1)S(1)}, u32[]{:S(2)}, u32[]{:S(2)}) collective-permute-start(bf16[2,4,96,384]{3,2,1,0:T(8,128)(2,1)S(1)} %add_convert_fusion.1), channel_id=1, source_target_pairs={{0,64},{64,0},{128,192},{192,128},{32,224},{96,160},{160,96},{224,... | collective-permute-start | bytes 1769480 | tf_op jit(solution)/shard_map/ppermute | solution.py:43
  83.1 14.9 %collective-permute-start.15 = (bf16[2,4,96,384]{3,2,1,0:T(8,128)(2,1)S(1)}, bf16[2,4,96,384]{3,2,1,0:T(8,128)(2,1)S(1)}, u32[]{:S(2)}, u32[]{:S(2)}) collective-permute-start(bf16[2,4,96,384]{3,2,1,0:T(8,128)(2,1)S(1)} %add_convert_fusion), channel_id=1, source_target_pairs={{0,64},{64,0},{128,192},{192,128},{32,224},{96,160},{160,96},{224,... | collective-permute-start | bytes 1769480 | tf_op jit(solution)/shard_map/ppermute | solution.py:43
  88.0 11.8 %collective-permute-start.14 = (bf16[2,48,3072]{2,1,0:T(8,128)(2,1)S(1)}, bf16[2,48,3072]{2,1,0:T(8,128)(2,1)S(1)}, u32[]{:S(2)}, u32[]{:S(2)}) collective-permute-start(bf16[2,48,3072]{2,1,0:T(8,128)(2,1)S(1)} %slice.226), channel_id=1, source_target_pairs={{0,8},{8,0},{16,24},{24,16},{32,56},{40,48},{48,40},{56,32},{1,9},... | collective-permute-start | bytes 1769480 | tf_op jit(solution)/shard_map/ppermute | solution.py:43
  92.8 9.8 %collective-permute-start.13 = (bf16[4,96,384]{2,1,0:T(8,128)(2,1)S(1)}, bf16[4,96,384]{2,1,0:T(8,128)(2,1)S(1)}, u32[]{:S(2)}, u32[]{:S(2)}) collective-permute-start(bf16[4,96,384]{2,1,0:T(8,128)(2,1)S(1)} %fusion.1), channel_id=1, source_target_pairs={{0,192},{64,128},{128,64},{192,0},{32,96},{96,32},{160,224},{224,1... | collective-permute-start | bytes 884744 | tf_op jit(solution)/shard_map/ppermute | solution.py:43
  102.7 21.7 %collective-permute-start.19 = (bf16[48,3072]{1,0:T(8,128)(2,1)S(1)}, bf16[48,3072]{1,0:T(8,128)(2,1)S(1)}, u32[]{:S(2)}, u32[]{:S(2)}) collective-permute-start(bf16[48,3072]{1,0:T(8,128)(2,1)S(1)} %fusion.3), channel_id=1, source_target_pairs={{0,24},{8,16},{16,8},{24,0},{32,40},{40,32},{48,56},{56,48},{1,25}... | collective-permute-start | bytes 884744 | tf_op jit(solution)/shard_map/ppermute | solution.py:43
  109.3 39.6 %collective-permute-start.18 = (bf16[2,96,384]{2,1,0:T(8,128)(2,1)S(1)}, bf16[2,96,384]{2,1,0:T(8,128)(2,1)S(1)}, u32[]{:S(2)}, u32[]{:S(2)}) collective-permute-start(bf16[2,96,384]{2,1,0:T(8,128)(2,1)S(1)} %fusion.4), channel_id=1, source_target_pairs={{0,256},{256,0},{512,768},{768,512},{32,800},{288,544},{544,288},{... | collective-permute-start | bytes 442376 | tf_op jit(solution)/shard_map/ppermute | solution.py:43
  119.5 9.8 %collective-permute-start.16 = (bf16[4,96,384]{2,1,0:T(8,128)(2,1)S(1)}, bf16[4,96,384]{2,1,0:T(8,128)(2,1)S(1)}, u32[]{:S(2)}, u32[]{:S(2)}) collective-permute-start(bf16[4,96,384]{2,1,0:T(8,128)(2,1)S(1)} %fusion.2), channel_id=1, source_target_pairs={{0,192},{64,128},{128,64},{192,0},{32,96},{96,32},{160,224},{224,1... | collective-permute-start | bytes 884744 | tf_op jit(solution)/shard_map/ppermute | solution.py:43
  124.5 24.3 %collective-permute-start.20 = (bf16[24,3072]{1,0:T(8,128)(2,1)S(1)}, bf16[24,3072]{1,0:T(8,128)(2,1)S(1)}, u32[]{:S(2)}, u32[]{:S(2)}) collective-permute-start(bf16[24,3072]{1,0:T(8,128)(2,1)S(1)} %slice.306), channel_id=1, source_target_pairs={{0,1},{1,0},{2,3},{3,2},{4,5},{5,4},{6,7},{7,6},{8,9},{9,8},{10,11... | collective-permute-start | bytes 442376 | tf_op jit(solution)/shard_map/ppermute | solution.py:22
  130.3 28.1 %collective-permute-start.17 = (bf16[2,96,384]{2,1,0:T(8,128)(2,1)S(1)}, bf16[2,96,384]{2,1,0:T(8,128)(2,1)S(1)}, u32[]{:S(2)}, u32[]{:S(2)}) collective-permute-start(bf16[2,96,384]{2,1,0:T(8,128)(2,1)S(1)} %fusion.5), channel_id=1, source_target_pairs={{0,256},{256,0},{512,768},{768,512},{32,800},{288,544},{544,288},{... | collective-permute-start | bytes 442376 | tf_op jit(solution)/shard_map/ppermute | solution.py:43
  148.9 39.6 %copy-start.4 = (bf16[6,3072]{1,0:T(8,128)(2,1)S(1)}, bf16[6,3072]{1,0:T(8,128)(2,1)}, u32[]{:S(2)}) copy-start(bf16[6,3072]{1,0:T(8,128)(2,1)} %layer_input.1) | copy-start | bytes 110596
  148.9 39.6 %copy-start.8 = (f32[3072]{0:T(1024)S(1)}, f32[3072]{0:T(1024)}, u32[]{:S(2)}) copy-start(f32[3072]{0:T(1024)} %param.7) | copy-start | bytes 36868
  148.9 39.8 %copy-start.6 = (bf16[6,3072]{1,0:T(8,128)(2,1)S(1)}, bf16[6,3072]{1,0:T(8,128)(2,1)}, u32[]{:S(2)}) copy-start(bf16[6,3072]{1,0:T(8,128)(2,1)} %out_grad.1) | copy-start | bytes 110596
  148.9 9.4 %collective-permute-start.21 = (bf16[12,3072]{1,0:T(8,128)(2,1)S(1)}, bf16[12,3072]{1,0:T(8,128)(2,1)S(1)}, u32[]{:S(2)}, u32[]{:S(2)}) collective-permute-start(bf16[12,3072]{1,0:T(8,128)(2,1)S(1)} %slice.307), channel_id=1, source_target_pairs={{0,2},{1,3},{2,0},{3,1},{4,6},{5,7},{6,4},{7,5},{8,10},{9,11},{10,... | collective-permute-start | bytes 221192 | tf_op jit(solution)/shard_map/ppermute | solution.py:22
  151.9 28.5 %collective-permute-start.24 = (bf16[96,384]{1,0:T(8,128)(2,1)S(1)}, bf16[96,384]{1,0:T(8,128)(2,1)S(1)}, u32[]{:S(2)}, u32[]{:S(2)}) collective-permute-start(bf16[96,384]{1,0:T(8,128)(2,1)S(1)} %fusion.6), channel_id=1, source_target_pairs={{0,768},{256,512},{512,256},{768,0},{32,288},{288,32},{544,800},{8... | collective-permute-start | bytes 221192 | tf_op jit(solution)/shard_map/ppermute | solution.py:43
  159.3 30.1 %collective-permute-start.23 = (bf16[96,384]{1,0:T(8,128)(2,1)S(1)}, bf16[96,384]{1,0:T(8,128)(2,1)S(1)}, u32[]{:S(2)}, u32[]{:S(2)}) collective-permute-start(bf16[96,384]{1,0:T(8,128)(2,1)S(1)} %fusion.9), channel_id=1, source_target_pairs={{0,768},{256,512},{512,256},{768,0},{32,288},{288,32},{544,800},{8... | collective-permute-start | bytes 221192 | tf_op jit(solution)/shard_map/ppermute | solution.py:43
  178.6 9.9 %collective-permute-start.22 = (bf16[6,3072]{1,0:T(8,128)(2,1)S(1)}, bf16[6,3072]{1,0:T(8,128)(2,1)S(1)}, u32[]{:S(2)}, u32[]{:S(2)}) collective-permute-start(bf16[6,3072]{1,0:T(8,128)(2,1)S(1)} %slice.308), channel_id=1, source_target_pairs={{0,4},{1,5},{2,6},{3,7},{4,0},{5,1},{6,2},{7,3},{8,12},{9,13},{10,... | collective-permute-start | bytes 110600 | tf_op jit(solution)/shard_map/ppermute | solution.py:22
  (4 other events, 3.0 us)
